TPU v7x, 32 devices: a whole 2x2x4 slice. The times are simulated.
32 devices in a mesh: rep: 2 (over x), shard: 16 (over z, y, core).
Axes of the slice: x: 2, y: 2, z: 4, core: 2. Of those that a mesh axis runs over, the one named last changes fastest.
Arguments:
- hidden_in: bfloat16 [4096, 2048], P(('rep', 'shard')), may hold values from -6 to 6
- segments: int32 [32, 128], P(('rep', 'shard')), may hold values from 0 to 7, never falling along the last dimension, each value on 1 to 64 neighbouring positions
- w_query: bfloat16 [2048, 2048], P('shard'), may hold values from -0.125 to 0.125
- w_key: bfloat16 [2048, 2048], P('shard'), may hold values from -0.125 to 0.125
- w_value: bfloat16 [2048, 2048], P('shard'), may hold values from -0.125 to 0.125
- w_output: bfloat16 [2048, 2048], P('shard'), may hold values from -0.125 to 0.125
- query_gain: bfloat16 [2048], P('shard'), may hold values from 0.099609375 to 1.8984375
- key_gain: bfloat16 [2048], P('shard'), may hold values from 0.099609375 to 1.8984375
- attn_gain: bfloat16 [2048], P('shard'), may hold values from 0.099609375 to 1.8984375
- w_gate: bfloat16 [2048, 8192], P('shard'), may hold values from -0.125 to 0.125
- w_up: bfloat16 [2048, 8192], P('shard'), may hold values from -0.125 to 0.125
- w_down: bfloat16 [8192, 2048], P('shard'), may hold values from -0.0625 to 0.0625
- ffn_gain: bfloat16 [2048], P('shard'), may hold values from 0.099609375 to 1.8984375
- out_cotangent: bfloat16 [4096, 2048], P(('rep', 'shard')), may hold values from -6 to 6
Outputs:
- hidden_out: bfloat16 [4096, 2048], P(('rep', 'shard'))
- hidden_grad: bfloat16 [4096, 2048], P(('rep', 'shard'))
- grad_query: float32 [2048, 2048], P('shard')
- grad_key: float32 [2048, 2048], P('shard')
- grad_value: float32 [2048, 2048], P('shard')
- grad_output: float32 [2048, 2048], P('shard')
- grad_query_gain: float32 [2048], P('shard')
- grad_key_gain: float32 [2048], P('shard')
- grad_attn_gain: float32 [2048], P('shard')
- grad_gate: float32 [2048, 8192], P('shard')
- grad_up: float32 [2048, 8192], P('shard')
- grad_down: float32 [8192, 2048], P('shard')
- grad_ffn_gain: float32 [2048], P('shard')
Inputs may be any that keep to these rules, and one draw needn't show every extreme that they name: `segments`: in each sequence the document numbers never fall; each document has 1 to 64 tokens, and one document of each sequence has exactly that many.
All inputs are finite; a program needn't handle non-finite values.
Results may differ from a plain program's by a relative error of at most 0.018.
Values may be sent and summed in bfloat16 or wider, within the bound.
A program may use at most 512 MiB of HBM per device.

v0:
```python
import math

import jax
import jax.numpy as jnp
from jax import lax
from jax.sharding import PartitionSpec as P

HEADS = 16
HEAD_DIM = 128


epsilon = 1e-06
theta_base = 500000.0
neg_fill = -1e30


def rms_scale(values):
    return lax.rsqrt(jnp.mean(values * values, axis=-1, keepdims=True) + epsilon)


def rms_back(upstream, normed, row_scale):
    return row_scale * (upstream - normed * jnp.mean(upstream * normed, axis=-1, keepdims=True))


def rotate(values, cosines, sines):
    half_dim = values.shape[-1] // 2
    first_half = values[..., :half_dim]
    second = values[..., half_dim:]
    return jnp.concatenate(
        [first_half * cosines - second * sines, second * cosines + first_half * sines], axis=-1
    )


def dot_back(left_side, right_side):
    return lax.dot_general(
        left_side, right_side, (((1,), (1,)), ((), ())), preferred_element_type=jnp.float32
    )


def col_term(left_side, right_side):

    def block_term(row_start, row_count):
        return lax.dot_general(
            left_side, right_side, (((0,), (0,)), ((), ())), preferred_element_type=jnp.float32
        )

    return block_term


def on_device(
    hidden_in,
    segments,
    w_query,
    w_key,
    w_value,
    w_output,
    query_gain,
    key_gain,
    attn_gain,
    w_gate,
    w_up,
    w_down,
    ffn_gain,
    out_cotangent,
):
    length = hidden_in.shape[0]
    model_width = hidden_in.shape[1]
    ffn_width = w_gate.shape[1]
    factor = HEAD_DIM ** (-0.5)
    doc_row = segments[0]
    earlier = jnp.sum((doc_row[None, :] < doc_row[:, None]).astype(jnp.int32), axis=1)
    positions = jnp.arange(length, dtype=jnp.int32) - earlier
    half_dim = HEAD_DIM // 2
    inverse = jnp.exp(
        jnp.arange(half_dim, dtype=jnp.float32) * (-2.0 * math.log(theta_base) / HEAD_DIM)
    )
    angles = positions.astype(jnp.float32)[:, None] * inverse[None, :]
    cosines = jnp.cos(angles)[:, None, :]
    sines = jnp.sin(angles)[:, None, :]
    token_idx = jnp.arange(length)
    allowed = (doc_row[:, None] == doc_row[None, :]) & (token_idx[:, None] >= token_idx[None, :])

    def reduce_rows(term_fn, local_rows):
        return lax.psum_scatter(
            term_fn(jnp.int32(0), local_rows * lax.axis_size("shard")),
            "shard",
            scatter_dimension=0,
            tiled=True,
        )

    def norm_rope(raw_proj, gain_vec):
        normed = raw_proj * rms_scale(raw_proj) * gain_vec
        return rotate(normed.reshape(length, HEADS, HEAD_DIM), cosines, sines)

    def attend_scores(query_low, key_low):
        scores = (
            jnp.einsum("qhd,khd->hqk", query_low, key_low, preferred_element_type=jnp.float32)
            * factor
        )
        return jnp.where(allowed[None], scores, neg_fill)

    full_query, full_key, full_value, gain_query, gain_key = (
        lax.all_gather(w_query, "shard", axis=0, tiled=True),
        lax.all_gather(w_key, "shard", axis=0, tiled=True),
        lax.all_gather(w_value, "shard", axis=0, tiled=True),
        lax.all_gather(query_gain, "shard", axis=0, tiled=True),
        lax.all_gather(key_gain, "shard", axis=0, tiled=True),
    )
    query_raw = jnp.dot(hidden_in, full_query, preferred_element_type=jnp.float32)
    key_raw = jnp.dot(hidden_in, full_key, preferred_element_type=jnp.float32)
    query_low = norm_rope(query_raw, gain_query.astype(jnp.float32)).astype(jnp.bfloat16)
    key_low = norm_rope(key_raw, gain_key.astype(jnp.float32)).astype(jnp.bfloat16)
    value_low = (
        jnp.dot(hidden_in, full_value, preferred_element_type=jnp.float32)
        .astype(jnp.bfloat16)
        .reshape(length, HEADS, HEAD_DIM)
    )
    scores = attend_scores(query_low, key_low)
    row_peak = jnp.max(scores, axis=-1, keepdims=True)
    log_norm = row_peak + jnp.log(jnp.sum(jnp.exp(scores - row_peak), axis=-1, keepdims=True))
    attn_prob = jnp.exp(scores - log_norm)
    mixed_low = (
        jnp.einsum(
            "hqk,khd->qhd",
            attn_prob.astype(jnp.bfloat16),
            value_low,
            preferred_element_type=jnp.float32,
        )
        .reshape(length, model_width)
        .astype(jnp.bfloat16)
    )
    full_output, gain_attn = (
        lax.all_gather(w_output, "shard", axis=0, tiled=True),
        lax.all_gather(attn_gain, "shard", axis=0, tiled=True),
    )
    attn_out = jnp.dot(mixed_low, full_output, preferred_element_type=jnp.float32)
    attn_rms = rms_scale(attn_out)
    attn_normed = attn_out * attn_rms
    resid = hidden_in.astype(jnp.float32) + attn_normed * gain_attn.astype(jnp.float32)
    resid_low = resid.astype(jnp.bfloat16)
    full_gate, full_up = (
        lax.all_gather(w_gate, "shard", axis=0, tiled=True),
        lax.all_gather(w_up, "shard", axis=0, tiled=True),
    )
    gate_proj = jnp.dot(resid_low, full_gate, preferred_element_type=jnp.float32)
    up_proj = jnp.dot(resid_low, full_up, preferred_element_type=jnp.float32)
    gate_sig = jax.nn.sigmoid(gate_proj)
    hidden_ffn = (gate_proj * gate_sig * up_proj).astype(jnp.bfloat16)
    full_down, gain_ffn = (
        lax.all_gather(w_down, "shard", axis=0, tiled=True),
        lax.all_gather(ffn_gain, "shard", axis=0, tiled=True),
    )
    ffn_out = jnp.dot(hidden_ffn, full_down, preferred_element_type=jnp.float32)
    ffn_rms = rms_scale(ffn_out)
    ffn_normed = ffn_out * ffn_rms
    hidden_out = (resid + ffn_normed * gain_ffn.astype(jnp.float32)).astype(jnp.bfloat16)
    grad_out = out_cotangent.astype(jnp.float32)
    back_down, back_fgain = (
        lax.all_gather(w_down, "shard", axis=0, tiled=True),
        lax.all_gather(ffn_gain, "shard", axis=0, tiled=True),
    )
    ffn_gain_term = jnp.sum(grad_out * ffn_normed, axis=0)
    d_ffn_low = rms_back(grad_out * back_fgain.astype(jnp.float32), ffn_normed, ffn_rms).astype(
        jnp.bfloat16
    )
    down_grad = reduce_rows(col_term(hidden_ffn, d_ffn_low), w_down.shape[0])
    d_hidden_ffn = dot_back(d_ffn_low, back_down)
    d_gate_low = (d_hidden_ffn * up_proj * gate_sig * (1.0 + gate_proj * (1.0 - gate_sig))).astype(
        jnp.bfloat16
    )
    d_up_low = (d_hidden_ffn * gate_proj * gate_sig).astype(jnp.bfloat16)
    ffn_in_grad = reduce_rows(
        col_term(resid_low, jnp.concatenate([d_gate_low, d_up_low], axis=1)), w_gate.shape[0]
    )
    back_gate, back_up = (
        lax.all_gather(w_gate, "shard", axis=0, tiled=True),
        lax.all_gather(w_up, "shard", axis=0, tiled=True),
    )
    d_resid = grad_out + dot_back(d_gate_low, back_gate) + dot_back(d_up_low, back_up)
    back_output, back_again = (
        lax.all_gather(w_output, "shard", axis=0, tiled=True),
        lax.all_gather(attn_gain, "shard", axis=0, tiled=True),
    )
    attn_gain_term = jnp.sum(d_resid * attn_normed, axis=0)
    d_attn_low = rms_back(d_resid * back_again.astype(jnp.float32), attn_normed, attn_rms).astype(
        jnp.bfloat16
    )
    out_grad = reduce_rows(col_term(mixed_low, d_attn_low), w_output.shape[0])
    d_mixed_low = (
        dot_back(d_attn_low, back_output).astype(jnp.bfloat16).reshape(length, HEADS, HEAD_DIM)
    )
    scores_again = attend_scores(query_low, key_low)
    prob_again = jnp.exp(scores_again - log_norm)
    d_value = jnp.einsum(
        "hqk,qhd->khd",
        prob_again.astype(jnp.bfloat16),
        d_mixed_low,
        preferred_element_type=jnp.float32,
    )
    d_prob = jnp.einsum("qhd,khd->hqk", d_mixed_low, value_low, preferred_element_type=jnp.float32)
    d_scores_low = (
        prob_again * (d_prob - jnp.sum(d_prob * prob_again, axis=-1, keepdims=True))
    ).astype(jnp.bfloat16)
    d_query_rot = (
        jnp.einsum("hqk,khd->qhd", d_scores_low, key_low, preferred_element_type=jnp.float32)
        * factor
    )
    d_key_rot = (
        jnp.einsum("hqk,qhd->khd", d_scores_low, query_low, preferred_element_type=jnp.float32)
        * factor
    )
    back_query, back_key, back_value, back_qgain, back_kgain = (
        lax.all_gather(w_query, "shard", axis=0, tiled=True),
        lax.all_gather(w_key, "shard", axis=0, tiled=True),
        lax.all_gather(w_value, "shard", axis=0, tiled=True),
        lax.all_gather(query_gain, "shard", axis=0, tiled=True),
        lax.all_gather(key_gain, "shard", axis=0, tiled=True),
    )
    unused_query, query_pull = jax.vjp(norm_rope, query_raw, back_qgain.astype(jnp.float32))
    d_query_raw, query_gain_term = query_pull(d_query_rot)
    unused_key, key_pull = jax.vjp(norm_rope, key_raw, back_kgain.astype(jnp.float32))
    d_key_raw, key_gain_term = key_pull(d_key_rot)
    d_query_low = d_query_raw.astype(jnp.bfloat16)
    d_key_low = d_key_raw.astype(jnp.bfloat16)
    d_value_low = d_value.reshape(length, model_width).astype(jnp.bfloat16)
    qkv_grad = reduce_rows(
        col_term(hidden_in, jnp.concatenate([d_query_low, d_key_low, d_value_low], axis=1)),
        w_query.shape[0],
    )
    hidden_grad = (
        d_resid
        + dot_back(d_query_low, back_query)
        + dot_back(d_key_low, back_key)
        + dot_back(d_value_low, back_value)
    ).astype(jnp.bfloat16)
    gain_sums = (
        lax.psum_scatter(query_gain_term, "shard", scatter_dimension=0, tiled=True),
        lax.psum_scatter(key_gain_term, "shard", scatter_dimension=0, tiled=True),
        lax.psum_scatter(attn_gain_term, "shard", scatter_dimension=0, tiled=True),
        lax.psum_scatter(ffn_gain_term, "shard", scatter_dimension=0, tiled=True),
    )
    totals = (
        lax.psum(qkv_grad[:, :model_width].astype(jnp.bfloat16), "rep").astype(jnp.float32),
        lax.psum(qkv_grad[:, model_width : 2 * model_width].astype(jnp.bfloat16), "rep").astype(
            jnp.float32
        ),
        lax.psum(qkv_grad[:, 2 * model_width :].astype(jnp.bfloat16), "rep").astype(jnp.float32),
        lax.psum(out_grad.astype(jnp.bfloat16), "rep").astype(jnp.float32),
        lax.psum(gain_sums[0].astype(jnp.bfloat16), "rep").astype(jnp.float32),
        lax.psum(gain_sums[1].astype(jnp.bfloat16), "rep").astype(jnp.float32),
        lax.psum(gain_sums[2].astype(jnp.bfloat16), "rep").astype(jnp.float32),
        lax.psum(ffn_in_grad[:, :ffn_width].astype(jnp.bfloat16), "rep").astype(jnp.float32),
        lax.psum(ffn_in_grad[:, ffn_width:].astype(jnp.bfloat16), "rep").astype(jnp.float32),
        lax.psum(down_grad.astype(jnp.bfloat16), "rep").astype(jnp.float32),
        lax.psum(gain_sums[3].astype(jnp.bfloat16), "rep").astype(jnp.float32),
    )
    return (
        hidden_out,
        hidden_grad,
        totals[0],
        totals[1],
        totals[2],
        totals[3],
        totals[4],
        totals[5],
        totals[6],
        totals[7],
        totals[8],
        totals[9],
        totals[10],
    )


def solution(mesh):
    placed = (
        P(("rep", "shard"), None),
        P(("rep", "shard"), None),
        P("shard", None),
        P("shard", None),
        P("shard", None),
        P("shard", None),
        P("shard"),
        P("shard"),
        P("shard"),
        P("shard", None),
        P("shard", None),
        P("shard", None),
        P("shard"),
        P(("rep", "shard"), None),
    )
    return jax.shard_map(
        on_device,
        mesh=mesh,
        in_specs=placed,
        out_specs=(
            P(("rep", "shard"), None),
            P(("rep", "shard"), None),
            P("shard", None),
            P("shard", None),
            P("shard", None),
            P("shard", None),
            P("shard"),
            P("shard"),
            P("shard"),
            P("shard", None),
            P("shard", None),
            P("shard", None),
            P("shard"),
        ),
        check_vma=False,
    )
```

profile of v0, /device:TPU:0, one launch (start us, length us, event | category | flops | bytes accessed | tf_op | source)
XLA Modules:
  0.0 3663.1 jit_solution(7185058125295206287)
XLA Ops:
  12.0 23.2 all-gather
  35.2 17.5 all-gather.1
  52.8 18.9 all-gather.2
  71.6 17.4 all-gather.3
  89.6 4.7 multiply_reduce_fusion.8
  95.7 67.7 %all-gather.16.cloned.1.call-done = bf16[2048,2048]{1,0:T(8,128)(2,1)} async-done(((bf16[128,2048]{1,0:T(8,128)(2,1)}), bf16[2048,2048]{1,0:T(8,128)(2,1)}) %all-gather.16.cloned.1.call-update) | async-done | bytes 8388624 | tf_op jit(solution)/shard_map/all_gather | solution.py:104
  173.3 65.5 %all-gather.12.cloned.1.call-done = bf16[2048,2048]{1,0:T(8,128)(2,1)} async-done(((bf16[128,2048]{1,0:T(8,128)(2,1)}), bf16[2048,2048]{1,0:T(8,128)(2,1)}) %all-gather.12.cloned.1.call-update) | async-done | bytes 8388624 | tf_op jit(solution)/shard_map/all_gather | solution.py:105
  243.8 70.1 %all-gather.18.cloned.1.call-done = bf16[2048,2048]{1,0:T(8,128)(2,1)} async-done(((bf16[128,2048]{1,0:T(8,128)(2,1)}), bf16[2048,2048]{1,0:T(8,128)(2,1)}) %all-gather.18.cloned.1.call-update) | async-done | bytes 8388624 | tf_op jit(solution)/shard_map/all_gather | solution.py:133
  314.0 4.7 multiply_reduce_fusion.6
  319.7 162.0 %all-gather.20.cloned.1.call-done = bf16[2048,8192]{1,0:T(8,128)(2,1)} async-done(((bf16[128,8192]{1,0:T(8,128)(2,1)}), bf16[2048,8192]{1,0:T(8,128)(2,1)}) %all-gather.20.cloned.1.call-update) | async-done | bytes 33554448 | tf_op jit(solution)/shard_map/all_gather | solution.py:142
  481.7 18.9 fusion.46
  500.6 150.7 %all-gather.22.cloned.1.call-done = bf16[2048,8192]{1,0:T(8,128)(2,1)} async-done(((bf16[128,8192]{1,0:T(8,128)(2,1)}), bf16[2048,8192]{1,0:T(8,128)(2,1)}) %all-gather.22.cloned.1.call-update) | async-done | bytes 33554448 | tf_op jit(solution)/shard_map/all_gather | solution.py:143
  651.3 21.1 multiply_convert_fusion.2
  672.4 148.6 %all-gather.24.cloned.1.call-done = bf16[8192,2048]{1,0:T(8,128)(2,1)} async-done(((bf16[512,2048]{1,0:T(8,128)(2,1)}), bf16[8192,2048]{1,0:T(8,128)(2,1)}) %all-gather.24.cloned.1.call-update) | async-done | bytes 33554448 | tf_op jit(solution)/shard_map/all_gather | solution.py:150
  821.0 14.0 multiply_reduce_fusion.5
  837.0 19.9 multiply_convert_fusion
  856.9 17.4 convolution_add_fusion.1
  874.3 18.7 multiply_reduce_fusion
  896.4 8.1 fusion.47
  905.5 6.2 convolution_convert_fusion
  923.2 22.0 convolution_bitcast_fusion
  946.9 23.6 fusion.48
  972.3 46.4 %fusion = f32[2048,16384]{1,0:T(8,128)} fusion(bf16[128,2048]{1,0:T(8,128)(2,1)S(1)} %copy-done.10, bf16[128,8192]{1,0:T(8,128)(2,1)S(1)} %copy-done.8, bf16[128,8192]{1,0:T(8,128)(2,1)} %get-tuple-element.63), kind=kOutput, calls=%fused_computation.1 | convolution fusion | flops 8598323200 | bytes 138936320 | tf_op jit(solution)/shard_map/dot_general | solution.py:43
  1018.8 64.3 %reduce-scatter.7.cloned.1.call-done = f32[128,2048]{1,0:T(8,128)} async-done(((f32[2048,2048]{1,0:T(8,128)}), f32[128,2048]{1,0:T(8,128)}) %reduce-scatter.7.cloned.1.call-update) | async-done | bytes 1048592 | tf_op jit(solution)/shard_map/reduce_scatter | solution.py:84
  1085.3 468.9 %reduce-scatter.5.cloned.1.call-done = f32[128,6144]{0,1:T(8,128)} async-done(((f32[2048,6144]{0,1:T(8,128)}), f32[128,6144]{0,1:T(8,128)}) %reduce-scatter.5.cloned.1.call-update) | async-done | bytes 3145744 | tf_op jit(solution)/shard_map/reduce_scatter | solution.py:84
  1557.5 637.0 %reduce-scatter.11.cloned.1.call-done = f32[512,2048]{1,0:T(8,128)} async-done(((f32[8192,2048]{1,0:T(8,128)}), f32[512,2048]{1,0:T(8,128)}) %reduce-scatter.11.cloned.1.call-update) | async-done | bytes 4194320 | tf_op jit(solution)/shard_map/reduce_scatter | solution.py:84
  2198.3 1235.7 %reduce-scatter.9.cloned.1.call-done = f32[128,16384]{1,0:T(8,128)} async-done(((f32[2048,16384]{1,0:T(8,128)}), f32[128,16384]{1,0:T(8,128)}) %reduce-scatter.9.cloned.1.call-update) | async-done | bytes 8388624 | tf_op jit(solution)/shard_map/reduce_scatter | solution.py:84
  3442.0 59.5 %all-reduce.8 = (bf16[2048]{0:T(1024)(128)(2,1)S(1)}, bf16[2048]{0:T(1024)(128)(2,1)S(1)}, bf16[2048]{0:T(1024)(128)(2,1)S(1)}, bf16[2048]{0:T(1024)(128)(2,1)S(1)}) all-reduce(f32[2048]{0:T(1024)S(1)} %copy-done.35, f32[2048]{0:T(1024)S(1)} %copy-done.36, ...), channel_id=4, replica_groups=mesh['rep'=2,'shard'=16] {'shard'}, use_global_device_ids=true, to_apply=%region_19.20.clone | all-reduce | flops 8192 | bytes 49152
  3501.8 5.2 all-reduce.9
  3509.1 6.6 convolution_add_fusion.4
  3515.7 6.5 convolution_add_fusion.3
  3526.0 114.5 %all-reduce.13.cloned.1.call-done = (bf16[128,2048]{0,1:T(8,128)(2,1)}, bf16[128,2048]{0,1:T(8,128)(2,1)}, bf16[128,2048]{0,1:T(8,128)(2,1)}, bf16[128,2048]{1,0...) async-done(((bf16[128,2048]{0,1:T(8,128)(2,1)}, bf16[128,2048]{0,1:T(8,128)(2,1)}, bf16[128,2048]{0,1:T(8,128)(2,1)}, ...) | async-done | bytes 8388624 | tf_op jit(solution)/shard_map/psum | solution.py:243
  (184 shorter events, 81.6 us)
Async XLA Ops:
  7.2 4.8 copy-start.38
  7.2 28.0 copy-start.39
  7.2 45.5 %copy-start.40 = (bf16[128]{0:T(256)(128)(2,1)S(1)}, bf16[128]{0:T(256)(128)(2,1)}, u32[]{:S(2)}) copy-start(bf16[128]{0:T(256)(128)(2,1)} %param.22) | copy-start | bytes 772
  7.2 64.4 %copy-start.41 = (bf16[128]{0:T(256)(128)(2,1)S(1)}, bf16[128]{0:T(256)(128)(2,1)}, u32[]{:S(2)}) copy-start(bf16[128]{0:T(256)(128)(2,1)} %param.26) | copy-start | bytes 772
  7.2 81.8 %copy-start.37 = (s32[1,128]{1,0:T(1,128)S(1)}, s32[1,128]{1,0:T(1,128)}, u32[]{:S(2)}) copy-start(s32[1,128]{1,0:T(1,128)} %param.15) | copy-start | bytes 1540
  7.2 82.4 %all-gather.14.cloned.1.call-start = ((), (), s32[]{:S(2)}) async-start(), calls=%async_computation.5 | async-start | bytes 8912896 | tf_op jit(solution)/shard_map/all_gather | solution.py:103
  8.0 81.7 %copy-start = (bf16[128,2048]{1,0:T(8,128)(2,1)S(1)}, bf16[128,2048]{1,0:T(8,128)(2,1)}, u32[]{:S(2)}) copy-start(bf16[128,2048]{1,0:T(8,128)(2,1)} %param.14) | copy-start | bytes 1572868
  8.0 155.4 %all-gather.16.cloned.1.call-start = ((), (), s32[]{:S(2)}) async-start(), calls=%async_computation.6 | async-start | bytes 8912896 | tf_op jit(solution)/shard_map/all_gather | solution.py:104
  8.7 230.0 %all-gather.12.cloned.1.call-start = ((), (), s32[]{:S(2)}) async-start(), calls=%async_computation.4 | async-start | bytes 8912896 | tf_op jit(solution)/shard_map/all_gather | solution.py:105
  9.5 304.5 %all-gather.18.cloned.1.call-start = ((), (), s32[]{:S(2)}) async-start(), calls=%async_computation.7 | async-start | bytes 8912896 | tf_op jit(solution)/shard_map/all_gather | solution.py:133
  10.0 471.7 %all-gather.20.cloned.1.call-start = ((), (), s32[]{:S(2)}) async-start(), calls=%async_computation.8 | async-start | bytes 35651584 | tf_op jit(solution)/shard_map/all_gather | solution.py:142
  10.6 640.7 %all-gather.22.cloned.1.call-start = ((), (), s32[]{:S(2)}) async-start(), calls=%async_computation.9 | async-start | bytes 35651584 | tf_op jit(solution)/shard_map/all_gather | solution.py:143
  11.2 809.8 %all-gather.24.cloned.1.call-start = ((), (), s32[]{:S(2)}) async-start(), calls=%async_computation.10 | async-start | bytes 35651584 | tf_op jit(solution)/shard_map/all_gather | solution.py:150
  11.9 1071.2 %reduce-scatter.7.cloned.1.call-start = ((), (), s32[]{:S(2)}) async-start(), calls=%async_computation.12 | async-start | bytes 17825792 | tf_op jit(solution)/shard_map/reduce_scatter | solution.py:84
  243.4 70.5 %copy-start.23 = (bf16[16,16,8,128]{3,2,1,0:T(8,128)(2,1)}, bf16[16,16,8,128]{3,2,1,0:T(8,128)(2,1)S(1)}, u32[]{:S(2)}) copy-start(bf16[16,16,8,128]{3,2,1,0:T(8,128)(2,1)S(1)} %fusion.15) | copy-start | bytes 1572868
  821.0 14.0 copy-start.26
  874.3 18.7 copy-start.6
  904.4 649.8 %reduce-scatter.5.cloned.1.call-start = ((), (), s32[]{:S(2)}) async-start(), calls=%async_computation.11 | async-start | bytes 53477376 | tf_op jit(solution)/shard_map/reduce_scatter | solution.py:84
  912.7 4.8 copy-start.18
  912.7 4.8 copy-start.20
  914.4 3.6 copy-start.21
  923.2 22.1 copy-start.11
  945.3 1249.2 %reduce-scatter.11.cloned.1.call-start = ((), (), s32[]{:S(2)}) async-start(), calls=%async_computation.14 | async-start | bytes 71303168 | tf_op jit(solution)/shard_map/reduce_scatter | solution.py:84
  970.5 2463.5 %reduce-scatter.9.cloned.1.call-start = ((), (), s32[]{:S(2)}) async-start(), calls=%async_computation.13 | async-start | bytes 142606336 | tf_op jit(solution)/shard_map/reduce_scatter | solution.py:84
  1018.8 2621.7 %all-reduce.13.cloned.1.call-start = ((), (), s32[]{:S(2)}) async-start(), calls=%async_computation.15 | async-start | bytes 16777216 | tf_op jit(solution)/shard_map/psum | solution.py:243
  3440.1 69.0 %copy-start.9 = (f32[128,2048]{1,0:T(8,128)S(1)}, f32[128,2048]{1,0:T(8,128)}, u32[]{:S(2)}) copy-start(f32[128,2048]{1,0:T(8,128)} %get-tuple-element.101) | copy-start | bytes 3145732
  3509.1 6.6 copy-start.12
  3509.1 13.2 slice-start
  3515.7 6.6 slice-start.1
  3515.7 6.6 copy-start.22
  3640.5 6.8 copy-start.32
  3640.5 7.9 copy-start.31
  (25 other events, 41.4 us)
Sparse Core Ops, SparseCore 0:
  10.2 77.7 all-gather.13
  90.2 73.2 all-gather.15
  165.6 73.1 all-gather.11
  240.8 73.1 all-gather.17
  315.4 166.2 all-gather.19
  483.2 168.0 all-gather.21
  652.9 168.0 all-gather.23
  904.6 178.5 reduce-scatter.6
  1087.4 466.7 reduce-scatter.4
  1558.3 636.1 reduce-scatter.10
  2198.7 1235.1 reduce-scatter.8
  3440.3 200.2 all-reduce.12
where the time goes:
time: 3670 us; the launch traced here: 3660 us
  waiting for transfers between devices  3190 us (87%)
  matrix products  258 us (7%)
  blocking collectives  142 us (4%)
    reduce_scatter x4, waiting for transfers between devices, reduce_rows(): lax.psum_scatter(term_fn(jnp.int32(0), local_rows * lax.axis_size('shard'...  2410 us
    all_gather x1, waiting for transfers between devices, on_device(): lax.all_gather(w_gate, 'shard', axis=0, tiled=True)  162 us
    all_gather x1, waiting for transfers between devices, on_device(): lax.all_gather(w_up, 'shard', axis=0, tiled=True)  151 us
    all_gather x1, waiting for transfers between devices, on_device(): lax.all_gather(w_down, 'shard', axis=0, tiled=True)  149 us
    psum x1, waiting for transfers between devices, on_device(): lax.psum(qkv_grad[:, :model_width].astype(jnp.bfloat16), 'rep')  115 us
    dot_general x4, matrix products, block_term(): lax.dot_general(left_side, right_side, (((0,), (0,)), ((), ())), preferre...  100 us
    dot_general x7, matrix products, dot_back(): lax.dot_general(left_side, right_side, (((1,), (1,)), ((), ())), preferre...  79 us
  transfers between devices with their start and end apart: 12, of which 11 were waited for; matrix products, arithmetic and copies ran while one was open for 6% of the time, Pallas kernels for 0%

commit v1 on v0

--- a/solution.py
+++ b/solution.py
@@ -47,7 +47,7 @@
     return block_term
 
 
-def on_device(
+def on_device_general(
     hidden_in,
     segments,
     w_query,
@@ -271,6 +271,305 @@
     )
 
 
+LINE = 4
+
+
+def shard_perm(move):
+    return [(index, move(index)) for index in range(16)]
+
+
+def core_swap(values):
+    return lax.ppermute(values, "shard", shard_perm(lambda index: index ^ 1))
+
+
+def pair_swap(values):
+    return lax.ppermute(values, "shard", shard_perm(lambda index: index ^ 2))
+
+
+def rep_swap(values):
+    return lax.ppermute(values, "rep", [(0, 1), (1, 0)])
+
+
+def line_shift(values, steps):
+    return lax.ppermute(values, "shard", shard_perm(lambda index: (index + 4 * steps) % 16))
+
+
+def line_groups():
+    return [[line * 4 + pair * 2 + core for line in range(4) for core in range(2)] for pair in range(2)]
+
+
+def gather_tokens(block):
+    mine = [block] + [line_shift(block, steps) for steps in range(1, LINE)]
+    return jnp.stack(mine + [core_swap(piece) for piece in mine])
+
+
+def scatter_tokens(parts):
+    theirs = [core_swap(parts[LINE + k].astype(jnp.bfloat16)) for k in range(LINE)]
+    joint = [parts[k] + theirs[k].astype(jnp.float32) for k in range(LINE)]
+    total = joint[0]
+    for k in range(1, LINE):
+        total = total + line_shift(joint[k].astype(jnp.bfloat16), -k).astype(jnp.float32)
+    return total
+
+
+def group_sum(values):
+    count, tokens = values.shape
+    split = values.reshape(count, 2, LINE, tokens // (2 * LINE))
+    both = split + core_swap(split)[:, ::-1]
+    total = both
+    for steps in range(1, LINE):
+        total = total + jnp.roll(line_shift(both, steps), steps, axis=2)
+    return total.reshape(count, tokens)
+
+
+def by_pair(pair, own, other):
+    return jnp.where(pair == 0, own, other), jnp.where(pair == 0, other, own)
+
+
+def gather_columns(weight, pair):
+    rows, width = weight.shape
+    n = width // 16
+    pieces = weight.reshape(rows, 4, 2, 2, n).transpose(1, 3, 0, 2, 4).reshape(8, rows, 2, n)
+    own = lax.all_to_all(pieces, "shard", 0, 0, axis_index_groups=line_groups(), tiled=True)
+    first, second = by_pair(pair, own, pair_swap(own))
+    full = jnp.stack([first.reshape(4, 2, rows, 2 * n), second.reshape(4, 2, rows, 2 * n)], axis=1)
+    return full.reshape(16 * rows, 2 * n)
+
+
+def gather_rows(weight, pair):
+    return jnp.concatenate(by_pair(pair, weight, pair_swap(weight)), axis=0)
+
+
+def rep_total(values):
+    low = values.astype(jnp.bfloat16)
+    return low.astype(jnp.float32) + rep_swap(low).astype(jnp.float32)
+
+
+def pair_total(first, second, pair):
+    own, other = by_pair(pair, first, second)
+    return own + pair_swap(other.astype(jnp.bfloat16)).astype(jnp.float32)
+
+
+def reduce_columns(partial, pair):
+    rows = partial.shape[0] // 16
+    n = partial.shape[1] // 2
+    split = partial.reshape(4, 2, 2, rows, 2 * n)
+    mine = pair_total(split[:, 0], split[:, 1], pair).astype(jnp.bfloat16).reshape(8, rows, 2, n)
+    got = lax.all_to_all(mine, "shard", 0, 0, axis_index_groups=line_groups(), tiled=True)
+    return rep_total(got.reshape(4, 2, rows, 2, n).transpose(2, 0, 3, 1, 4).reshape(rows, 16 * n))
+
+
+def reduce_rows_of(partial, pair):
+    half = partial.shape[0] // 2
+    return rep_total(pair_total(partial[:half], partial[half:], pair))
+
+
+def on_device(
+    hidden_in,
+    segments,
+    w_query,
+    w_key,
+    w_value,
+    w_output,
+    query_gain,
+    key_gain,
+    attn_gain,
+    w_gate,
+    w_up,
+    w_down,
+    ffn_gain,
+    out_cotangent,
+):
+    length, model_width = hidden_in.shape
+    blocks = 2 * LINE
+    heads = HEADS // blocks
+    factor = HEAD_DIM ** (-0.5)
+    pair = (lax.axis_index("shard") // 2) % 2
+    f32 = jnp.float32
+
+    docs = gather_tokens(segments)[:, 0]
+    tokens = gather_tokens(hidden_in).reshape(blocks * length, model_width)
+    width = heads * HEAD_DIM
+    full_query = gather_columns(w_query, pair)
+    full_key = gather_columns(w_key, pair)
+    full_value = gather_columns(w_value, pair)
+    head_gains = gather_rows(jnp.stack([query_gain, key_gain])[None], pair).astype(f32)
+    gain_query = head_gains[:, 0].reshape(width)
+    gain_key = head_gains[:, 1].reshape(width)
+    wide_gains = lax.all_gather(
+        jnp.stack([attn_gain, ffn_gain]), "shard", axis=1, tiled=True
+    ).astype(f32)
+    gain_attn, gain_ffn = wide_gains[0], wide_gains[1]
+
+    earlier = jnp.sum((docs[:, None, :] < docs[:, :, None]).astype(jnp.int32), axis=2)
+    positions = jnp.arange(length, dtype=jnp.int32)[None] - earlier
+    half_dim = HEAD_DIM // 2
+    inverse = jnp.exp(
+        jnp.arange(half_dim, dtype=f32) * (-2.0 * math.log(theta_base) / HEAD_DIM)
+    )
+    angles = positions.astype(f32)[:, :, None] * inverse[None, None, :]
+    cosines = jnp.cos(angles)[:, :, None, :]
+    sines = jnp.sin(angles)[:, :, None, :]
+    token_idx = jnp.arange(length)
+    allowed = (docs[:, :, None] == docs[:, None, :]) & (
+        token_idx[:, None] >= token_idx[None, :]
+    )[None]
+
+    def split_heads(values):
+        return values.reshape(blocks, length, heads, HEAD_DIM)
+
+    query_raw = jnp.dot(tokens, full_query, preferred_element_type=f32)
+    key_raw = jnp.dot(tokens, full_key, preferred_element_type=f32)
+    squares = group_sum(
+        jnp.stack([jnp.sum(query_raw * query_raw, axis=-1), jnp.sum(key_raw * key_raw, axis=-1)])
+    )
+    head_scales = lax.rsqrt(squares / model_width + epsilon)
+    query_unit = query_raw * head_scales[0][:, None]
+    key_unit = key_raw * head_scales[1][:, None]
+    query_low = rotate(split_heads(query_unit * gain_query), cosines, sines).astype(jnp.bfloat16)
+    key_low = rotate(split_heads(key_unit * gain_key), cosines, sines).astype(jnp.bfloat16)
+    value_low = split_heads(
+        jnp.dot(tokens, full_value, preferred_element_type=f32).astype(jnp.bfloat16)
+    )
+    scores = (
+        jnp.einsum("sqhd,skhd->shqk", query_low, key_low, preferred_element_type=f32) * factor
+    )
+    scores = jnp.where(allowed[:, None], scores, neg_fill)
+    row_peak = jnp.max(scores, axis=-1, keepdims=True)
+    log_norm = row_peak + jnp.log(jnp.sum(jnp.exp(scores - row_peak), axis=-1, keepdims=True))
+    attn_prob = jnp.exp(scores - log_norm)
+    prob_low = attn_prob.astype(jnp.bfloat16)
+    mixed_low = (
+        jnp.einsum("shqk,skhd->sqhd", prob_low, value_low, preferred_element_type=f32)
+        .reshape(blocks * length, width)
+        .astype(jnp.bfloat16)
+    )
+    full_output = gather_rows(w_output, pair)
+
+    def to_blocks(values):
+        return values.reshape(blocks, length, model_width)
+
+    attn_out = scatter_tokens(
+        to_blocks(jnp.dot(mixed_low, full_output, preferred_element_type=f32))
+    )
+    attn_rms = rms_scale(attn_out)
+    attn_normed = attn_out * attn_rms
+    resid = hidden_in.astype(f32) + attn_normed * gain_attn
+    resid_low = gather_tokens(resid.astype(jnp.bfloat16)).reshape(blocks * length, model_width)
+
+    full_gate = gather_columns(w_gate, pair)
+    full_up = gather_columns(w_up, pair)
+    gate_proj = jnp.dot(resid_low, full_gate, preferred_element_type=f32)
+    up_proj = jnp.dot(resid_low, full_up, preferred_element_type=f32)
+    gate_sig = jax.nn.sigmoid(gate_proj)
+    hidden_ffn = (gate_proj * gate_sig * up_proj).astype(jnp.bfloat16)
+    full_down = gather_rows(w_down, pair)
+    ffn_out = scatter_tokens(
+        to_blocks(jnp.dot(hidden_ffn, full_down, preferred_element_type=f32))
+    )
+    ffn_rms = rms_scale(ffn_out)
+    ffn_normed = ffn_out * ffn_rms
+    hidden_out = (resid + ffn_normed * gain_ffn).astype(jnp.bfloat16)
+    grad_out = out_cotangent.astype(f32)
+    ffn_gain_term = jnp.sum(grad_out * ffn_normed, axis=0)
+    d_ffn_low = gather_tokens(
+        rms_back(grad_out * gain_ffn, ffn_normed, ffn_rms).astype(jnp.bfloat16)
+    ).reshape(blocks * length, model_width)
+
+    d_hidden_ffn = dot_back(d_ffn_low, full_down)
+    d_gate_low = (d_hidden_ffn * up_proj * gate_sig * (1.0 + gate_proj * (1.0 - gate_sig))).astype(
+        jnp.bfloat16
+    )
+    d_up_low = (d_hidden_ffn * gate_proj * gate_sig).astype(jnp.bfloat16)
+    d_resid = grad_out + scatter_tokens(
+        to_blocks(dot_back(d_gate_low, full_gate) + dot_back(d_up_low, full_up))
+    )
+
+    def outer(left_side, right_side):
+        return lax.dot_general(
+            left_side, right_side, (((0,), (0,)), ((), ())), preferred_element_type=f32
+        )
+
+    grad_down = reduce_rows_of(outer(hidden_ffn, d_ffn_low), pair)
+    grad_gate = reduce_columns(outer(resid_low, d_gate_low), pair)
+    grad_up = reduce_columns(outer(resid_low, d_up_low), pair)
+    attn_gain_term = jnp.sum(d_resid * attn_normed, axis=0)
+    d_attn_low = gather_tokens(
+        rms_back(d_resid * gain_attn, attn_normed, attn_rms).astype(jnp.bfloat16)
+    ).reshape(blocks * length, model_width)
+    grad_output = reduce_rows_of(outer(mixed_low, d_attn_low), pair)
+    d_mixed_low = split_heads(dot_back(d_attn_low, full_output).astype(jnp.bfloat16))
+    d_value = jnp.einsum("shqk,sqhd->skhd", prob_low, d_mixed_low, preferred_element_type=f32)
+    d_prob = jnp.einsum("sqhd,skhd->shqk", d_mixed_low, value_low, preferred_element_type=f32)
+    d_scores_low = (
+        attn_prob * (d_prob - jnp.sum(d_prob * attn_prob, axis=-1, keepdims=True))
+    ).astype(jnp.bfloat16)
+    d_query_rot = (
+        jnp.einsum("shqk,skhd->sqhd", d_scores_low, key_low, preferred_element_type=f32) * factor
+    )
+    d_key_rot = (
+        jnp.einsum("shqk,sqhd->skhd", d_scores_low, query_low, preferred_element_type=f32)
+        * factor
+    )
+    d_query_normed = rotate(d_query_rot, cosines, -sines).reshape(blocks * length, width)
+    d_key_normed = rotate(d_key_rot, cosines, -sines).reshape(blocks * length, width)
+    query_gain_term = jnp.sum(d_query_normed * query_unit, axis=0)
+    key_gain_term = jnp.sum(d_key_normed * key_unit, axis=0)
+    query_up = d_query_normed * gain_query
+    key_up = d_key_normed * gain_key
+    means = (
+        group_sum(
+            jnp.stack(
+                [jnp.sum(query_up * query_unit, axis=-1), jnp.sum(key_up * key_unit, axis=-1)]
+            )
+        )
+        / model_width
+    )
+    d_query_low = (head_scales[0][:, None] * (query_up - query_unit * means[0][:, None])).astype(
+        jnp.bfloat16
+    )
+    d_key_low = (head_scales[1][:, None] * (key_up - key_unit * means[1][:, None])).astype(
+        jnp.bfloat16
+    )
+    d_value_low = d_value.reshape(blocks * length, width).astype(jnp.bfloat16)
+    hidden_grad = (
+        d_resid
+        + scatter_tokens(
+            to_blocks(
+                dot_back(d_query_low, full_query)
+                + dot_back(d_key_low, full_key)
+                + dot_back(d_value_low, full_value)
+            )
+        )
+    ).astype(jnp.bfloat16)
+    grad_query = reduce_columns(outer(tokens, d_query_low), pair)
+    grad_key = reduce_columns(outer(tokens, d_key_low), pair)
+    grad_value = reduce_columns(outer(tokens, d_value_low), pair)
+    head_terms = jnp.stack([query_gain_term, key_gain_term]).reshape(2, 2, HEAD_DIM)
+    own_term, other_term = by_pair(pair, head_terms[:, 0], head_terms[:, 1])
+    head_grads = own_term + pair_swap(other_term)
+    wide_grads = lax.psum_scatter(
+        jnp.stack([attn_gain_term, ffn_gain_term]), "shard", scatter_dimension=1, tiled=True
+    )
+    gain_grads = jnp.concatenate([head_grads, wide_grads])
+    gain_grads = gain_grads + rep_swap(gain_grads)
+    return (
+        hidden_out,
+        hidden_grad,
+        grad_query,
+        grad_key,
+        grad_value,
+        grad_output,
+        gain_grads[0],
+        gain_grads[1],
+        gain_grads[2],
+        grad_gate,
+        grad_up,
+        grad_down,
+        gain_grads[3],
+    )
+
+
 def solution(mesh):
     placed = (
         P(("rep", "shard"), None),
@@ -289,7 +588,7 @@
         P(("rep", "shard"), None),
     )
     return jax.shard_map(
-        on_device,
+        on_device if mesh.shape["shard"] == 16 else on_device_general,
         mesh=mesh,
         in_specs=placed,
         out_specs=(

time: 3670 us -> 1260 us (0.34)
  waiting for transfers between devices: 3190 us -> 608 us
  starting transfers between devices: 0.47 us -> 154 us
  matrix products: 258 us -> 109 us
  local copies, waits for them, and re-layouts: 23.5 us -> 171 us
  other arithmetic: 34.4 us -> 112 us
  blocking collectives: 142 us -> 76.1 us
    reduce_scatter x4 -> x0, waiting for transfers between devices: 2410 us -> none  [reduce_rows(): lax.psum_scatter(term_fn(jnp.int32(0), local_rows * lax.axis_size('shard'...]
    all_gather x7 -> x0, waiting for transfers between devices: 665 us -> none  [the longest x1 162 us: on_device(): lax.all_gather(w_gate, 'shard', axis=0, tiled=True)]
    ppermute x0 -> x95, waiting for transfers between devices: none -> 485 us  [the longest x33 292 us: line_shift(): lax.ppermute(values, 'shard', shard_perm(lambda index: (index + 4 * steps...]
    psum x1 -> x0, waiting for transfers between devices: 115 us -> none  [on_device(): lax.psum(qkv_grad[:, :model_width].astype(jnp.bfloat16), 'rep')]
    dot_general x17 -> x20, matrix products: 179 us -> 69.6 us  [the longest x7 29.8 us: outer(): lax.dot_general(left_side, right_side, (((0,), (0,)), ((), ())), preferre...]
    ppermute x0 -> x95, starting transfers between devices: none -> 104 us  [the longest x33 73.5 us: line_shift(): lax.ppermute(values, 'shard', shard_perm(lambda index: (index + 4 * steps...]
    all_to_all x0 -> x10, waiting for transfers between devices: none -> 61.6 us  [the longest x5 38.4 us: reduce_columns(): lax.all_to_all(mine, 'shard', 0, 0, axis_index_groups=line_groups(), tile...]
    unnamed x1 -> x0, blocking collectives: 59.5 us -> none
  transfers between devices with their start and end apart: 12 -> 106, of which waited for: 11 -> 48; matrix products, arithmetic and copies ran while one was open for 6% -> 23% of each run, Pallas kernels for 0% -> 0%
where the time goes in v1:
time: 1260 us; the launch traced here: 1250 us
  waiting for transfers between devices  608 us (48%)
  local copies, waits for them, and re-layouts  171 us (14%)
  starting transfers between devices  154 us (12%)
  other arithmetic  112 us (9%)
  matrix products  109 us (9%)
  blocking collectives  76.1 us (6%)
  between operations  16.1 us (1%)
    ppermute x33, waiting for transfers between devices, line_shift(): lax.ppermute(values, 'shard', shard_perm(lambda index: (index + 4 * steps...  292 us
    ppermute x16, waiting for transfers between devices, pair_swap(): return lax.ppermute(values, 'shard', shard_perm(lambda index: index ^ 2))  116 us
    all_gather x1, blocking collectives, on_device(): lax.all_gather(jnp.stack([attn_gain, ffn_gain]), 'shard', axis=1, tiled=T...  76.1 us
    ppermute x33, starting transfers between devices, line_shift(): lax.ppermute(values, 'shard', shard_perm(lambda index: (index + 4 * steps...  73.5 us
    ppermute x8, waiting for transfers between devices, rep_swap(): return lax.ppermute(values, 'rep', [(0, 1), (1, 0)])  68.1 us
    unnamed x2, waiting for transfers between devices  61.5 us
    unnamed x225, local copies, waits for them, and re-layouts  57.2 us
    dot_general x7, matrix products, dot_back(): lax.dot_general(left_side, right_side, (((1,), (1,)), ((), ())), preferre...  39.3 us
  transfers between devices with their start and end apart: 106, of which 48 were waited for; matrix products, arithmetic and copies ran while one was open for 23% of the time, Pallas kernels for 0%

profile of v1, /device:TPU:0, one launch (start us, length us, event | category | flops | bytes accessed | tf_op | source)
XLA Modules:
  0.0 1246.8 jit_solution(17709474278991235393)
XLA Ops:
  48.9 24.4 %collective-permute-done.1 = bf16[128,2048]{1,0:T(8,128)(2,1)S(1)} collective-permute-done((bf16[128,2048]{1,0:T(8,128)(2,1)S(1)}, bf16[128,2048]{1,0:T(8,128)(2,1)S(1)}, u32[]{:S(2)}, u32[]{:S(2)}) %collective-permute-start.1) | collective-permute-done | bytes 524320 | tf_op jit(solution)/shard_map/ppermute | solution.py:294
  77.4 12.4 all-to-all-start
  91.5 13.7 %all-to-all-done = bf16[8,128,2,128]{3,1,2,0:T(8,128)(2,1)S(1)} async-done(((bf16[8,128,2,128]{3,1,2,0:T(8,128)(2,1)}), bf16[8,128,2,128]{3,1,2,0:T(8,128)(2,1)S(1)}, u32[]{:S(2)}, u32[]{:S(2)}) %all-to-all-start) | async-done | bytes 524320 | tf_op jit(solution)/shard_map/all_to_all | solution.py:333
  114.5 9.5 all-to-all-done.1
  139.2 10.1 collective-permute-done.15
  221.5 76.1 %all_gather.3 = bf16[2,2048]{1,0:T(2,128)(2,1)S(1)} all-gather(bf16[2,128]{1,0:T(2,128)(2,1)S(1)} %pad_maximum_fusion.24), channel_id=1, replica_groups=mesh['rep'=2,'shard'=16] {'shard'}, dimensions={1}, use_global_device_ids=true | all-gather | bytes 8704 | tf_op jit(solution)/shard_map/all_gather | solution.py:399
  297.7 10.0 collective-permute-done.27
  310.6 11.3 collective-permute-start.32
  334.5 23.8 %collective-permute-done.30 = bf16[128,2048]{1,0:T(8,128)(2,1)} collective-permute-done((bf16[128,2048]{1,0:T(8,128)(2,1)}, bf16[128,2048]{1,0:T(8,128)(2,1)}, u32[]{:S(2)}, u32[]{:S(2)}) %collective-permute-start.30) | collective-permute-done | bytes 524320 | tf_op jit(solution)/shard_map/ppermute | solution.py:294
  360.2 8.2 collective-permute-done.31
  378.6 39.5 %collective-permute-done.38 = bf16[8,128,2,512]{3,1,2,0:T(8,128)(2,1)} collective-permute-done((bf16[8,128,2,512]{3,1,2,0:T(8,128)(2,1)}, bf16[8,128,2,512]{3,1,2,0:T(8,128)(2,1)}, u32[]{:S(2)}, u32[]{:S(2)}) %collective-permute-start.38) | collective-permute-done | bytes 2097184 | tf_op jit(solution)/shard_map/ppermute | solution.py:286
  418.2 43.3 %collective-permute-done.37 = bf16[8,128,2,512]{3,1,2,0:T(8,128)(2,1)S(1)} collective-permute-done((bf16[8,128,2,512]{3,1,2,0:T(8,128)(2,1)}, bf16[8,128,2,512]{3,1,2,0:T(8,128)(2,1)S(1)}, u32[]{:S(2)}, u32[]{:S(2)}) %collective-permute-start.37) | collective-permute-done | bytes 2097184 | tf_op jit(solution)/shard_map/ppermute | solution.py:286
  512.1 10.3 multiply_convert_fusion.2
  539.1 7.8 collective-permute-done.42
  546.9 15.2 %collective-permute-done.46 = bf16[128,2048]{1,0:T(8,128)(2,1)S(1)} collective-permute-done((bf16[128,2048]{1,0:T(8,128)(2,1)S(1)}, bf16[128,2048]{1,0:T(8,128)(2,1)S(1)}, u32[]{:S(2)}, u32[]{:S(2)}) %collective-permute-start.46) | collective-permute-done | bytes 524320 | tf_op jit(solution)/shard_map/ppermute | solution.py:294
  562.1 20.4 %collective-permute-done.44 = bf16[128,2048]{1,0:T(8,128)(2,1)S(1)} collective-permute-done((bf16[128,2048]{1,0:T(8,128)(2,1)S(1)}, bf16[128,2048]{1,0:T(8,128)(2,1)S(1)}, u32[]{:S(2)}, u32[]{:S(2)}) %collective-permute-start.44) | collective-permute-done | bytes 524320 | tf_op jit(solution)/shard_map/ppermute | solution.py:294
  600.0 30.0 %collective-permute-done.48 = bf16[128,2048]{1,0:T(8,128)(2,1)} collective-permute-done((bf16[128,2048]{1,0:T(8,128)(2,1)}, bf16[128,2048]{1,0:T(8,128)(2,1)}, u32[]{:S(2)}, u32[]{:S(2)}) %collective-permute-start.48) | collective-permute-done | bytes 524320 | tf_op jit(solution)/shard_map/ppermute | solution.py:294
  646.4 14.4 %multiply_convert_fusion = (bf16[1024,1024]{1,0:T(8,128)(2,1)S(1)}, bf16[1024,1024]{1,0:T(8,128)(2,1)}) fusion(f32[1024,1024]{1,0:T(8,128)} %copy-done.88, f32[1024,1024]{1,0:T(8,128)} %get-tuple-element.123, bf16[1024,2048]{1,0:T(8,128)(2,1)} %bitcast.465, bf16[512,2048]{1,0:T(8,128)(2,1)S(1)} %copy-done.70, bf16[512,2048]{1,0:T(8,128)(2,1)S(1)} %copy-done.68), kind=kOutput, calls=%fused_computation.19 | convolution fusion | flops 4316987392 | bytes 20971520 | tf_op jit(solution)/shard_map/dot_general | solution.py:35
  671.3 9.3 fusion.120
  707.8 14.6 %collective-permute-done.60 = bf16[128,2048]{1,0:T(8,128)(2,1)S(1)} collective-permute-done((bf16[128,2048]{1,0:T(8,128)(2,1)S(1)}, bf16[128,2048]{1,0:T(8,128)(2,1)S(1)}, u32[]{:S(2)}, u32[]{:S(2)}) %collective-permute-start.60) | collective-permute-done | bytes 524320 | tf_op jit(solution)/shard_map/ppermute | solution.py:294
  722.4 20.8 %collective-permute-done.58 = bf16[128,2048]{1,0:T(8,128)(2,1)S(1)} collective-permute-done((bf16[128,2048]{1,0:T(8,128)(2,1)S(1)}, bf16[128,2048]{1,0:T(8,128)(2,1)S(1)}, u32[]{:S(2)}, u32[]{:S(2)}) %collective-permute-start.58) | collective-permute-done | bytes 524320 | tf_op jit(solution)/shard_map/ppermute | solution.py:294
  753.6 10.2 collective-permute-done.61
  764.0 21.2 %collective-permute-done.62 = bf16[128,2048]{1,0:T(8,128)(2,1)S(1)} collective-permute-done((bf16[128,2048]{1,0:T(8,128)(2,1)S(1)}, bf16[128,2048]{1,0:T(8,128)(2,1)S(1)}, u32[]{:S(2)}, u32[]{:S(2)}) %collective-permute-start.62) | collective-permute-done | bytes 524320 | tf_op jit(solution)/shard_map/ppermute | solution.py:294
  812.7 9.1 collective-permute-start.70
  833.8 22.7 %collective-permute-done.83 = bf16[4,2,128,256]{3,2,1,0:T(8,128)(2,1)S(1)} collective-permute-done((bf16[4,2,128,256]{3,2,1,0:T(8,128)(2,1)S(1)}, bf16[4,2,128,256]{3,2,1,0:T(8,128)(2,1)S(1)}, u32[]{:S(2)}, u32[]{:S(2)}) %collective-permute-start.83) | collective-permute-done | bytes 524320 | tf_op jit(solution)/shard_map/ppermute | solution.py:286
  883.1 61.5 %reduce-scatter.4.cloned.1.call-done = f32[128,2]{1,0:T(8,128)} async-done(((f32[2048,2]{1,0:T(8,128)}), f32[128,2]{1,0:T(8,128)}) %reduce-scatter.4.cloned.1.call-update) | async-done | bytes 1040
  998.9 30.3 %all-to-all-done.9 = bf16[8,128,2,512]{3,2,1,0:T(2,128)(2,1)} async-done(((bf16[8,128,2,512]{3,2,1,0:T(2,128)(2,1)}), bf16[8,128,2,512]{3,2,1,0:T(2,128)(2,1)}, u32[]{:S(2)}, u32[]{:S(2)}) %all-to-all-start.9) | async-done | bytes 2097184 | tf_op jit(solution)/shard_map/all_to_all | solution.py:358
  1061.7 18.3 %collective-permute-done.74 = bf16[128,2048]{1,0:T(8,128)(2,1)} collective-permute-done((bf16[128,2048]{1,0:T(8,128)(2,1)}, bf16[128,2048]{1,0:T(8,128)(2,1)}, u32[]{:S(2)}, u32[]{:S(2)}) %collective-permute-start.74) | collective-permute-done | bytes 524320 | tf_op jit(solution)/shard_map/ppermute | solution.py:294
  1081.5 14.0 %collective-permute-done.78 = bf16[128,2048]{1,0:T(8,128)(2,1)} collective-permute-done((bf16[128,2048]{1,0:T(8,128)(2,1)}, bf16[128,2048]{1,0:T(8,128)(2,1)}, u32[]{:S(2)}, u32[]{:S(2)}) %collective-permute-start.78) | collective-permute-done | bytes 524320 | tf_op jit(solution)/shard_map/ppermute | solution.py:294
  1095.5 32.1 %collective-permute-done.76 = bf16[128,2048]{1,0:T(8,128)(2,1)} collective-permute-done((bf16[128,2048]{1,0:T(8,128)(2,1)}, bf16[128,2048]{1,0:T(8,128)(2,1)}, u32[]{:S(2)}, u32[]{:S(2)}) %collective-permute-start.76) | collective-permute-done | bytes 524320 | tf_op jit(solution)/shard_map/ppermute | solution.py:294
  1168.7 25.3 %collective-permute-done.92 = bf16[128,8192]{1,0:T(8,128)(2,1)} collective-permute-done((bf16[128,8192]{1,0:T(8,128)(2,1)}, bf16[128,8192]{1,0:T(8,128)(2,1)}, u32[]{:S(2)}, u32[]{:S(2)}) %collective-permute-start.92) | collective-permute-done | bytes 2097184 | tf_op jit(solution)/shard_map/ppermute | solution.py:290
  1198.1 39.1 %collective-permute-done.90 = bf16[128,8192]{1,0:T(8,128)(2,1)S(1)} collective-permute-done((bf16[128,8192]{1,0:T(8,128)(2,1)}, bf16[128,8192]{1,0:T(8,128)(2,1)S(1)}, u32[]{:S(2)}, u32[]{:S(2)}) %collective-permute-start.90) | collective-permute-done | bytes 2097184 | tf_op jit(solution)/shard_map/ppermute | solution.py:290
  (583 shorter events, 521.9 us)
Async XLA Ops:
  19.7 57.8 %all-to-all-start.2 = ((bf16[8,128,2,128]{3,1,2,0:T(8,128)(2,1)}), bf16[8,128,2,128]{3,1,2,0:T(8,128)(2,1)}, u32[]{:S(2)}, u32[]{:S(2)}) async-start(bf16[8,128,2,128]{3,1,2,0:T(8,128)(2,1)} %bitcast.33), calls=%async_computation.2 | async-start | bytes 1048576 | tf_op jit(solution)/shard_map/all_to_all | solution.py:333
  39.0 71.6 %collective-permute-start.3 = (bf16[128,2048]{1,0:T(8,128)(2,1)S(1)}, bf16[128,2048]{1,0:T(8,128)(2,1)}, u32[]{:S(2)}, u32[]{:S(2)}) collective-permute-start(bf16[128,2048]{1,0:T(8,128)(2,1)S(1)} %copy-done.30), channel_id=1, source_target_pairs={{0,1},{1,0},{2,3},{3,2},{4,5},{5,4},{6,7},{7,6},{8,9},{9,8},{10,11... | collective-permute-start | bytes 1572872 | tf_op jit(solution)/shard_map/ppermute | solution.py:282
  73.3 58.1 %collective-permute-start.5 = (bf16[128,2048]{1,0:T(8,128)(2,1)S(1)}, bf16[128,2048]{1,0:T(8,128)(2,1)}, u32[]{:S(2)}, u32[]{:S(2)}) collective-permute-start(bf16[128,2048]{1,0:T(8,128)(2,1)S(1)} %collective-permute-done.1), channel_id=1, source_target_pairs={{0,1},{1,0},{2,3},{3,2},{4,5},{5,4},{6,7},{7,6},{8,9},{9,8},{10,11... | collective-permute-start | bytes 1572872 | tf_op jit(solution)/shard_map/ppermute | solution.py:282
  73.3 55.6 %collective-permute-start.4 = (bf16[128,2048]{1,0:T(8,128)(2,1)S(1)}, bf16[128,2048]{1,0:T(8,128)(2,1)}, u32[]{:S(2)}, u32[]{:S(2)}) collective-permute-start(bf16[128,2048]{1,0:T(8,128)(2,1)S(1)} %collective-permute-done), channel_id=1, source_target_pairs={{0,1},{1,0},{2,3},{3,2},{4,5},{5,4},{6,7},{7,6},{8,9},{9,8},{10,11... | collective-permute-start | bytes 1572872 | tf_op jit(solution)/shard_map/ppermute | solution.py:282
  75.3 58.0 %collective-permute-start.6 = (bf16[128,2048]{1,0:T(8,128)(2,1)}, bf16[128,2048]{1,0:T(8,128)(2,1)}, u32[]{:S(2)}, u32[]{:S(2)}) collective-permute-start(bf16[128,2048]{1,0:T(8,128)(2,1)} %collective-permute-done.2), channel_id=1, source_target_pairs={{0,1},{1,0},{2,3},{3,2},{4,5},{5,4},{6,7},{7,6},{8,9},{9,8},{10,11... | collective-permute-start | bytes 1572872 | tf_op jit(solution)/shard_map/ppermute | solution.py:282
  124.0 85.4 %all-to-all-start.4 = ((bf16[8,128,2,512]{3,1,2,0:T(8,128)(2,1)}), bf16[8,128,2,512]{3,1,2,0:T(8,128)(2,1)}, u32[]{:S(2)}, u32[]{:S(2)}) async-start(bf16[8,128,2,512]{3,1,2,0:T(8,128)(2,1)} %bitcast.66), calls=%async_computation.4 | async-start | bytes 4194304 | tf_op jit(solution)/shard_map/all_to_all | solution.py:333
  203.1 121.0 %collective-permute-start.39 = (bf16[512,2048]{1,0:T(8,128)(2,1)}, bf16[512,2048]{1,0:T(8,128)(2,1)}, u32[]{:S(2)}, u32[]{:S(2)}) collective-permute-start(bf16[512,2048]{1,0:T(8,128)(2,1)} %param.25), channel_id=1, source_target_pairs={{0,2},{1,3},{2,0},{3,1},{4,6},{5,7},{6,4},{7,5},{8,10},{9,11},{10,... | collective-permute-start | bytes 6291464 | tf_op jit(solution)/shard_map/ppermute | solution.py:286
  209.2 88.5 %collective-permute-start.23 = (bf16[128,2048]{1,0:T(8,128)(2,1)}, bf16[128,2048]{1,0:T(8,128)(2,1)S(1)}, u32[]{:S(2)}, u32[]{:S(2)}) collective-permute-start(bf16[128,2048]{1,0:T(8,128)(2,1)} %get-tuple-element.64), channel_id=1, source_target_pairs={{0,1},{1,0},{2,3},{3,2},{4,5},{5,4},{6,7},{7,6},{8,9},{9,8},{10,11... | collective-permute-start | bytes 1572872 | tf_op jit(solution)/shard_map/ppermute | solution.py:282
  209.4 160.3 %all-to-all-start.3 = ((bf16[8,128,2,512]{3,1,2,0:T(8,128)(2,1)}), bf16[8,128,2,512]{3,1,2,0:T(8,128)(2,1)}, u32[]{:S(2)}, u32[]{:S(2)}) async-start(bf16[8,128,2,512]{3,1,2,0:T(8,128)(2,1)} %bitcast.60), calls=%async_computation.3 | async-start | bytes 4194304 | tf_op jit(solution)/shard_map/all_to_all | solution.py:333
  216.7 81.0 %collective-permute-start.25 = (bf16[128,2048]{1,0:T(8,128)(2,1)S(1)}, bf16[128,2048]{1,0:T(8,128)(2,1)S(1)}, u32[]{:S(2)}, u32[]{:S(2)}) collective-permute-start(bf16[128,2048]{1,0:T(8,128)(2,1)S(1)} %get-tuple-element.43), channel_id=1, source_target_pairs={{0,12},{1,13},{2,14},{3,15},{4,0},{5,1},{6,2},{7,3},{8,4},{9,5},{1... | collective-permute-start | bytes 1572872 | tf_op jit(solution)/shard_map/ppermute | solution.py:294
  220.4 77.3 %collective-permute-start.29 = (bf16[128,2048]{1,0:T(8,128)(2,1)S(1)}, bf16[128,2048]{1,0:T(8,128)(2,1)S(1)}, u32[]{:S(2)}, u32[]{:S(2)}) collective-permute-start(bf16[128,2048]{1,0:T(8,128)(2,1)S(1)} %get-tuple-element.44), channel_id=1, source_target_pairs={{0,4},{1,5},{2,6},{3,7},{4,8},{5,9},{6,10},{7,11},{8,12},{9,13},{1... | collective-permute-start | bytes 1572872 | tf_op jit(solution)/shard_map/ppermute | solution.py:294
  220.4 87.2 %collective-permute-start.27 = (bf16[128,2048]{1,0:T(8,128)(2,1)S(1)}, bf16[128,2048]{1,0:T(8,128)(2,1)S(1)}, u32[]{:S(2)}, u32[]{:S(2)}) collective-permute-start(bf16[128,2048]{1,0:T(8,128)(2,1)S(1)} %get-tuple-element.45), channel_id=1, source_target_pairs={{0,8},{1,9},{2,10},{3,11},{4,12},{5,13},{6,14},{7,15},{8,0},{9,1},... | collective-permute-start | bytes 1572872 | tf_op jit(solution)/shard_map/ppermute | solution.py:294
  369.3 48.9 %collective-permute-start.38 = (bf16[8,128,2,512]{3,1,2,0:T(8,128)(2,1)}, bf16[8,128,2,512]{3,1,2,0:T(8,128)(2,1)}, u32[]{:S(2)}, u32[]{:S(2)}) collective-permute-start(bf16[8,128,2,512]{3,1,2,0:T(8,128)(2,1)} %all-to-all-done.4), channel_id=1, source_target_pairs={{0,2},{1,3},{2,0},{3,1},{4,6},{5,7},{6,4},{7,5},{8,10},{9,11},{10,... | collective-permute-start | bytes 6291464 | tf_op jit(solution)/shard_map/ppermute | solution.py:286
  369.7 91.7 %collective-permute-start.37 = (bf16[8,128,2,512]{3,1,2,0:T(8,128)(2,1)}, bf16[8,128,2,512]{3,1,2,0:T(8,128)(2,1)S(1)}, u32[]{:S(2)}, u32[]{:S(2)}) collective-permute-start(bf16[8,128,2,512]{3,1,2,0:T(8,128)(2,1)} %all-to-all-done.3), channel_id=1, source_target_pairs={{0,2},{1,3},{2,0},{3,1},{4,6},{5,7},{6,4},{7,5},{8,10},{9,11},{10,... | collective-permute-start | bytes 6291464 | tf_op jit(solution)/shard_map/ppermute | solution.py:286
  535.2 47.3 %collective-permute-start.44 = (bf16[128,2048]{1,0:T(8,128)(2,1)S(1)}, bf16[128,2048]{1,0:T(8,128)(2,1)S(1)}, u32[]{:S(2)}, u32[]{:S(2)}) collective-permute-start(bf16[128,2048]{1,0:T(8,128)(2,1)S(1)} %get-tuple-element.42), channel_id=1, source_target_pairs={{0,8},{1,9},{2,10},{3,11},{4,12},{5,13},{6,14},{7,15},{8,0},{9,1},... | collective-permute-start | bytes 1572872 | tf_op jit(solution)/shard_map/ppermute | solution.py:294
  662.4 305.6 %collective-permute-start.93 = (bf16[512,2048]{1,0:T(8,128)(2,1)}, bf16[512,2048]{1,0:T(8,128)(2,1)}, u32[]{:S(2)}, u32[]{:S(2)}) collective-permute-start(bf16[512,2048]{1,0:T(8,128)(2,1)} %select_convert_fusion), channel_id=1, source_target_pairs={{0,2},{1,3},{2,0},{3,1},{4,6},{5,7},{6,4},{7,5},{8,10},{9,11},{10,... | collective-permute-start | bytes 6291464 | tf_op jit(solution)/shard_map/ppermute | solution.py:286
  751.6 193.9 %collective-permute-start.91 = (bf16[4,2,128,1024]{3,2,1,0:T(8,128)(2,1)}, bf16[4,2,128,1024]{3,2,1,0:T(8,128)(2,1)}, u32[]{:S(2)}, u32[]{:S(2)}) collective-permute-start(bf16[4,2,128,1024]{3,2,1,0:T(8,128)(2,1)} %fusion.13), channel_id=1, source_target_pairs={{0,2},{1,3},{2,0},{3,1},{4,6},{5,7},{6,4},{7,5},{8,10},{9,11},{10,... | collective-permute-start | bytes 6291464 | tf_op jit(solution)/shard_map/ppermute | solution.py:286
  752.0 208.0 %collective-permute-start.89 = (bf16[4,2,128,1024]{3,2,1,0:T(8,128)(2,1)}, bf16[4,2,128,1024]{3,2,1,0:T(8,128)(2,1)}, u32[]{:S(2)}, u32[]{:S(2)}) collective-permute-start(bf16[4,2,128,1024]{3,2,1,0:T(8,128)(2,1)} %fusion.12), channel_id=1, source_target_pairs={{0,2},{1,3},{2,0},{3,1},{4,6},{5,7},{6,4},{7,5},{8,10},{9,11},{10,... | collective-permute-start | bytes 6291464 | tf_op jit(solution)/shard_map/ppermute | solution.py:286
  867.9 85.7 %collective-permute-start.81 = (bf16[4,2,128,256]{3,2,1,0:T(8,128)(2,1)S(1)}, bf16[4,2,128,256]{3,2,1,0:T(8,128)(2,1)}, u32[]{:S(2)}, u32[]{:S(2)}) collective-permute-start(bf16[4,2,128,256]{3,2,1,0:T(8,128)(2,1)S(1)} %fusion.65), channel_id=1, source_target_pairs={{0,2},{1,3},{2,0},{3,1},{4,6},{5,7},{6,4},{7,5},{8,10},{9,11},{10,... | collective-permute-start | bytes 1572872 | tf_op jit(solution)/shard_map/ppermute | solution.py:286
  878.1 78.3 %all-to-all-start.5 = ((bf16[8,128,2,128]{3,2,1,0:T(2,128)(2,1)}), bf16[8,128,2,128]{3,2,1,0:T(2,128)(2,1)S(1)}, u32[]{:S(2)}, u32[]{:S(2)}) async-start(bf16[8,128,2,128]{3,2,1,0:T(2,128)(2,1)} %reshape.390), calls=%async_computation.5 | async-start | bytes 1048576 | tf_op jit(solution)/shard_map/all_to_all | solution.py:358
  881.6 62.9 %reduce-scatter.4.cloned.1.call-start = ((), (), s32[]{:S(2)}) async-start(), calls=%async_computation.11 | async-start | bytes 1114112
  975.3 53.9 %all-to-all-start.9 = ((bf16[8,128,2,512]{3,2,1,0:T(2,128)(2,1)}), bf16[8,128,2,512]{3,2,1,0:T(2,128)(2,1)}, u32[]{:S(2)}, u32[]{:S(2)}) async-start(bf16[8,128,2,512]{3,2,1,0:T(2,128)(2,1)} %reshape.402), calls=%async_computation.9 | async-start | bytes 4194304 | tf_op jit(solution)/shard_map/all_to_all | solution.py:358
  985.9 47.7 %collective-permute-start.85 = (bf16[128,2048]{1,0:T(8,128)(2,1)}, bf16[128,2048]{1,0:T(8,128)(2,1)}, u32[]{:S(2)}, u32[]{:S(2)}) collective-permute-start(bf16[128,2048]{1,0:T(8,128)(2,1)} %select_convert_fusion.3), channel_id=1, source_target_pairs={{0,2},{1,3},{2,0},{3,1},{4,6},{5,7},{6,4},{7,5},{8,10},{9,11},{10,... | collective-permute-start | bytes 1572872 | tf_op jit(solution)/shard_map/ppermute | solution.py:286
  998.3 62.8 %collective-permute-start.72 = (bf16[128,2048]{1,0:T(8,128)(2,1)}, bf16[128,2048]{1,0:T(8,128)(2,1)}, u32[]{:S(2)}, u32[]{:S(2)}) collective-permute-start(bf16[128,2048]{1,0:T(8,128)(2,1)} %get-tuple-element.46), channel_id=1, source_target_pairs={{0,1},{1,0},{2,3},{3,2},{4,5},{5,4},{6,7},{7,6},{8,9},{9,8},{10,11... | collective-permute-start | bytes 1572872 | tf_op jit(solution)/shard_map/ppermute | solution.py:282
  1029.2 123.0 %all-to-all-start.8 = ((bf16[8,128,2,512]{3,2,1,0:T(2,128)(2,1)}), bf16[8,128,2,512]{3,2,1,0:T(2,128)(2,1)}, u32[]{:S(2)}, u32[]{:S(2)}) async-start(bf16[8,128,2,512]{3,2,1,0:T(2,128)(2,1)} %reshape.399), calls=%async_computation.8 | async-start | bytes 4194304 | tf_op jit(solution)/shard_map/all_to_all | solution.py:358
  1044.3 51.1 %collective-permute-start.78 = (bf16[128,2048]{1,0:T(8,128)(2,1)}, bf16[128,2048]{1,0:T(8,128)(2,1)}, u32[]{:S(2)}, u32[]{:S(2)}) collective-permute-start(bf16[128,2048]{1,0:T(8,128)(2,1)} %get-tuple-element.33), channel_id=1, source_target_pairs={{0,4},{1,5},{2,6},{3,7},{4,8},{5,9},{6,10},{7,11},{8,12},{9,13},{1... | collective-permute-start | bytes 1572872 | tf_op jit(solution)/shard_map/ppermute | solution.py:294
  1044.5 83.1 %collective-permute-start.76 = (bf16[128,2048]{1,0:T(8,128)(2,1)}, bf16[128,2048]{1,0:T(8,128)(2,1)}, u32[]{:S(2)}, u32[]{:S(2)}) collective-permute-start(bf16[128,2048]{1,0:T(8,128)(2,1)} %get-tuple-element.34), channel_id=1, source_target_pairs={{0,8},{1,9},{2,10},{3,11},{4,12},{5,13},{6,14},{7,15},{8,0},{9,1},... | collective-permute-start | bytes 1572872 | tf_op jit(solution)/shard_map/ppermute | solution.py:294
  1049.9 114.4 %collective-permute-start.94 = (bf16[512,2048]{1,0:T(8,128)(2,1)S(1)}, bf16[512,2048]{1,0:T(8,128)(2,1)}, u32[]{:S(2)}, u32[]{:S(2)}) collective-permute-start(bf16[512,2048]{1,0:T(8,128)(2,1)S(1)} %copy-done.10), channel_id=1, source_target_pairs={{0,16},{16,0},{1,17},{17,1},{2,18},{18,2},{3,19},{19,3},{4,20},{20... | collective-permute-start | bytes 6291464 | tf_op jit(solution)/shard_map/ppermute | solution.py:290
  1061.2 84.4 %collective-permute-start.84 = (bf16[128,2048]{1,0:T(8,128)(2,1)}, bf16[128,2048]{1,0:T(8,128)(2,1)}, u32[]{:S(2)}, u32[]{:S(2)}) collective-permute-start(bf16[128,2048]{1,0:T(8,128)(2,1)} %reshape.398), channel_id=1, source_target_pairs={{0,16},{16,0},{1,17},{17,1},{2,18},{18,2},{3,19},{19,3},{4,20},{20... | collective-permute-start | bytes 1572872 | tf_op jit(solution)/shard_map/ppermute | solution.py:290
  1080.0 67.8 %collective-permute-start.80 = (bf16[128,2048]{1,0:T(8,128)(2,1)}, bf16[128,2048]{1,0:T(8,128)(2,1)}, u32[]{:S(2)}, u32[]{:S(2)}) collective-permute-start(bf16[128,2048]{1,0:T(8,128)(2,1)} %reshape.392), channel_id=1, source_target_pairs={{0,16},{16,0},{1,17},{17,1},{2,18},{18,2},{3,19},{19,3},{4,20},{20... | collective-permute-start | bytes 1572872 | tf_op jit(solution)/shard_map/ppermute | solution.py:290
  1145.1 48.9 %collective-permute-start.92 = (bf16[128,8192]{1,0:T(8,128)(2,1)}, bf16[128,8192]{1,0:T(8,128)(2,1)}, u32[]{:S(2)}, u32[]{:S(2)}) collective-permute-start(bf16[128,8192]{1,0:T(8,128)(2,1)} %reshape.404), channel_id=1, source_target_pairs={{0,16},{16,0},{1,17},{17,1},{2,18},{18,2},{3,19},{19,3},{4,20},{20... | collective-permute-start | bytes 6291464 | tf_op jit(solution)/shard_map/ppermute | solution.py:290
  1162.8 74.3 %collective-permute-start.90 = (bf16[128,8192]{1,0:T(8,128)(2,1)}, bf16[128,8192]{1,0:T(8,128)(2,1)S(1)}, u32[]{:S(2)}, u32[]{:S(2)}) collective-permute-start(bf16[128,8192]{1,0:T(8,128)(2,1)} %reshape.401), channel_id=1, source_target_pairs={{0,16},{16,0},{1,17},{17,1},{2,18},{18,2},{3,19},{19,3},{4,20},{20... | collective-permute-start | bytes 6291464 | tf_op jit(solution)/shard_map/ppermute | solution.py:290
  (164 other events, 3202.0 us)
Sparse Core Ops, SparseCore 0:
  886.6 57.8 reduce-scatter.3

commit v2 on v1

--- a/solution.py
+++ b/solution.py
@@ -3,6 +3,8 @@
 import jax
 import jax.numpy as jnp
 from jax import lax
+from jax.experimental import pallas as pl
+from jax.experimental.pallas import tpu as pltpu
 from jax.sharding import PartitionSpec as P
 
 HEADS = 16
@@ -298,28 +300,9 @@
     return [[line * 4 + pair * 2 + core for line in range(4) for core in range(2)] for pair in range(2)]
 
 
-def gather_tokens(block):
-    mine = [block] + [line_shift(block, steps) for steps in range(1, LINE)]
-    return jnp.stack(mine + [core_swap(piece) for piece in mine])
-
-
-def scatter_tokens(parts):
-    theirs = [core_swap(parts[LINE + k].astype(jnp.bfloat16)) for k in range(LINE)]
-    joint = [parts[k] + theirs[k].astype(jnp.float32) for k in range(LINE)]
-    total = joint[0]
-    for k in range(1, LINE):
-        total = total + line_shift(joint[k].astype(jnp.bfloat16), -k).astype(jnp.float32)
-    return total
-
-
 def group_sum(values):
-    count, tokens = values.shape
-    split = values.reshape(count, 2, LINE, tokens // (2 * LINE))
-    both = split + core_swap(split)[:, ::-1]
-    total = both
-    for steps in range(1, LINE):
-        total = total + jnp.roll(line_shift(both, steps), steps, axis=2)
-    return total.reshape(count, tokens)
+    both = values + core_swap(values)
+    return both + line_shift(both, 1) + line_shift(both, 2) + line_shift(both, 3)
 
 
 def by_pair(pair, own, other):
@@ -362,6 +345,521 @@
 def reduce_rows_of(partial, pair):
     half = partial.shape[0] // 2
     return rep_total(pair_total(partial[:half], partial[half:], pair))
+
+
+MESH_ID = pl.DeviceIdType.MESH
+
+
+class Line:
+    def __init__(self):
+        index = lax.axis_index("shard")
+        self.rep = lax.axis_index("rep")
+        self.place = index // 4
+        self.pair = (index // 2) % 2
+        self.core = index % 2
+        self.block = self.place * 2 + self.core
+        self.sibling = self.at(self.place, self.pair, 1 - self.core)
+        self.right = self.at(jnp.minimum(self.place + 1, LINE - 1), self.pair, self.core)
+        self.left = self.at(jnp.maximum(self.place - 1, 0), self.pair, self.core)
+        self.across = self.at(self.place, 1 - self.pair, self.core)
+        self.partner = (1 - self.rep, index)
+        self.has_right = self.place < LINE - 1
+        self.has_left = self.place > 0
+
+    def at(self, place, pair, core):
+        return (self.rep, place * 4 + pair * 2 + core)
+
+    def piece(self, p, sign):
+        return (self.place + sign * (p // 2) + LINE) % LINE, (self.core + p % 2) % 2
+
+    def meet(self, wide):
+        barrier = pltpu.get_barrier_semaphore()
+
+        def greet(device):
+            pl.semaphore_signal(barrier, inc=1, device_id=device, device_id_type=MESH_ID)
+
+        if wide:
+            for p in range(1, 2 * LINE):
+                place, core = self.piece(p, 1)
+                greet(self.at(place, self.pair, core))
+            greet(self.across)
+            greet(self.partner)
+            pl.semaphore_wait(barrier, 2 * LINE + 1)
+            return
+        greet(self.sibling)
+        pl.when(self.has_right)(lambda: greet(self.right))
+        pl.when(self.has_left)(lambda: greet(self.left))
+        pl.semaphore_wait(
+            barrier, 1 + self.has_right.astype(jnp.int32) + self.has_left.astype(jnp.int32)
+        )
+
+
+def remote(source, target, send_sem, recv_sem, device):
+    return pltpu.make_async_remote_copy(
+        src_ref=source,
+        dst_ref=target,
+        send_sem=send_sem,
+        recv_sem=recv_sem,
+        device_id=device,
+        device_id_type=MESH_ID,
+    )
+
+
+class Spread:
+    SEMAPHORES = ((2 * LINE,),) * 4 + ((2 * LINE, 2),) * 2
+
+    def __init__(self, line, sources, target, sems):
+        self.line, self.sources, self.target = line, sources, target
+        self.z_send, self.z_recv, self.y_send, self.y_recv, self.x_send, self.x_recv = sems
+        self.half = sources[0].shape[0] // 2
+
+    def rows(self, place, pair, core, rep):
+        start = ((place * 4 + pair * 2 + core) * 2 + rep) * self.half
+        return self.target.at[pl.ds(pl.multiple_of(start, self.half), self.half), :]
+
+    def start(self, p):
+        line, half = self.line, self.half
+        place, core = line.piece(p, 1)
+        here = self.rows(line.place, line.pair, line.core, line.rep)
+        mine = pl.ds(pl.multiple_of(line.rep * half, half), half)
+        at = 0
+        for source in self.sources:
+            n = source.shape[1] // 16
+            for q in range(2):
+                column = pl.multiple_of((place * 4 + q * 2 + core) * n, n)
+                piece, goal = source.at[mine, pl.ds(column, n)], here.at[:, pl.ds(at, n)]
+                if p == 0:
+                    pltpu.make_async_copy(piece, goal, self.z_recv.at[0]).start()
+                else:
+                    remote(
+                        piece, goal, self.z_send.at[p], self.z_recv.at[p], line.at(place, line.pair, core)
+                    ).start()
+                at += n
+
+    def cross(self, p, pair):
+        place, core = self.line.piece(p, -1)
+        ref = self.rows(place, pair, core, self.line.rep)
+        return remote(ref, ref, self.y_send.at[p], self.y_recv.at[p], self.line.across)
+
+    def over(self, p, pair, rep, which):
+        place, core = self.line.piece(p, -1)
+        ref = self.rows(place, pair, core, rep)
+        return remote(ref, ref, self.x_send.at[p, which], self.x_recv.at[p, which], self.line.partner)
+
+    def came(self, p):
+        line = self.line
+        place, core = line.piece(p, -1)
+        ref = self.rows(place, line.pair, core, line.rep)
+        if p == 0:
+            pltpu.make_async_copy(ref, ref, self.z_recv.at[0]).wait()
+        else:
+            remote(ref, ref, self.z_send.at[p], self.z_recv.at[p], line.sibling).wait_recv()
+        self.cross(p, line.pair).start()
+        self.over(p, line.pair, line.rep, 0).start()
+
+    def onward(self, p):
+        line = self.line
+        self.cross(p, 1 - line.pair).wait_recv()
+        self.over(p, 1 - line.pair, line.rep, 1).start()
+
+    def finish(self):
+        line = self.line
+        for p in range(2 * LINE):
+            if p > 0:
+                ref = self.rows(line.place, line.pair, line.core, line.rep)
+                remote(ref, ref, self.z_send.at[p], self.z_recv.at[p], line.sibling).wait_send()
+            self.cross(p, line.pair).wait_send()
+            for which, pair in ((0, line.pair), (1, 1 - line.pair)):
+                self.over(p, pair, line.rep, which).wait_send()
+                self.over(p, pair, 1 - line.rep, which).wait_recv()
+
+
+class Stack:
+    SEMAPHORES = ((3,),)
+
+    def __init__(self, line, source, target, sems):
+        self.line, self.sems = line, sems[0]
+        self.source = source
+        size = source.shape[0]
+        self.mine = target.at[pl.ds(pl.multiple_of(line.pair * size, size), size), :]
+
+    def here(self):
+        return pltpu.make_async_copy(self.source, self.mine, self.sems.at[0])
+
+    def there(self):
+        return remote(self.source, self.mine, self.sems.at[1], self.sems.at[2], self.line.across)
+
+    def start(self):
+        self.there().start()
+        self.here().start()
+
+    def finish(self):
+        self.here().wait()
+        self.there().wait()
+
+
+def line_scatter_joint(line, k, rows, parts, sib):
+    return parts[2 * k + line.core, rows, :].astype(jnp.float32) + sib[k, rows, :].astype(jnp.float32)
+
+
+def line_scatter_pass(line, j, step, way, parts, sib, sums, came, sib_recv, send_sem, came_sem):
+    rows = pl.ds(pl.multiple_of(j * step, step), step)
+    device = line.right if way == 0 else line.left
+    ends = line.place == 0 if way == 0 else line.place == LINE - 1
+
+    def copy(k):
+        return remote(sums.at[k, rows], came.at[k, rows], send_sem.at[k, j], came_sem.at[k, j], device)
+
+    for k in range(LINE - 1, 0, -1) if way == 0 else range(LINE - 1):
+
+        @pl.when(line.place < k if way == 0 else line.place > k)
+        def _():
+            remote(
+                parts.at[2 * k + line.core, rows], sib.at[k, rows], sib_recv.at[k, j], sib_recv.at[k, j], line.sibling
+            ).wait_recv()
+
+            @pl.when(ends)
+            def _():
+                sums[k, rows, :] = line_scatter_joint(line, k, rows, parts, sib).astype(jnp.bfloat16)
+
+            @pl.when(jnp.logical_not(ends))
+            def _():
+                copy(k).wait_recv()
+                sums[k, rows, :] = (
+                    line_scatter_joint(line, k, rows, parts, sib) + came[k, rows, :].astype(jnp.float32)
+                ).astype(jnp.bfloat16)
+
+            copy(k).start()
+
+
+def line_scatter_total(line, j, step, parts, sib, rights, lefts, sums, sib_recv, sends, right_recv, left_recv):
+    rows = pl.ds(pl.multiple_of(j * step, step), step)
+    me = line.place
+    remote(
+        parts.at[2 * me + line.core, rows], sib.at[me, rows], sib_recv.at[me, j], sib_recv.at[me, j], line.sibling
+    ).wait_recv()
+
+    @pl.when(line.has_left)
+    def _():
+        remote(sums.at[me, rows], rights.at[me, rows], sends.at[me, j], right_recv.at[me, j], line.left).wait_recv()
+
+    @pl.when(line.has_right)
+    def _():
+        remote(sums.at[me, rows], lefts.at[me, rows], sends.at[me, j], left_recv.at[me, j], line.right).wait_recv()
+
+    total = line_scatter_joint(line, me, rows, parts, sib)
+    total = total + jnp.where(line.has_left, rights[me, rows, :].astype(jnp.float32), 0.0)
+    return total + jnp.where(line.has_right, lefts[me, rows, :].astype(jnp.float32), 0.0)
+
+
+def line_scatter_start(line, pieces, step, parts, sib, sib_send, sib_recv):
+    def piece(j, carry):
+        rows = pl.ds(pl.multiple_of(j * step, step), step)
+        for k in range(LINE):
+            remote(
+                parts.at[2 * k + 1 - line.core, rows],
+                sib.at[k, rows],
+                sib_send.at[k, j],
+                sib_recv.at[k, j],
+                line.sibling,
+            ).start()
+        return carry
+
+    lax.fori_loop(0, pieces, piece, 0)
+
+
+def line_scatter_end(line, pieces, step, parts, sib, rights, lefts, sums, sib_send, right_send, left_send):
+    def piece(j, carry):
+        rows = pl.ds(pl.multiple_of(j * step, step), step)
+        for k in range(LINE):
+            remote(
+                parts.at[2 * k + 1 - line.core, rows],
+                sib.at[k, rows],
+                sib_send.at[k, j],
+                sib_send.at[k, j],
+                line.sibling,
+            ).wait_send()
+
+            @pl.when(line.place < k)
+            def _():
+                remote(
+                    sums.at[k, rows], rights.at[k, rows], right_send.at[k, j], right_send.at[k, j], line.right
+                ).wait_send()
+
+            @pl.when(line.place > k)
+            def _():
+                remote(
+                    sums.at[k, rows], lefts.at[k, rows], left_send.at[k, j], left_send.at[k, j], line.left
+                ).wait_send()
+
+        return carry
+
+    lax.fori_loop(0, pieces, piece, 0)
+
+
+def gather_copy(line, k, j, step, core, gathered, way, sends, recvs):
+    rows = pl.ds(pl.multiple_of(j * step, step), step)
+    block = 2 * k + core
+    device = (line.right, line.left, line.sibling)[way]
+    ref = gathered.at[block, rows]
+    return remote(ref, ref, sends.at[k, way, j], recvs.at[block, j], device)
+
+
+def line_gather_own(line, j, step, gathered, sends, recvs):
+    def copy(way):
+        return gather_copy(line, line.place, j, step, line.core, gathered, way, sends, recvs)
+
+    pl.when(line.has_right)(lambda: copy(0).start())
+    pl.when(line.has_left)(lambda: copy(1).start())
+    copy(2).start()
+
+
+def line_gather_pass(line, hop, j, step, gathered, sends, recvs):
+    for way in (0, 1):
+        k = line.place - hop if way == 0 else line.place + hop
+        there = k >= 0 if way == 0 else k < LINE
+        onward = line.has_right if way == 0 else line.has_left
+        k = jnp.clip(k, 0, LINE - 1)
+
+        @pl.when(there)
+        def _():
+            gather_copy(line, k, j, step, line.core, gathered, way, sends, recvs).wait_recv()
+            pl.when(onward)(
+                lambda: gather_copy(line, k, j, step, line.core, gathered, way, sends, recvs).start()
+            )
+            gather_copy(line, k, j, step, line.core, gathered, 2, sends, recvs).start()
+
+
+def line_gather_end(line, pieces, step, gathered, sends, recvs):
+    def piece(j, carry):
+        for k in range(LINE):
+            gather_copy(line, k, j, step, 1 - line.core, gathered, 2, sends, recvs).wait_recv()
+            gather_copy(line, k, j, step, line.core, gathered, 2, sends, recvs).wait_send()
+
+            @pl.when((line.place >= k) & line.has_right)
+            def _():
+                gather_copy(line, k, j, step, line.core, gathered, 0, sends, recvs).wait_send()
+
+            @pl.when((line.place <= k) & line.has_left)
+            def _():
+                gather_copy(line, k, j, step, line.core, gathered, 1, sends, recvs).wait_send()
+
+        return carry
+
+    lax.fori_loop(0, pieces, piece, 0)
+
+
+def take_from(items, count):
+    taken = items[:count]
+    del items[:count]
+    return taken
+
+
+def line_call(collective_id, pieces, middle, inputs, outputs, scatter, gather, spreads=(), stacks=()):
+    block = inputs[0].shape[-2:]
+    step = block[0] // pieces
+    n_in, n_out = len(inputs), len(outputs)
+    weights = [w for group in spreads for w in group] + list(stacks)
+    n_weights, n_extra = len(weights), len(spreads) + len(stacks)
+    extras = [
+        jax.ShapeDtypeStruct((16 * group[0].shape[0], sum(w.shape[1] for w in group) // 8), jnp.bfloat16)
+        for group in spreads
+    ] + [jax.ShapeDtypeStruct((2 * w.shape[0], w.shape[1]), jnp.bfloat16) for w in stacks]
+    low = jnp.bfloat16
+    scratch = []
+    if scatter:
+        scratch += [pltpu.VMEM((LINE,) + block, low) for _ in range(4)]
+        scratch += [pltpu.SemaphoreType.DMA((LINE, pieces)) for _ in range(6)]
+    if gather:
+        scratch += [pltpu.SemaphoreType.DMA((LINE, 3, pieces)), pltpu.SemaphoreType.DMA((2 * LINE, pieces))]
+
+    n_scratch = len(scratch)
+    kinds = [Spread] * len(spreads) + [Stack] * len(stacks)
+    scratch += [pltpu.SemaphoreType.DMA(shape) for kind in kinds for shape in kind.SEMAPHORES]
+
+    def kernel(*refs):
+        refs = list(refs)
+
+        def take(count):
+            taken = refs[:count]
+            del refs[:count]
+            return taken
+
+        ins, given, outs, extra = take(n_in), take(n_weights), take(n_out), take(n_extra)
+        rest = take(n_scratch)
+        line = Line()
+        moves = []
+        for group in spreads:
+            moves.append(Spread(line, take_from(given, len(group)), extra.pop(0), take(6)))
+        heaps = [Stack(line, given.pop(0), extra.pop(0), take(1)) for _ in stacks]
+        line.meet(bool(moves or heaps))
+        if scatter:
+            sib, rights, lefts, sums, sib_send, sib_recv, right_send, left_send, right_recv, left_recv = rest[:10]
+            parts = ins[0]
+            line_scatter_start(line, pieces, step, parts, sib, sib_send, sib_recv)
+        if gather:
+            sends, recvs = rest[-2:]
+
+        def during(j, act):
+            pl.when((j >= 0) & (j < pieces))(lambda: act(j))
+
+        def finish(j):
+            rows = pl.ds(pl.multiple_of(j * step, step), step)
+            total = None
+            if scatter:
+                total = line_scatter_total(
+                    line, j, step, parts, sib, rights, lefts, sums, sib_recv, right_send, right_recv, left_recv
+                )
+            values = middle(total, rows, j, ins, outs)
+            if gather:
+                outs[0][line.block, rows, :] = values.astype(low)
+                line_gather_own(line, j, step, outs[0], sends, recvs)
+
+        def slot(t, carry):
+            if scatter:
+                during(
+                    t - line.place,
+                    lambda j: line_scatter_pass(
+                        line, j, step, 0, parts, sib, sums, rights, sib_recv, right_send, right_recv
+                    ),
+                )
+                during(
+                    t - (LINE - 1 - line.place),
+                    lambda j: line_scatter_pass(
+                        line, j, step, 1, parts, sib, sums, lefts, sib_recv, left_send, left_recv
+                    ),
+                )
+                during(t - (LINE - 1), finish)
+            if gather:
+                for hop in range(1, LINE):
+                    during(
+                        t - hop - (LINE - 1 if scatter else 0),
+                        lambda j, hop=hop: line_gather_pass(line, hop, j, step, outs[0], sends, recvs),
+                    )
+            return carry
+
+        if not scatter:
+            lax.fori_loop(0, pieces, lambda j, carry: (finish(j), carry)[1], 0)
+        hops = (LINE - 1) * (int(scatter) + int(gather))
+        if moves:
+            for t in range(pieces + hops):
+                for move in moves:
+                    if t < 2 * LINE:
+                        move.start(t)
+                    if 3 <= t < 3 + 2 * LINE:
+                        move.came(t - 3)
+                    if 6 <= t < 6 + 2 * LINE:
+                        move.onward(t - 6)
+                if t == 2:
+                    for heap in heaps:
+                        heap.start()
+                slot(t, 0)
+            for move in moves:
+                for t in range(pieces + hops, 6 + 2 * LINE):
+                    if t < 3 + 2 * LINE:
+                        move.came(t - 3)
+                    move.onward(t - 6)
+                move.finish()
+            for heap in heaps:
+                heap.finish()
+        else:
+            lax.fori_loop(0, pieces + hops, slot, 0)
+        if scatter:
+            line_scatter_end(
+                line, pieces, step, parts, sib, rights, lefts, sums, sib_send, right_send, left_send
+            )
+        if gather:
+            line_gather_end(line, pieces, step, outs[0], sends, recvs)
+
+    vmem = pl.BlockSpec(memory_space=pltpu.VMEM)
+    return pl.pallas_call(
+        kernel,
+        out_shape=[jax.ShapeDtypeStruct(shape, kind) for shape, kind in outputs] + extras,
+        in_specs=[vmem] * n_in + [pl.BlockSpec(memory_space=pl.ANY)] * n_weights,
+        out_specs=[vmem] * n_out + [pl.BlockSpec(memory_space=pl.ANY)] * n_extra,
+        scratch_shapes=scratch,
+        compiler_params=pltpu.CompilerParams(
+            collective_id=collective_id, has_side_effects=True, vmem_limit_bytes=40 << 20
+        ),
+        cost_estimate=pl.CostEstimate(flops=10_000_000, bytes_accessed=200_000_000, transcendentals=0),
+    )(*inputs, *weights)
+
+
+def gather_blocks(payload, spreads, stacks, collective_id):
+    def middle(total, rows, j, ins, outs):
+        return ins[0][rows, :]
+
+    shape = (2 * LINE,) + payload.shape
+    return line_call(collective_id, 9, middle, [payload], [(shape, jnp.bfloat16)], False, True, spreads, stacks)
+
+
+def attention_block(parts, hidden, gain, spreads, stacks, collective_id):
+    def middle(total, rows, j, ins, outs):
+        outs[1][rows, :] = total
+        resid = ins[1][rows, :].astype(jnp.float32) + total * rms_scale(total) * ins[2][...]
+        outs[2][rows, :] = resid
+        return resid
+
+    shape = hidden.shape
+    return line_call(
+        collective_id, 8, middle, [parts, hidden, gain],
+        [(parts.shape, jnp.bfloat16), (shape, jnp.float32), (shape, jnp.float32)], True, True, spreads, stacks,
+    )
+
+
+def add_rows(ref, values, j):
+    folded = jnp.sum(values.reshape(values.shape[0] // 8, 8, values.shape[1]), axis=0)
+
+    @pl.when(j == 0)
+    def _():
+        ref[...] = folded
+
+    @pl.when(j > 0)
+    def _():
+        ref[...] += folded
+
+
+def ffn_block(parts, resid, cotangent, gain, collective_id):
+    def middle(total, rows, j, ins, outs):
+        scale = rms_scale(total)
+        normed = total * scale
+        grad = ins[2][rows, :].astype(jnp.float32)
+        gains = ins[3][...]
+        outs[1][rows, :] = (ins[1][rows, :] + normed * gains).astype(jnp.bfloat16)
+        add_rows(outs[2], grad * normed, j)
+        return rms_back(grad * gains, normed, scale)
+
+    shape = resid.shape
+    return line_call(
+        collective_id, 8, middle, [parts, resid, cotangent, gain],
+        [(parts.shape, jnp.bfloat16), (shape, jnp.bfloat16), ((8, shape[1]), jnp.float32)], True, True,
+    )
+
+
+def back_block(parts, cotangent, attn_out, gain, collective_id):
+    def middle(total, rows, j, ins, outs):
+        d_resid = ins[1][rows, :].astype(jnp.float32) + total
+        outs[1][rows, :] = d_resid
+        attn = ins[2][rows, :]
+        scale = rms_scale(attn)
+        normed = attn * scale
+        add_rows(outs[2], d_resid * normed, j)
+        return rms_back(d_resid * ins[3][...], normed, scale)
+
+    shape = cotangent.shape
+    return line_call(
+        collective_id, 8, middle, [parts, cotangent, attn_out, gain],
+        [(parts.shape, jnp.bfloat16), (shape, jnp.float32), ((8, shape[1]), jnp.float32)], True, True,
+    )
+
+
+def last_block(parts, d_resid, collective_id):
+    def middle(total, rows, j, ins, outs):
+        outs[0][rows, :] = (ins[1][rows, :] + total).astype(jnp.bfloat16)
+
+    return line_call(
+        collective_id, 8, middle, [parts, d_resid], [(d_resid.shape, jnp.bfloat16)], True, False
+    )[0]
 
 
 def on_device(
@@ -387,19 +885,23 @@
     pair = (lax.axis_index("shard") // 2) % 2
     f32 = jnp.float32
 
-    docs = gather_tokens(segments)[:, 0]
-    tokens = gather_tokens(hidden_in).reshape(blocks * length, model_width)
+    extra = jnp.concatenate(
+        [query_gain, key_gain, attn_gain, ffn_gain, segments[0].astype(jnp.bfloat16)]
+    )
+    extra = jnp.pad(extra[None], ((0, 15), (0, model_width - extra.shape[0])))
+    payload, full_qkv, full_output = gather_blocks(
+        jnp.concatenate([hidden_in, extra]), [[w_query, w_key, w_value]], [w_output], 0
+    )
+    tokens = payload[:, :length].reshape(blocks * length, model_width)
+    docs = payload[:, length, 4 * length : 5 * length].astype(jnp.int32)
+    gains = payload[:, length, : 4 * length].reshape(LINE, 2, 4, length)
+    gains = jnp.stack(by_pair(pair, gains, pair_swap(gains)), axis=1)
+    gains = jnp.moveaxis(gains, 3, 0).reshape(4, 1, model_width).astype(f32)
+    gain_attn, gain_ffn = gains[2], gains[3]
     width = heads * HEAD_DIM
-    full_query = gather_columns(w_query, pair)
-    full_key = gather_columns(w_key, pair)
-    full_value = gather_columns(w_value, pair)
     head_gains = gather_rows(jnp.stack([query_gain, key_gain])[None], pair).astype(f32)
     gain_query = head_gains[:, 0].reshape(width)
     gain_key = head_gains[:, 1].reshape(width)
-    wide_gains = lax.all_gather(
-        jnp.stack([attn_gain, ffn_gain]), "shard", axis=1, tiled=True
-    ).astype(f32)
-    gain_attn, gain_ffn = wide_gains[0], wide_gains[1]
 
     earlier = jnp.sum((docs[:, None, :] < docs[:, :, None]).astype(jnp.int32), axis=2)
     positions = jnp.arange(length, dtype=jnp.int32)[None] - earlier
@@ -418,8 +920,8 @@
     def split_heads(values):
         return values.reshape(blocks, length, heads, HEAD_DIM)
 
-    query_raw = jnp.dot(tokens, full_query, preferred_element_type=f32)
-    key_raw = jnp.dot(tokens, full_key, preferred_element_type=f32)
+    all_raw = jnp.dot(tokens, full_qkv, preferred_element_type=f32)
+    query_raw, key_raw = all_raw[:, :width], all_raw[:, width : 2 * width]
     squares = group_sum(
         jnp.stack([jnp.sum(query_raw * query_raw, axis=-1), jnp.sum(key_raw * key_raw, axis=-1)])
     )
@@ -428,9 +930,7 @@
     key_unit = key_raw * head_scales[1][:, None]
     query_low = rotate(split_heads(query_unit * gain_query), cosines, sines).astype(jnp.bfloat16)
     key_low = rotate(split_heads(key_unit * gain_key), cosines, sines).astype(jnp.bfloat16)
-    value_low = split_heads(
-        jnp.dot(tokens, full_value, preferred_element_type=f32).astype(jnp.bfloat16)
-    )
+    value_low = split_heads(all_raw[:, 2 * width :].astype(jnp.bfloat16))
     scores = (
         jnp.einsum("sqhd,skhd->shqk", query_low, key_low, preferred_element_type=f32) * factor
     )
@@ -444,46 +944,46 @@
         .reshape(blocks * length, width)
         .astype(jnp.bfloat16)
     )
-    full_output = gather_rows(w_output, pair)
 
     def to_blocks(values):
-        return values.reshape(blocks, length, model_width)
-
-    attn_out = scatter_tokens(
-        to_blocks(jnp.dot(mixed_low, full_output, preferred_element_type=f32))
-    )
-    attn_rms = rms_scale(attn_out)
-    attn_normed = attn_out * attn_rms
-    resid = hidden_in.astype(f32) + attn_normed * gain_attn
-    resid_low = gather_tokens(resid.astype(jnp.bfloat16)).reshape(blocks * length, model_width)
-
-    full_gate = gather_columns(w_gate, pair)
-    full_up = gather_columns(w_up, pair)
+        return values.astype(jnp.bfloat16).reshape(blocks, length, model_width)
+
+    resid_low, attn_out, resid, full_gate, full_up, full_down = attention_block(
+        to_blocks(jnp.dot(mixed_low, full_output, preferred_element_type=f32)),
+        hidden_in,
+        gain_attn,
+        [[w_gate], [w_up]],
+        [w_down],
+        1,
+    )
+    resid_low = resid_low.reshape(blocks * length, model_width)
+
     gate_proj = jnp.dot(resid_low, full_gate, preferred_element_type=f32)
     up_proj = jnp.dot(resid_low, full_up, preferred_element_type=f32)
     gate_sig = jax.nn.sigmoid(gate_proj)
     hidden_ffn = (gate_proj * gate_sig * up_proj).astype(jnp.bfloat16)
-    full_down = gather_rows(w_down, pair)
-    ffn_out = scatter_tokens(
-        to_blocks(jnp.dot(hidden_ffn, full_down, preferred_element_type=f32))
-    )
-    ffn_rms = rms_scale(ffn_out)
-    ffn_normed = ffn_out * ffn_rms
-    hidden_out = (resid + ffn_normed * gain_ffn).astype(jnp.bfloat16)
-    grad_out = out_cotangent.astype(f32)
-    ffn_gain_term = jnp.sum(grad_out * ffn_normed, axis=0)
-    d_ffn_low = gather_tokens(
-        rms_back(grad_out * gain_ffn, ffn_normed, ffn_rms).astype(jnp.bfloat16)
-    ).reshape(blocks * length, model_width)
+    d_ffn_low, hidden_out, ffn_gain_term = ffn_block(
+        to_blocks(jnp.dot(hidden_ffn, full_down, preferred_element_type=f32)),
+        resid,
+        out_cotangent,
+        gain_ffn,
+        2,
+    )
+    d_ffn_low = d_ffn_low.reshape(blocks * length, model_width)
 
     d_hidden_ffn = dot_back(d_ffn_low, full_down)
     d_gate_low = (d_hidden_ffn * up_proj * gate_sig * (1.0 + gate_proj * (1.0 - gate_sig))).astype(
         jnp.bfloat16
     )
     d_up_low = (d_hidden_ffn * gate_proj * gate_sig).astype(jnp.bfloat16)
-    d_resid = grad_out + scatter_tokens(
-        to_blocks(dot_back(d_gate_low, full_gate) + dot_back(d_up_low, full_up))
-    )
+    d_attn_low, d_resid, attn_gain_term = back_block(
+        to_blocks(dot_back(d_gate_low, full_gate) + dot_back(d_up_low, full_up)),
+        out_cotangent,
+        attn_out,
+        gain_attn,
+        3,
+    )
+    d_attn_low = d_attn_low.reshape(blocks * length, model_width)
 
     def outer(left_side, right_side):
         return lax.dot_general(
@@ -493,10 +993,6 @@
     grad_down = reduce_rows_of(outer(hidden_ffn, d_ffn_low), pair)
     grad_gate = reduce_columns(outer(resid_low, d_gate_low), pair)
     grad_up = reduce_columns(outer(resid_low, d_up_low), pair)
-    attn_gain_term = jnp.sum(d_resid * attn_normed, axis=0)
-    d_attn_low = gather_tokens(
-        rms_back(d_resid * gain_attn, attn_normed, attn_rms).astype(jnp.bfloat16)
-    ).reshape(blocks * length, model_width)
     grad_output = reduce_rows_of(outer(mixed_low, d_attn_low), pair)
     d_mixed_low = split_heads(dot_back(d_attn_low, full_output).astype(jnp.bfloat16))
     d_value = jnp.einsum("shqk,sqhd->skhd", prob_low, d_mixed_low, preferred_element_type=f32)
@@ -532,16 +1028,13 @@
         jnp.bfloat16
     )
     d_value_low = d_value.reshape(blocks * length, width).astype(jnp.bfloat16)
-    hidden_grad = (
-        d_resid
-        + scatter_tokens(
-            to_blocks(
-                dot_back(d_query_low, full_query)
-                + dot_back(d_key_low, full_key)
-                + dot_back(d_value_low, full_value)
-            )
-        )
-    ).astype(jnp.bfloat16)
+    hidden_grad = last_block(
+        to_blocks(
+            dot_back(jnp.concatenate([d_query_low, d_key_low, d_value_low], axis=1), full_qkv)
+        ),
+        d_resid,
+        4,
+    )
     grad_query = reduce_columns(outer(tokens, d_query_low), pair)
     grad_key = reduce_columns(outer(tokens, d_key_low), pair)
     grad_value = reduce_columns(outer(tokens, d_value_low), pair)
@@ -549,7 +1042,10 @@
     own_term, other_term = by_pair(pair, head_terms[:, 0], head_terms[:, 1])
     head_grads = own_term + pair_swap(other_term)
     wide_grads = lax.psum_scatter(
-        jnp.stack([attn_gain_term, ffn_gain_term]), "shard", scatter_dimension=1, tiled=True
+        jnp.stack([jnp.sum(attn_gain_term, axis=0), jnp.sum(ffn_gain_term, axis=0)]),
+        "shard",
+        scatter_dimension=1,
+        tiled=True,
     )
     gain_grads = jnp.concatenate([head_grads, wide_grads])
     gain_grads = gain_grads + rep_swap(gain_grads)

time: 1260 us -> 1040 us (0.83)
  Pallas kernels: 0 us -> 413 us
  waiting for transfers between devices: 608 us -> 257 us
  starting transfers between devices: 154 us -> 51.8 us
  blocking collectives: 76.1 us -> 0 us
  local copies, waits for them, and re-layouts: 171 us -> 109 us
  other arithmetic: 112 us -> 81.5 us
    pallas_call x0 -> x5, Pallas kernels: none -> 413 us  [line_call(): pl.pallas_call(kernel, out_shape=[jax.ShapeDtypeStruct(shape, kind) for s...]
    ppermute x33 -> x6, waiting for transfers between devices: 292 us -> 4.85 us  [line_shift(): lax.ppermute(values, 'shard', shard_perm(lambda index: (index + 4 * steps...]
    all_gather x1 -> x0, blocking collectives: 76.1 us -> none  [on_device(): lax.all_gather(jnp.stack([attn_gain, ffn_gain]), 'shard', axis=1, tiled=T...]
    ppermute x33 -> x6, starting transfers between devices: 73.5 us -> 7.83 us  [line_shift(): lax.ppermute(values, 'shard', shard_perm(lambda index: (index + 4 * steps...]
    unnamed x2, waiting for transfers between devices: 61.5 us -> 0.04 us
    ppermute x8, waiting for transfers between devices: 68.1 us -> 118 us  [rep_swap(): return lax.ppermute(values, 'rep', [(0, 1), (1, 0)])]
    all_to_all x5, waiting for transfers between devices: 38.4 us -> 4.02 us  [reduce_columns(): lax.all_to_all(mine, 'shard', 0, 0, axis_index_groups=line_groups(), tile...]
    all_to_all x5 -> x0, starting transfers between devices: 29.4 us -> none  [gather_columns(): lax.all_to_all(pieces, 'shard', 0, 0, axis_index_groups=line_groups(), ti...]
  transfers between devices with their start and end apart: 106 -> 32, of which waited for: 48 -> 9; matrix products, arithmetic and copies ran while one was open for 23% -> 18% of each run, Pallas kernels for 0% -> 14%
where the time goes in v2:
time: 1040 us; the launch traced here: 1030 us
  Pallas kernels  413 us (40%)
  waiting for transfers between devices  257 us (25%)
  local copies, waits for them, and re-layouts  109 us (10%)
  matrix products  101 us (10%)
  other arithmetic  81.5 us (8%)
  starting transfers between devices  51.8 us (5%)
  between operations  15.6 us (2%)
    pallas_call x5, Pallas kernels, line_call(): pl.pallas_call(kernel, out_shape=[jax.ShapeDtypeStruct(shape, kind) for s...  413 us
    ppermute x10, waiting for transfers between devices, pair_swap(): return lax.ppermute(values, 'shard', shard_perm(lambda index: index ^ 2))  130 us
    ppermute x8, waiting for transfers between devices, rep_swap(): return lax.ppermute(values, 'rep', [(0, 1), (1, 0)])  118 us
    unnamed x141, local copies, waits for them, and re-layouts  37.8 us
    dot_general x7, matrix products, outer(): lax.dot_general(left_side, right_side, (((0,), (0,)), ((), ())), preferre...  34.9 us
    dot_general x5, matrix products, dot_back(): lax.dot_general(left_side, right_side, (((1,), (1,)), ((), ())), preferre...  34 us
    reshape x10, local copies, waits for them, and re-layouts, reduce_columns(): got.reshape(4, 2, rows, 2, n).transpose(2, 0, 3, 1, 4).reshape(rows, 16 * n)  32.1 us
    all_to_all x5, starting transfers between devices, reduce_columns(): lax.all_to_all(mine, 'shard', 0, 0, axis_index_groups=line_groups(), tile...  22.9 us
  transfers between devices with their start and end apart: 32, of which 9 were waited for; matrix products, arithmetic and copies ran while one was open for 18% of the time, Pallas kernels for 14%

profile of v2, /device:TPU:0, one launch (start us, length us, event | category | flops | bytes accessed | tf_op | source)
XLA Modules:
  0.0 1029.0 jit_solution(12487060375582830512)
XLA Ops:
  20.3 68.1 %shard_map.237 = (bf16[8,144,2048]{2,1,0:T(8,128)(2,1)S(1)}, bf16[2048,768]{1,0:T(8,128)(2,1)S(1)}, bf16[256,2048]{1,0:T(8,128)(2,1)S(1)}) custom-call(bf16[144,2048]{1,0:T(8,128)(2,1)S(1)} %fusion.34.refs_0_, bf16[128,2048]{1,0:T(8,128)(2,1)S(1)} %copy-done.7, bf16[128,2048]{1,0:T(8,128)(2,1)S(1)} %copy-done.8, bf16[128,2048]{1,0:T(8,128)(2,1)S(1)} %copy-done.9, ...), custom_call_target="tpu_custom_call" | custom-call | flops 10000000 | bytes 200000000 | tf_op jit(solution)/shard_map/pallas_call | solution.py:775
  108.0 6.4 copy.142
  144.2 133.7 %shard_map.238 = (bf16[8,128,2048]{2,1,0:T(8,128)(2,1)S(1)}, f32[128,2048]{1,0:T(8,128)S(1)}, f32[128,2048]{1,0:T(8,128)S(1)}, bf16[2048,1024]{1,0:T(8,128)(2,1)...) custom-call(bf16[8,128,2048]{2,1,0:T(8,128)(2,1)} %bitcast.294, bf16[128,2048]{1,0:T(8,128)(2,1)S(1)} %copy-done.2, ...), custom_call_target="tpu_custom_call" | custom-call | flops 10000000 | bytes 200000000 | tf_op jit(solution)/shard_map/pallas_call | solution.py:775
  277.9 7.8 fusion.67
  285.8 6.5 multiply_convert_fusion.2
  292.3 4.8 convolution_convert_fusion.2
  297.1 70.9 %shard_map.239 = (bf16[8,128,2048]{2,1,0:T(8,128)(2,1)S(1)}, bf16[128,2048]{1,0:T(8,128)(2,1)S(1)}, f32[8,2048]{1,0:T(8,128)S(1)}) custom-call(bf16[8,128,2048]{2,1,0:T(8,128)(2,1)S(1)} %bitcast.286, f32[128,2048]{1,0:T(8,128)S(1)} %get-tuple-element.35.refs_1_, bf16[128,2048]{1,0:T(8,128)(2,1)S(1)} %copy-done.6, f32[1,2048]{1,0:T(1,128)S(1)} %bitcast.289), custom_call_target="tpu_custom_call" | custom-call | flops 10000000 | bytes 200000000 | tf_op jit(solution)/shard_map/pallas_call | solution.py:775
  368.0 11.8 %multiply_convert_fusion = (bf16[1024,1024]{1,0:T(8,128)(2,1)}, bf16[1024,1024]{1,0:T(8,128)(2,1)S(1)}) fusion(f32[1024,1024]{1,0:T(8,128)} %copy-done.60, f32[1024,1024]{1,0:T(8,128)} %get-tuple-element.95, bf16[1024,2048]{1,0:T(8,128)(2,1)S(1)} %bitcast.290, bf16[1024,2048]{1,0:T(8,128)(2,1)} %get-tuple-element.34), kind=kOutput, calls=%fused_computation.16 | convolution fusion | flops 4308598784 | bytes 20971520 | tf_op jit(solution)/shard_map/dot_general | solution.py:37
  379.8 6.9 fusion.68
  386.7 7.7 add_convert_fusion
  394.4 67.2 %shard_map.240 = (bf16[8,128,2048]{2,1,0:T(8,128)(2,1)S(1)}, f32[128,2048]{1,0:T(8,128)S(1)}, f32[8,2048]{1,0:T(8,128)S(1)}) custom-call(bf16[8,128,2048]{2,1,0:T(8,128)(2,1)S(1)} %bitcast.284, bf16[128,2048]{1,0:T(8,128)(2,1)S(1)} %copy-done.6, f32[128,2048]{1,0:T(8,128)S(1)} %get-tuple-element.38.refs_2_, f32[1,2048]{1,0:T(1,128)S(1)} %bitcast.288), custom_call_target="tpu_custom_call" | custom-call | flops 10000000 | bytes 200000000 | tf_op jit(solution)/shard_map/pallas_call | solution.py:775
  488.8 6.4 copy.157
  498.8 10.8 %fusion.4 = f32[4,2,2,128,1024]{4,3,2,0,1:T(8,128)} fusion(bf16[4,2,2,128,1024]{4,3,2,1,0:T(8,128)(2,1)} %bitcast.306, bf16[1024,1024]{1,0:T(8,128)(2,1)} %get-tuple-element.51), kind=kOutput, calls=%fused_computation.7 | convolution fusion | flops 4294967296 | bytes 14680064 | tf_op jit(solution)/shard_map/dot_general | solution.py:989
  521.9 5.3 fusion.11
  543.7 43.0 %collective-permute-done.12 = bf16[4,2,128,256]{3,2,1,0:T(8,128)(2,1)S(1)} collective-permute-done((bf16[4,2,128,256]{3,2,1,0:T(8,128)(2,1)S(1)}, bf16[4,2,128,256]{3,2,1,0:T(8,128)(2,1)S(1)}, u32[]{:S(2)}, u32[]{:S(2)}) %collective-permute-start.12) | collective-permute-done | bytes 524320 | tf_op jit(solution)/shard_map/ppermute | solution.py:288
  591.2 5.3 all-to-all-start.1
  596.5 10.7 %fusion.13 = f32[4,2,2,128,1024]{4,3,2,1,0:T(8,128)} fusion(bf16[4,2,2,128,1024]{4,3,2,1,0:T(8,128)(2,1)} %bitcast.307, bf16[1024,1024]{1,0:T(8,128)(2,1)} %copy-done.61), kind=kOutput, calls=%fused_computation.30 | convolution fusion | flops 4294967296 | bytes 14680064 | tf_op jit(solution)/shard_map/dot_general | solution.py:989
  607.2 6.7 fusion.3
  618.4 5.1 all-to-all-start.4
  623.7 5.3 fusion.10
  650.8 87.2 %collective-permute-done.18 = f32[2,128]{1,0:T(2,128)S(1)} collective-permute-done((f32[2,128]{1,0:T(2,128)S(1)}, f32[2,128]{1,0:T(2,128)S(1)}, u32[]{:S(2)}, u32[]{:S(2)}) %collective-permute-start.18) | collective-permute-done | bytes 1056 | tf_op jit(solution)/shard_map/ppermute | solution.py:288
  741.1 6.6 fusion.2
  752.3 4.7 all-to-all-start.3
  757.0 5.5 convolution_convert_fusion.1
  762.6 73.0 %shard_map.241 = bf16[128,2048]{1,0:T(8,128)(2,1)S(1)} custom-call(bf16[8,128,2048]{2,1,0:T(8,128)(2,1)S(1)} %bitcast.285, f32[128,2048]{1,0:T(8,128)S(1)} %get-tuple-element.40.refs_1_), custom_call_target="tpu_custom_call" | custom-call | flops 10000000 | bytes 200000000 | tf_op jit(solution)/shard_map/pallas_call | solution.py:775
  841.6 5.3 add_convert_fusion.1
  860.6 6.1 copy.233
  875.7 44.4 %collective-permute-done.11 = bf16[128,2048]{1,0:T(8,128)(2,1)} collective-permute-done((bf16[128,2048]{1,0:T(8,128)(2,1)}, bf16[128,2048]{1,0:T(8,128)(2,1)}, u32[]{:S(2)}, u32[]{:S(2)}) %collective-permute-start.11) | collective-permute-done | bytes 524320 | tf_op jit(solution)/shard_map/ppermute | solution.py:292
  922.5 8.9 collective-permute-done.13
  933.6 6.1 copy.234
  948.7 27.6 %collective-permute-done.23 = bf16[128,8192]{1,0:T(8,128)(2,1)} collective-permute-done((bf16[128,8192]{1,0:T(8,128)(2,1)}, bf16[128,8192]{1,0:T(8,128)(2,1)}, u32[]{:S(2)}, u32[]{:S(2)}) %collective-permute-start.23) | collective-permute-done | bytes 2097184 | tf_op jit(solution)/shard_map/ppermute | solution.py:292
  980.5 37.1 %collective-permute-done.21 = bf16[128,8192]{1,0:T(8,128)(2,1)S(1)} collective-permute-done((bf16[128,8192]{1,0:T(8,128)(2,1)}, bf16[128,8192]{1,0:T(8,128)(2,1)S(1)}, u32[]{:S(2)}, u32[]{:S(2)}) %collective-permute-start.21) | collective-permute-done | bytes 2097184 | tf_op jit(solution)/shard_map/ppermute | solution.py:292
  (299 shorter events, 210.4 us)
Async XLA Ops:
  7.9 106.6 %collective-permute-start.4 = (bf16[1,2,128]{2,1,0:T(2,128)(2,1)S(1)}, bf16[1,2,128]{2,1,0:T(2,128)(2,1)S(1)}, u32[]{:S(2)}, u32[]{:S(2)}) collective-permute-start(bf16[1,2,128]{2,1,0:T(2,128)(2,1)S(1)} %maximum_bitcast_fusion), channel_id=1, source_target_pairs={{0,2},{1,3},{2,0},{3,1},{4,6},{5,7},{6,4},{7,5},{8,10},{9,11},{10,... | collective-permute-start | bytes 1544 | tf_op jit(solution)/shard_map/ppermute | solution.py:288
  92.3 27.7 %collective-permute-start.5 = (bf16[4,2,4,128]{3,2,1,0:T(4,128)(2,1)S(1)}, bf16[4,2,4,128]{3,2,1,0:T(4,128)(2,1)S(1)}, u32[]{:S(2)}, u32[]{:S(2)}) collective-permute-start(bf16[4,2,4,128]{3,2,1,0:T(4,128)(2,1)S(1)} %reshape_squeeze.3), channel_id=1, source_target_pairs={{0,2},{1,3},{2,0},{3,1},{4,6},{5,7},{6,4},{7,5},{8,10},{9,11},{10,... | collective-permute-start | bytes 24584 | tf_op jit(solution)/shard_map/ppermute | solution.py:288
  101.2 13.3 %collective-permute-start = (f32[2,1024]{1,0:T(2,128)S(1)}, f32[2,1024]{1,0:T(2,128)S(1)}, u32[]{:S(2)}, u32[]{:S(2)}) collective-permute-start(f32[2,1024]{1,0:T(2,128)S(1)} %pad_maximum_fusion.9), channel_id=1, source_target_pairs={{0,1},{1,0},{2,3},{3,2},{4,5},{5,4},{6,7},{7,6},{8,9},{9,8},{10,11... | collective-permute-start | bytes 24584 | tf_op jit(solution)/shard_map/ppermute | solution.py:284
  114.5 5.5 collective-permute-start.2
  116.4 5.0 collective-permute-start.3
  119.3 5.6 collective-permute-start.1
  484.9 11.5 %collective-permute-start.6 = (f32[2,1024]{1,0:T(2,128)S(1)}, f32[2,1024]{1,0:T(2,128)S(1)}, u32[]{:S(2)}, u32[]{:S(2)}) collective-permute-start(f32[2,1024]{1,0:T(2,128)S(1)} %pad_maximum_fusion.10), channel_id=1, source_target_pairs={{0,1},{1,0},{2,3},{3,2},{4,5},{5,4},{6,7},{7,6},{8,9},{9,8},{10,11... | collective-permute-start | bytes 24584 | tf_op jit(solution)/shard_map/ppermute | solution.py:284
  495.2 21.3 %collective-permute-start.14 = (bf16[4,2,128,256]{3,2,1,0:T(8,128)(2,1)}, bf16[4,2,128,256]{3,2,1,0:T(8,128)(2,1)S(1)}, u32[]{:S(2)}, u32[]{:S(2)}) collective-permute-start(bf16[4,2,128,256]{3,2,1,0:T(8,128)(2,1)} %fusion.37), channel_id=1, source_target_pairs={{0,2},{1,3},{2,0},{3,1},{4,6},{5,7},{6,4},{7,5},{8,10},{9,11},{10,... | collective-permute-start | bytes 1572872 | tf_op jit(solution)/shard_map/ppermute | solution.py:288
  496.4 13.2 %collective-permute-start.8 = (f32[2,1024]{1,0:T(2,128)S(1)}, f32[2,1024]{1,0:T(2,128)S(1)}, u32[]{:S(2)}, u32[]{:S(2)}) collective-permute-start(f32[2,1024]{1,0:T(2,128)S(1)} %fusion.57), channel_id=1, source_target_pairs={{0,8},{1,9},{2,10},{3,11},{4,12},{5,13},{6,14},{7,15},{8,0},{9,1},... | collective-permute-start | bytes 24584 | tf_op jit(solution)/shard_map/ppermute | solution.py:296
  496.5 13.2 %collective-permute-start.9 = (f32[2,1024]{1,0:T(2,128)S(1)}, f32[2,1024]{1,0:T(2,128)S(1)}, u32[]{:S(2)}, u32[]{:S(2)}) collective-permute-start(f32[2,1024]{1,0:T(2,128)S(1)} %fusion.57), channel_id=1, source_target_pairs={{0,12},{1,13},{2,14},{3,15},{4,0},{5,1},{6,2},{7,3},{8,4},{9,5},{1... | collective-permute-start | bytes 24584 | tf_op jit(solution)/shard_map/ppermute | solution.py:296
  497.5 12.2 %collective-permute-start.7 = (f32[2,1024]{1,0:T(2,128)S(1)}, f32[2,1024]{1,0:T(2,128)S(1)}, u32[]{:S(2)}, u32[]{:S(2)}) collective-permute-start(f32[2,1024]{1,0:T(2,128)S(1)} %fusion.57), channel_id=1, source_target_pairs={{0,4},{1,5},{2,6},{3,7},{4,8},{5,9},{6,10},{7,11},{8,12},{9,13},{1... | collective-permute-start | bytes 24584 | tf_op jit(solution)/shard_map/ppermute | solution.py:296
  515.6 15.4 %collective-permute-start.10 = (bf16[4,2,128,256]{3,2,1,0:T(8,128)(2,1)}, bf16[4,2,128,256]{3,2,1,0:T(8,128)(2,1)}, u32[]{:S(2)}, u32[]{:S(2)}) collective-permute-start(bf16[4,2,128,256]{3,2,1,0:T(8,128)(2,1)} %fusion.35), channel_id=1, source_target_pairs={{0,2},{1,3},{2,0},{3,1},{4,6},{5,7},{6,4},{7,5},{8,10},{9,11},{10,... | collective-permute-start | bytes 1572872 | tf_op jit(solution)/shard_map/ppermute | solution.py:288
  517.7 19.6 %all-to-all-start.2 = ((bf16[8,128,2,128]{3,2,1,0:T(2,128)(2,1)}), bf16[8,128,2,128]{3,2,1,0:T(2,128)(2,1)S(1)}, u32[]{:S(2)}, u32[]{:S(2)}) async-start(bf16[8,128,2,128]{3,2,1,0:T(2,128)(2,1)} %reshape.258), calls=%async_computation.2 | async-start | bytes 1048576 | tf_op jit(solution)/shard_map/all_to_all | solution.py:341
  527.2 80.0 %collective-permute-start.22 = (bf16[4,2,128,1024]{3,2,1,0:T(8,128)(2,1)}, bf16[4,2,128,1024]{3,2,1,0:T(8,128)(2,1)}, u32[]{:S(2)}, u32[]{:S(2)}) collective-permute-start(bf16[4,2,128,1024]{3,2,1,0:T(8,128)(2,1)} %fusion.11), channel_id=1, source_target_pairs={{0,2},{1,3},{2,0},{3,1},{4,6},{5,7},{6,4},{7,5},{8,10},{9,11},{10,... | collective-permute-start | bytes 6291464 | tf_op jit(solution)/shard_map/ppermute | solution.py:288
  537.3 53.9 %all-to-all-start = ((bf16[8,128,2,128]{3,2,1,0:T(2,128)(2,1)}), bf16[8,128,2,128]{3,2,1,0:T(2,128)(2,1)S(1)}, u32[]{:S(2)}, u32[]{:S(2)}) async-start(bf16[8,128,2,128]{3,2,1,0:T(2,128)(2,1)} %reshape.252), calls=%async_computation | async-start | bytes 1048576 | tf_op jit(solution)/shard_map/all_to_all | solution.py:341
  542.4 44.3 %collective-permute-start.12 = (bf16[4,2,128,256]{3,2,1,0:T(8,128)(2,1)S(1)}, bf16[4,2,128,256]{3,2,1,0:T(8,128)(2,1)S(1)}, u32[]{:S(2)}, u32[]{:S(2)}) collective-permute-start(bf16[4,2,128,256]{3,2,1,0:T(8,128)(2,1)S(1)} %fusion.36), channel_id=1, source_target_pairs={{0,2},{1,3},{2,0},{3,1},{4,6},{5,7},{6,4},{7,5},{8,10},{9,11},{10,... | collective-permute-start | bytes 1572872 | tf_op jit(solution)/shard_map/ppermute | solution.py:288
  591.2 27.2 %all-to-all-start.1 = ((bf16[8,128,2,128]{3,2,1,0:T(2,128)(2,1)}), bf16[8,128,2,128]{3,2,1,0:T(2,128)(2,1)}, u32[]{:S(2)}, u32[]{:S(2)}) async-start(bf16[8,128,2,128]{3,2,1,0:T(2,128)(2,1)} %reshape.255), calls=%async_computation.1 | async-start | bytes 1048576 | tf_op jit(solution)/shard_map/all_to_all | solution.py:341
  618.4 133.9 %all-to-all-start.4 = ((bf16[8,128,2,512]{3,2,1,0:T(2,128)(2,1)}), bf16[8,128,2,512]{3,2,1,0:T(2,128)(2,1)}, u32[]{:S(2)}, u32[]{:S(2)}) async-start(bf16[8,128,2,512]{3,2,1,0:T(2,128)(2,1)} %reshape.264), calls=%async_computation.4 | async-start | bytes 4194304 | tf_op jit(solution)/shard_map/all_to_all | solution.py:341
  623.5 114.5 %reduce-scatter.4.cloned.1.call-start = ((), (), s32[]{:S(2)}) async-start(), calls=%async_computation.6 | async-start | bytes 1114112
  629.9 111.1 %collective-permute-start.20 = (bf16[4,2,128,1024]{3,2,1,0:T(8,128)(2,1)}, bf16[4,2,128,1024]{3,2,1,0:T(8,128)(2,1)}, u32[]{:S(2)}, u32[]{:S(2)}) collective-permute-start(bf16[4,2,128,1024]{3,2,1,0:T(8,128)(2,1)} %fusion.10), channel_id=1, source_target_pairs={{0,2},{1,3},{2,0},{3,1},{4,6},{5,7},{6,4},{7,5},{8,10},{9,11},{10,... | collective-permute-start | bytes 6291464 | tf_op jit(solution)/shard_map/ppermute | solution.py:288
  640.8 200.8 %collective-permute-start.24 = (bf16[512,2048]{1,0:T(8,128)(2,1)}, bf16[512,2048]{1,0:T(8,128)(2,1)}, u32[]{:S(2)}, u32[]{:S(2)}) collective-permute-start(bf16[512,2048]{1,0:T(8,128)(2,1)} %select_convert_fusion), channel_id=1, source_target_pairs={{0,2},{1,3},{2,0},{3,1},{4,6},{5,7},{6,4},{7,5},{8,10},{9,11},{10,... | collective-permute-start | bytes 6291464 | tf_op jit(solution)/shard_map/ppermute | solution.py:288
  647.3 188.2 %collective-permute-start.16 = (bf16[128,2048]{1,0:T(8,128)(2,1)}, bf16[128,2048]{1,0:T(8,128)(2,1)}, u32[]{:S(2)}, u32[]{:S(2)}) collective-permute-start(bf16[128,2048]{1,0:T(8,128)(2,1)} %select_convert_fusion.3), channel_id=1, source_target_pairs={{0,2},{1,3},{2,0},{3,1},{4,6},{5,7},{6,4},{7,5},{8,10},{9,11},{10,... | collective-permute-start | bytes 1572872 | tf_op jit(solution)/shard_map/ppermute | solution.py:288
  648.5 89.4 %collective-permute-start.18 = (f32[2,128]{1,0:T(2,128)S(1)}, f32[2,128]{1,0:T(2,128)S(1)}, u32[]{:S(2)}, u32[]{:S(2)}) collective-permute-start(f32[2,128]{1,0:T(2,128)S(1)} %select_bitcast_fusion.2), channel_id=1, source_target_pairs={{0,2},{1,3},{2,0},{3,1},{4,6},{5,7},{6,4},{7,5},{8,10},{9,11},{10,... | collective-permute-start | bytes 3080 | tf_op jit(solution)/shard_map/ppermute | solution.py:288
  738.9 96.6 %collective-permute-start.19 = (f32[4,128]{1,0:T(4,128)S(1)}, f32[4,128]{1,0:T(4,128)S(1)}, u32[]{:S(2)}, u32[]{:S(2)}) collective-permute-start(f32[4,128]{1,0:T(4,128)S(1)} %pad_maximum_fusion.11), channel_id=1, source_target_pairs={{0,16},{16,0},{1,17},{17,1},{2,18},{18,2},{3,19},{19,3},{4,20},{20... | collective-permute-start | bytes 6152 | tf_op jit(solution)/shard_map/ppermute | solution.py:292
  752.3 181.3 %all-to-all-start.3 = ((bf16[8,128,2,512]{3,2,1,0:T(2,128)(2,1)}), bf16[8,128,2,512]{3,2,1,0:T(2,128)(2,1)}, u32[]{:S(2)}, u32[]{:S(2)}) async-start(bf16[8,128,2,512]{3,2,1,0:T(2,128)(2,1)} %reshape.261), calls=%async_computation.3 | async-start | bytes 4194304 | tf_op jit(solution)/shard_map/all_to_all | solution.py:341
  837.6 15.7 %collective-permute-start.17 = (bf16[128,2048]{1,0:T(8,128)(2,1)}, bf16[128,2048]{1,0:T(8,128)(2,1)}, u32[]{:S(2)}, u32[]{:S(2)}) collective-permute-start(bf16[128,2048]{1,0:T(8,128)(2,1)} %add_convert_fusion.2), channel_id=1, source_target_pairs={{0,16},{16,0},{1,17},{17,1},{2,18},{18,2},{3,19},{19,3},{4,20},{20... | collective-permute-start | bytes 1572872 | tf_op jit(solution)/shard_map/ppermute | solution.py:292
  839.6 33.8 %collective-permute-start.15 = (bf16[128,2048]{1,0:T(8,128)(2,1)}, bf16[128,2048]{1,0:T(8,128)(2,1)}, u32[]{:S(2)}, u32[]{:S(2)}) collective-permute-start(bf16[128,2048]{1,0:T(8,128)(2,1)} %reshape.260), channel_id=1, source_target_pairs={{0,16},{16,0},{1,17},{17,1},{2,18},{18,2},{3,19},{19,3},{4,20},{20... | collective-permute-start | bytes 1572872 | tf_op jit(solution)/shard_map/ppermute | solution.py:292
  846.9 97.3 %collective-permute-start.25 = (bf16[512,2048]{1,0:T(8,128)(2,1)S(1)}, bf16[512,2048]{1,0:T(8,128)(2,1)}, u32[]{:S(2)}, u32[]{:S(2)}) collective-permute-start(bf16[512,2048]{1,0:T(8,128)(2,1)S(1)} %add_convert_fusion.1), channel_id=1, source_target_pairs={{0,16},{16,0},{1,17},{17,1},{2,18},{18,2},{3,19},{19,3},{4,20},{20... | collective-permute-start | bytes 6291464 | tf_op jit(solution)/shard_map/ppermute | solution.py:292
  851.4 68.8 %collective-permute-start.11 = (bf16[128,2048]{1,0:T(8,128)(2,1)}, bf16[128,2048]{1,0:T(8,128)(2,1)}, u32[]{:S(2)}, u32[]{:S(2)}) collective-permute-start(bf16[128,2048]{1,0:T(8,128)(2,1)} %reshape.254), channel_id=1, source_target_pairs={{0,16},{16,0},{1,17},{17,1},{2,18},{18,2},{3,19},{19,3},{4,20},{20... | collective-permute-start | bytes 1572872 | tf_op jit(solution)/shard_map/ppermute | solution.py:292
  860.5 70.9 %collective-permute-start.13 = (bf16[128,2048]{1,0:T(8,128)(2,1)}, bf16[128,2048]{1,0:T(8,128)(2,1)}, u32[]{:S(2)}, u32[]{:S(2)}) collective-permute-start(bf16[128,2048]{1,0:T(8,128)(2,1)} %reshape.257), channel_id=1, source_target_pairs={{0,16},{16,0},{1,17},{17,1},{2,18},{18,2},{3,19},{19,3},{4,20},{20... | collective-permute-start | bytes 1572872 | tf_op jit(solution)/shard_map/ppermute | solution.py:292
  871.4 104.9 %collective-permute-start.23 = (bf16[128,8192]{1,0:T(8,128)(2,1)}, bf16[128,8192]{1,0:T(8,128)(2,1)}, u32[]{:S(2)}, u32[]{:S(2)}) collective-permute-start(bf16[128,8192]{1,0:T(8,128)(2,1)} %reshape.266), channel_id=1, source_target_pairs={{0,16},{16,0},{1,17},{17,1},{2,18},{18,2},{3,19},{19,3},{4,20},{20... | collective-permute-start | bytes 6291464 | tf_op jit(solution)/shard_map/ppermute | solution.py:292
  944.2 73.4 %collective-permute-start.21 = (bf16[128,8192]{1,0:T(8,128)(2,1)}, bf16[128,8192]{1,0:T(8,128)(2,1)S(1)}, u32[]{:S(2)}, u32[]{:S(2)}) collective-permute-start(bf16[128,8192]{1,0:T(8,128)(2,1)} %reshape.263), channel_id=1, source_target_pairs={{0,16},{16,0},{1,17},{17,1},{2,18},{18,2},{3,19},{19,3},{4,20},{20... | collective-permute-start | bytes 6291464 | tf_op jit(solution)/shard_map/ppermute | solution.py:292
  (62 other events, 544.6 us)
Sparse Core Ops, SparseCore 0:
  650.9 62.2 reduce-scatter.3

commit v3 on v2

--- a/solution.py
+++ b/solution.py
@@ -296,10 +296,6 @@
     return lax.ppermute(values, "shard", shard_perm(lambda index: (index + 4 * steps) % 16))
 
 
-def line_groups():
-    return [[line * 4 + pair * 2 + core for line in range(4) for core in range(2)] for pair in range(2)]
-
-
 def group_sum(values):
     both = values + core_swap(values)
     return both + line_shift(both, 1) + line_shift(both, 2) + line_shift(both, 3)
@@ -309,42 +305,8 @@
     return jnp.where(pair == 0, own, other), jnp.where(pair == 0, other, own)
 
 
-def gather_columns(weight, pair):
-    rows, width = weight.shape
-    n = width // 16
-    pieces = weight.reshape(rows, 4, 2, 2, n).transpose(1, 3, 0, 2, 4).reshape(8, rows, 2, n)
-    own = lax.all_to_all(pieces, "shard", 0, 0, axis_index_groups=line_groups(), tiled=True)
-    first, second = by_pair(pair, own, pair_swap(own))
-    full = jnp.stack([first.reshape(4, 2, rows, 2 * n), second.reshape(4, 2, rows, 2 * n)], axis=1)
-    return full.reshape(16 * rows, 2 * n)
-
-
 def gather_rows(weight, pair):
     return jnp.concatenate(by_pair(pair, weight, pair_swap(weight)), axis=0)
-
-
-def rep_total(values):
-    low = values.astype(jnp.bfloat16)
-    return low.astype(jnp.float32) + rep_swap(low).astype(jnp.float32)
-
-
-def pair_total(first, second, pair):
-    own, other = by_pair(pair, first, second)
-    return own + pair_swap(other.astype(jnp.bfloat16)).astype(jnp.float32)
-
-
-def reduce_columns(partial, pair):
-    rows = partial.shape[0] // 16
-    n = partial.shape[1] // 2
-    split = partial.reshape(4, 2, 2, rows, 2 * n)
-    mine = pair_total(split[:, 0], split[:, 1], pair).astype(jnp.bfloat16).reshape(8, rows, 2, n)
-    got = lax.all_to_all(mine, "shard", 0, 0, axis_index_groups=line_groups(), tiled=True)
-    return rep_total(got.reshape(4, 2, rows, 2, n).transpose(2, 0, 3, 1, 4).reshape(rows, 16 * n))
-
-
-def reduce_rows_of(partial, pair):
-    half = partial.shape[0] // 2
-    return rep_total(pair_total(partial[:half], partial[half:], pair))
 
 
 MESH_ID = pl.DeviceIdType.MESH
@@ -406,12 +368,26 @@
 
 
 class Spread:
-    SEMAPHORES = ((2 * LINE,),) * 4 + ((2 * LINE, 2),) * 2
-
-    def __init__(self, line, sources, target, sems):
-        self.line, self.sources, self.target = line, sources, target
+    semaphores = ((2 * LINE,),) * 4 + ((2 * LINE, 2),) * 2
+    slots = 6 + 2 * LINE
+
+    def __init__(self, *weights):
+        self.inputs = list(weights)
+        shape = (16 * weights[0].shape[0], sum(weight.shape[1] for weight in weights) // 8)
+        self.outputs = [jax.ShapeDtypeStruct(shape, jnp.bfloat16)]
+
+    def bind(self, line, sources, targets, sems):
+        self.line, self.sources, self.target = line, sources, targets[0]
         self.z_send, self.z_recv, self.y_send, self.y_recv, self.x_send, self.x_recv = sems
         self.half = sources[0].shape[0] // 2
+
+    def slot(self, t):
+        if t < 2 * LINE:
+            self.start(t)
+        if 3 <= t < 3 + 2 * LINE:
+            self.came(t - 3)
+        if 6 <= t < 6 + 2 * LINE:
+            self.onward(t - 6)
 
     def rows(self, place, pair, core, rep):
         start = ((place * 4 + pair * 2 + core) * 2 + rep) * self.half
@@ -475,13 +451,22 @@
 
 
 class Stack:
-    SEMAPHORES = ((3,),)
-
-    def __init__(self, line, source, target, sems):
+    semaphores = ((3,),)
+    slots = 3
+
+    def __init__(self, weight):
+        self.inputs = [weight]
+        self.outputs = [jax.ShapeDtypeStruct((2 * weight.shape[0], weight.shape[1]), weight.dtype)]
+
+    def bind(self, line, sources, targets, sems):
         self.line, self.sems = line, sems[0]
-        self.source = source
-        size = source.shape[0]
-        self.mine = target.at[pl.ds(pl.multiple_of(line.pair * size, size), size), :]
+        self.source = sources[0]
+        size = self.source.shape[0]
+        self.mine = targets[0].at[pl.ds(pl.multiple_of(line.pair * size, size), size), :]
+
+    def slot(self, t):
+        if t == 2:
+            self.start()
 
     def here(self):
         return pltpu.make_async_copy(self.source, self.mine, self.sems.at[0])
@@ -496,6 +481,98 @@
     def finish(self):
         self.here().wait()
         self.there().wait()
+
+
+class Swap:
+    semaphores = ((2,),)
+    slots = 1
+
+    def __init__(self, values, shape, pick, to):
+        self.inputs, self.pick, self.to = [values], pick, to
+        self.outputs = [jax.ShapeDtypeStruct(shape, values.dtype)]
+
+    def bind(self, line, sources, targets, sems):
+        self.copy = remote(
+            self.pick(line, sources[0]), targets[0], sems[0].at[0], sems[0].at[1], getattr(line, self.to)
+        )
+
+    def slot(self, t):
+        if t == 0:
+            self.copy.start()
+
+    def finish(self):
+        self.copy.wait()
+
+
+class Deal:
+    semaphores = ((2 * LINE,),) * 4
+    slots = 3 + 2 * LINE
+
+    def __init__(self, values, count, joint):
+        rows, width = values.shape[1:]
+        self.inputs, self.joint, self.count = [values], joint, count
+        self.n = width // count if joint else width // (2 * count)
+        shape = jax.ShapeDtypeStruct((rows, 16 * count * self.n), values.dtype)
+        self.outputs = [shape] if joint else [shape, shape]
+
+    def bind(self, line, sources, targets, sems):
+        self.line, self.source, self.targets = line, sources[0], targets
+        self.z_send, self.z_recv, self.x_send, self.x_recv = sems
+
+    def columns(self, place, core, rep):
+        n = self.n
+        at = 0
+        for index in range(self.count):
+            for q in (rep,) if self.joint else (0, 1):
+                yield at, pl.multiple_of((index * 16 + place * 4 + q * 2 + core) * n, n)
+                at += n
+
+    def whole(self, sem_send, sem_recv):
+        ref = self.source.at[0]
+        return remote(ref, ref, sem_send, sem_recv, self.line.partner)
+
+    def start(self, p):
+        line = self.line
+        place, core = line.piece(p, 1)
+        for at, column in self.columns(line.place, line.core, line.rep):
+            piece = self.source.at[2 * place + core, :, pl.ds(at, self.n)]
+            goal = self.targets[0].at[:, pl.ds(column, self.n)]
+            if p == 0:
+                pltpu.make_async_copy(piece, goal, self.z_recv.at[0]).start()
+            else:
+                remote(
+                    piece, goal, self.z_send.at[p], self.z_recv.at[p], line.at(place, line.pair, core)
+                ).start()
+
+    def came(self, p):
+        line = self.line
+        if p == 0:
+            ref = self.source.at[0]
+            pltpu.make_async_copy(ref, ref, self.z_recv.at[0]).wait()
+        else:
+            self.whole(self.z_send.at[p], self.z_recv.at[p]).wait_recv()
+        place, core = line.piece(p, -1)
+        for _, column in self.columns(place, core, line.rep):
+            there = pl.ds(column, self.n)
+            remote(
+                self.targets[0].at[:, there],
+                self.targets[-1].at[:, there],
+                self.x_send.at[p],
+                self.x_recv.at[p],
+                line.partner,
+            ).start()
+
+    def slot(self, t):
+        if t < 2 * LINE:
+            self.start(t)
+        if 3 <= t < 3 + 2 * LINE:
+            self.came(t - 3)
+
+    def finish(self):
+        for p in range(2 * LINE):
+            if p > 0:
+                self.whole(self.z_send.at[p], self.z_recv.at[p]).wait_send()
+            self.whole(self.x_send.at[p], self.x_recv.at[p]).wait()
 
 
 def line_scatter_joint(line, k, rows, parts, sib):
@@ -649,33 +726,20 @@
     lax.fori_loop(0, pieces, piece, 0)
 
 
-def take_from(items, count):
-    taken = items[:count]
-    del items[:count]
-    return taken
-
-
-def line_call(collective_id, pieces, middle, inputs, outputs, scatter, gather, spreads=(), stacks=()):
-    block = inputs[0].shape[-2:]
-    step = block[0] // pieces
-    n_in, n_out = len(inputs), len(outputs)
-    weights = [w for group in spreads for w in group] + list(stacks)
-    n_weights, n_extra = len(weights), len(spreads) + len(stacks)
-    extras = [
-        jax.ShapeDtypeStruct((16 * group[0].shape[0], sum(w.shape[1] for w in group) // 8), jnp.bfloat16)
-        for group in spreads
-    ] + [jax.ShapeDtypeStruct((2 * w.shape[0], w.shape[1]), jnp.bfloat16) for w in stacks]
+def line_call(collective_id, pieces, middle, inputs, outputs, scatter, gather, moves=()):
+    step = inputs[0].shape[-2] // pieces if inputs else 0
     low = jnp.bfloat16
     scratch = []
     if scatter:
+        block = inputs[0].shape[-2:]
         scratch += [pltpu.VMEM((LINE,) + block, low) for _ in range(4)]
         scratch += [pltpu.SemaphoreType.DMA((LINE, pieces)) for _ in range(6)]
     if gather:
         scratch += [pltpu.SemaphoreType.DMA((LINE, 3, pieces)), pltpu.SemaphoreType.DMA((2 * LINE, pieces))]
-
     n_scratch = len(scratch)
-    kinds = [Spread] * len(spreads) + [Stack] * len(stacks)
-    scratch += [pltpu.SemaphoreType.DMA(shape) for kind in kinds for shape in kind.SEMAPHORES]
+    scratch += [pltpu.SemaphoreType.DMA(shape) for move in moves for shape in move.semaphores]
+    moved = [values for move in moves for values in move.inputs]
+    extras = [shape for move in moves for shape in move.outputs]
 
     def kernel(*refs):
         refs = list(refs)
@@ -685,14 +749,15 @@
             del refs[:count]
             return taken
 
-        ins, given, outs, extra = take(n_in), take(n_weights), take(n_out), take(n_extra)
+        ins = take(len(inputs))
+        given = [take(len(move.inputs)) for move in moves]
+        outs = take(len(outputs))
+        extra = [take(len(move.outputs)) for move in moves]
         rest = take(n_scratch)
         line = Line()
-        moves = []
-        for group in spreads:
-            moves.append(Spread(line, take_from(given, len(group)), extra.pop(0), take(6)))
-        heaps = [Stack(line, given.pop(0), extra.pop(0), take(1)) for _ in stacks]
-        line.meet(bool(moves or heaps))
+        for move, sources, targets in zip(moves, given, extra):
+            move.bind(line, sources, targets, take(len(move.semaphores)))
+        line.meet(bool(moves))
         if scatter:
             sib, rights, lefts, sums, sib_send, sib_recv, right_send, left_send, right_recv, left_recv = rest[:10]
             parts = ins[0]
@@ -738,32 +803,23 @@
                     )
             return carry
 
-        if not scatter:
+        if gather and not scatter:
             lax.fori_loop(0, pieces, lambda j, carry: (finish(j), carry)[1], 0)
-        hops = (LINE - 1) * (int(scatter) + int(gather))
-        if moves:
-            for t in range(pieces + hops):
+        slots = pieces + (LINE - 1) * (int(scatter) + int(gather)) if inputs else 0
+        apart = max([move.slots for move in moves] + [0])
+        if apart <= 1:
+            for move in moves:
+                move.slot(0)
+            if inputs:
+                lax.fori_loop(0, slots, slot, 0)
+        else:
+            for t in range(max(slots, apart)):
                 for move in moves:
-                    if t < 2 * LINE:
-                        move.start(t)
-                    if 3 <= t < 3 + 2 * LINE:
-                        move.came(t - 3)
-                    if 6 <= t < 6 + 2 * LINE:
-                        move.onward(t - 6)
-                if t == 2:
-                    for heap in heaps:
-                        heap.start()
-                slot(t, 0)
-            for move in moves:
-                for t in range(pieces + hops, 6 + 2 * LINE):
-                    if t < 3 + 2 * LINE:
-                        move.came(t - 3)
-                    move.onward(t - 6)
-                move.finish()
-            for heap in heaps:
-                heap.finish()
-        else:
-            lax.fori_loop(0, pieces + hops, slot, 0)
+                    move.slot(t)
+                if t < slots:
+                    slot(t, 0)
+        for move in moves:
+            move.finish()
         if scatter:
             line_scatter_end(
                 line, pieces, step, parts, sib, rights, lefts, sums, sib_send, right_send, left_send
@@ -772,28 +828,29 @@
             line_gather_end(line, pieces, step, outs[0], sends, recvs)
 
     vmem = pl.BlockSpec(memory_space=pltpu.VMEM)
+    whole = pl.BlockSpec(memory_space=pl.ANY)
     return pl.pallas_call(
         kernel,
         out_shape=[jax.ShapeDtypeStruct(shape, kind) for shape, kind in outputs] + extras,
-        in_specs=[vmem] * n_in + [pl.BlockSpec(memory_space=pl.ANY)] * n_weights,
-        out_specs=[vmem] * n_out + [pl.BlockSpec(memory_space=pl.ANY)] * n_extra,
+        in_specs=[vmem] * len(inputs) + [whole] * len(moved),
+        out_specs=[vmem] * len(outputs) + [whole] * len(extras),
         scratch_shapes=scratch,
         compiler_params=pltpu.CompilerParams(
             collective_id=collective_id, has_side_effects=True, vmem_limit_bytes=40 << 20
         ),
         cost_estimate=pl.CostEstimate(flops=10_000_000, bytes_accessed=200_000_000, transcendentals=0),
-    )(*inputs, *weights)
-
-
-def gather_blocks(payload, spreads, stacks, collective_id):
+    )(*inputs, *moved)
+
+
+def gather_blocks(payload, moves, collective_id):
     def middle(total, rows, j, ins, outs):
         return ins[0][rows, :]
 
     shape = (2 * LINE,) + payload.shape
-    return line_call(collective_id, 9, middle, [payload], [(shape, jnp.bfloat16)], False, True, spreads, stacks)
-
-
-def attention_block(parts, hidden, gain, spreads, stacks, collective_id):
+    return line_call(collective_id, 9, middle, [payload], [(shape, jnp.bfloat16)], False, True, moves)
+
+
+def attention_block(parts, hidden, gain, moves, collective_id):
     def middle(total, rows, j, ins, outs):
         outs[1][rows, :] = total
         resid = ins[1][rows, :].astype(jnp.float32) + total * rms_scale(total) * ins[2][...]
@@ -803,7 +860,7 @@
     shape = hidden.shape
     return line_call(
         collective_id, 8, middle, [parts, hidden, gain],
-        [(parts.shape, jnp.bfloat16), (shape, jnp.float32), (shape, jnp.float32)], True, True, spreads, stacks,
+        [(parts.shape, jnp.bfloat16), (shape, jnp.float32), (shape, jnp.float32)], True, True, moves,
     )
 
 
@@ -836,7 +893,7 @@
     )
 
 
-def back_block(parts, cotangent, attn_out, gain, collective_id):
+def back_block(parts, cotangent, attn_out, gain, moves, collective_id):
     def middle(total, rows, j, ins, outs):
         d_resid = ins[1][rows, :].astype(jnp.float32) + total
         outs[1][rows, :] = d_resid
@@ -849,17 +906,17 @@
     shape = cotangent.shape
     return line_call(
         collective_id, 8, middle, [parts, cotangent, attn_out, gain],
-        [(parts.shape, jnp.bfloat16), (shape, jnp.float32), ((8, shape[1]), jnp.float32)], True, True,
-    )
-
-
-def last_block(parts, d_resid, collective_id):
+        [(parts.shape, jnp.bfloat16), (shape, jnp.float32), ((8, shape[1]), jnp.float32)], True, True, moves,
+    )
+
+
+def last_block(parts, d_resid, moves, collective_id):
     def middle(total, rows, j, ins, outs):
         outs[0][rows, :] = (ins[1][rows, :] + total).astype(jnp.bfloat16)
 
     return line_call(
-        collective_id, 8, middle, [parts, d_resid], [(d_resid.shape, jnp.bfloat16)], True, False
-    )[0]
+        collective_id, 8, middle, [parts, d_resid], [(d_resid.shape, jnp.bfloat16)], True, False, moves
+    )
 
 
 def on_device(
@@ -890,7 +947,7 @@
     )
     extra = jnp.pad(extra[None], ((0, 15), (0, model_width - extra.shape[0])))
     payload, full_qkv, full_output = gather_blocks(
-        jnp.concatenate([hidden_in, extra]), [[w_query, w_key, w_value]], [w_output], 0
+        jnp.concatenate([hidden_in, extra]), [Spread(w_query, w_key, w_value), Stack(w_output)], 0
     )
     tokens = payload[:, :length].reshape(blocks * length, model_width)
     docs = payload[:, length, 4 * length : 5 * length].astype(jnp.int32)
@@ -952,8 +1009,7 @@
         to_blocks(jnp.dot(mixed_low, full_output, preferred_element_type=f32)),
         hidden_in,
         gain_attn,
-        [[w_gate], [w_up]],
-        [w_down],
+        [Spread(w_gate), Spread(w_up), Stack(w_down)],
         1,
     )
     resid_low = resid_low.reshape(blocks * length, model_width)
@@ -976,24 +1032,58 @@
         jnp.bfloat16
     )
     d_up_low = (d_hidden_ffn * gate_proj * gate_sig).astype(jnp.bfloat16)
-    d_attn_low, d_resid, attn_gain_term = back_block(
+    def outer(left_side, right_side):
+        return lax.dot_general(
+            left_side, right_side, (((0,), (0,)), ((), ())), preferred_element_type=f32
+        ).astype(jnp.bfloat16)
+
+    def joined(first, second):
+        return (first.astype(f32) + second.astype(f32)).astype(jnp.bfloat16)
+
+    ff_rows = w_down.shape[0]
+    part_gate = outer(resid_low, d_gate_low)
+    part_up = outer(resid_low, d_up_low)
+    part_down = outer(hidden_ffn, d_ffn_low).reshape(2, ff_rows, model_width)
+
+    def other_columns(line, ref):
+        return ref.at[:, pl.ds(pl.multiple_of((1 - line.rep) * ff_rows, ff_rows), ff_rows)]
+
+    def other_pair(line, ref):
+        return ref.at[1 - line.pair]
+
+    def other_rows(line, ref):
+        return ref.at[:, 1 - line.pair]
+
+    def same(line, ref):
+        return ref
+
+    columns = (model_width, ff_rows)
+    d_attn_low, d_resid, attn_gain_term, there_gate, there_up, there_down = back_block(
         to_blocks(dot_back(d_gate_low, full_gate) + dot_back(d_up_low, full_up)),
         out_cotangent,
         attn_out,
         gain_attn,
+        [
+            Swap(part_gate, columns, other_columns, "partner"),
+            Swap(part_up, columns, other_columns, "partner"),
+            Swap(part_down, part_down.shape[1:], other_pair, "across"),
+        ],
         3,
     )
+
+    def own_columns(values):
+        return lax.dynamic_slice_in_dim(values, lax.axis_index("rep") * ff_rows, ff_rows, 1)
+
+    def own_pair(values, axis):
+        return lax.dynamic_index_in_dim(values, pair, axis, keepdims=False)
+
+    ffn_part = jnp.concatenate(
+        [joined(own_columns(part_gate), there_gate), joined(own_columns(part_up), there_up)], axis=1
+    ).reshape(LINE, 2, 2 * length, 2 * ff_rows)
+    ffn_part = joined(own_pair(ffn_part, 1), pair_swap(own_pair(ffn_part[:, ::-1], 1)))
+    down_part = joined(own_pair(part_down, 0), there_down)
     d_attn_low = d_attn_low.reshape(blocks * length, model_width)
 
-    def outer(left_side, right_side):
-        return lax.dot_general(
-            left_side, right_side, (((0,), (0,)), ((), ())), preferred_element_type=f32
-        )
-
-    grad_down = reduce_rows_of(outer(hidden_ffn, d_ffn_low), pair)
-    grad_gate = reduce_columns(outer(resid_low, d_gate_low), pair)
-    grad_up = reduce_columns(outer(resid_low, d_up_low), pair)
-    grad_output = reduce_rows_of(outer(mixed_low, d_attn_low), pair)
     d_mixed_low = split_heads(dot_back(d_attn_low, full_output).astype(jnp.bfloat16))
     d_value = jnp.einsum("shqk,sqhd->skhd", prob_low, d_mixed_low, preferred_element_type=f32)
     d_prob = jnp.einsum("sqhd,skhd->shqk", d_mixed_low, value_low, preferred_element_type=f32)
@@ -1028,16 +1118,36 @@
         jnp.bfloat16
     )
     d_value_low = d_value.reshape(blocks * length, width).astype(jnp.bfloat16)
-    hidden_grad = last_block(
+    d_qkv_low = jnp.concatenate([d_query_low, d_key_low, d_value_low], axis=1)
+    part_qkv = outer(tokens, d_qkv_low).reshape(LINE, 2, 2 * length, 3 * width)
+    part_output = outer(mixed_low, d_attn_low).reshape(2, length, model_width)
+    hidden_grad, there_qkv, there_output, there_down, ffn_total = last_block(
         to_blocks(
-            dot_back(jnp.concatenate([d_query_low, d_key_low, d_value_low], axis=1), full_qkv)
+            dot_back(d_qkv_low, full_qkv)
         ),
         d_resid,
+        [
+            Swap(part_qkv, (LINE, 2 * length, 3 * width), other_rows, "across"),
+            Swap(part_output, (length, model_width), other_pair, "across"),
+            Swap(down_part, down_part.shape, same, "partner"),
+            Deal(ffn_part.reshape(blocks, length, 2 * ff_rows), 2, True),
+        ],
         4,
     )
-    grad_query = reduce_columns(outer(tokens, d_query_low), pair)
-    grad_key = reduce_columns(outer(tokens, d_key_low), pair)
-    grad_value = reduce_columns(outer(tokens, d_value_low), pair)
+    qkv_part = joined(own_pair(part_qkv, 1), there_qkv).reshape(blocks, length, 3 * width)
+    output_part = joined(own_pair(part_output, 0), there_output)
+    qkv_own, qkv_there, there_output = line_call(
+        5, 1, None, [], [], False, False,
+        [Deal(qkv_part, 3, False), Swap(output_part, output_part.shape, same, "partner")],
+    )
+
+    def total_of(first, second):
+        return first.astype(f32) + second.astype(f32)
+
+    grad_query, grad_key, grad_value = jnp.split(total_of(qkv_own, qkv_there), 3, axis=1)
+    grad_gate, grad_up = jnp.split(ffn_total.astype(f32), 2, axis=1)
+    grad_output = total_of(output_part, there_output)
+    grad_down = total_of(down_part, there_down)
     head_terms = jnp.stack([query_gain_term, key_gain_term]).reshape(2, 2, HEAD_DIM)
     own_term, other_term = by_pair(pair, head_terms[:, 0], head_terms[:, 1])
     head_grads = own_term + pair_swap(other_term)

time: 1040 us -> 788 us (0.76)
  waiting for transfers between devices: 257 us -> 32.7 us
  Pallas kernels: 413 us -> 522 us
  local copies, waits for them, and re-layouts: 109 us -> 62.4 us
  other arithmetic: 81.5 us -> 38.5 us
  starting transfers between devices: 51.8 us -> 15.9 us
    ppermute x8 -> x1, waiting for transfers between devices: 118 us -> 0.01 us  [rep_swap(): return lax.ppermute(values, 'rep', [(0, 1), (1, 0)])]
    ppermute x10 -> x4, waiting for transfers between devices: 130 us -> 13.4 us  [pair_swap(): return lax.ppermute(values, 'shard', shard_perm(lambda index: index ^ 2))]
    pallas_call x5 -> x6, Pallas kernels: 413 us -> 522 us  [line_call(): pl.pallas_call(kernel, out_shape=[jax.ShapeDtypeStruct(shape, kind) for s...]
    reshape x15 -> x0, local copies, waits for them, and re-layouts: 45 us -> none  [the longest x10 32.1 us: reduce_columns(): got.reshape(4, 2, rows, 2, n).transpose(2, 0, 3, 1, 4).reshape(rows, 16 * n)]
    convert_element_type x14 -> x5, other arithmetic: 41.2 us -> 9.72 us  [joined(): return (first.astype(f32) + second.astype(f32)).astype(jnp.bfloat16)]
    all_to_all x5 -> x0, starting transfers between devices: 22.9 us -> none  [reduce_columns(): lax.all_to_all(mine, 'shard', 0, 0, axis_index_groups=line_groups(), tile...]
    add x7 -> x3, other arithmetic: 20.2 us -> 4.25 us  [total_of(): return first.astype(f32) + second.astype(f32)]
    dot_general x2 -> x0, local copies, waits for them, and re-layouts: 12.8 us -> none  [outer(): lax.dot_general(left_side, right_side, (((0,), (0,)), ((), ())), preferre...]
  transfers between devices with their start and end apart: 32 -> 14, of which waited for: 9 -> 6; matrix products, arithmetic and copies ran while one was open for 18% -> 8% of each run, Pallas kernels for 14% -> 9%
where the time goes in v3:
time: 788 us; the launch traced here: 780 us
  Pallas kernels  522 us (66%)
  matrix products  92.6 us (12%)
  local copies, waits for them, and re-layouts  62.4 us (8%)
  other arithmetic  38.5 us (5%)
  waiting for transfers between devices  32.7 us (4%)
  starting transfers between devices  15.9 us (2%)
  between operations  15.2 us (2%)
    pallas_call x6, Pallas kernels, line_call(): pl.pallas_call(kernel, out_shape=[jax.ShapeDtypeStruct(shape, kind) for s...  522 us
    dot_general x5, matrix products, dot_back(): lax.dot_general(left_side, right_side, (((1,), (1,)), ((), ())), preferre...  33.7 us
    unnamed x121, local copies, waits for them, and re-layouts  32.9 us
    dot_general x5, matrix products, outer(): lax.dot_general(left_side, right_side, (((0,), (0,)), ((), ())), preferre...  25.2 us
  transfers between devices with their start and end apart: 14, of which 6 were waited for; matrix products, arithmetic and copies ran while one was open for 8% of the time, Pallas kernels for 9%

profile of v3, /device:TPU:0, one launch (start us, length us, event | category | flops | bytes accessed | tf_op | source)
XLA Modules:
  0.0 779.5 jit_solution(13774268528870627203)
XLA Ops:
  7.9 3.0 collective-permute-start.4
  20.3 68.1 %shard_map.237 = (bf16[8,144,2048]{2,1,0:T(8,128)(2,1)S(1)}, bf16[2048,768]{1,0:T(8,128)(2,1)S(1)}, bf16[256,2048]{1,0:T(8,128)(2,1)S(1)}) custom-call(bf16[144,2048]{1,0:T(8,128)(2,1)S(1)} %fusion.13.refs_0_, bf16[128,2048]{1,0:T(8,128)(2,1)S(1)} %copy-done.14, bf16[128,2048]{1,0:T(8,128)(2,1)S(1)} %copy-done.15, bf16[128,2048]{1,0:T(8,128)(2,1)S(1)} %copy-done.16, ...), custom_call_target="tpu_custom_call" | custom-call | flops 10000000 | bytes 200000000 | tf_op jit(solution)/shard_map/pallas_call | solution.py:832
  95.7 3.6 fusion.40
  103.9 3.1 fusion.19
  109.4 2.9 collective-permute-start.3
  114.5 3.5 collective-permute-done.1
  137.8 3.4 convolution_convert_fusion
  142.3 133.7 %shard_map.238 = (bf16[8,128,2048]{2,1,0:T(8,128)(2,1)S(1)}, f32[128,2048]{1,0:T(8,128)S(1)}, f32[128,2048]{1,0:T(8,128)S(1)}, bf16[2048,1024]{1,0:T(8,128)(2,1)...) custom-call(bf16[8,128,2048]{2,1,0:T(8,128)(2,1)} %bitcast.198, bf16[128,2048]{1,0:T(8,128)(2,1)S(1)} %copy-done.5, ...), custom_call_target="tpu_custom_call" | custom-call | flops 10000000 | bytes 200000000 | tf_op jit(solution)/shard_map/pallas_call | solution.py:832
  276.0 6.4 fusion.41
  282.4 6.5 multiply_convert_fusion.2
  288.9 4.8 convolution_convert_fusion.5
  293.7 70.8 %shard_map.239 = (bf16[8,128,2048]{2,1,0:T(8,128)(2,1)S(1)}, bf16[128,2048]{1,0:T(8,128)(2,1)S(1)}, f32[8,2048]{1,0:T(8,128)S(1)}) custom-call(bf16[8,128,2048]{2,1,0:T(8,128)(2,1)S(1)} %bitcast.182, f32[128,2048]{1,0:T(8,128)S(1)} %get-tuple-element.46.refs_1_, bf16[128,2048]{1,0:T(8,128)(2,1)S(1)} %copy-done.9, f32[1,2048]{1,0:T(1,128)S(1)} %bitcast.187), custom_call_target="tpu_custom_call" | custom-call | flops 10000000 | bytes 200000000 | tf_op jit(solution)/shard_map/pallas_call | solution.py:832
  364.6 6.3 convolution_convert_fusion.2
  370.9 8.2 %multiply_convert_fusion = (bf16[1024,1024]{1,0:T(8,128)(2,1)S(1)}, bf16[1024,1024]{1,0:T(8,128)(2,1)S(1)}) fusion(f32[1024,1024]{1,0:T(8,128)} %copy-done.51, f32[1024,1024]{1,0:T(8,128)} %get-tuple-element.122, bf16[1024,2048]{1,0:T(8,128)(2,1)S(1)} %bitcast.193, bf16[1024,2048]{1,0:T(8,128)(2,1)S(1)} %copy-done.50), kind=kOutput, calls=%fused_computation.9 | convolution fusion | flops 4308598784 | bytes 20971520 | tf_op jit(solution)/shard_map/dot_general | solution.py:37
  379.1 6.2 convolution_convert_fusion.4.refs_4_
  385.3 6.9 fusion.42
  392.2 6.4 convolution_convert_fusion.3.refs_5_
  398.6 8.3 %add_convert_fusion = bf16[1024,2048]{1,0:T(8,128)(2,1)} fusion(f32[1024,2048]{1,0:T(8,128)} %fusion.42, bf16[1024,1024]{1,0:T(8,128)(2,1)S(1)} %get-tuple-element.73, bf16[2048,1024]{1,0:T(8,128)(2,1)S(1)} %copy-done.47), kind=kOutput, calls=%fused_computation | convolution fusion | flops 4299161600 | bytes 18874368 | tf_op jit(solution)/shard_map/dot_general | solution.py:37
  406.9 101.7 %shard_map.240 = (bf16[8,128,2048]{2,1,0:T(8,128)(2,1)S(1)}, f32[128,2048]{1,0:T(8,128)S(1)}, f32[8,2048]{1,0:T(8,128)S(1)}, bf16[2048,512]{1,0:T(8,128)(2,1)S(1...) custom-call(bf16[8,128,2048]{2,1,0:T(8,128)(2,1)} %bitcast.211, bf16[128,2048]{1,0:T(8,128)(2,1)S(1)} %copy-done.9, ...), custom_call_target="tpu_custom_call" | custom-call | flops 10000000 | bytes 200000000 | tf_op jit(solution)/shard_map/pallas_call | solution.py:832
  528.6 3.2 multiply_subtract_fusion.1
  538.8 3.2 fusion.10
  543.8 3.5 add_convert_fusion.1
  549.9 4.6 rev.3
  554.6 3.2 fusion.1.refs_4_
  565.0 3.6 collective-permute-done.7
  570.3 5.0 convolution_convert_fusion.6
  575.3 9.0 %reduce-scatter.4.cloned.1.call-done = f32[128,2]{1,0:T(8,128)} async-done(((f32[2048,2]{1,0:T(8,128)}), f32[128,2]{1,0:T(8,128)}) %reduce-scatter.4.cloned.1.call-update) | async-done | bytes 1040
  586.8 7.9 %convolution_convert_fusion.1 = bf16[1024,2048]{1,0:T(8,128)(2,1)} fusion(bf16[2048,768]{1,0:T(8,128)(2,1)} %copy-done.18, bf16[1024,256]{0,1:T(8,128)(2,1)} %bitcast.216, bf16[1024,256]{0,1:T(8,128)(2,1)} %copy-done.42, bf16[1024,256]{0,1:T(8,128)(2,1)} %copy-done.41), kind=kOutput, calls=%fused_computation.14 | convolution fusion | flops 3228041216 | bytes 8912896 | tf_op jit(solution)/shard_map/dot_general | solution.py:37
  595.2 13.4 %collective-permute-done.10 = bf16[4,256,1024]{2,1,0:T(8,128)(2,1)} collective-permute-done((bf16[4,256,1024]{2,1,0:T(8,128)(2,1)}, bf16[4,256,1024]{2,1,0:T(8,128)(2,1)}, u32[]{:S(2)}, u32[]{:S(2)}) %collective-permute-start.10) | collective-permute-done | bytes 2097184 | tf_op jit(solution)/shard_map/ppermute | solution.py:288
  611.2 97.8 %shard_map.241 = (bf16[128,2048]{1,0:T(8,128)(2,1)S(1)}, bf16[4,256,768]{2,1,0:T(8,128)(2,1)S(1)}, bf16[128,2048]{1,0:T(8,128)(2,1)S(1)}, bf16[512,2048]{1,0:T(8,128)(2,1)S(1)}, bf16[128,16384]{1,0:T(8,128)(2,1)}) custom-call(bf16[8,128,2048]{2,1,0:T(8,128)(2,1)} %bitcast.207, f32[128,2048]{1,0:T(8,128)S(1)} %copy-done.11, ...), custom_call_target="tpu_custom_call" | custom-call | flops 10000000 | bytes 200000000 | tf_op jit(solution)/shard_map/pallas_call | solution.py:832
  712.3 50.1 %shard_map.242 = (bf16[128,6144]{1,0:T(8,128)(2,1)S(1)}, bf16[128,6144]{1,0:T(8,128)(2,1)S(1)}, bf16[128,2048]{1,0:T(8,128)(2,1)S(1)}) custom-call(bf16[8,128,768]{2,1,0:T(8,128)(2,1)S(1)} %bitcast.181, bf16[128,2048]{1,0:T(8,128)(2,1)S(1)} %fusion.11.refs_1_), custom_call_target="tpu_custom_call" | custom-call | flops 10000000 | bytes 200000000 | tf_op jit(solution)/shard_map/pallas_call | solution.py:832
  766.5 4.4 fusion.31
  (217 shorter events, 101.7 us)
Async XLA Ops:
  7.2 577.2 %reduce-scatter.4.cloned.1.call-start = ((), (), s32[]{:S(2)}) async-start(), calls=%async_computation.1 | async-start | bytes 1114112
  7.9 99.6 %collective-permute-start.4 = (bf16[1,2,128]{2,1,0:T(2,128)(2,1)S(1)}, bf16[1,2,128]{2,1,0:T(2,128)(2,1)S(1)}, u32[]{:S(2)}, u32[]{:S(2)}) collective-permute-start(bf16[1,2,128]{2,1,0:T(2,128)(2,1)S(1)} %maximum_bitcast_fusion), channel_id=1, source_target_pairs={{0,2},{1,3},{2,0},{3,1},{4,6},{5,7},{6,4},{7,5},{8,10},{9,11},{10,... | collective-permute-start | bytes 1544 | tf_op jit(solution)/shard_map/ppermute | solution.py:288
  92.3 20.8 %collective-permute-start.5 = (bf16[4,2,4,128]{3,2,1,0:T(4,128)(2,1)S(1)}, bf16[4,2,4,128]{3,2,1,0:T(4,128)(2,1)S(1)}, u32[]{:S(2)}, u32[]{:S(2)}) collective-permute-start(bf16[4,2,4,128]{3,2,1,0:T(4,128)(2,1)S(1)} %reshape_squeeze.3), channel_id=1, source_target_pairs={{0,2},{1,3},{2,0},{3,1},{4,6},{5,7},{6,4},{7,5},{8,10},{9,11},{10,... | collective-permute-start | bytes 24584 | tf_op jit(solution)/shard_map/ppermute | solution.py:288
  101.0 6.4 copy-start.44
  101.0 6.5 copy-start.45
  101.3 6.3 collective-permute-start
  107.0 25.9 %copy-start.37 = (f32[8,128,64]{2,1,0:T(8,128)}, f32[8,128,64]{2,1,0:T(8,128)S(1)}, u32[]{:S(2)}) copy-start(f32[8,128,64]{2,1,0:T(8,128)S(1)} %get-tuple-element.110) | copy-start | bytes 786436
  107.5 29.1 %copy-start.38 = (bf16[8,128,2,128]{3,1,2,0:T(8,128)(2,1)}, bf16[8,128,2,128]{3,1,2,0:T(8,128)(2,1)S(1)}, u32[]{:S(2)}) copy-start(bf16[8,128,2,128]{3,1,2,0:T(8,128)(2,1)S(1)} %copy.90) | copy-start | bytes 1572868
  107.6 5.5 collective-permute-start.2
  109.4 5.0 collective-permute-start.3
  112.3 5.6 collective-permute-start.1
  276.0 6.5 copy-start.46
  282.4 6.5 copy-start.51
  282.4 6.5 copy-start.49
  364.5 6.3 copy-start.12
  364.6 6.3 copy-start.50
  392.2 6.4 copy-start.47
  542.0 21.2 %collective-permute-start.11 = (f32[2,128]{1,0:T(2,128)S(1)}, f32[2,128]{1,0:T(2,128)S(1)}, u32[]{:S(2)}, u32[]{:S(2)}) collective-permute-start(f32[2,128]{1,0:T(2,128)S(1)} %select_bitcast_fusion.2), channel_id=1, source_target_pairs={{0,2},{1,3},{2,0},{3,1},{4,6},{5,7},{6,4},{7,5},{8,10},{9,11},{10,... | collective-permute-start | bytes 3080 | tf_op jit(solution)/shard_map/ppermute | solution.py:288
  543.7 16.5 %collective-permute-start.6 = (f32[2,1024]{1,0:T(2,128)S(1)}, f32[2,1024]{1,0:T(2,128)S(1)}, u32[]{:S(2)}, u32[]{:S(2)}) collective-permute-start(f32[2,1024]{1,0:T(2,128)S(1)} %pad_maximum_fusion.14), channel_id=1, source_target_pairs={{0,1},{1,0},{2,3},{3,2},{4,5},{5,4},{6,7},{7,6},{8,9},{9,8},{10,11... | collective-permute-start | bytes 24584 | tf_op jit(solution)/shard_map/ppermute | solution.py:284
  554.6 14.1 %copy-start.24 = (f32[1024,768]{0,1:T(8,128)S(1)}, f32[1024,768]{0,1:T(8,128)}, u32[]{:S(2)}) copy-start(f32[1024,768]{0,1:T(8,128)} %copy-done.23) | copy-start | bytes 9437188
  554.6 14.1 %copy-start.26 = (f32[8,128,2,128]{1,0,3,2:T(8,128)S(1)}, f32[8,128,2,128]{1,0,3,2:T(8,128)}, u32[]{:S(2)}) copy-start(f32[8,128,2,128]{1,0,3,2:T(8,128)} %copy.94) | copy-start | bytes 3145732
  554.6 14.1 %copy-start.27 = (f32[8,128,2,128]{1,0,3,2:T(8,128)S(1)}, f32[8,128,2,128]{1,0,3,2:T(8,128)}, u32[]{:S(2)}) copy-start(f32[8,128,2,128]{1,0,3,2:T(8,128)} %copy.98) | copy-start | bytes 3145732
  558.0 12.2 %copy-start.40 = (bf16[8,128,2048]{2,1,0:T(8,128)(2,1)S(1)}, bf16[8,128,2048]{2,1,0:T(8,128)(2,1)}, u32[]{:S(2)}) copy-start(bf16[8,128,2048]{2,1,0:T(8,128)(2,1)} %copy-done.39) | copy-start | bytes 12582916
  558.0 12.2 %copy-start.43 = (bf16[32,8,8,128]{3,1,2,0:T(8,128)(2,1)S(1)}, bf16[32,8,8,128]{3,1,2,0:T(8,128)(2,1)}, u32[]{:S(2)}) copy-start(bf16[32,8,8,128]{3,1,2,0:T(8,128)(2,1)} %copy.142) | copy-start | bytes 1572868
  559.5 49.0 %collective-permute-start.10 = (bf16[4,256,1024]{2,1,0:T(8,128)(2,1)}, bf16[4,256,1024]{2,1,0:T(8,128)(2,1)}, u32[]{:S(2)}, u32[]{:S(2)}) collective-permute-start(bf16[4,256,1024]{2,1,0:T(8,128)(2,1)} %dynamic-slice_bitcast_fusion), channel_id=1, source_target_pairs={{0,2},{1,3},{2,0},{3,1},{4,6},{5,7},{6,4},{7,5},{8,10},{9,11},{10,... | collective-permute-start | bytes 6291464 | tf_op jit(solution)/shard_map/ppermute | solution.py:288
  560.1 4.8 collective-permute-start.8
  560.8 4.2 collective-permute-start.9
  563.1 5.4 collective-permute-start.7
  585.3 23.3 %copy-start.22 = (bf16[2048,1024]{1,0:T(8,128)(2,1)S(1)}, bf16[2048,1024]{1,0:T(8,128)(2,1)}, u32[]{:S(2)}) copy-start(bf16[2048,1024]{1,0:T(8,128)(2,1)} %pad_maximum_fusion) | copy-start | bytes 12582916
  585.3 9.4 %collective-permute-start.12 = (f32[4,128]{1,0:T(4,128)S(1)}, f32[4,128]{1,0:T(4,128)S(1)}, u32[]{:S(2)}, u32[]{:S(2)}) collective-permute-start(f32[4,128]{1,0:T(4,128)S(1)} %pad_maximum_fusion.15), channel_id=1, source_target_pairs={{0,16},{16,0},{1,17},{17,1},{2,18},{18,2},{3,19},{19,3},{4,20},{20... | collective-permute-start | bytes 6152 | tf_op jit(solution)/shard_map/ppermute | solution.py:292
  594.7 16.5 %copy-start = (bf16[2048,768]{1,0:T(8,128)(2,1)S(1)}, bf16[2048,768]{1,0:T(8,128)(2,1)}, u32[]{:S(2)}) copy-start(bf16[2048,768]{1,0:T(8,128)(2,1)} %convolution_convert_fusion.6) | copy-start | bytes 9437188
  594.7 16.5 %copy-start.11 = (f32[128,2048]{1,0:T(8,128)S(1)}, f32[128,2048]{1,0:T(8,128)}, u32[]{:S(2)}) copy-start(f32[128,2048]{1,0:T(8,128)} %copy-done.10) | copy-start | bytes 3145732
  (34 other events, 114.4 us)
Sparse Core Ops, SparseCore 0:
  528.7 55.6 reduce-scatter.3

commit v4 on v3

--- a/solution.py
+++ b/solution.py
@@ -280,25 +280,12 @@
     return [(index, move(index)) for index in range(16)]
 
 
-def core_swap(values):
-    return lax.ppermute(values, "shard", shard_perm(lambda index: index ^ 1))
-
-
 def pair_swap(values):
     return lax.ppermute(values, "shard", shard_perm(lambda index: index ^ 2))
 
 
 def rep_swap(values):
     return lax.ppermute(values, "rep", [(0, 1), (1, 0)])
-
-
-def line_shift(values, steps):
-    return lax.ppermute(values, "shard", shard_perm(lambda index: (index + 4 * steps) % 16))
-
-
-def group_sum(values):
-    both = values + core_swap(values)
-    return both + line_shift(both, 1) + line_shift(both, 2) + line_shift(both, 3)
 
 
 def by_pair(pair, own, other):
@@ -368,13 +355,15 @@
 
 
 class Spread:
-    semaphores = ((2 * LINE,),) * 4 + ((2 * LINE, 2),) * 2
-    slots = 6 + 2 * LINE
-
-    def __init__(self, *weights):
-        self.inputs = list(weights)
+    semaphores = ((2 * LINE,),) * 2 + ((2 * LINE, 2),) * 4
+    buffers = ()
+    near = True
+
+    def __init__(self, *weights, begin=0, burst=False):
+        self.inputs, self.begin, self.burst = list(weights), begin, burst
         shape = (16 * weights[0].shape[0], sum(weight.shape[1] for weight in weights) // 8)
         self.outputs = [jax.ShapeDtypeStruct(shape, jnp.bfloat16)]
+        self.slots = begin + 3 + 2 * LINE
 
     def bind(self, line, sources, targets, sems):
         self.line, self.sources, self.target = line, sources, targets[0]
@@ -382,12 +371,16 @@
         self.half = sources[0].shape[0] // 2
 
     def slot(self, t):
-        if t < 2 * LINE:
-            self.start(t)
-        if 3 <= t < 3 + 2 * LINE:
-            self.came(t - 3)
-        if 6 <= t < 6 + 2 * LINE:
-            self.onward(t - 6)
+        t -= self.begin
+        for p in range(2 * LINE):
+            if t == (0 if self.burst else (p + 1) // 3):
+                self.start(p)
+        for p in range(2 * LINE):
+            if t == (p + 1 if p else 0):
+                self.came(p)
+        for p in range(2 * LINE):
+            if t == p + 3:
+                self.onward(p)
 
     def rows(self, place, pair, core, rep):
         start = ((place * 4 + pair * 2 + core) * 2 + rep) * self.half
@@ -399,9 +392,9 @@
         here = self.rows(line.place, line.pair, line.core, line.rep)
         mine = pl.ds(pl.multiple_of(line.rep * half, half), half)
         at = 0
-        for source in self.sources:
-            n = source.shape[1] // 16
-            for q in range(2):
+        for q in range(2):
+            for source in self.sources:
+                n = source.shape[1] // 16
                 column = pl.multiple_of((place * 4 + q * 2 + core) * n, n)
                 piece, goal = source.at[mine, pl.ds(column, n)], here.at[:, pl.ds(at, n)]
                 if p == 0:
@@ -412,10 +405,10 @@
                     ).start()
                 at += n
 
-    def cross(self, p, pair):
+    def cross(self, p, pair, rep, which):
         place, core = self.line.piece(p, -1)
-        ref = self.rows(place, pair, core, self.line.rep)
-        return remote(ref, ref, self.y_send.at[p], self.y_recv.at[p], self.line.across)
+        ref = self.rows(place, pair, core, rep)
+        return remote(ref, ref, self.y_send.at[p, which], self.y_recv.at[p, which], self.line.across)
 
     def over(self, p, pair, rep, which):
         place, core = self.line.piece(p, -1)
@@ -430,71 +423,102 @@
             pltpu.make_async_copy(ref, ref, self.z_recv.at[0]).wait()
         else:
             remote(ref, ref, self.z_send.at[p], self.z_recv.at[p], line.sibling).wait_recv()
-        self.cross(p, line.pair).start()
+        self.cross(p, line.pair, line.rep, 0).start()
         self.over(p, line.pair, line.rep, 0).start()
 
     def onward(self, p):
         line = self.line
-        self.cross(p, 1 - line.pair).wait_recv()
-        self.over(p, 1 - line.pair, line.rep, 1).start()
+        if p % 2:
+            self.over(p, line.pair, 1 - line.rep, 0).wait_recv()
+            self.cross(p, line.pair, 1 - line.rep, 1).start()
+        else:
+            self.cross(p, 1 - line.pair, line.rep, 0).wait_recv()
+            self.over(p, 1 - line.pair, line.rep, 1).start()
 
     def finish(self):
         line = self.line
+        pair, rep = line.pair, line.rep
         for p in range(2 * LINE):
             if p > 0:
-                ref = self.rows(line.place, line.pair, line.core, line.rep)
+                ref = self.rows(line.place, pair, line.core, rep)
                 remote(ref, ref, self.z_send.at[p], self.z_recv.at[p], line.sibling).wait_send()
-            self.cross(p, line.pair).wait_send()
-            for which, pair in ((0, line.pair), (1, 1 - line.pair)):
-                self.over(p, pair, line.rep, which).wait_send()
-                self.over(p, pair, 1 - line.rep, which).wait_recv()
+            self.cross(p, pair, rep, 0).wait_send()
+            self.over(p, pair, rep, 0).wait_send()
+            if p % 2:
+                self.cross(p, 1 - pair, rep, 0).wait_recv()
+                self.cross(p, pair, 1 - rep, 1).wait_send()
+                self.cross(p, 1 - pair, 1 - rep, 1).wait_recv()
+            else:
+                self.over(p, pair, 1 - rep, 0).wait_recv()
+                self.over(p, 1 - pair, rep, 1).wait_send()
+                self.over(p, 1 - pair, 1 - rep, 1).wait_recv()
 
 
 class Stack:
-    semaphores = ((3,),)
-    slots = 3
-
-    def __init__(self, weight):
-        self.inputs = [weight]
+    buffers = ()
+    near = True
+
+    def __init__(self, weight, count):
+        self.inputs, self.count = [weight], count
         self.outputs = [jax.ShapeDtypeStruct((2 * weight.shape[0], weight.shape[1]), weight.dtype)]
+        self.semaphores = ((1,),) + ((count,),) * 4
+        self.slots = 1 + count
 
     def bind(self, line, sources, targets, sems):
-        self.line, self.sems = line, sems[0]
-        self.source = sources[0]
-        size = self.source.shape[0]
-        self.mine = targets[0].at[pl.ds(pl.multiple_of(line.pair * size, size), size), :]
+        self.line, self.source, self.target = line, sources[0], targets[0]
+        self.local, self.y_send, self.y_recv, self.x_send, self.x_recv = sems
+        self.size = self.source.shape[0]
+
+    def here(self):
+        size = self.size
+        mine = self.target.at[pl.ds(pl.multiple_of(self.line.pair * size, size), size), :]
+        return pltpu.make_async_copy(self.source, mine, self.local.at[0])
+
+    def there(self, p):
+        line, part = self.line, self.size // (2 * self.count)
+        start = pl.multiple_of((line.rep * self.count + p) * part, part)
+        goal = self.target.at[pl.ds(pl.multiple_of(line.pair * self.size + start, part), part), :]
+        return remote(
+            self.source.at[pl.ds(start, part), :], goal, self.y_send.at[p], self.y_recv.at[p], line.across
+        )
+
+    def onward(self, p, rep):
+        line, part = self.line, self.size // (2 * self.count)
+        start = (1 - line.pair) * self.size + (rep * self.count + p) * part
+        ref = self.target.at[pl.ds(pl.multiple_of(start, part), part), :]
+        return remote(ref, ref, self.x_send.at[p], self.x_recv.at[p], line.partner)
 
     def slot(self, t):
-        if t == 2:
-            self.start()
-
-    def here(self):
-        return pltpu.make_async_copy(self.source, self.mine, self.sems.at[0])
-
-    def there(self):
-        return remote(self.source, self.mine, self.sems.at[1], self.sems.at[2], self.line.across)
-
-    def start(self):
-        self.there().start()
-        self.here().start()
+        if t == 0:
+            for k in range(self.count):
+                self.there(k).start()
+            self.here().start()
+        if 1 <= t < 1 + self.count:
+            self.there(t - 1).wait_recv()
+            self.onward(t - 1, self.line.rep).start()
 
     def finish(self):
         self.here().wait()
-        self.there().wait()
+        for p in range(self.count):
+            self.there(p).wait_send()
+            self.onward(p, self.line.rep).wait_send()
+            self.onward(p, 1 - self.line.rep).wait_recv()
 
 
 class Swap:
     semaphores = ((2,),)
+    buffers = ()
+    near = True
     slots = 1
 
-    def __init__(self, values, shape, pick, to):
-        self.inputs, self.pick, self.to = [values], pick, to
-        self.outputs = [jax.ShapeDtypeStruct(shape, values.dtype)]
-
-    def bind(self, line, sources, targets, sems):
-        self.copy = remote(
-            self.pick(line, sources[0]), targets[0], sems[0].at[0], sems[0].at[1], getattr(line, self.to)
-        )
+    def __init__(self, values, start, count):
+        self.inputs, self.start, self.count = [values], start, count
+        self.outputs = [jax.ShapeDtypeStruct((count, values.shape[1]), values.dtype)]
+
+    def bind(self, line, sources, targets, scratch):
+        sends, recvs = scratch[0].at[0], scratch[0].at[1]
+        rows = sources[0].at[pl.ds(self.start, self.count), :]
+        self.copy = remote(rows, targets[0], sends, recvs, line.partner)
 
     def slot(self, t):
         if t == 0:
@@ -506,37 +530,36 @@
 
 class Deal:
     semaphores = ((2 * LINE,),) * 4
+    buffers = ()
+    near = True
     slots = 3 + 2 * LINE
 
-    def __init__(self, values, count, joint):
-        rows, width = values.shape[1:]
-        self.inputs, self.joint, self.count = [values], joint, count
-        self.n = width // count if joint else width // (2 * count)
-        shape = jax.ShapeDtypeStruct((rows, 16 * count * self.n), values.dtype)
-        self.outputs = [shape] if joint else [shape, shape]
-
-    def bind(self, line, sources, targets, sems):
-        self.line, self.source, self.targets = line, sources[0], targets
-        self.z_send, self.z_recv, self.x_send, self.x_recv = sems
-
-    def columns(self, place, core, rep):
-        n = self.n
-        at = 0
-        for index in range(self.count):
-            for q in (rep,) if self.joint else (0, 1):
-                yield at, pl.multiple_of((index * 16 + place * 4 + q * 2 + core) * n, n)
-                at += n
-
-    def whole(self, sem_send, sem_recv):
-        ref = self.source.at[0]
-        return remote(ref, ref, sem_send, sem_recv, self.line.partner)
+    def __init__(self, sources, per):
+        rows, width = sources[0].shape[1:]
+        self.inputs, self.per = list(sources), per
+        self.n = width // per
+        self.width = width * len(sources)
+        self.outputs = [jax.ShapeDtypeStruct((rows, 16 * self.width), sources[0].dtype)]
+
+    def bind(self, line, sources, targets, scratch):
+        self.line, self.sources, self.target = line, sources, targets[0]
+        self.z_send, self.z_recv, self.x_send, self.x_recv = scratch
+
+    def runs(self, place, core):
+        for index, source in enumerate(self.sources):
+            for run in range(self.per):
+                block = (index * self.per + run) * 16 + place * 4 + self.line.rep * 2 + core
+                yield source, run * self.n, pl.ds(pl.multiple_of(block * self.n, self.n), self.n)
+
+    def whole(self):
+        return self.target.at[:, pl.ds(0, self.width)]
 
     def start(self, p):
         line = self.line
         place, core = line.piece(p, 1)
-        for at, column in self.columns(line.place, line.core, line.rep):
-            piece = self.source.at[2 * place + core, :, pl.ds(at, self.n)]
-            goal = self.targets[0].at[:, pl.ds(column, self.n)]
+        for source, at, there in self.runs(line.place, line.core):
+            piece = source.at[2 * place + core, :, pl.ds(at, self.n)]
+            goal = self.target.at[:, there]
             if p == 0:
                 pltpu.make_async_copy(piece, goal, self.z_recv.at[0]).start()
             else:
@@ -545,34 +568,157 @@
                 ).start()
 
     def came(self, p):
-        line = self.line
+        line, ref = self.line, self.whole()
         if p == 0:
-            ref = self.source.at[0]
             pltpu.make_async_copy(ref, ref, self.z_recv.at[0]).wait()
         else:
-            self.whole(self.z_send.at[p], self.z_recv.at[p]).wait_recv()
+            remote(ref, ref, self.z_send.at[p], self.z_recv.at[p], line.partner).wait_recv()
         place, core = line.piece(p, -1)
-        for _, column in self.columns(place, core, line.rep):
-            there = pl.ds(column, self.n)
-            remote(
-                self.targets[0].at[:, there],
-                self.targets[-1].at[:, there],
-                self.x_send.at[p],
-                self.x_recv.at[p],
-                line.partner,
-            ).start()
+        for _, _, there in self.runs(place, core):
+            goal = self.target.at[:, there]
+            remote(goal, goal, self.x_send.at[p], self.x_recv.at[p], line.partner).start()
 
     def slot(self, t):
         if t < 2 * LINE:
             self.start(t)
-        if 3 <= t < 3 + 2 * LINE:
-            self.came(t - 3)
+        if t == 0:
+            self.came(0)
+        if 3 <= t < 2 + 2 * LINE:
+            self.came(t - 2)
 
     def finish(self):
+        ref = self.whole()
         for p in range(2 * LINE):
             if p > 0:
-                self.whole(self.z_send.at[p], self.z_recv.at[p]).wait_send()
-            self.whole(self.x_send.at[p], self.x_recv.at[p]).wait()
+                remote(ref, ref, self.z_send.at[p], self.z_recv.at[p], self.line.partner).wait_send()
+            remote(ref, ref, self.x_send.at[p], self.x_recv.at[p], self.line.partner).wait()
+
+
+def add_into(target, first, second):
+    step = 64
+
+    def some(index, carry):
+        rows = pl.ds(pl.multiple_of(index * step, step), step)
+        target[rows, :] = first[rows, :] + second[rows, :]
+        return carry
+
+    lax.fori_loop(0, target.shape[0] // step, some, 0)
+
+
+class Reduce:
+    near = True
+
+    def __init__(self, values, first):
+        rows, n = values.shape[0] // 8, values.shape[1] // 2
+        self.inputs, self.first, self.size, self.n = [values], first, rows, n
+        self.outputs = [jax.ShapeDtypeStruct((LINE, rows, n), values.dtype)]
+        self.chunks = 2 * LINE if first == "partner" else LINE
+        wide = n if first == "partner" else 2 * n
+        self.semaphores = ((self.chunks,),) * 2 + ((LINE,),) * 2
+        self.buffers = ((self.chunks, rows, wide), (LINE, rows, n), (LINE, rows, n))
+        self.join_at = [3 + (5 * k) // 2 for k in range(8)] if first == "partner" else [2, 4, 6, 8]
+        self.last_at = self.join_at[LINE:] if first == "partner" else [7, 8, 9, 10]
+        self.slots = max(self.last_at) + 1
+
+    def bind(self, line, sources, targets, scratch):
+        self.line, self.values, self.target = line, sources[0], targets[0]
+        self.send1, self.recv1, self.send2, self.recv2, self.came1, self.out2, self.came2 = scratch
+
+    def part(self, place, pair, rep=None):
+        rows = pl.ds(pl.multiple_of((place * 2 + pair) * self.size, self.size), self.size)
+        if rep is None:
+            return self.values.at[rows, :]
+        return self.values.at[rows, pl.ds(pl.multiple_of(rep * self.n, self.n), self.n)]
+
+    def leg1(self, k):
+        line = self.line
+        if self.first == "partner":
+            pair = 1 - line.pair if k < LINE else line.pair
+            return remote(
+                self.part(k % LINE, pair, 1 - line.rep), self.came1.at[k], self.send1.at[k], self.recv1.at[k], line.partner
+            )
+        return remote(self.part(k, 1 - line.pair), self.came1.at[k], self.send1.at[k], self.recv1.at[k], line.across)
+
+    def leg2(self, k):
+        device = self.line.across if self.first == "partner" else self.line.partner
+        return remote(self.out2.at[k], self.came2.at[k], self.send2.at[k], self.recv2.at[k], device)
+
+    def join(self, k):
+        line, n = self.line, self.n
+        self.leg1(k).wait_recv()
+        if self.first == "partner":
+            own = self.part(k % LINE, 1 - line.pair if k < LINE else line.pair, line.rep)
+            add_into(self.out2.at[k] if k < LINE else self.target.at[k - LINE], own, self.came1.at[k])
+            if k < LINE:
+                self.leg2(k).start()
+            return
+        for rep, goal in ((1 - line.rep, self.out2.at[k]), (line.rep, self.target.at[k])):
+            columns = pl.ds(pl.multiple_of(rep * n, n), n)
+            add_into(goal, self.part(k, line.pair, rep), self.came1.at[k, :, columns])
+        self.leg2(k).start()
+
+    def last(self, k):
+        self.leg2(k).wait_recv()
+        add_into(self.target.at[k], self.target.at[k], self.came2.at[k])
+
+    def slot(self, t):
+        if t == 0:
+            for k in range(self.chunks):
+                self.leg1(k).start()
+        for k in range(self.chunks):
+            if t == self.join_at[k]:
+                self.join(k)
+        for k in range(LINE):
+            if t == self.last_at[k]:
+                self.last(k)
+
+    def finish(self):
+        for k in range(self.chunks):
+            self.leg1(k).wait_send()
+        for k in range(LINE):
+            self.leg2(k).wait_send()
+
+
+class PairSum:
+    near = True
+
+    def __init__(self, values, count, at):
+        self.inputs, self.count, self.at = [values], count, at
+        self.outputs = [jax.ShapeDtypeStruct(values.shape[1:], values.dtype)]
+        self.semaphores = ((count,),) * 2
+        self.buffers = (values.shape[1:],)
+        self.slots = at + 2 * count
+
+    def bind(self, line, sources, targets, scratch):
+        self.line, self.values, self.target = line, sources[0], targets[0]
+        self.sends, self.recvs, self.came = scratch
+        self.size = self.target.shape[0] // self.count
+
+    def copy(self, k):
+        rows = pl.ds(k * self.size, self.size)
+        return remote(
+            self.values.at[1 - self.line.pair, rows, :],
+            self.came.at[rows, :],
+            self.sends.at[k],
+            self.recvs.at[k],
+            self.line.across,
+        )
+
+    def slot(self, t):
+        if t == 0:
+            for k in range(self.count):
+                self.copy(k).start()
+        for k in range(self.count):
+            if t == self.at + 2 * k:
+                rows = pl.ds(k * self.size, self.size)
+                self.copy(k).wait_recv()
+                add_into(
+                    self.target.at[rows, :], self.values.at[self.line.pair, rows, :], self.came.at[rows, :]
+                )
+
+    def finish(self):
+        for k in range(self.count):
+            self.copy(k).wait_send()
 
 
 def line_scatter_joint(line, k, rows, parts, sib):
@@ -726,7 +872,26 @@
     lax.fori_loop(0, pieces, piece, 0)
 
 
-def line_call(collective_id, pieces, middle, inputs, outputs, scatter, gather, moves=()):
+def take_from(items, count):
+    taken = items[:count]
+    del items[:count]
+    return taken
+
+
+def moves_scratch(moves):
+    scratch = []
+    for move in moves:
+        scratch += [pltpu.SemaphoreType.DMA(shape) for shape in move.semaphores]
+        scratch += [pltpu.VMEM(shape, jnp.bfloat16) for shape in move.buffers]
+    return scratch
+
+
+def moves_specs(moves, side):
+    near, far = pl.BlockSpec(memory_space=pltpu.VMEM), pl.BlockSpec(memory_space=pl.ANY)
+    return [near if move.near else far for move in moves for _ in getattr(move, side)]
+
+
+def line_call(collective_id, pieces, middle, inputs, outputs, scatter, gather, moves=(), limit=44):
     step = inputs[0].shape[-2] // pieces if inputs else 0
     low = jnp.bfloat16
     scratch = []
@@ -737,7 +902,7 @@
     if gather:
         scratch += [pltpu.SemaphoreType.DMA((LINE, 3, pieces)), pltpu.SemaphoreType.DMA((2 * LINE, pieces))]
     n_scratch = len(scratch)
-    scratch += [pltpu.SemaphoreType.DMA(shape) for move in moves for shape in move.semaphores]
+    scratch += moves_scratch(moves)
     moved = [values for move in moves for values in move.inputs]
     extras = [shape for move in moves for shape in move.outputs]
 
@@ -756,7 +921,7 @@
         rest = take(n_scratch)
         line = Line()
         for move, sources, targets in zip(moves, given, extra):
-            move.bind(line, sources, targets, take(len(move.semaphores)))
+            move.bind(line, sources, targets, take(len(move.semaphores) + len(move.buffers)))
         line.meet(bool(moves))
         if scatter:
             sib, rights, lefts, sums, sib_send, sib_recv, right_send, left_send, right_recv, left_recv = rest[:10]
@@ -828,15 +993,14 @@
             line_gather_end(line, pieces, step, outs[0], sends, recvs)
 
     vmem = pl.BlockSpec(memory_space=pltpu.VMEM)
-    whole = pl.BlockSpec(memory_space=pl.ANY)
     return pl.pallas_call(
         kernel,
         out_shape=[jax.ShapeDtypeStruct(shape, kind) for shape, kind in outputs] + extras,
-        in_specs=[vmem] * len(inputs) + [whole] * len(moved),
-        out_specs=[vmem] * len(outputs) + [whole] * len(extras),
+        in_specs=[vmem] * len(inputs) + moves_specs(moves, "inputs"),
+        out_specs=[vmem] * len(outputs) + moves_specs(moves, "outputs"),
         scratch_shapes=scratch,
         compiler_params=pltpu.CompilerParams(
-            collective_id=collective_id, has_side_effects=True, vmem_limit_bytes=40 << 20
+            collective_id=collective_id, has_side_effects=True, vmem_limit_bytes=limit << 20
         ),
         cost_estimate=pl.CostEstimate(flops=10_000_000, bytes_accessed=200_000_000, transcendentals=0),
     )(*inputs, *moved)
@@ -906,7 +1070,7 @@
     shape = cotangent.shape
     return line_call(
         collective_id, 8, middle, [parts, cotangent, attn_out, gain],
-        [(parts.shape, jnp.bfloat16), (shape, jnp.float32), ((8, shape[1]), jnp.float32)], True, True, moves,
+        [(parts.shape, jnp.bfloat16), (shape, jnp.float32), ((8, shape[1]), jnp.float32)], True, True, moves, 56,
     )
 
 
@@ -916,6 +1080,261 @@
 
     return line_call(
         collective_id, 8, middle, [parts, d_resid], [(d_resid.shape, jnp.bfloat16)], True, False, moves
+    )
+
+
+def line_exchange(line, mine, came, sends, recvs):
+    def copy(p):
+        place, core = line.piece(p, 1)
+        return remote(mine, came.at[p], sends.at[p], recvs.at[p], line.at(place, line.pair, core))
+
+    for p in range(1, 2 * LINE):
+        copy(p).start()
+    total = mine[...]
+    for p in range(1, 2 * LINE):
+        copy(p).wait_recv()
+        total = total + came[p]
+    for p in range(1, 2 * LINE):
+        copy(p).wait_send()
+    return total
+
+
+def spot(head, index):
+    start = (3 * head + index) * HEAD_DIM
+    return slice(start, start + HEAD_DIM)
+
+
+def turn_tables(turns):
+    half = turns.shape[1] // 2
+    swapped = pltpu.roll(turns, half, 1)
+    first = lax.broadcasted_iota(jnp.int32, turns.shape, 1) < half
+    return jnp.where(first, turns, swapped), jnp.where(first, -swapped, turns)
+
+
+def as_row(column):
+    return jnp.broadcast_to(column, (column.shape[0], column.shape[0])).T[0:1, :]
+
+
+def as_columns(row):
+    return jnp.broadcast_to(row, (row.shape[1], row.shape[1])).T
+
+
+def dot(left, right, left_dim, right_dim):
+    return lax.dot_general(
+        left, right, (((left_dim,), (right_dim,)), ((), ())), preferred_element_type=jnp.float32
+    )
+
+
+def heads_call(collective_id, body, inputs, outputs, scratch, rows, moves):
+    blocks, length = 2 * LINE, HEAD_DIM
+    scratch = [
+        pltpu.VMEM((rows, length), jnp.float32),
+        pltpu.VMEM((blocks, rows, length), jnp.float32),
+        pltpu.SemaphoreType.DMA((blocks,)),
+        pltpu.SemaphoreType.DMA((blocks,)),
+    ] + scratch
+    n_scratch = len(scratch)
+    moved = [values for move in moves for values in move.inputs]
+    extras = [shape for move in moves for shape in move.outputs]
+
+    def kernel(*refs):
+        refs = list(refs)
+        ins = take_from(refs, len(inputs))
+        given = [take_from(refs, len(move.inputs)) for move in moves]
+        outs = take_from(refs, len(outputs))
+        extra = [take_from(refs, len(move.outputs)) for move in moves]
+        rest = take_from(refs, n_scratch)
+        line = Line()
+        for move, sources, targets in zip(moves, given, extra):
+            move.bind(line, sources, targets, take_from(refs, len(move.semaphores) + len(move.buffers)))
+        line.meet(True)
+        passed = [0]
+
+        def tick():
+            for move in moves:
+                move.slot(passed[0])
+            passed[0] += 1
+
+        body(line, ins, outs, rest, tick)
+        while passed[0] < max([move.slots for move in moves] + [0]):
+            tick()
+        for move in moves:
+            move.finish()
+
+    vmem = pl.BlockSpec(memory_space=pltpu.VMEM)
+    return pl.pallas_call(
+        kernel,
+        out_shape=[jax.ShapeDtypeStruct(shape, kind) for shape, kind in outputs] + extras,
+        in_specs=[vmem] * len(inputs) + moves_specs(moves, "inputs"),
+        out_specs=[vmem] * len(outputs) + moves_specs(moves, "outputs"),
+        scratch_shapes=scratch + moves_scratch(moves),
+        compiler_params=pltpu.CompilerParams(
+            collective_id=collective_id, has_side_effects=True, vmem_limit_bytes=44 << 20
+        ),
+        cost_estimate=pl.CostEstimate(flops=10_000_000, bytes_accessed=80_000_000, transcendentals=0),
+    )(*inputs, *moved)
+
+
+def attend(raw, turns, bias, gains, weight, moves, collective_id):
+    blocks, length = bias.shape[:2]
+    width = raw.shape[2] // 3
+    heads = width // HEAD_DIM
+    model_width = weight.shape[1]
+    low = jnp.bfloat16
+
+    def body(line, ins, outs, scratch, tick):
+        raw, turns, bias, gains, weight = ins
+        parts, lows, probs, mixed, squares = outs
+        mine, came, sends, recvs = scratch
+
+        def squares_of(b, carry):
+            for index in range(2):
+                total = jnp.zeros((length, 1), jnp.float32)
+                for h in range(heads):
+                    values = raw[b, :length, spot(h, index)]
+                    total = total + jnp.sum(values * values, axis=1, keepdims=True)
+                mine[pl.ds(index * blocks + b, 1), :] = as_row(total)
+            return carry
+
+        tick()
+        lax.fori_loop(0, blocks, squares_of, 0)
+        tick()
+        squares[...] = line_exchange(line, mine, came, sends, recvs)
+        tick()
+
+        def block(b, carry):
+            scales = [
+                lax.rsqrt(as_columns(squares[pl.ds(index * blocks + b, 1), :]) / model_width + epsilon)
+                for index in range(2)
+            ]
+            cos, sin = turn_tables(turns[b])
+            for h in range(heads):
+                here = slice(h * HEAD_DIM, (h + 1) * HEAD_DIM)
+                turned = []
+                for index in range(2):
+                    there = spot(h, index)
+                    normed = raw[b, :length, there] * scales[index] * gains[index : index + 1, here]
+                    turned.append((normed * cos + pltpu.roll(normed, HEAD_DIM // 2, 1) * sin).astype(low))
+                    lows[b, :, there] = turned[index]
+                there = spot(h, 2)
+                value = raw[b, :length, there].astype(low)
+                lows[b, :, there] = value
+                scores = dot(turned[0], turned[1], 1, 1) * HEAD_DIM**-0.5 + bias[b]
+                powers = jnp.exp(scores - jnp.max(scores, axis=1, keepdims=True))
+                prob = powers / jnp.sum(powers, axis=1, keepdims=True)
+                probs[b, h] = prob
+                mixed[b, :, here] = dot(prob.astype(low), value, 1, 0).astype(low)
+            parts[b] = dot(mixed[b], weight[...], 1, 0).astype(low)
+            return carry
+
+        for part in range(LINE):
+            lax.fori_loop(2 * part, 2 * part + 2, block, 0)
+            tick()
+
+    return heads_call(
+        collective_id,
+        body,
+        [raw, turns, bias, gains, weight],
+        [
+            ((blocks, length, model_width), low),
+            ((blocks, length, 3 * width), low),
+            ((blocks, heads, length, length), jnp.float32),
+            ((blocks, length, width), low),
+            ((2 * blocks, length), jnp.float32),
+        ],
+        [],
+        2 * blocks,
+        moves,
+    )
+
+
+def attend_back(d_attn, weight, raw, turns, gains, lows, probs, squares, wide_terms, moves, collective_id):
+    blocks, rows = raw.shape[:2]
+    length = lows.shape[1]
+    width = raw.shape[2] // 3
+    heads = width // HEAD_DIM
+    model_width = weight.shape[1]
+    low = jnp.bfloat16
+
+    def body(line, ins, outs, scratch, tick):
+        d_attn, weight, raw, turns, gains, lows, probs, squares = ins[:8]
+        d_low, terms, wide = outs
+        mine, came, sends, recvs, upstream, unit = scratch
+        tick()
+        terms[...] = jnp.zeros_like(terms)
+        for which in range(2):
+            total = jnp.sum(ins[8 + which][...], axis=0, keepdims=True)
+            for index in range(model_width // length):
+                row = 2 * blocks + which * (model_width // length) + index
+                mine[row : row + 1, :] = total[:, index * length : (index + 1) * length]
+
+        def block(b, carry):
+            scales = [
+                lax.rsqrt(as_columns(squares[pl.ds(index * blocks + b, 1), :]) / model_width + epsilon)
+                for index in range(2)
+            ]
+            cos, sin = turn_tables(turns[b])
+            d_mixed = dot(d_attn[b], weight[...], 1, 1).astype(low)
+            means = [jnp.zeros((length, 1), jnp.float32)] * 2
+            for h in range(heads):
+                here = slice(h * HEAD_DIM, (h + 1) * HEAD_DIM)
+                places = [spot(h, index) for index in range(3)]
+                query, key, value = [lows[b, :, there] for there in places]
+                prob = probs[b, h]
+                d_out = d_mixed[:, here]
+                d_low[b, :length, places[2]] = dot(prob.astype(low), d_out, 0, 0).astype(low)
+                d_prob = dot(d_out, value, 1, 1)
+                d_scores = (
+                    prob * (d_prob - jnp.sum(d_prob * prob, axis=1, keepdims=True))
+                ).astype(low)
+                turned = [dot(d_scores, key, 1, 0), dot(d_scores, query, 0, 0)]
+                for index in range(2):
+                    d_rot = turned[index] * HEAD_DIM**-0.5
+                    d_normed = d_rot * cos - pltpu.roll(d_rot, HEAD_DIM // 2, 1) * sin
+                    units = raw[b, :length, places[index]] * scales[index]
+                    ups = d_normed * gains[index : index + 1, here]
+                    folded = (d_normed * units).reshape(length // 8, 8, HEAD_DIM)
+                    side = slice((index * heads + h) * HEAD_DIM, (index * heads + h + 1) * HEAD_DIM)
+                    terms[:, side] += jnp.sum(folded, axis=0)
+                    upstream[b, :, side] = ups
+                    unit[b, :, side] = units
+                    means[index] = means[index] + jnp.sum(ups * units, axis=1, keepdims=True)
+            for index in range(2):
+                mine[pl.ds(index * blocks + b, 1), :] = as_row(means[index])
+            return carry
+
+        lax.fori_loop(0, blocks, block, 0)
+        mine[...] = line_exchange(line, mine, came, sends, recvs)
+        wide[...] = mine[2 * blocks :, :]
+
+        def last(b, carry):
+            d_low[b, length:, :] = jnp.zeros((rows - length, 3 * width), low)
+            for index in range(2):
+                scale = lax.rsqrt(
+                    as_columns(squares[pl.ds(index * blocks + b, 1), :]) / model_width + epsilon
+                )
+                mean = as_columns(mine[pl.ds(index * blocks + b, 1), :]) / model_width
+                for h in range(heads):
+                    side = slice((index * heads + h) * HEAD_DIM, (index * heads + h + 1) * HEAD_DIM)
+                    d_low[b, :length, spot(h, index)] = (
+                        scale * (upstream[b, :, side] - unit[b, :, side] * mean)
+                    ).astype(low)
+            return carry
+
+        lax.fori_loop(0, blocks, last, 0)
+
+    return heads_call(
+        collective_id,
+        body,
+        [d_attn, weight, raw, turns, gains, lows, probs, squares, *wide_terms],
+        [
+            (raw.shape, low),
+            ((8, 2 * width), jnp.float32),
+            ((2 * model_width // length, length), jnp.float32),
+        ],
+        [pltpu.VMEM((blocks, length, 2 * width), jnp.float32) for _ in range(2)],
+        2 * blocks + 2 * model_width // length,
+        moves,
     )
 
 
@@ -947,9 +1366,8 @@
     )
     extra = jnp.pad(extra[None], ((0, 15), (0, model_width - extra.shape[0])))
     payload, full_qkv, full_output = gather_blocks(
-        jnp.concatenate([hidden_in, extra]), [Spread(w_query, w_key, w_value), Stack(w_output)], 0
-    )
-    tokens = payload[:, :length].reshape(blocks * length, model_width)
+        jnp.concatenate([hidden_in, extra]), [Spread(w_query, w_key, w_value), Stack(w_output, 2)], 0
+    )
     docs = payload[:, length, 4 * length : 5 * length].astype(jnp.int32)
     gains = payload[:, length, : 4 * length].reshape(LINE, 2, 4, length)
     gains = jnp.stack(by_pair(pair, gains, pair_swap(gains)), axis=1)
@@ -957,8 +1375,7 @@
     gain_attn, gain_ffn = gains[2], gains[3]
     width = heads * HEAD_DIM
     head_gains = gather_rows(jnp.stack([query_gain, key_gain])[None], pair).astype(f32)
-    gain_query = head_gains[:, 0].reshape(width)
-    gain_key = head_gains[:, 1].reshape(width)
+    head_gains = head_gains.transpose(1, 0, 2).reshape(2, width)
 
     earlier = jnp.sum((docs[:, None, :] < docs[:, :, None]).astype(jnp.int32), axis=2)
     positions = jnp.arange(length, dtype=jnp.int32)[None] - earlier
@@ -967,49 +1384,27 @@
         jnp.arange(half_dim, dtype=f32) * (-2.0 * math.log(theta_base) / HEAD_DIM)
     )
     angles = positions.astype(f32)[:, :, None] * inverse[None, None, :]
-    cosines = jnp.cos(angles)[:, :, None, :]
-    sines = jnp.sin(angles)[:, :, None, :]
+    turns = jnp.cos(jnp.concatenate([angles, angles - 0.5 * math.pi], axis=-1))
     token_idx = jnp.arange(length)
     allowed = (docs[:, :, None] == docs[:, None, :]) & (
         token_idx[:, None] >= token_idx[None, :]
     )[None]
-
-    def split_heads(values):
-        return values.reshape(blocks, length, heads, HEAD_DIM)
-
-    all_raw = jnp.dot(tokens, full_qkv, preferred_element_type=f32)
-    query_raw, key_raw = all_raw[:, :width], all_raw[:, width : 2 * width]
-    squares = group_sum(
-        jnp.stack([jnp.sum(query_raw * query_raw, axis=-1), jnp.sum(key_raw * key_raw, axis=-1)])
-    )
-    head_scales = lax.rsqrt(squares / model_width + epsilon)
-    query_unit = query_raw * head_scales[0][:, None]
-    key_unit = key_raw * head_scales[1][:, None]
-    query_low = rotate(split_heads(query_unit * gain_query), cosines, sines).astype(jnp.bfloat16)
-    key_low = rotate(split_heads(key_unit * gain_key), cosines, sines).astype(jnp.bfloat16)
-    value_low = split_heads(all_raw[:, 2 * width :].astype(jnp.bfloat16))
-    scores = (
-        jnp.einsum("sqhd,skhd->shqk", query_low, key_low, preferred_element_type=f32) * factor
-    )
-    scores = jnp.where(allowed[:, None], scores, neg_fill)
-    row_peak = jnp.max(scores, axis=-1, keepdims=True)
-    log_norm = row_peak + jnp.log(jnp.sum(jnp.exp(scores - row_peak), axis=-1, keepdims=True))
-    attn_prob = jnp.exp(scores - log_norm)
-    prob_low = attn_prob.astype(jnp.bfloat16)
-    mixed_low = (
-        jnp.einsum("shqk,skhd->sqhd", prob_low, value_low, preferred_element_type=f32)
-        .reshape(blocks * length, width)
-        .astype(jnp.bfloat16)
-    )
+    bias = jnp.where(allowed, 0.0, neg_fill)
 
     def to_blocks(values):
-        return values.astype(jnp.bfloat16).reshape(blocks, length, model_width)
-
-    resid_low, attn_out, resid, full_gate, full_up, full_down = attention_block(
-        to_blocks(jnp.dot(mixed_low, full_output, preferred_element_type=f32)),
+        return values.astype(jnp.bfloat16).reshape(blocks, -1, model_width)
+
+    raw = jnp.dot(payload.reshape(-1, model_width), full_qkv, preferred_element_type=f32)
+    raw = raw.reshape(blocks, -1, 3 * width)
+    attn_parts, lows, probs, mixed_low, squares, full_gate = attend(
+        raw, turns, bias, head_gains, full_output, [Spread(w_gate, begin=2, burst=True)], 6
+    )
+    mixed_low = mixed_low.reshape(blocks * length, width)
+    resid_low, attn_out, resid, full_up, full_down = attention_block(
+        attn_parts,
         hidden_in,
         gain_attn,
-        [Spread(w_gate), Spread(w_up), Stack(w_down)],
+        [Spread(w_up), Stack(w_down, 8)],
         1,
     )
     resid_low = resid_low.reshape(blocks * length, model_width)
@@ -1037,126 +1432,66 @@
             left_side, right_side, (((0,), (0,)), ((), ())), preferred_element_type=f32
         ).astype(jnp.bfloat16)
 
-    def joined(first, second):
-        return (first.astype(f32) + second.astype(f32)).astype(jnp.bfloat16)
-
     ff_rows = w_down.shape[0]
     part_gate = outer(resid_low, d_gate_low)
     part_up = outer(resid_low, d_up_low)
     part_down = outer(hidden_ffn, d_ffn_low).reshape(2, ff_rows, model_width)
 
-    def other_columns(line, ref):
-        return ref.at[:, pl.ds(pl.multiple_of((1 - line.rep) * ff_rows, ff_rows), ff_rows)]
-
-    def other_pair(line, ref):
-        return ref.at[1 - line.pair]
-
-    def other_rows(line, ref):
-        return ref.at[:, 1 - line.pair]
-
-    def same(line, ref):
-        return ref
-
-    columns = (model_width, ff_rows)
-    d_attn_low, d_resid, attn_gain_term, there_gate, there_up, there_down = back_block(
+    d_attn_low, d_resid, attn_gain_term, gate_sum, up_sum, down_part = back_block(
         to_blocks(dot_back(d_gate_low, full_gate) + dot_back(d_up_low, full_up)),
         out_cotangent,
         attn_out,
         gain_attn,
         [
-            Swap(part_gate, columns, other_columns, "partner"),
-            Swap(part_up, columns, other_columns, "partner"),
-            Swap(part_down, part_down.shape[1:], other_pair, "across"),
+            Reduce(part_gate, "partner"),
+            Reduce(part_up, "partner"),
+            PairSum(part_down, 4, 13),
         ],
         3,
     )
 
-    def own_columns(values):
-        return lax.dynamic_slice_in_dim(values, lax.axis_index("rep") * ff_rows, ff_rows, 1)
-
-    def own_pair(values, axis):
-        return lax.dynamic_index_in_dim(values, pair, axis, keepdims=False)
-
-    ffn_part = jnp.concatenate(
-        [joined(own_columns(part_gate), there_gate), joined(own_columns(part_up), there_up)], axis=1
-    ).reshape(LINE, 2, 2 * length, 2 * ff_rows)
-    ffn_part = joined(own_pair(ffn_part, 1), pair_swap(own_pair(ffn_part[:, ::-1], 1)))
-    down_part = joined(own_pair(part_down, 0), there_down)
+    d_qkv, head_terms, wide_terms, there_first = attend_back(
+        d_attn_low, full_output, raw, turns, head_gains, lows, probs, squares,
+        [attn_gain_term, ffn_gain_term], [Swap(down_part, 0, ff_rows // 2)], 7,
+    )
     d_attn_low = d_attn_low.reshape(blocks * length, model_width)
-
-    d_mixed_low = split_heads(dot_back(d_attn_low, full_output).astype(jnp.bfloat16))
-    d_value = jnp.einsum("shqk,sqhd->skhd", prob_low, d_mixed_low, preferred_element_type=f32)
-    d_prob = jnp.einsum("sqhd,skhd->shqk", d_mixed_low, value_low, preferred_element_type=f32)
-    d_scores_low = (
-        attn_prob * (d_prob - jnp.sum(d_prob * attn_prob, axis=-1, keepdims=True))
-    ).astype(jnp.bfloat16)
-    d_query_rot = (
-        jnp.einsum("shqk,skhd->sqhd", d_scores_low, key_low, preferred_element_type=f32) * factor
-    )
-    d_key_rot = (
-        jnp.einsum("shqk,sqhd->skhd", d_scores_low, query_low, preferred_element_type=f32)
-        * factor
-    )
-    d_query_normed = rotate(d_query_rot, cosines, -sines).reshape(blocks * length, width)
-    d_key_normed = rotate(d_key_rot, cosines, -sines).reshape(blocks * length, width)
-    query_gain_term = jnp.sum(d_query_normed * query_unit, axis=0)
-    key_gain_term = jnp.sum(d_key_normed * key_unit, axis=0)
-    query_up = d_query_normed * gain_query
-    key_up = d_key_normed * gain_key
-    means = (
-        group_sum(
-            jnp.stack(
-                [jnp.sum(query_up * query_unit, axis=-1), jnp.sum(key_up * key_unit, axis=-1)]
-            )
-        )
-        / model_width
-    )
-    d_query_low = (head_scales[0][:, None] * (query_up - query_unit * means[0][:, None])).astype(
-        jnp.bfloat16
-    )
-    d_key_low = (head_scales[1][:, None] * (key_up - key_unit * means[1][:, None])).astype(
-        jnp.bfloat16
-    )
-    d_value_low = d_value.reshape(blocks * length, width).astype(jnp.bfloat16)
-    d_qkv_low = jnp.concatenate([d_query_low, d_key_low, d_value_low], axis=1)
-    part_qkv = outer(tokens, d_qkv_low).reshape(LINE, 2, 2 * length, 3 * width)
+    part_qkv = outer(
+        payload.reshape(-1, model_width), d_qkv.reshape(-1, 3 * width)
+    )
     part_output = outer(mixed_low, d_attn_low).reshape(2, length, model_width)
-    hidden_grad, there_qkv, there_output, there_down, ffn_total = last_block(
+    hidden_grad, qkv_sum, output_part, ffn_total, there_second = last_block(
         to_blocks(
-            dot_back(d_qkv_low, full_qkv)
+            dot_back(d_qkv[:, :length].reshape(-1, 3 * width), full_qkv)
         ),
         d_resid,
         [
-            Swap(part_qkv, (LINE, 2 * length, 3 * width), other_rows, "across"),
-            Swap(part_output, (length, model_width), other_pair, "across"),
-            Swap(down_part, down_part.shape, same, "partner"),
-            Deal(ffn_part.reshape(blocks, length, 2 * ff_rows), 2, True),
+            Reduce(part_qkv, "across"),
+            PairSum(part_output, 1, 5),
+            Deal([gate_sum.reshape(blocks, length, -1), up_sum.reshape(blocks, length, -1)], 1),
+            Swap(down_part, ff_rows // 2, ff_rows // 2),
         ],
         4,
     )
-    qkv_part = joined(own_pair(part_qkv, 1), there_qkv).reshape(blocks, length, 3 * width)
-    output_part = joined(own_pair(part_output, 0), there_output)
-    qkv_own, qkv_there, there_output = line_call(
+    qkv_total, there_output = line_call(
         5, 1, None, [], [], False, False,
-        [Deal(qkv_part, 3, False), Swap(output_part, output_part.shape, same, "partner")],
+        [
+            Deal([qkv_sum.reshape(blocks, length, -1)], 3),
+            Swap(output_part, 0, length),
+        ],
     )
 
     def total_of(first, second):
         return first.astype(f32) + second.astype(f32)
 
-    grad_query, grad_key, grad_value = jnp.split(total_of(qkv_own, qkv_there), 3, axis=1)
+    grad_query, grad_key, grad_value = jnp.split(qkv_total.astype(f32), 3, axis=1)
     grad_gate, grad_up = jnp.split(ffn_total.astype(f32), 2, axis=1)
     grad_output = total_of(output_part, there_output)
-    grad_down = total_of(down_part, there_down)
-    head_terms = jnp.stack([query_gain_term, key_gain_term]).reshape(2, 2, HEAD_DIM)
+    grad_down = total_of(down_part, jnp.concatenate([there_first, there_second]))
+    head_terms = jnp.sum(head_terms, axis=0).reshape(2, 2, HEAD_DIM)
     own_term, other_term = by_pair(pair, head_terms[:, 0], head_terms[:, 1])
     head_grads = own_term + pair_swap(other_term)
-    wide_grads = lax.psum_scatter(
-        jnp.stack([jnp.sum(attn_gain_term, axis=0), jnp.sum(ffn_gain_term, axis=0)]),
-        "shard",
-        scatter_dimension=1,
-        tiled=True,
-    )
+    wide_terms = (wide_terms + pair_swap(wide_terms)).reshape(2, 16, length)
+    wide_grads = lax.dynamic_index_in_dim(wide_terms, lax.axis_index("shard"), 1, keepdims=False)
     gain_grads = jnp.concatenate([head_grads, wide_grads])
     gain_grads = gain_grads + rep_swap(gain_grads)
     return (

time: 788 us -> 710 us (0.901)
  Pallas kernels: 522 us -> 564 us
  local copies, waits for them, and re-layouts: 62.4 us -> 24.5 us
  waiting for transfers between devices: 32.7 us -> 0.25 us
  other arithmetic: 38.5 us -> 10.9 us
  between operations: 15.2 us -> 1.37 us
  starting transfers between devices: 15.9 us -> 7.93 us
    pallas_call x0 -> x2, Pallas kernels: none -> 84 us  [heads_call(): pl.pallas_call(kernel, out_shape=[jax.ShapeDtypeStruct(shape, kind) for s...]
    pallas_call x6, Pallas kernels: 522 us -> 480 us  [line_call(): pl.pallas_call(kernel, out_shape=[jax.ShapeDtypeStruct(shape, kind) for s...]
    unnamed x121 -> x70, local copies, waits for them, and re-layouts: 32.9 us -> 15 us
    ppermute x4, waiting for transfers between devices: 13.4 us -> 0.01 us  [pair_swap(): return lax.ppermute(values, 'shard', shard_perm(lambda index: index ^ 2))]
    convert_element_type x9 -> x0, other arithmetic: 11.3 us -> none  [the longest x5 9.72 us: joined(): return (first.astype(f32) + second.astype(f32)).astype(jnp.bfloat16)]
    ppermute x8 -> x0, waiting for transfers between devices: 10.3 us -> none  [the longest x6 10.3 us: line_shift(): lax.ppermute(values, 'shard', shard_perm(lambda index: (index + 4 * steps...]
    unnamed x2 -> x0, waiting for transfers between devices: 9.06 us -> none
    ppermute x8 -> x0, starting transfers between devices: 8.58 us -> none  [the longest x6 8.44 us: line_shift(): lax.ppermute(values, 'shard', shard_perm(lambda index: (index + 4 * steps...]
  transfers between devices with their start and end apart: 14 -> 5, of which waited for: 6 -> 1; matrix products, arithmetic and copies ran while one was open for 8% -> 5% of each run, Pallas kernels for 9% -> 35%
where the time goes in v4:
time: 710 us; the launch traced here: 701 us
  Pallas kernels  564 us (79%)
  matrix products  92.1 us (13%)
  local copies, waits for them, and re-layouts  24.5 us (3%)
  other arithmetic  10.9 us (2%)
  starting transfers between devices  7.93 us (1%)
    pallas_call x6, Pallas kernels, line_call(): pl.pallas_call(kernel, out_shape=[jax.ShapeDtypeStruct(shape, kind) for s...  480 us
    pallas_call x2, Pallas kernels, heads_call(): pl.pallas_call(kernel, out_shape=[jax.ShapeDtypeStruct(shape, kind) for s...  84 us
    dot_general x4, matrix products, dot_back(): lax.dot_general(left_side, right_side, (((1,), (1,)), ((), ())), preferre...  34 us
    dot_general x5, matrix products, outer(): lax.dot_general(left_side, right_side, (((0,), (0,)), ((), ())), preferre...  29.9 us
    unnamed x70, local copies, waits for them, and re-layouts  15 us
  transfers between devices with their start and end apart: 5, of which 1 were waited for; matrix products, arithmetic and copies ran while one was open for 5% of the time, Pallas kernels for 35%

profile of v4, /device:TPU:0, one launch (start us, length us, event | category | flops | bytes accessed | tf_op | source)
XLA Modules:
  0.0 701.0 jit_solution(8386364911912384896)
XLA Ops:
  1.3 3.0 collective-permute-start
  13.7 64.8 %shard_map.237 = (bf16[8,144,2048]{2,1,0:T(8,128)(2,1)}, bf16[2048,768]{1,0:T(8,128)(2,1)S(1)}, bf16[256,2048]{1,0:T(8,128)(2,1)S(1)}) custom-call(bf16[144,2048]{1,0:T(8,128)(2,1)S(1)} %fusion.4.refs_0_, bf16[128,2048]{1,0:T(8,128)(2,1)S(1)} %copy-done.13, bf16[128,2048]{1,0:T(8,128)(2,1)S(1)} %copy-done.14, bf16[128,2048]{1,0:T(8,128)(2,1)S(1)} %copy-done.15, ...), custom_call_target="tpu_custom_call" | custom-call | flops 10000000 | bytes 200000000 | tf_op jit(solution)/shard_map/pallas_call | solution.py:996
  78.5 1.6 copy-done.19
  81.0 1.6 collective-permute-start.1
  84.0 9.0 %fusion.refs_0_.refs_2_ = f32[8,144,768]{2,1,0:T(8,128)} fusion(bf16[8,144,2048]{2,1,0:T(8,128)(2,1)} %get-tuple-element.47, bf16[2048,768]{1,0:T(8,128)(2,1)} %copy-done.19), kind=kOutput, calls=%fused_computation.12 | convolution fusion | flops 3623878656 | bytes 11403264 | tf_op jit(solution)/shard_map/dot_general | solution.py:1397
  93.2 1.9 maximum_cosine_fusion.refs_1_.refs_3_
  95.2 1.7 copy-done.5
  96.9 53.5 %shard_map.238 = (bf16[8,128,2048]{2,1,0:T(8,128)(2,1)}, bf16[8,128,768]{2,1,0:T(8,128)(2,1)S(1)}, f32[8,2,128,128]{3,2,1,0:T(8,128)S(1)}, bf16[8,128,256]{2,1,0...) custom-call(f32[8,144,768]{2,1,0:T(8,128)} %fusion.refs_0_.refs_2_, ...), custom_call_target="tpu_custom_call" | custom-call | flops 10000000 | bytes 80000000 | tf_op jit(solution)/shard_map/pallas_call | solution.py:1165
  150.6 99.1 %shard_map.239 = (bf16[8,128,2048]{2,1,0:T(8,128)(2,1)}, f32[128,2048]{1,0:T(8,128)S(1)}, f32[128,2048]{1,0:T(8,128)S(1)}, bf16[2048,1024]{1,0:T(8,128)(2,1)}, bf16[1024,2048]{1,0:T(8,128)(2,1)}) custom-call(bf16[8,128,2048]{2,1,0:T(8,128)(2,1)} %get-tuple-element.50.refs_0_, bf16[128,2048]{1,0:T(8,128)(2,1)S(1)} %copy-done.4, f32[1,2048]{1,0:T(1,128)S(1)} %bitcast.88, ...), custom_call_target="tpu_custom_call" | custom-call | flops 10000000 | bytes 200000000 | tf_op jit(solution)/shard_map/pallas_call | solution.py:996
  249.7 6.7 fusion.10
  256.5 6.5 multiply_convert_fusion.2
  262.9 6.1 convolution_convert_fusion.4
  269.0 69.3 %shard_map.240 = (bf16[8,128,2048]{2,1,0:T(8,128)(2,1)S(1)}, bf16[128,2048]{1,0:T(8,128)(2,1)S(1)}, f32[8,2048]{1,0:T(8,128)S(1)}) custom-call(bf16[8,128,2048]{2,1,0:T(8,128)(2,1)} %bitcast.94, f32[128,2048]{1,0:T(8,128)S(1)} %get-tuple-element.55.refs_1_, bf16[128,2048]{1,0:T(8,128)(2,1)S(1)} %copy-done.6, f32[1,2048]{1,0:T(1,128)S(1)} %bitcast.90), custom_call_target="tpu_custom_call" | custom-call | flops 10000000 | bytes 200000000 | tf_op jit(solution)/shard_map/pallas_call | solution.py:996
  338.4 6.2 convolution_convert_fusion.1
  344.6 10.8 %multiply_convert_fusion = (bf16[1024,1024]{1,0:T(8,128)(2,1)}, bf16[1024,1024]{1,0:T(8,128)(2,1)}) fusion(f32[1024,1024]{1,0:T(8,128)} %copy-done.29, f32[1024,1024]{1,0:T(8,128)} %get-tuple-element.104, bf16[1024,2048]{1,0:T(8,128)(2,1)S(1)} %bitcast.92, bf16[1024,2048]{1,0:T(8,128)(2,1)} %get-tuple-element.54), kind=kOutput, calls=%fused_computation.3 | convolution fusion | flops 4308598784 | bytes 20971520 | tf_op jit(solution)/shard_map/dot_general | solution.py:37
  355.4 7.9 %convolution_convert_fusion.3.refs_4_ = bf16[2048,1024]{1,0:T(8,128)(2,1)} fusion(bf16[1024,2048]{1,0:T(8,128)(2,1)S(1)} %bitcast.113, bf16[1024,1024]{1,0:T(8,128)(2,1)} %get-tuple-element.82), kind=kOutput, calls=%fused_computation.10 | convolution fusion | flops 4297064448 | bytes 10485760 | tf_op jit(solution)/shard_map/dot_general | solution.py:1431
  363.3 6.9 fusion.11
  370.1 6.3 convolution_convert_fusion.2.refs_5_
  376.5 8.3 %add_convert_fusion = bf16[1024,2048]{1,0:T(8,128)(2,1)} fusion(f32[1024,2048]{1,0:T(8,128)} %fusion.11, bf16[1024,1024]{1,0:T(8,128)(2,1)S(1)} %copy-done.31, bf16[2048,1024]{1,0:T(8,128)(2,1)S(1)} %copy-done.25), kind=kOutput, calls=%fused_computation | convolution fusion | flops 4299161600 | bytes 18874368 | tf_op jit(solution)/shard_map/dot_general | solution.py:37
  384.8 116.7 %shard_map.241 = (bf16[8,128,2048]{2,1,0:T(8,128)(2,1)}, f32[128,2048]{1,0:T(8,128)}, f32[8,2048]{1,0:T(8,128)}, bf16[4,256,512]{2,1,0:T(8,128)(2,1)}, bf16[4,25...) custom-call(bf16[8,128,2048]{2,1,0:T(8,128)(2,1)} %bitcast.96, bf16[128,2048]{1,0:T(8,128)(2,1)} %refs_1_.5, ...), custom_call_target="tpu_custom_call" | custom-call | flops 10000000 | bytes 200000000 | tf_op jit(solution)/shard_map/pallas_call | solution.py:996
  501.5 1.6 copy-done
  503.9 30.4 %shard_map.242 = (bf16[8,144,768]{2,1,0:T(8,128)(2,1)S(1)}, f32[8,512]{1,0:T(8,128)S(1)}, f32[32,128]{1,0:T(8,128)S(1)}, bf16[256,2048]{1,0:T(8,128)(2,1)S(1)}) custom-call(bf16[8,128,2048]{2,1,0:T(8,128)(2,1)} %get-tuple-element.59.refs_0_, bf16[256,2048]{1,0:T(8,128)(2,1)S(1)} %get-tuple-element.49.refs_4_.refs_1_, f32[8,144,768]{2,1,0:T(8,128)} %fusion.refs_0_.refs_2_, ...), custom_call_target="tpu_custom_call" | custom-call | flops 10000000 | bytes 80000000 | tf_op jit(solution)/shard_map/pallas_call | solution.py:1165
  534.3 8.3 %bitcast_convert_fusion.refs_2_ = bf16[2048,768]{1,0:T(8,128)(2,1)} fusion(bf16[8,144,2048]{2,1,0:T(8,128)(2,1)} %get-tuple-element.47, bf16[8,144,768]{2,1,0:T(8,128)(2,1)S(1)} %get-tuple-element.66), kind=kOutput, calls=%fused_computation.1 | convolution fusion | flops 3625451520 | bytes 9633792 | tf_op jit(solution)/shard_map/dot_general | solution.py:1431
  542.6 1.2 slice.39
  543.9 1.3 fusion.2
  547.3 8.0 %convolution_convert_fusion = bf16[1024,2048]{1,0:T(8,128)(2,1)} fusion(bf16[1024,768]{1,0:T(8,128)(2,1)} %bitcast.97, bf16[2048,768]{1,0:T(8,128)(2,1)} %copy-done.19), kind=kOutput, calls=%fused_computation.7 | convolution fusion | flops 3223322624 | bytes 8912896 | tf_op jit(solution)/shard_map/dot_general | solution.py:37
  555.3 95.3 %shard_map.243 = (bf16[128,2048]{1,0:T(8,128)(2,1)S(1)}, bf16[4,256,384]{2,1,0:T(8,128)(2,1)S(1)}, bf16[128,2048]{1,0:T(8,128)(2,1)S(1)}, bf16[128,16384]{1,0:T(8,128)(2,1)}, bf16[256,2048]{1,0:T(8,128)(2,1)S(1)}) custom-call(bf16[8,128,2048]{2,1,0:T(8,128)(2,1)} %bitcast.93, f32[128,2048]{1,0:T(8,128)S(1)} %copy-done.8, ...), custom_call_target="tpu_custom_call" | custom-call | flops 10000000 | bytes 200000000 | tf_op jit(solution)/shard_map/pallas_call | solution.py:996
  650.5 6.6 fusion.6
  657.1 2.8 convert_add_fusion
  659.9 35.0 %shard_map.244 = (bf16[128,6144]{1,0:T(8,128)(2,1)S(1)}, bf16[128,2048]{1,0:T(8,128)(2,1)S(1)}) custom-call(bf16[8,128,384]{2,1,0:T(8,128)(2,1)S(1)} %bitcast.87, bf16[128,2048]{1,0:T(8,128)(2,1)S(1)} %get-tuple-element.73.refs_1_), custom_call_target="tpu_custom_call" | custom-call | flops 10000000 | bytes 200000000 | tf_op jit(solution)/shard_map/pallas_call | solution.py:996
  695.0 1.3 collective-permute-start.4
  696.3 2.1 fusion.7
  (104 shorter events, 18.1 us)
Async XLA Ops:
  1.3 93.8 %collective-permute-start = (bf16[1,2,128]{2,1,0:T(2,128)(2,1)S(1)}, bf16[1,2,128]{2,1,0:T(2,128)(2,1)S(1)}, u32[]{:S(2)}, u32[]{:S(2)}) collective-permute-start(bf16[1,2,128]{2,1,0:T(2,128)(2,1)S(1)} %maximum_bitcast_fusion), channel_id=1, source_target_pairs={{0,2},{1,3},{2,0},{3,1},{4,6},{5,7},{6,4},{7,5},{8,10},{9,11},{10,... | collective-permute-start | bytes 1544 | tf_op jit(solution)/shard_map/ppermute | solution.py:284
  78.5 1.6 copy-start.19
  81.0 69.4 %collective-permute-start.1 = (bf16[4,2,4,128]{3,2,1,0:T(4,128)(2,1)S(1)}, bf16[4,2,4,128]{3,2,1,0:T(4,128)(2,1)S(1)}, u32[]{:S(2)}, u32[]{:S(2)}) collective-permute-start(bf16[4,2,4,128]{3,2,1,0:T(4,128)(2,1)S(1)} %reshape_squeeze.3), channel_id=1, source_target_pairs={{0,2},{1,3},{2,0},{3,1},{4,6},{5,7},{6,4},{7,5},{8,10},{9,11},{10,... | collective-permute-start | bytes 24584 | tf_op jit(solution)/shard_map/ppermute | solution.py:284
  84.0 11.2 %copy-start.21 = (bf16[128]{0:T(256)(128)(2,1)S(1)}, bf16[128]{0:T(256)(128)(2,1)}, u32[]{:S(2)}) copy-start(bf16[128]{0:T(256)(128)(2,1)} %param.20) | copy-start | bytes 772
  84.0 11.1 %copy-start.22 = (bf16[128]{0:T(256)(128)(2,1)S(1)}, bf16[128]{0:T(256)(128)(2,1)}, u32[]{:S(2)}) copy-start(bf16[128]{0:T(256)(128)(2,1)} %param.21) | copy-start | bytes 772
  95.1 55.5 %copy-start.4 = (bf16[128,2048]{1,0:T(8,128)(2,1)S(1)}, bf16[128,2048]{1,0:T(8,128)(2,1)}, u32[]{:S(2)}) copy-start(bf16[128,2048]{1,0:T(8,128)(2,1)} %refs_1_.4) | copy-start | bytes 1572868
  95.1 55.5 %copy-start.2 = (bf16[128,8192]{1,0:T(8,128)(2,1)S(1)}, bf16[128,8192]{1,0:T(8,128)(2,1)}, u32[]{:S(2)}) copy-start(bf16[128,8192]{1,0:T(8,128)(2,1)} %refs_3_.3) | copy-start | bytes 6291460
  95.1 55.5 %copy-start.3 = (bf16[512,2048]{1,0:T(8,128)(2,1)S(1)}, bf16[512,2048]{1,0:T(8,128)(2,1)}, u32[]{:S(2)}) copy-start(bf16[512,2048]{1,0:T(8,128)(2,1)} %refs_4_.3) | copy-start | bytes 6291460
  95.2 1.7 copy-start.5
  150.6 99.1 %copy-start.17 = (f32[1,4,2,2,128]{4,3,2,1,0:T(2,128)}, f32[1,4,2,2,128]{4,3,2,1,0:T(2,128)S(1)}, u32[]{:S(2)}) copy-start(f32[1,4,2,2,128]{4,3,2,1,0:T(2,128)S(1)} %copy.32) | copy-start | bytes 24580
  150.6 99.1 %copy-start.23 = (bf16[2048,1024]{1,0:T(8,128)(2,1)S(1)}, bf16[2048,1024]{1,0:T(8,128)(2,1)}, u32[]{:S(2)}) copy-start(bf16[2048,1024]{1,0:T(8,128)(2,1)} %get-tuple-element.52) | copy-start | bytes 12582916
  249.7 6.7 copy-start.7
  249.7 6.7 copy-start.24
  249.7 6.7 copy-start.26
  256.4 6.5 copy-start.29
  256.5 6.5 copy-start.28
  262.9 6.1 copy-start.6
  338.4 6.2 copy-start.11
  344.6 10.8 %copy-start.27 = (bf16[8,128,2048]{2,1,0:T(8,128)(2,1)S(1)}, bf16[8,128,2048]{2,1,0:T(8,128)(2,1)}, u32[]{:S(2)}) copy-start(bf16[8,128,2048]{2,1,0:T(8,128)(2,1)} %get-tuple-element.51) | copy-start | bytes 12582916
  355.4 7.9 %copy-start.30 = (bf16[1024,1024]{1,0:T(8,128)(2,1)S(1)}, bf16[1024,1024]{1,0:T(8,128)(2,1)}, u32[]{:S(2)}) copy-start(bf16[1024,1024]{1,0:T(8,128)(2,1)} %get-tuple-element.82) | copy-start | bytes 6291460
  363.3 6.9 copy-start.31
  370.1 6.3 copy-start.25
  501.4 1.6 copy-start
  534.3 9.5 %copy-start.20 = (bf16[8,128,2048]{2,1,0:T(8,128)(2,1)S(1)}, bf16[8,128,2048]{2,1,0:T(8,128)(2,1)}, u32[]{:S(2)}) copy-start(bf16[8,128,2048]{2,1,0:T(8,128)(2,1)} %get-tuple-element.59.refs_0_) | copy-start | bytes 12582916
  545.2 149.8 %collective-permute-start.2 = (f32[2,128]{1,0:T(2,128)S(1)}, f32[2,128]{1,0:T(2,128)S(1)}, u32[]{:S(2)}, u32[]{:S(2)}) collective-permute-start(f32[2,128]{1,0:T(2,128)S(1)} %bitcast.110), channel_id=1, source_target_pairs={{0,2},{1,3},{2,0},{3,1},{4,6},{5,7},{6,4},{7,5},{8,10},{9,11},{10,... | collective-permute-start | bytes 3080 | tf_op jit(solution)/shard_map/ppermute | solution.py:284
  546.1 148.9 %collective-permute-start.3 = (f32[32,128]{1,0:T(8,128)S(1)}, f32[32,128]{1,0:T(8,128)S(1)}, u32[]{:S(2)}, u32[]{:S(2)}) collective-permute-start(f32[32,128]{1,0:T(8,128)S(1)} %get-tuple-element.77), channel_id=1, source_target_pairs={{0,2},{1,3},{2,0},{3,1},{4,6},{5,7},{6,4},{7,5},{8,10},{9,11},{10,... | collective-permute-start | bytes 49160 | tf_op jit(solution)/shard_map/ppermute | solution.py:284
  547.3 8.0 %copy-start.1 = (bf16[512,2048]{1,0:T(8,128)(2,1)S(1)}, bf16[512,2048]{1,0:T(8,128)(2,1)}, u32[]{:S(2)}) copy-start(bf16[512,2048]{1,0:T(8,128)(2,1)} %get-tuple-element.65.refs_10_.refs_6_) | copy-start | bytes 6291460
  547.3 8.0 %copy-start.8 = (f32[128,2048]{1,0:T(8,128)S(1)}, f32[128,2048]{1,0:T(8,128)}, u32[]{:S(2)}) copy-start(f32[128,2048]{1,0:T(8,128)} %get-tuple-element.67.refs_1_) | copy-start | bytes 3145732
  547.3 8.0 %copy-start.9 = (bf16[4,256,512]{2,1,0:T(8,128)(2,1)S(1)}, bf16[4,256,512]{2,1,0:T(8,128)(2,1)}, u32[]{:S(2)}) copy-start(bf16[4,256,512]{2,1,0:T(8,128)(2,1)} %get-tuple-element.69) | copy-start | bytes 3145732
  547.3 8.0 %copy-start.10 = (bf16[4,256,512]{2,1,0:T(8,128)(2,1)S(1)}, bf16[4,256,512]{2,1,0:T(8,128)(2,1)}, u32[]{:S(2)}) copy-start(bf16[4,256,512]{2,1,0:T(8,128)(2,1)} %get-tuple-element.70) | copy-start | bytes 3145732
  695.0 3.7 collective-permute-start.4
  696.3 2.9 copy-start.12
  (5 other events, 5.0 us)

commit v5 on v4

--- a/solution.py
+++ b/solution.py
@@ -528,6 +528,39 @@
         self.copy.wait()
 
 
+class Share:
+    semaphores = ((2 * LINE,),) * 2
+    buffers = ()
+    near = True
+    slots = 1
+
+    def __init__(self, values):
+        self.inputs = [values]
+        self.outputs = [jax.ShapeDtypeStruct((2 * LINE,) + values.shape, values.dtype)]
+
+    def bind(self, line, sources, targets, scratch):
+        self.line, self.source, self.target = line, sources[0], targets[0]
+        self.sends, self.recvs = scratch
+
+    def copy(self, p):
+        goal = self.target.at[self.line.block]
+        if p == 0:
+            return pltpu.make_async_copy(self.source, goal, self.recvs.at[0])
+        place, core = self.line.piece(p, 1)
+        return remote(
+            self.source, goal, self.sends.at[p], self.recvs.at[p], self.line.at(place, self.line.pair, core)
+        )
+
+    def slot(self, t):
+        if t == 0:
+            for p in range(2 * LINE):
+                self.copy(p).start()
+
+    def finish(self):
+        for p in range(2 * LINE):
+            self.copy(p).wait()
+
+
 class Deal:
     semaphores = ((2 * LINE,),) * 4
     buffers = ()
@@ -594,78 +627,104 @@
             remote(ref, ref, self.x_send.at[p], self.x_recv.at[p], self.line.partner).wait()
 
 
-def add_into(target, first, second):
-    step = 64
+def outer_into(target, left, row, right, column, *more):
+    rows, n = target.shape
+    wide = 512 if n % 512 == 0 else 384
 
     def some(index, carry):
-        rows = pl.ds(pl.multiple_of(index * step, step), step)
-        target[rows, :] = first[rows, :] + second[rows, :]
+        across = n // wide
+        down, along = index // across, index % across
+        here = pl.ds(pl.multiple_of(down * 128, 128), 128)
+        there = pl.ds(pl.multiple_of(along * wide, wide), wide)
+        total = lax.dot_general(
+            left[:, pl.ds(pl.multiple_of(row + down * 128, 128), 128)],
+            right[:, pl.ds(pl.multiple_of(column + along * wide, 128), wide)],
+            (((0,), (0,)), ((), ())),
+            preferred_element_type=jnp.float32,
+        )
+        for ref in more:
+            total = total + ref[here, there].astype(jnp.float32)
+        target[here, there] = total.astype(target.dtype)
         return carry
 
-    lax.fori_loop(0, target.shape[0] // step, some, 0)
+    lax.fori_loop(0, (rows // 128) * (n // wide), some, 0)
 
 
 class Reduce:
     near = True
 
-    def __init__(self, values, first):
-        rows, n = values.shape[0] // 8, values.shape[1] // 2
-        self.inputs, self.first, self.size, self.n = [values], first, rows, n
-        self.outputs = [jax.ShapeDtypeStruct((LINE, rows, n), values.dtype)]
+    def __init__(self, left, rights, first):
+        rows, n = left.shape[1] // 8, rights[0].shape[1] // 2
+        self.inputs, self.first, self.size, self.n = [left, *rights], first, rows, n
+        self.outputs = [jax.ShapeDtypeStruct((LINE, rows, n), left.dtype) for _ in rights]
         self.chunks = 2 * LINE if first == "partner" else LINE
         wide = n if first == "partner" else 2 * n
-        self.semaphores = ((self.chunks,),) * 2 + ((LINE,),) * 2
-        self.buffers = ((self.chunks, rows, wide), (LINE, rows, n), (LINE, rows, n))
-        self.join_at = [3 + (5 * k) // 2 for k in range(8)] if first == "partner" else [2, 4, 6, 8]
-        self.last_at = self.join_at[LINE:] if first == "partner" else [7, 8, 9, 10]
+        self.semaphores = ((self.chunks,),) * (2 * len(rights)) + ((LINE,),) * (2 * len(rights))
+        self.buffers = ((self.chunks, rows, wide),) * (2 * len(rights))
+        self.join_at = [3, 5, 8, 10] if first == "partner" else [3, 5, 7, 9]
+        self.last_at = [12, 15, 16, 17] if first == "partner" else [10, 10, 10, 11]
         self.slots = max(self.last_at) + 1
 
     def bind(self, line, sources, targets, scratch):
-        self.line, self.values, self.target = line, sources[0], targets[0]
-        self.send1, self.recv1, self.send2, self.recv2, self.came1, self.out2, self.came2 = scratch
-
-    def part(self, place, pair, rep=None):
-        rows = pl.ds(pl.multiple_of((place * 2 + pair) * self.size, self.size), self.size)
-        if rep is None:
-            return self.values.at[rows, :]
-        return self.values.at[rows, pl.ds(pl.multiple_of(rep * self.n, self.n), self.n)]
-
-    def leg1(self, k):
+        self.line, self.left, self.parts = line, sources[0], []
+        count = len(targets)
+        sems1, sems2, buffers = scratch[: 2 * count], scratch[2 * count : 4 * count], scratch[4 * count :]
+        for index, target in enumerate(targets):
+            pick = slice(2 * index, 2 * index + 2)
+            self.parts.append((sources[1 + index], target, *sems1[pick], *sems2[pick], *buffers[pick]))
+
+    def row(self, place, pair):
+        return (place * 2 + pair) * self.size
+
+    def leg1(self, part, k):
+        _, _, send1, recv1, _, _, out, came = part
+        device = self.line.partner if self.first == "partner" else self.line.across
+        return remote(out.at[k], came.at[k], send1.at[k], recv1.at[k], device)
+
+    def leg2(self, part, k):
+        _, target, _, _, send2, recv2, out, _ = part
+        device = self.line.across if self.first == "partner" else self.line.partner
+        return remote(out.at[k, :, pl.ds(0, self.n)], target.at[k], send2.at[k], recv2.at[k], device)
+
+    def produce(self, k):
         line = self.line
-        if self.first == "partner":
-            pair = 1 - line.pair if k < LINE else line.pair
-            return remote(
-                self.part(k % LINE, pair, 1 - line.rep), self.came1.at[k], self.send1.at[k], self.recv1.at[k], line.partner
-            )
-        return remote(self.part(k, 1 - line.pair), self.came1.at[k], self.send1.at[k], self.recv1.at[k], line.across)
-
-    def leg2(self, k):
-        device = self.line.across if self.first == "partner" else self.line.partner
-        return remote(self.out2.at[k], self.came2.at[k], self.send2.at[k], self.recv2.at[k], device)
+        for part in self.parts:
+            if self.first == "partner":
+                pair = 1 - line.pair if k < LINE else line.pair
+                outer_into(part[6].at[k], self.left, self.row(k % LINE, pair), part[0], (1 - line.rep) * self.n)
+            else:
+                outer_into(part[6].at[k], self.left, self.row(k, 1 - line.pair), part[0], 0)
+            self.leg1(part, k).start()
 
     def join(self, k):
         line, n = self.line, self.n
-        self.leg1(k).wait_recv()
-        if self.first == "partner":
-            own = self.part(k % LINE, 1 - line.pair if k < LINE else line.pair, line.rep)
-            add_into(self.out2.at[k] if k < LINE else self.target.at[k - LINE], own, self.came1.at[k])
-            if k < LINE:
-                self.leg2(k).start()
-            return
-        for rep, goal in ((1 - line.rep, self.out2.at[k]), (line.rep, self.target.at[k])):
-            columns = pl.ds(pl.multiple_of(rep * n, n), n)
-            add_into(goal, self.part(k, line.pair, rep), self.came1.at[k, :, columns])
-        self.leg2(k).start()
+        for part in self.parts:
+            right, _, _, _, _, _, out, came = part
+            self.leg1(part, k).wait()
+            goal = out.at[k, :, pl.ds(0, n)]
+            if self.first == "partner":
+                outer_into(goal, self.left, self.row(k, 1 - line.pair), right, line.rep * n, came.at[k])
+            else:
+                column = pl.multiple_of((1 - line.rep) * n, n)
+                outer_into(goal, self.left, self.row(k, line.pair), right, column, came.at[k, :, pl.ds(column, n)])
+            self.leg2(part, k).start()
 
     def last(self, k):
-        self.leg2(k).wait_recv()
-        add_into(self.target.at[k], self.target.at[k], self.came2.at[k])
+        line, n = self.line, self.n
+        for part in self.parts:
+            right, target, _, _, _, _, _, came = part
+            if self.first == "partner":
+                self.leg1(part, LINE + k).wait()
+                mine = came.at[LINE + k]
+            else:
+                mine = came.at[k, :, pl.ds(pl.multiple_of(line.rep * n, n), n)]
+            self.leg2(part, k).wait()
+            outer_into(target.at[k], self.left, self.row(k, line.pair), right, line.rep * n, mine, target.at[k])
 
     def slot(self, t):
-        if t == 0:
-            for k in range(self.chunks):
-                self.leg1(k).start()
-        for k in range(self.chunks):
+        if t < self.chunks:
+            self.produce(t)
+        for k in range(LINE):
             if t == self.join_at[k]:
                 self.join(k)
         for k in range(LINE):
@@ -673,52 +732,46 @@
                 self.last(k)
 
     def finish(self):
-        for k in range(self.chunks):
-            self.leg1(k).wait_send()
-        for k in range(LINE):
-            self.leg2(k).wait_send()
+        pass
 
 
 class PairSum:
     near = True
 
-    def __init__(self, values, count, at):
-        self.inputs, self.count, self.at = [values], count, at
-        self.outputs = [jax.ShapeDtypeStruct(values.shape[1:], values.dtype)]
+    def __init__(self, left, right, count, at):
+        self.inputs, self.count, self.at = [left, right], count, at
+        shape = (left.shape[1] // 2, right.shape[1])
+        self.outputs = [jax.ShapeDtypeStruct(shape, left.dtype)]
         self.semaphores = ((count,),) * 2
-        self.buffers = (values.shape[1:],)
-        self.slots = at + 2 * count
+        self.buffers = (shape,)
+        self.slots = at + count
 
     def bind(self, line, sources, targets, scratch):
-        self.line, self.values, self.target = line, sources[0], targets[0]
-        self.sends, self.recvs, self.came = scratch
+        self.line, self.target = line, targets[0]
+        self.left, self.right = sources
+        self.sends, self.recvs, self.out = scratch
         self.size = self.target.shape[0] // self.count
 
     def copy(self, k):
         rows = pl.ds(k * self.size, self.size)
         return remote(
-            self.values.at[1 - self.line.pair, rows, :],
-            self.came.at[rows, :],
-            self.sends.at[k],
-            self.recvs.at[k],
-            self.line.across,
+            self.out.at[rows, :], self.target.at[rows, :], self.sends.at[k], self.recvs.at[k], self.line.across
         )
 
     def slot(self, t):
-        if t == 0:
-            for k in range(self.count):
+        pair, size = self.line.pair, self.size
+        for k in range(self.count):
+            rows = pl.ds(k * size, size)
+            if t == k:
+                outer_into(self.out.at[rows, :], self.left, (1 - pair) * self.count * size + k * size, self.right, 0)
                 self.copy(k).start()
-        for k in range(self.count):
-            if t == self.at + 2 * k:
-                rows = pl.ds(k * self.size, self.size)
-                self.copy(k).wait_recv()
-                add_into(
-                    self.target.at[rows, :], self.values.at[self.line.pair, rows, :], self.came.at[rows, :]
-                )
+            if t == self.at + k:
+                self.copy(k).wait()
+                goal = self.target.at[rows, :]
+                outer_into(goal, self.left, pair * self.count * size + k * size, self.right, 0, goal)
 
     def finish(self):
-        for k in range(self.count):
-            self.copy(k).wait_send()
+        pass
 
 
 def line_scatter_joint(line, k, rows, parts, sib):
@@ -891,7 +944,7 @@
     return [near if move.near else far for move in moves for _ in getattr(move, side)]
 
 
-def line_call(collective_id, pieces, middle, inputs, outputs, scatter, gather, moves=(), limit=44):
+def line_call(collective_id, pieces, middle, inputs, outputs, scatter, gather, moves=(), limit=46):
     step = inputs[0].shape[-2] // pieces if inputs else 0
     low = jnp.bfloat16
     scratch = []
@@ -1011,7 +1064,7 @@
         return ins[0][rows, :]
 
     shape = (2 * LINE,) + payload.shape
-    return line_call(collective_id, 9, middle, [payload], [(shape, jnp.bfloat16)], False, True, moves)
+    return line_call(collective_id, 8, middle, [payload], [(shape, jnp.bfloat16)], False, True, moves)
 
 
 def attention_block(parts, hidden, gain, moves, collective_id):
@@ -1175,19 +1228,20 @@
     )(*inputs, *moved)
 
 
-def attend(raw, turns, bias, gains, weight, moves, collective_id):
+def attend(tokens, full_qkv, turns, bias, gains, weight, moves, collective_id):
     blocks, length = bias.shape[:2]
-    width = raw.shape[2] // 3
+    width = full_qkv.shape[1] // 3
     heads = width // HEAD_DIM
     model_width = weight.shape[1]
     low = jnp.bfloat16
 
     def body(line, ins, outs, scratch, tick):
-        raw, turns, bias, gains, weight = ins
-        parts, lows, probs, mixed, squares = outs
+        tokens, full_qkv, turns, bias, gains, weight = ins
+        parts, lows, probs, mixed, squares, raw = outs
         mine, came, sends, recvs = scratch
 
         def squares_of(b, carry):
+            raw[b] = dot(tokens[b], full_qkv[...], 1, 0)
             for index in range(2):
                 total = jnp.zeros((length, 1), jnp.float32)
                 for h in range(heads):
@@ -1197,8 +1251,9 @@
             return carry
 
         tick()
-        lax.fori_loop(0, blocks, squares_of, 0)
-        tick()
+        for part in range(LINE):
+            lax.fori_loop(2 * part, 2 * part + 2, squares_of, 0)
+            tick()
         squares[...] = line_exchange(line, mine, came, sends, recvs)
         tick()
 
@@ -1234,13 +1289,14 @@
     return heads_call(
         collective_id,
         body,
-        [raw, turns, bias, gains, weight],
+        [tokens, full_qkv, turns, bias, gains, weight],
         [
             ((blocks, length, model_width), low),
             ((blocks, length, 3 * width), low),
             ((blocks, heads, length, length), jnp.float32),
             ((blocks, length, width), low),
             ((2 * blocks, length), jnp.float32),
+            ((blocks, length, 3 * width), jnp.float32),
         ],
         [],
         2 * blocks,
@@ -1248,9 +1304,8 @@
     )
 
 
-def attend_back(d_attn, weight, raw, turns, gains, lows, probs, squares, wide_terms, moves, collective_id):
-    blocks, rows = raw.shape[:2]
-    length = lows.shape[1]
+def attend_back(d_attn, weight, raw, turns, gains, lows, probs, squares, wide_terms, full_qkv, moves, collective_id):
+    blocks, length = raw.shape[:2]
     width = raw.shape[2] // 3
     heads = width // HEAD_DIM
     model_width = weight.shape[1]
@@ -1258,7 +1313,8 @@
 
     def body(line, ins, outs, scratch, tick):
         d_attn, weight, raw, turns, gains, lows, probs, squares = ins[:8]
-        d_low, terms, wide = outs
+        d_low, terms, wide, parts = outs
+        full_qkv = ins[10]
         mine, came, sends, recvs, upstream, unit = scratch
         tick()
         terms[...] = jnp.zeros_like(terms)
@@ -1308,7 +1364,6 @@
         wide[...] = mine[2 * blocks :, :]
 
         def last(b, carry):
-            d_low[b, length:, :] = jnp.zeros((rows - length, 3 * width), low)
             for index in range(2):
                 scale = lax.rsqrt(
                     as_columns(squares[pl.ds(index * blocks + b, 1), :]) / model_width + epsilon
@@ -1319,6 +1374,7 @@
                     d_low[b, :length, spot(h, index)] = (
                         scale * (upstream[b, :, side] - unit[b, :, side] * mean)
                     ).astype(low)
+            parts[b] = dot(d_low[b], full_qkv[...], 1, 1).astype(low)
             return carry
 
         lax.fori_loop(0, blocks, last, 0)
@@ -1326,11 +1382,12 @@
     return heads_call(
         collective_id,
         body,
-        [d_attn, weight, raw, turns, gains, lows, probs, squares, *wide_terms],
+        [d_attn, weight, raw, turns, gains, lows, probs, squares, *wide_terms, full_qkv],
         [
             (raw.shape, low),
             ((8, 2 * width), jnp.float32),
             ((2 * model_width // length, length), jnp.float32),
+            ((blocks, length, model_width), low),
         ],
         [pltpu.VMEM((blocks, length, 2 * width), jnp.float32) for _ in range(2)],
         2 * blocks + 2 * model_width // length,
@@ -1364,12 +1421,18 @@
     extra = jnp.concatenate(
         [query_gain, key_gain, attn_gain, ffn_gain, segments[0].astype(jnp.bfloat16)]
     )
-    extra = jnp.pad(extra[None], ((0, 15), (0, model_width - extra.shape[0])))
-    payload, full_qkv, full_output = gather_blocks(
-        jnp.concatenate([hidden_in, extra]), [Spread(w_query, w_key, w_value), Stack(w_output, 2)], 0
-    )
-    docs = payload[:, length, 4 * length : 5 * length].astype(jnp.int32)
-    gains = payload[:, length, : 4 * length].reshape(LINE, 2, 4, length)
+    payload, extras, full_qkv, full_output = gather_blocks(
+        hidden_in,
+        [
+            Share(jnp.pad(extra[None], ((0, 15), (0, 0)))),
+            Spread(w_query, w_key, w_value),
+            Stack(w_output, 2),
+        ],
+        0,
+    )
+    tokens = payload.reshape(-1, model_width)
+    docs = extras[:, 0, 4 * length :].astype(jnp.int32)
+    gains = extras[:, 0, : 4 * length].reshape(LINE, 2, 4, length)
     gains = jnp.stack(by_pair(pair, gains, pair_swap(gains)), axis=1)
     gains = jnp.moveaxis(gains, 3, 0).reshape(4, 1, model_width).astype(f32)
     gain_attn, gain_ffn = gains[2], gains[3]
@@ -1394,10 +1457,8 @@
     def to_blocks(values):
         return values.astype(jnp.bfloat16).reshape(blocks, -1, model_width)
 
-    raw = jnp.dot(payload.reshape(-1, model_width), full_qkv, preferred_element_type=f32)
-    raw = raw.reshape(blocks, -1, 3 * width)
-    attn_parts, lows, probs, mixed_low, squares, full_gate = attend(
-        raw, turns, bias, head_gains, full_output, [Spread(w_gate, begin=2, burst=True)], 6
+    attn_parts, lows, probs, mixed_low, squares, raw, full_gate = attend(
+        payload, full_qkv, turns, bias, head_gains, full_output, [Spread(w_gate, burst=True)], 6
     )
     mixed_low = mixed_low.reshape(blocks * length, width)
     resid_low, attn_out, resid, full_up, full_down = attention_block(
@@ -1427,46 +1488,30 @@
         jnp.bfloat16
     )
     d_up_low = (d_hidden_ffn * gate_proj * gate_sig).astype(jnp.bfloat16)
-    def outer(left_side, right_side):
-        return lax.dot_general(
-            left_side, right_side, (((0,), (0,)), ((), ())), preferred_element_type=f32
-        ).astype(jnp.bfloat16)
-
     ff_rows = w_down.shape[0]
-    part_gate = outer(resid_low, d_gate_low)
-    part_up = outer(resid_low, d_up_low)
-    part_down = outer(hidden_ffn, d_ffn_low).reshape(2, ff_rows, model_width)
-
     d_attn_low, d_resid, attn_gain_term, gate_sum, up_sum, down_part = back_block(
         to_blocks(dot_back(d_gate_low, full_gate) + dot_back(d_up_low, full_up)),
         out_cotangent,
         attn_out,
         gain_attn,
         [
-            Reduce(part_gate, "partner"),
-            Reduce(part_up, "partner"),
-            PairSum(part_down, 4, 13),
+            Reduce(resid_low, [d_gate_low, d_up_low], "partner"),
+            PairSum(hidden_ffn, d_ffn_low, 4, 13),
         ],
         3,
     )
 
-    d_qkv, head_terms, wide_terms, there_first = attend_back(
+    d_qkv, head_terms, wide_terms, back_parts, there_first = attend_back(
         d_attn_low, full_output, raw, turns, head_gains, lows, probs, squares,
-        [attn_gain_term, ffn_gain_term], [Swap(down_part, 0, ff_rows // 2)], 7,
+        [attn_gain_term, ffn_gain_term], full_qkv, [Swap(down_part, 0, ff_rows // 2)], 7,
     )
     d_attn_low = d_attn_low.reshape(blocks * length, model_width)
-    part_qkv = outer(
-        payload.reshape(-1, model_width), d_qkv.reshape(-1, 3 * width)
-    )
-    part_output = outer(mixed_low, d_attn_low).reshape(2, length, model_width)
     hidden_grad, qkv_sum, output_part, ffn_total, there_second = last_block(
-        to_blocks(
-            dot_back(d_qkv[:, :length].reshape(-1, 3 * width), full_qkv)
-        ),
+        back_parts,
         d_resid,
         [
-            Reduce(part_qkv, "across"),
-            PairSum(part_output, 1, 5),
+            Reduce(tokens, [d_qkv.reshape(-1, 3 * width)], "across"),
+            PairSum(mixed_low, d_attn_low, 1, 5),
             Deal([gate_sum.reshape(blocks, length, -1), up_sum.reshape(blocks, length, -1)], 1),
             Swap(down_part, ff_rows // 2, ff_rows // 2),
         ],

time: 710 us -> 675 us (0.951)
  matrix products: 92.1 us -> 46.5 us
  local copies, waits for them, and re-layouts: 24.5 us -> 32 us
    dot_general x6 -> x0, matrix products: 38.9 us -> none  [the longest x5 29.9 us: outer(): lax.dot_general(left_side, right_side, (((0,), (0,)), ((), ())), preferre...]
    pallas_call x2, Pallas kernels: 84 us -> 94.1 us  [heads_call(): pl.pallas_call(kernel, out_shape=[jax.ShapeDtypeStruct(shape, kind) for s...]
    unnamed x70 -> x88, local copies, waits for them, and re-layouts: 15 us -> 24.4 us
    dot_general x4 -> x3, matrix products: 34 us -> 26.1 us  [dot_back(): lax.dot_general(left_side, right_side, (((1,), (1,)), ((), ())), preferre...]
  transfers between devices with their start and end apart: 5 -> 5, of which waited for: 1 -> 0; matrix products, arithmetic and copies ran while one was open for 5% -> 3% of each run, Pallas kernels for 35% -> 39%
where the time goes in v5:
time: 675 us; the launch traced here: 666 us
  Pallas kernels  568 us (84%)
  matrix products  46.5 us (7%)
  local copies, waits for them, and re-layouts  32 us (5%)
  other arithmetic  9.12 us (1%)
  starting transfers between devices  8.17 us (1%)
    pallas_call x6, Pallas kernels, line_call(): pl.pallas_call(kernel, out_shape=[jax.ShapeDtypeStruct(shape, kind) for s...  474 us
    pallas_call x2, Pallas kernels, heads_call(): pl.pallas_call(kernel, out_shape=[jax.ShapeDtypeStruct(shape, kind) for s...  94.1 us
    dot_general x3, matrix products, dot_back(): lax.dot_general(left_side, right_side, (((1,), (1,)), ((), ())), preferre...  26.1 us
    unnamed x88, local copies, waits for them, and re-layouts  24.4 us
  transfers between devices with their start and end apart: 5, of which 0 were waited for; matrix products, arithmetic and copies ran while one was open for 3% of the time, Pallas kernels for 39%

profile of v5, /device:TPU:0, one launch (start us, length us, event | category | flops | bytes accessed | tf_op | source)
XLA Modules:
  0.0 665.6 jit_solution(12924292245459011491)
XLA Ops:
  1.4 3.0 collective-permute-start
  10.6 1.0 copy-done.21
  11.7 1.0 copy-done.22
  13.8 65.4 %shard_map.237 = (bf16[8,128,2048]{2,1,0:T(8,128)(2,1)}, bf16[8,16,640]{2,1,0:T(8,128)(2,1)S(1)}, bf16[2048,768]{1,0:T(8,128)(2,1)S(1)}, bf16[256,2048]{1,0:T(8,128)(2,1)S(1)}) custom-call(bf16[128,2048]{1,0:T(8,128)(2,1)S(1)} %copy-done.6, bf16[16,640]{1,0:T(8,128)(2,1)S(1)} %pad.4.refs_1_, bf16[128,2048]{1,0:T(8,128)(2,1)S(1)} %copy-done.20, ...), custom_call_target="tpu_custom_call" | custom-call | flops 10000000 | bytes 200000000 | tf_op jit(solution)/shard_map/pallas_call | solution.py:1049
  79.2 1.6 copy-done.2
  80.8 1.4 collective-permute-start.1
  83.1 1.9 maximum_cosine_fusion.refs_2_.refs_3_
  85.1 1.6 copy-done.8
  86.7 59.2 %shard_map.238 = (bf16[8,128,2048]{2,1,0:T(8,128)(2,1)}, bf16[8,128,768]{2,1,0:T(8,128)(2,1)S(1)}, f32[8,2,128,128]{3,2,1,0:T(8,128)S(1)}, bf16[8,128,256]{2,1,0...) custom-call(bf16[8,128,2048]{2,1,0:T(8,128)(2,1)} %get-tuple-element.50.refs_0_, ...), custom_call_target="tpu_custom_call" | custom-call | flops 10000000 | bytes 80000000 | tf_op jit(solution)/shard_map/pallas_call | solution.py:1218
  145.9 1.1 copy-done.10
  148.9 93.9 %shard_map.239 = (bf16[8,128,2048]{2,1,0:T(8,128)(2,1)}, f32[128,2048]{1,0:T(8,128)S(1)}, f32[128,2048]{1,0:T(8,128)S(1)}, bf16[2048,1024]{1,0:T(8,128)(2,1)}, bf16[1024,2048]{1,0:T(8,128)(2,1)}) custom-call(bf16[8,128,2048]{2,1,0:T(8,128)(2,1)} %get-tuple-element.54.refs_0_, bf16[128,2048]{1,0:T(8,128)(2,1)S(1)} %copy-done.7, f32[1,2048]{1,0:T(1,128)S(1)} %bitcast.69, ...), custom_call_target="tpu_custom_call" | custom-call | flops 10000000 | bytes 200000000 | tf_op jit(solution)/shard_map/pallas_call | solution.py:1049
  242.9 7.9 %fusion.5 = f32[1024,1024]{1,0:T(8,128)S(1)} fusion(bf16[1024,2048]{1,0:T(8,128)(2,1)} %bitcast.75, bf16[2048,1024]{1,0:T(8,128)(2,1)} %get-tuple-element.56), kind=kOutput, calls=%fused_computation.39 | convolution fusion | flops 4294967296 | bytes 12582912 | tf_op jit(solution)/shard_map/dot_general | solution.py:1473
  250.8 6.5 multiply_convert_fusion.2
  257.3 6.0 convolution_convert_fusion
  263.4 69.3 %shard_map.240 = (bf16[8,128,2048]{2,1,0:T(8,128)(2,1)S(1)}, bf16[128,2048]{1,0:T(8,128)(2,1)S(1)}, f32[8,2048]{1,0:T(8,128)S(1)}) custom-call(bf16[8,128,2048]{2,1,0:T(8,128)(2,1)} %bitcast.74, f32[128,2048]{1,0:T(8,128)S(1)} %get-tuple-element.59.refs_1_, bf16[128,2048]{1,0:T(8,128)(2,1)S(1)} %copy-done.9, f32[1,2048]{1,0:T(1,128)S(1)} %bitcast.71), custom_call_target="tpu_custom_call" | custom-call | flops 10000000 | bytes 200000000 | tf_op jit(solution)/shard_map/pallas_call | solution.py:1049
  332.7 11.0 %multiply_convert_fusion = (bf16[1024,1024]{1,0:T(8,128)(2,1)S(1)}, bf16[1024,1024]{1,0:T(8,128)(2,1)S(1)}) fusion(f32[1024,1024]{1,0:T(8,128)} %copy-done.40, f32[1024,1024]{1,0:T(8,128)} %get-tuple-element.110, bf16[1024,2048]{1,0:T(8,128)(2,1)S(1)} %bitcast.62, bf16[1024,2048]{1,0:T(8,128)(2,1)} %get-tuple-element.58), kind=kOutput, calls=%fused_computation.2 | convolution fusion | flops 4308598784 | bytes 20971520 | tf_op jit(solution)/shard_map/dot_general | solution.py:37
  343.8 6.8 %fusion.6 = f32[1024,2048]{1,0:T(8,128)} fusion(bf16[1024,1024]{1,0:T(8,128)(2,1)S(1)} %get-tuple-element.88.refs_5_, bf16[2048,1024]{1,0:T(8,128)(2,1)S(1)} %copy-done.36), kind=kOutput, calls=%fused_computation.40 | convolution fusion | flops 4294967296 | bytes 14680064 | tf_op jit(solution)/shard_map/dot_general | solution.py:37
  350.6 8.3 %add_convert_fusion = bf16[1024,2048]{1,0:T(8,128)(2,1)} fusion(f32[1024,2048]{1,0:T(8,128)} %fusion.6, bf16[1024,1024]{1,0:T(8,128)(2,1)S(1)} %get-tuple-element.87.refs_6_, bf16[2048,1024]{1,0:T(8,128)(2,1)S(1)} %copy-done.38), kind=kOutput, calls=%fused_computation | convolution fusion | flops 4299161600 | bytes 18874368 | tf_op jit(solution)/shard_map/dot_general | solution.py:37
  358.9 112.4 %shard_map.241 = (bf16[8,128,2048]{2,1,0:T(8,128)(2,1)}, f32[128,2048]{1,0:T(8,128)}, f32[8,2048]{1,0:T(8,128)}, bf16[4,256,512]{2,1,0:T(8,128)(2,1)}, bf16[4,25...) custom-call(bf16[8,128,2048]{2,1,0:T(8,128)(2,1)} %bitcast.78, bf16[128,2048]{1,0:T(8,128)(2,1)} %refs_1_.3, ...), custom_call_target="tpu_custom_call" | custom-call | flops 10000000 | bytes 200000000 | tf_op jit(solution)/shard_map/pallas_call | solution.py:1049
  471.4 1.6 copy-done
  473.8 34.9 %shard_map.242 = (bf16[8,128,768]{2,1,0:T(8,128)(2,1)S(1)}, f32[8,512]{1,0:T(8,128)S(1)}, f32[32,128]{1,0:T(8,128)S(1)}, bf16[8,128,2048]{2,1,0:T(8,128)(2,1)}, bf16[256,2048]{1,0:T(8,128)(2,1)S(1)}) custom-call(bf16[8,128,2048]{2,1,0:T(8,128)(2,1)} %get-tuple-element.63.refs_0_, bf16[256,2048]{1,0:T(8,128)(2,1)S(1)} %get-tuple-element.53.refs_5_.refs_1_, ...), custom_call_target="tpu_custom_call" | custom-call | flops 10000000 | bytes 80000000 | tf_op jit(solution)/shard_map/pallas_call | solution.py:1218
  510.3 1.6 collective-permute-start.3
  511.8 1.2 copy-done.14
  513.1 1.2 copy-done.15
  514.3 1.2 copy-done.16
  515.5 1.0 copy-done.25
  516.6 102.5 %shard_map.243 = (bf16[128,2048]{1,0:T(8,128)(2,1)S(1)}, bf16[4,256,384]{2,1,0:T(8,128)(2,1)S(1)}, bf16[128,2048]{1,0:T(8,128)(2,1)S(1)}, bf16[128,16384]{1,0:T(8,128)(2,1)}, bf16[256,2048]{1,0:T(8,128)(2,1)S(1)}) custom-call(bf16[8,128,2048]{2,1,0:T(8,128)(2,1)} %get-tuple-element.71.refs_0_, f32[128,2048]{1,0:T(8,128)S(1)} %copy-done.14, ...), custom_call_target="tpu_custom_call" | custom-call | flops 10000000 | bytes 200000000 | tf_op jit(solution)/shard_map/pallas_call | solution.py:1049
  619.1 6.8 %fusion.1 = (f32[128,8192]{1,0:T(8,128)}, f32[128,8192]{1,0:T(8,128)}) fusion(bf16[128,16384]{1,0:T(8,128)(2,1)} %get-tuple-element.84), kind=kLoop, calls=%fused_computation.35 | loop fusion | bytes 16777216 | tf_op jit(solution)/shard_map/split | solution.py:1532
  625.8 2.8 convert_add_fusion
  628.6 30.8 %shard_map.244 = (bf16[128,6144]{1,0:T(8,128)(2,1)S(1)}, bf16[128,2048]{1,0:T(8,128)(2,1)S(1)}) custom-call(bf16[8,128,384]{2,1,0:T(8,128)(2,1)S(1)} %bitcast.67, bf16[128,2048]{1,0:T(8,128)(2,1)S(1)} %get-tuple-element.79.refs_1_), custom_call_target="tpu_custom_call" | custom-call | flops 10000000 | bytes 200000000 | tf_op jit(solution)/shard_map/pallas_call | solution.py:1049
  659.5 1.7 collective-permute-start.4
  661.2 2.1 fusion.2
  (114 shorter events, 15.4 us)
Async XLA Ops:
  0.6 84.4 %copy-start.35 = (bf16[128]{0:T(256)(128)(2,1)S(1)}, bf16[128]{0:T(256)(128)(2,1)}, u32[]{:S(2)}) copy-start(bf16[128]{0:T(256)(128)(2,1)} %param.21) | copy-start | bytes 772
  0.7 84.4 %copy-start.34 = (bf16[128]{0:T(256)(128)(2,1)S(1)}, bf16[128]{0:T(256)(128)(2,1)}, u32[]{:S(2)}) copy-start(bf16[128]{0:T(256)(128)(2,1)} %param.20) | copy-start | bytes 772
  1.4 83.6 %collective-permute-start = (bf16[1,2,128]{2,1,0:T(2,128)(2,1)S(1)}, bf16[1,2,128]{2,1,0:T(2,128)(2,1)S(1)}, u32[]{:S(2)}, u32[]{:S(2)}) collective-permute-start(bf16[1,2,128]{2,1,0:T(2,128)(2,1)S(1)} %maximum_bitcast_fusion), channel_id=1, source_target_pairs={{0,2},{1,3},{2,0},{3,1},{4,6},{5,7},{6,4},{7,5},{8,10},{9,11},{10,... | collective-permute-start | bytes 1544 | tf_op jit(solution)/shard_map/ppermute | solution.py:284
  79.1 1.6 copy-start.2
  80.8 68.0 %collective-permute-start.1 = (bf16[4,2,4,128]{3,2,1,0:T(4,128)(2,1)S(1)}, bf16[4,2,4,128]{3,2,1,0:T(4,128)(2,1)S(1)}, u32[]{:S(2)}, u32[]{:S(2)}) collective-permute-start(bf16[4,2,4,128]{3,2,1,0:T(4,128)(2,1)S(1)} %reshape_squeeze.3), channel_id=1, source_target_pairs={{0,2},{1,3},{2,0},{3,1},{4,6},{5,7},{6,4},{7,5},{8,10},{9,11},{10,... | collective-permute-start | bytes 24584 | tf_op jit(solution)/shard_map/ppermute | solution.py:284
  85.1 1.6 copy-start.8
  86.7 62.2 %copy-start.4 = (bf16[128,8192]{1,0:T(8,128)(2,1)S(1)}, bf16[128,8192]{1,0:T(8,128)(2,1)}, u32[]{:S(2)}) copy-start(bf16[128,8192]{1,0:T(8,128)(2,1)} %refs_3_.3) | copy-start | bytes 6291460
  86.7 62.2 %copy-start.5 = (bf16[512,2048]{1,0:T(8,128)(2,1)S(1)}, bf16[512,2048]{1,0:T(8,128)(2,1)}, u32[]{:S(2)}) copy-start(bf16[512,2048]{1,0:T(8,128)(2,1)} %refs_4_.3) | copy-start | bytes 6291460
  86.7 62.2 %copy-start.7 = (bf16[128,2048]{1,0:T(8,128)(2,1)S(1)}, bf16[128,2048]{1,0:T(8,128)(2,1)}, u32[]{:S(2)}) copy-start(bf16[128,2048]{1,0:T(8,128)(2,1)} %refs_1_.2) | copy-start | bytes 1572868
  148.9 94.0 %copy-start.28 = (f32[1,4,2,2,128]{4,3,2,1,0:T(2,128)}, f32[1,4,2,2,128]{4,3,2,1,0:T(2,128)S(1)}, u32[]{:S(2)}) copy-start(f32[1,4,2,2,128]{4,3,2,1,0:T(2,128)S(1)} %copy.31) | copy-start | bytes 24580
  242.8 8.0 %copy-start.17 = (f32[128,2048]{1,0:T(8,128)}, f32[128,2048]{1,0:T(8,128)S(1)}, u32[]{:S(2)}) copy-start(f32[128,2048]{1,0:T(8,128)S(1)} %get-tuple-element.62.refs_2_) | copy-start | bytes 3145732
  242.8 8.0 %copy-start.30 = (bf16[8,128,2048]{2,1,0:T(8,128)(2,1)S(1)}, bf16[8,128,2048]{2,1,0:T(8,128)(2,1)}, u32[]{:S(2)}) copy-start(bf16[8,128,2048]{2,1,0:T(8,128)(2,1)} %get-tuple-element.55) | copy-start | bytes 12582916
  242.9 8.0 %copy-start.37 = (bf16[2048,1024]{1,0:T(8,128)(2,1)S(1)}, bf16[2048,1024]{1,0:T(8,128)(2,1)}, u32[]{:S(2)}) copy-start(bf16[2048,1024]{1,0:T(8,128)(2,1)} %get-tuple-element.57) | copy-start | bytes 12582916
  250.8 6.5 copy-start.40
  250.8 6.5 copy-start.39
  257.3 6.0 copy-start.31
  257.3 6.0 copy-start.9
  332.7 11.0 %copy-start.3 = (bf16[8,128,2048]{2,1,0:T(8,128)(2,1)}, bf16[8,128,2048]{2,1,0:T(8,128)(2,1)S(1)}, u32[]{:S(2)}) copy-start(bf16[8,128,2048]{2,1,0:T(8,128)(2,1)S(1)} %get-tuple-element.61) | copy-start | bytes 12582916
  332.7 11.0 %copy-start.26 = (bf16[128,2048]{1,0:T(8,128)(2,1)}, bf16[128,2048]{1,0:T(8,128)(2,1)S(1)}, u32[]{:S(2)}) copy-start(bf16[128,2048]{1,0:T(8,128)(2,1)S(1)} %get-tuple-element.125) | copy-start | bytes 1572868
  332.7 11.1 %copy-start.36 = (bf16[2048,1024]{1,0:T(8,128)(2,1)S(1)}, bf16[2048,1024]{1,0:T(8,128)(2,1)}, u32[]{:S(2)}) copy-start(bf16[2048,1024]{1,0:T(8,128)(2,1)} %get-tuple-element.56) | copy-start | bytes 12582916
  343.8 6.8 %copy-start.33 = (bf16[1024,1024]{1,0:T(8,128)(2,1)}, bf16[1024,1024]{1,0:T(8,128)(2,1)S(1)}, u32[]{:S(2)}) copy-start(bf16[1024,1024]{1,0:T(8,128)(2,1)S(1)} %get-tuple-element.88.refs_5_) | copy-start | bytes 6291460
  343.8 6.8 %copy-start.32 = (bf16[1024,1024]{1,0:T(8,128)(2,1)}, bf16[1024,1024]{1,0:T(8,128)(2,1)S(1)}, u32[]{:S(2)}) copy-start(bf16[1024,1024]{1,0:T(8,128)(2,1)S(1)} %get-tuple-element.87.refs_6_) | copy-start | bytes 6291460
  343.8 6.8 %copy-start.38 = (bf16[2048,1024]{1,0:T(8,128)(2,1)S(1)}, bf16[2048,1024]{1,0:T(8,128)(2,1)}, u32[]{:S(2)}) copy-start(bf16[2048,1024]{1,0:T(8,128)(2,1)} %get-tuple-element.57) | copy-start | bytes 12582916
  358.9 112.5 %copy-start.11 = (bf16[8,128,768]{2,1,0:T(8,128)(2,1)S(1)}, bf16[8,128,768]{2,1,0:T(8,128)(2,1)}, u32[]{:S(2)}) copy-start(bf16[8,128,768]{2,1,0:T(8,128)(2,1)} %copy-done.10) | copy-start | bytes 4718596
  358.9 112.5 %copy-start.13 = (f32[8,2,128,128]{3,2,1,0:T(8,128)S(1)}, f32[8,2,128,128]{3,2,1,0:T(8,128)}, u32[]{:S(2)}) copy-start(f32[8,2,128,128]{3,2,1,0:T(8,128)} %copy-done.12) | copy-start | bytes 3145732
  471.4 1.6 copy-start
  509.7 149.7 %collective-permute-start.2 = (f32[2,128]{1,0:T(2,128)S(1)}, f32[2,128]{1,0:T(2,128)S(1)}, u32[]{:S(2)}, u32[]{:S(2)}) collective-permute-start(f32[2,128]{1,0:T(2,128)S(1)} %bitcast.91), channel_id=1, source_target_pairs={{0,2},{1,3},{2,0},{3,1},{4,6},{5,7},{6,4},{7,5},{8,10},{9,11},{10,... | collective-permute-start | bytes 3080 | tf_op jit(solution)/shard_map/ppermute | solution.py:284
  510.3 149.1 %collective-permute-start.3 = (f32[32,128]{1,0:T(8,128)S(1)}, f32[32,128]{1,0:T(8,128)S(1)}, u32[]{:S(2)}, u32[]{:S(2)}) collective-permute-start(f32[32,128]{1,0:T(8,128)S(1)} %get-tuple-element.83), channel_id=1, source_target_pairs={{0,2},{1,3},{2,0},{3,1},{4,6},{5,7},{6,4},{7,5},{8,10},{9,11},{10,... | collective-permute-start | bytes 49160 | tf_op jit(solution)/shard_map/ppermute | solution.py:284
  619.0 6.8 %copy-start.1 = (bf16[512,2048]{1,0:T(8,128)(2,1)S(1)}, bf16[512,2048]{1,0:T(8,128)(2,1)}, u32[]{:S(2)}) copy-start(bf16[512,2048]{1,0:T(8,128)(2,1)} %get-tuple-element.70.refs_11_.refs_8_) | copy-start | bytes 6291460
  619.0 6.8 %copy-start.19 = (bf16[256,2048]{1,0:T(8,128)(2,1)S(1)}, bf16[256,2048]{1,0:T(8,128)(2,1)}, u32[]{:S(2)}) copy-start(bf16[256,2048]{1,0:T(8,128)(2,1)} %copy-done.18) | copy-start | bytes 3145732
  659.5 3.8 collective-permute-start.4
  661.2 2.7 copy-start.27
  (14 other events, 14.6 us)

commit v6 on v5

--- a/solution.py
+++ b/solution.py
@@ -357,13 +357,16 @@
 class Spread:
     semaphores = ((2 * LINE,),) * 2 + ((2 * LINE, 2),) * 4
     buffers = ()
-    near = True
-
-    def __init__(self, *weights, begin=0, burst=False):
-        self.inputs, self.begin, self.burst = list(weights), begin, burst
+    near = False
+
+    BESIDE_LINE = ((0, 0, 1, 1, 1, 2, 2, 2), (0, 2, 3, 4, 5, 6, 7, 8), (3, 4, 5, 6, 7, 8, 9, 10))
+    BESIDE_HEADS = ((0, 0, 0, 0, 4, 4, 0, 0), (0, 1, 4, 4, 8, 8, 4, 4), (1, 2, 5, 5, 9, 9, 5, 5))
+
+    def __init__(self, *weights, plan=BESIDE_LINE):
+        self.inputs, self.plan = list(weights), plan
         shape = (16 * weights[0].shape[0], sum(weight.shape[1] for weight in weights) // 8)
         self.outputs = [jax.ShapeDtypeStruct(shape, jnp.bfloat16)]
-        self.slots = begin + 3 + 2 * LINE
+        self.slots = max(plan[2]) + 1
 
     def bind(self, line, sources, targets, sems):
         self.line, self.sources, self.target = line, sources, targets[0]
@@ -371,16 +374,10 @@
         self.half = sources[0].shape[0] // 2
 
     def slot(self, t):
-        t -= self.begin
-        for p in range(2 * LINE):
-            if t == (0 if self.burst else (p + 1) // 3):
-                self.start(p)
-        for p in range(2 * LINE):
-            if t == (p + 1 if p else 0):
-                self.came(p)
-        for p in range(2 * LINE):
-            if t == p + 3:
-                self.onward(p)
+        for when, act in zip(self.plan, (self.start, self.came, self.onward)):
+            for p in range(2 * LINE):
+                if t == when[p]:
+                    act(p)
 
     def rows(self, place, pair, core, rep):
         start = ((place * 4 + pair * 2 + core) * 2 + rep) * self.half
@@ -456,7 +453,7 @@
 
 class Stack:
     buffers = ()
-    near = True
+    near = False
 
     def __init__(self, weight, count):
         self.inputs, self.count = [weight], count
@@ -629,15 +626,16 @@
 
 def outer_into(target, left, row, right, column, *more):
     rows, n = target.shape
+    tall = min(rows, 256)
     wide = 512 if n % 512 == 0 else 384
 
     def some(index, carry):
         across = n // wide
         down, along = index // across, index % across
-        here = pl.ds(pl.multiple_of(down * 128, 128), 128)
+        here = pl.ds(pl.multiple_of(down * tall, tall), tall)
         there = pl.ds(pl.multiple_of(along * wide, wide), wide)
         total = lax.dot_general(
-            left[:, pl.ds(pl.multiple_of(row + down * 128, 128), 128)],
+            left[:, pl.ds(pl.multiple_of(row + down * tall, 128), tall)],
             right[:, pl.ds(pl.multiple_of(column + along * wide, 128), wide)],
             (((0,), (0,)), ((), ())),
             preferred_element_type=jnp.float32,
@@ -647,7 +645,7 @@
         target[here, there] = total.astype(target.dtype)
         return carry
 
-    lax.fori_loop(0, (rows // 128) * (n // wide), some, 0)
+    lax.fori_loop(0, (rows // tall) * (n // wide), some, 0)
 
 
 class Reduce:
@@ -828,49 +826,32 @@
     return total + jnp.where(line.has_right, lefts[me, rows, :].astype(jnp.float32), 0.0)
 
 
-def line_scatter_start(line, pieces, step, parts, sib, sib_send, sib_recv):
-    def piece(j, carry):
-        rows = pl.ds(pl.multiple_of(j * step, step), step)
-        for k in range(LINE):
+def line_scatter_start(line, j, step, parts, sib, sib_send, sib_recv):
+    rows = pl.ds(pl.multiple_of(j * step, step), step)
+    for k in range(LINE):
+        remote(
+            parts.at[2 * k + 1 - line.core, rows], sib.at[k, rows], sib_send.at[k, j], sib_recv.at[k, j], line.sibling
+        ).start()
+
+
+def line_scatter_end(line, j, step, parts, sib, rights, lefts, sums, sib_send, right_send, left_send):
+    rows = pl.ds(pl.multiple_of(j * step, step), step)
+    for k in range(LINE):
+        remote(
+            parts.at[2 * k + 1 - line.core, rows], sib.at[k, rows], sib_send.at[k, j], sib_send.at[k, j], line.sibling
+        ).wait_send()
+
+        @pl.when(line.place < k)
+        def _():
             remote(
-                parts.at[2 * k + 1 - line.core, rows],
-                sib.at[k, rows],
-                sib_send.at[k, j],
-                sib_recv.at[k, j],
-                line.sibling,
-            ).start()
-        return carry
-
-    lax.fori_loop(0, pieces, piece, 0)
-
-
-def line_scatter_end(line, pieces, step, parts, sib, rights, lefts, sums, sib_send, right_send, left_send):
-    def piece(j, carry):
-        rows = pl.ds(pl.multiple_of(j * step, step), step)
-        for k in range(LINE):
+                sums.at[k, rows], rights.at[k, rows], right_send.at[k, j], right_send.at[k, j], line.right
+            ).wait_send()
+
+        @pl.when(line.place > k)
+        def _():
             remote(
-                parts.at[2 * k + 1 - line.core, rows],
-                sib.at[k, rows],
-                sib_send.at[k, j],
-                sib_send.at[k, j],
-                line.sibling,
+                sums.at[k, rows], lefts.at[k, rows], left_send.at[k, j], left_send.at[k, j], line.left
             ).wait_send()
-
-            @pl.when(line.place < k)
-            def _():
-                remote(
-                    sums.at[k, rows], rights.at[k, rows], right_send.at[k, j], right_send.at[k, j], line.right
-                ).wait_send()
-
-            @pl.when(line.place > k)
-            def _():
-                remote(
-                    sums.at[k, rows], lefts.at[k, rows], left_send.at[k, j], left_send.at[k, j], line.left
-                ).wait_send()
-
-        return carry
-
-    lax.fori_loop(0, pieces, piece, 0)
 
 
 def gather_copy(line, k, j, step, core, gathered, way, sends, recvs):
@@ -906,23 +887,18 @@
             gather_copy(line, k, j, step, line.core, gathered, 2, sends, recvs).start()
 
 
-def line_gather_end(line, pieces, step, gathered, sends, recvs):
-    def piece(j, carry):
-        for k in range(LINE):
-            gather_copy(line, k, j, step, 1 - line.core, gathered, 2, sends, recvs).wait_recv()
-            gather_copy(line, k, j, step, line.core, gathered, 2, sends, recvs).wait_send()
-
-            @pl.when((line.place >= k) & line.has_right)
-            def _():
-                gather_copy(line, k, j, step, line.core, gathered, 0, sends, recvs).wait_send()
-
-            @pl.when((line.place <= k) & line.has_left)
-            def _():
-                gather_copy(line, k, j, step, line.core, gathered, 1, sends, recvs).wait_send()
-
-        return carry
-
-    lax.fori_loop(0, pieces, piece, 0)
+def line_gather_end(line, j, step, gathered, sends, recvs):
+    for k in range(LINE):
+        gather_copy(line, k, j, step, 1 - line.core, gathered, 2, sends, recvs).wait_recv()
+        gather_copy(line, k, j, step, line.core, gathered, 2, sends, recvs).wait_send()
+
+        @pl.when((line.place >= k) & line.has_right)
+        def _():
+            gather_copy(line, k, j, step, line.core, gathered, 0, sends, recvs).wait_send()
+
+        @pl.when((line.place <= k) & line.has_left)
+        def _():
+            gather_copy(line, k, j, step, line.core, gathered, 1, sends, recvs).wait_send()
 
 
 def take_from(items, count):
@@ -941,7 +917,9 @@
 
 def moves_specs(moves, side):
     near, far = pl.BlockSpec(memory_space=pltpu.VMEM), pl.BlockSpec(memory_space=pl.ANY)
-    return [near if move.near else far for move in moves for _ in getattr(move, side)]
+    return [
+        near if move.near or side == "outputs" else far for move in moves for _ in getattr(move, side)
+    ]
 
 
 def line_call(collective_id, pieces, middle, inputs, outputs, scatter, gather, moves=(), limit=46):
@@ -979,9 +957,12 @@
         if scatter:
             sib, rights, lefts, sums, sib_send, sib_recv, right_send, left_send, right_recv, left_recv = rest[:10]
             parts = ins[0]
-            line_scatter_start(line, pieces, step, parts, sib, sib_send, sib_recv)
+            for j in range(2):
+                line_scatter_start(line, j, step, parts, sib, sib_send, sib_recv)
         if gather:
             sends, recvs = rest[-2:]
+
+        hops = (LINE - 1) * (int(scatter) + int(gather))
 
         def during(j, act):
             pl.when((j >= 0) & (j < pieces))(lambda: act(j))
@@ -1000,6 +981,7 @@
 
         def slot(t, carry):
             if scatter:
+                during(t + 2, lambda j: line_scatter_start(line, j, step, parts, sib, sib_send, sib_recv))
                 during(
                     t - line.place,
                     lambda j: line_scatter_pass(
@@ -1019,11 +1001,19 @@
                         t - hop - (LINE - 1 if scatter else 0),
                         lambda j, hop=hop: line_gather_pass(line, hop, j, step, outs[0], sends, recvs),
                     )
+                during(t - hops - 1, lambda j: line_gather_end(line, j, step, outs[0], sends, recvs))
+            if scatter:
+                during(
+                    t - LINE,
+                    lambda j: line_scatter_end(
+                        line, j, step, parts, sib, rights, lefts, sums, sib_send, right_send, left_send
+                    ),
+                )
             return carry
 
         if gather and not scatter:
             lax.fori_loop(0, pieces, lambda j, carry: (finish(j), carry)[1], 0)
-        slots = pieces + (LINE - 1) * (int(scatter) + int(gather)) if inputs else 0
+        slots = pieces + hops + 1 if inputs else 0
         apart = max([move.slots for move in moves] + [0])
         if apart <= 1:
             for move in moves:
@@ -1038,12 +1028,6 @@
                     slot(t, 0)
         for move in moves:
             move.finish()
-        if scatter:
-            line_scatter_end(
-                line, pieces, step, parts, sib, rights, lefts, sums, sib_send, right_send, left_send
-            )
-        if gather:
-            line_gather_end(line, pieces, step, outs[0], sends, recvs)
 
     vmem = pl.BlockSpec(memory_space=pltpu.VMEM)
     return pl.pallas_call(
@@ -1064,7 +1048,7 @@
         return ins[0][rows, :]
 
     shape = (2 * LINE,) + payload.shape
-    return line_call(collective_id, 8, middle, [payload], [(shape, jnp.bfloat16)], False, True, moves)
+    return line_call(collective_id, 8, middle, [payload], [(shape, jnp.bfloat16)], False, True, moves, 58)
 
 
 def attention_block(parts, hidden, gain, moves, collective_id):
@@ -1240,9 +1224,11 @@
         parts, lows, probs, mixed, squares, raw = outs
         mine, came, sends, recvs = scratch
 
-        def squares_of(b, carry):
-            raw[b] = dot(tokens[b], full_qkv[...], 1, 0)
-            for index in range(2):
+        def squares_of(two, carry):
+            both = pl.ds(2 * two, 2)
+            product = dot(tokens[both].reshape(2 * length, model_width), full_qkv[...], 1, 0)
+            raw[both] = product.reshape(2, length, 3 * width)
+            for b, index in ((2 * two, 0), (2 * two, 1), (2 * two + 1, 0), (2 * two + 1, 1)):
                 total = jnp.zeros((length, 1), jnp.float32)
                 for h in range(heads):
                     values = raw[b, :length, spot(h, index)]
@@ -1252,7 +1238,7 @@
 
         tick()
         for part in range(LINE):
-            lax.fori_loop(2 * part, 2 * part + 2, squares_of, 0)
+            squares_of(part, 0)
             tick()
         squares[...] = line_exchange(line, mine, came, sends, recvs)
         tick()
@@ -1279,11 +1265,13 @@
                 prob = powers / jnp.sum(powers, axis=1, keepdims=True)
                 probs[b, h] = prob
                 mixed[b, :, here] = dot(prob.astype(low), value, 1, 0).astype(low)
-            parts[b] = dot(mixed[b], weight[...], 1, 0).astype(low)
             return carry
 
         for part in range(LINE):
             lax.fori_loop(2 * part, 2 * part + 2, block, 0)
+            both = pl.ds(2 * part, 2)
+            product = dot(mixed[both].reshape(2 * length, width), weight[...], 1, 0)
+            parts[both] = product.astype(low).reshape(2, length, model_width)
             tick()
 
     return heads_call(
@@ -1315,7 +1303,7 @@
         d_attn, weight, raw, turns, gains, lows, probs, squares = ins[:8]
         d_low, terms, wide, parts = outs
         full_qkv = ins[10]
-        mine, came, sends, recvs, upstream, unit = scratch
+        mine, came, sends, recvs, upstream, unit, d_mixed = scratch
         tick()
         terms[...] = jnp.zeros_like(terms)
         for which in range(2):
@@ -1330,14 +1318,13 @@
                 for index in range(2)
             ]
             cos, sin = turn_tables(turns[b])
-            d_mixed = dot(d_attn[b], weight[...], 1, 1).astype(low)
             means = [jnp.zeros((length, 1), jnp.float32)] * 2
             for h in range(heads):
                 here = slice(h * HEAD_DIM, (h + 1) * HEAD_DIM)
                 places = [spot(h, index) for index in range(3)]
                 query, key, value = [lows[b, :, there] for there in places]
                 prob = probs[b, h]
-                d_out = d_mixed[:, here]
+                d_out = d_mixed[b, :, here]
                 d_low[b, :length, places[2]] = dot(prob.astype(low), d_out, 0, 0).astype(low)
                 d_prob = dot(d_out, value, 1, 1)
                 d_scores = (
@@ -1359,6 +1346,13 @@
                 mine[pl.ds(index * blocks + b, 1), :] = as_row(means[index])
             return carry
 
+        def mix(two, carry):
+            both = pl.ds(2 * two, 2)
+            product = dot(d_attn[both].reshape(2 * length, model_width), weight[...], 1, 1)
+            d_mixed[both] = product.astype(low).reshape(2, length, width)
+            return carry
+
+        lax.fori_loop(0, LINE, mix, 0)
         lax.fori_loop(0, blocks, block, 0)
         mine[...] = line_exchange(line, mine, came, sends, recvs)
         wide[...] = mine[2 * blocks :, :]
@@ -1374,10 +1368,16 @@
                     d_low[b, :length, spot(h, index)] = (
                         scale * (upstream[b, :, side] - unit[b, :, side] * mean)
                     ).astype(low)
-            parts[b] = dot(d_low[b], full_qkv[...], 1, 1).astype(low)
             return carry
 
-        lax.fori_loop(0, blocks, last, 0)
+        def lasts(two, carry):
+            lax.fori_loop(2 * two, 2 * two + 2, last, 0)
+            both = pl.ds(2 * two, 2)
+            product = dot(d_low[both].reshape(2 * length, 3 * width), full_qkv[...], 1, 1)
+            parts[both] = product.astype(low).reshape(2, length, model_width)
+            return carry
+
+        lax.fori_loop(0, LINE, lasts, 0)
 
     return heads_call(
         collective_id,
@@ -1389,7 +1389,8 @@
             ((2 * model_width // length, length), jnp.float32),
             ((blocks, length, model_width), low),
         ],
-        [pltpu.VMEM((blocks, length, 2 * width), jnp.float32) for _ in range(2)],
+        [pltpu.VMEM((blocks, length, 2 * width), jnp.float32) for _ in range(2)]
+        + [pltpu.VMEM((blocks, length, width), low)],
         2 * blocks + 2 * model_width // length,
         moves,
     )
@@ -1418,21 +1419,19 @@
     pair = (lax.axis_index("shard") // 2) % 2
     f32 = jnp.float32
 
-    extra = jnp.concatenate(
-        [query_gain, key_gain, attn_gain, ffn_gain, segments[0].astype(jnp.bfloat16)]
-    )
+    extra = jnp.stack([query_gain, key_gain, attn_gain, ffn_gain, segments[0].astype(jnp.bfloat16)])
     payload, extras, full_qkv, full_output = gather_blocks(
         hidden_in,
         [
-            Share(jnp.pad(extra[None], ((0, 15), (0, 0)))),
+            Share(jnp.pad(extra, ((0, 11), (0, 0)))),
             Spread(w_query, w_key, w_value),
             Stack(w_output, 2),
         ],
         0,
     )
     tokens = payload.reshape(-1, model_width)
-    docs = extras[:, 0, 4 * length :].astype(jnp.int32)
-    gains = extras[:, 0, : 4 * length].reshape(LINE, 2, 4, length)
+    docs = extras[:, 4].astype(jnp.int32)
+    gains = extras[:, :4].reshape(LINE, 2, 4, length)
     gains = jnp.stack(by_pair(pair, gains, pair_swap(gains)), axis=1)
     gains = jnp.moveaxis(gains, 3, 0).reshape(4, 1, model_width).astype(f32)
     gain_attn, gain_ffn = gains[2], gains[3]
@@ -1458,7 +1457,7 @@
         return values.astype(jnp.bfloat16).reshape(blocks, -1, model_width)
 
     attn_parts, lows, probs, mixed_low, squares, raw, full_gate = attend(
-        payload, full_qkv, turns, bias, head_gains, full_output, [Spread(w_gate, burst=True)], 6
+        payload, full_qkv, turns, bias, head_gains, full_output, [Spread(w_gate, plan=Spread.BESIDE_HEADS)], 6
     )
     mixed_low = mixed_low.reshape(blocks * length, width)
     resid_low, attn_out, resid, full_up, full_down = attention_block(

time: 675 us -> 659 us (0.976)
  local copies, waits for them, and re-layouts: 32 us -> 19.2 us
    unnamed x88 -> x68, local copies, waits for them, and re-layouts: 24.4 us -> 9.81 us
  transfers between devices with their start and end apart: 5 -> 5, of which waited for: 0 -> 1; matrix products, arithmetic and copies ran while one was open for 3% -> 3% of each run, Pallas kernels for 39% -> 39%
where the time goes in v6:
time: 659 us; the launch traced here: 654 us
  Pallas kernels  569 us (86%)
  matrix products  46.9 us (7%)
  local copies, waits for them, and re-layouts  19.2 us (3%)
  other arithmetic  9.93 us (2%)
  starting transfers between devices  7.22 us (1%)
    pallas_call x6, Pallas kernels, line_call(): pl.pallas_call(kernel, out_shape=[jax.ShapeDtypeStruct(shape, kind) for s...  481 us
    pallas_call x2, Pallas kernels, heads_call(): pl.pallas_call(kernel, out_shape=[jax.ShapeDtypeStruct(shape, kind) for s...  88.2 us
    dot_general x3, matrix products, dot_back(): lax.dot_general(left_side, right_side, (((1,), (1,)), ((), ())), preferre...  26.4 us
  transfers between devices with their start and end apart: 5, of which 1 were waited for; matrix products, arithmetic and copies ran while one was open for 3% of the time, Pallas kernels for 39%

profile of v6, /device:TPU:0, one launch (start us, length us, event | category | flops | bytes accessed | tf_op | source)
XLA Modules:
  0.0 654.4 jit_solution(15028795468720994109)
XLA Ops:
  0.7 0.8 maximum_bitcast_fusion
  1.5 3.0 collective-permute-start
  6.5 65.2 %shard_map.237 = (bf16[8,128,2048]{2,1,0:T(8,128)(2,1)}, bf16[8,16,128]{2,1,0:T(8,128)(2,1)}, bf16[2048,768]{1,0:T(8,128)(2,1)}, bf16[256,2048]{1,0:T(8,128)(2,1)}) custom-call(bf16[128,2048]{1,0:T(8,128)(2,1)} %refs_1_.2, bf16[16,128]{1,0:T(8,128)(2,1)} %pad.4.refs_1_, bf16[128,2048]{1,0:T(8,128)(2,1)} %refs_2_.2, bf16[128,2048]{1,0:T(8,128)(2,1)} %refs_3_.2, ...), custom_call_target="tpu_custom_call" | custom-call | flops 10000000 | bytes 200000000 | tf_op jit(solution)/shard_map/pallas_call | solution.py:1033
  72.4 1.6 collective-permute-start.1
  75.6 1.9 maximum_cosine_fusion.refs_2_.refs_3_
  77.6 1.2 copy-done.2
  78.8 54.5 %shard_map.238 = (bf16[8,128,2048]{2,1,0:T(8,128)(2,1)}, bf16[8,128,768]{2,1,0:T(8,128)(2,1)S(1)}, f32[8,2,128,128]{3,2,1,0:T(8,128)S(1)}, bf16[8,128,256]{2,1,0...) custom-call(bf16[8,128,2048]{2,1,0:T(8,128)(2,1)} %get-tuple-element.50.refs_0_, ...), custom_call_target="tpu_custom_call" | custom-call | flops 10000000 | bytes 80000000 | tf_op jit(solution)/shard_map/pallas_call | solution.py:1202
  133.5 95.1 %shard_map.239 = (bf16[8,128,2048]{2,1,0:T(8,128)(2,1)}, f32[128,2048]{1,0:T(8,128)S(1)}, f32[128,2048]{1,0:T(8,128)S(1)}, bf16[2048,1024]{1,0:T(8,128)(2,1)}, bf16[1024,2048]{1,0:T(8,128)(2,1)}) custom-call(bf16[8,128,2048]{2,1,0:T(8,128)(2,1)} %get-tuple-element.54.refs_0_, bf16[128,2048]{1,0:T(8,128)(2,1)S(1)} %copy-done.7, f32[1,2048]{1,0:T(1,128)S(1)} %bitcast.72, ...), custom_call_target="tpu_custom_call" | custom-call | flops 10000000 | bytes 200000000 | tf_op jit(solution)/shard_map/pallas_call | solution.py:1033
  228.6 7.9 %fusion.7 = f32[1024,1024]{1,0:T(8,128)S(1)} fusion(bf16[1024,2048]{1,0:T(8,128)(2,1)} %bitcast.78, bf16[2048,1024]{1,0:T(8,128)(2,1)} %get-tuple-element.56), kind=kOutput, calls=%fused_computation.39 | convolution fusion | flops 4294967296 | bytes 12582912 | tf_op jit(solution)/shard_map/dot_general | solution.py:1472
  236.6 6.5 multiply_convert_fusion.2
  243.1 6.1 convolution_convert_fusion
  249.2 77.5 %shard_map.240 = (bf16[8,128,2048]{2,1,0:T(8,128)(2,1)S(1)}, bf16[128,2048]{1,0:T(8,128)(2,1)S(1)}, f32[8,2048]{1,0:T(8,128)S(1)}) custom-call(bf16[8,128,2048]{2,1,0:T(8,128)(2,1)} %bitcast.77, f32[128,2048]{1,0:T(8,128)S(1)} %get-tuple-element.59.refs_1_, bf16[128,2048]{1,0:T(8,128)(2,1)S(1)} %copy-done.9, f32[1,2048]{1,0:T(1,128)S(1)} %bitcast.74), custom_call_target="tpu_custom_call" | custom-call | flops 10000000 | bytes 200000000 | tf_op jit(solution)/shard_map/pallas_call | solution.py:1033
  326.8 11.0 %multiply_convert_fusion = (bf16[1024,1024]{1,0:T(8,128)(2,1)S(1)}, bf16[1024,1024]{1,0:T(8,128)(2,1)S(1)}) fusion(f32[1024,1024]{1,0:T(8,128)} %copy-done.32, f32[1024,1024]{1,0:T(8,128)} %get-tuple-element.110, bf16[1024,2048]{1,0:T(8,128)(2,1)S(1)} %bitcast.65, bf16[1024,2048]{1,0:T(8,128)(2,1)} %get-tuple-element.58), kind=kOutput, calls=%fused_computation.2 | convolution fusion | flops 4308598784 | bytes 20971520 | tf_op jit(solution)/shard_map/dot_general | solution.py:37
  337.8 7.0 %fusion.8 = f32[1024,2048]{1,0:T(8,128)} fusion(bf16[1024,1024]{1,0:T(8,128)(2,1)S(1)} %get-tuple-element.88.refs_5_, bf16[2048,1024]{1,0:T(8,128)(2,1)S(1)} %copy-done.28), kind=kOutput, calls=%fused_computation.40 | convolution fusion | flops 4294967296 | bytes 14680064 | tf_op jit(solution)/shard_map/dot_general | solution.py:37
  344.8 8.4 %add_convert_fusion = bf16[1024,2048]{1,0:T(8,128)(2,1)} fusion(f32[1024,2048]{1,0:T(8,128)} %fusion.8, bf16[1024,1024]{1,0:T(8,128)(2,1)S(1)} %get-tuple-element.87.refs_6_, bf16[2048,1024]{1,0:T(8,128)(2,1)S(1)} %copy-done.30), kind=kOutput, calls=%fused_computation | convolution fusion | flops 4299161600 | bytes 18874368 | tf_op jit(solution)/shard_map/dot_general | solution.py:37
  353.2 110.5 %shard_map.241 = (bf16[8,128,2048]{2,1,0:T(8,128)(2,1)}, f32[128,2048]{1,0:T(8,128)}, f32[8,2048]{1,0:T(8,128)}, bf16[4,256,512]{2,1,0:T(8,128)(2,1)}, bf16[4,25...) custom-call(bf16[8,128,2048]{2,1,0:T(8,128)(2,1)} %bitcast.81, bf16[128,2048]{1,0:T(8,128)(2,1)} %refs_1_.3, ...), custom_call_target="tpu_custom_call" | custom-call | flops 10000000 | bytes 200000000 | tf_op jit(solution)/shard_map/pallas_call | solution.py:1033
  463.8 1.6 copy-done
  465.4 0.8 copy-done.21
  466.2 33.7 %shard_map.242 = (bf16[8,128,768]{2,1,0:T(8,128)(2,1)S(1)}, f32[8,512]{1,0:T(8,128)S(1)}, f32[32,128]{1,0:T(8,128)S(1)}, bf16[8,128,2048]{2,1,0:T(8,128)(2,1)}, bf16[256,2048]{1,0:T(8,128)(2,1)S(1)}) custom-call(bf16[8,128,2048]{2,1,0:T(8,128)(2,1)} %get-tuple-element.63.refs_0_, bf16[256,2048]{1,0:T(8,128)(2,1)S(1)} %copy-done.3, ...), custom_call_target="tpu_custom_call" | custom-call | flops 10000000 | bytes 80000000 | tf_op jit(solution)/shard_map/pallas_call | solution.py:1202
  499.9 1.0 copy-done.14
  501.5 1.5 collective-permute-start.3
  503.0 1.2 copy-done.11
  504.2 1.2 copy-done.12
  505.4 1.0 copy-done.17
  506.5 98.9 %shard_map.243 = (bf16[128,2048]{1,0:T(8,128)(2,1)S(1)}, bf16[4,256,384]{2,1,0:T(8,128)(2,1)S(1)}, bf16[128,2048]{1,0:T(8,128)(2,1)S(1)}, bf16[128,16384]{1,0:T(8,128)(2,1)}, bf16[256,2048]{1,0:T(8,128)(2,1)S(1)}) custom-call(bf16[8,128,2048]{2,1,0:T(8,128)(2,1)} %get-tuple-element.71.refs_0_, f32[128,2048]{1,0:T(8,128)S(1)} %copy-done.10, ...), custom_call_target="tpu_custom_call" | custom-call | flops 10000000 | bytes 200000000 | tf_op jit(solution)/shard_map/pallas_call | solution.py:1033
  605.4 6.8 %fusion.3 = (f32[128,8192]{1,0:T(8,128)}, f32[128,8192]{1,0:T(8,128)}) fusion(bf16[128,16384]{1,0:T(8,128)(2,1)} %get-tuple-element.84), kind=kLoop, calls=%fused_computation.35 | loop fusion | bytes 16777216 | tf_op jit(solution)/shard_map/split | solution.py:1531
  612.2 2.8 convert_add_fusion
  615.0 33.3 %shard_map.244 = (bf16[128,6144]{1,0:T(8,128)(2,1)S(1)}, bf16[128,2048]{1,0:T(8,128)(2,1)S(1)}) custom-call(bf16[8,128,384]{2,1,0:T(8,128)(2,1)S(1)} %bitcast.70, bf16[128,2048]{1,0:T(8,128)(2,1)S(1)} %get-tuple-element.79.refs_1_), custom_call_target="tpu_custom_call" | custom-call | flops 10000000 | bytes 200000000 | tf_op jit(solution)/shard_map/pallas_call | solution.py:1033
  649.0 2.1 fusion.4
  651.1 0.9 collective-permute-done.4
  652.6 0.8 copy.44
  653.4 0.8 copy.45
  (90 shorter events, 6.2 us)
Async XLA Ops:
  0.6 76.8 %copy-start.27 = (bf16[128]{0:T(256)(128)(2,1)S(1)}, bf16[128]{0:T(256)(128)(2,1)}, u32[]{:S(2)}) copy-start(bf16[128]{0:T(256)(128)(2,1)} %param.21) | copy-start | bytes 772
  0.7 76.8 %copy-start.26 = (bf16[128]{0:T(256)(128)(2,1)S(1)}, bf16[128]{0:T(256)(128)(2,1)}, u32[]{:S(2)}) copy-start(bf16[128]{0:T(256)(128)(2,1)} %param.20) | copy-start | bytes 772
  0.7 76.9 %copy-start.8 = (bf16[128,8192]{1,0:T(8,128)(2,1)S(1)}, bf16[128,8192]{1,0:T(8,128)(2,1)}, u32[]{:S(2)}) copy-start(bf16[128,8192]{1,0:T(8,128)(2,1)} %refs_6_.1) | copy-start | bytes 6291460
  1.5 76.0 %collective-permute-start = (bf16[1,2,128]{2,1,0:T(2,128)(2,1)S(1)}, bf16[1,2,128]{2,1,0:T(2,128)(2,1)S(1)}, u32[]{:S(2)}, u32[]{:S(2)}) collective-permute-start(bf16[1,2,128]{2,1,0:T(2,128)(2,1)S(1)} %maximum_bitcast_fusion), channel_id=1, source_target_pairs={{0,2},{1,3},{2,0},{3,1},{4,6},{5,7},{6,4},{7,5},{8,10},{9,11},{10,... | collective-permute-start | bytes 1544 | tf_op jit(solution)/shard_map/ppermute | solution.py:284
  72.4 60.9 %collective-permute-start.1 = (bf16[4,2,4,128]{3,1,0,2:T(2,128)(2,1)S(1)}, bf16[4,2,4,128]{3,1,0,2:T(2,128)(2,1)S(1)}, u32[]{:S(2)}, u32[]{:S(2)}) collective-permute-start(bf16[4,2,4,128]{3,1,0,2:T(2,128)(2,1)S(1)} %copy.32), channel_id=1, source_target_pairs={{0,2},{1,3},{2,0},{3,1},{4,6},{5,7},{6,4},{7,5},{8,10},{9,11},{10,... | collective-permute-start | bytes 24584 | tf_op jit(solution)/shard_map/ppermute | solution.py:284
  78.8 54.7 %copy-start.5 = (bf16[128,8192]{1,0:T(8,128)(2,1)S(1)}, bf16[128,8192]{1,0:T(8,128)(2,1)}, u32[]{:S(2)}) copy-start(bf16[128,8192]{1,0:T(8,128)(2,1)} %refs_3_.3) | copy-start | bytes 6291460
  78.8 54.7 %copy-start.6 = (bf16[512,2048]{1,0:T(8,128)(2,1)S(1)}, bf16[512,2048]{1,0:T(8,128)(2,1)}, u32[]{:S(2)}) copy-start(bf16[512,2048]{1,0:T(8,128)(2,1)} %refs_4_.3) | copy-start | bytes 6291460
  78.8 54.7 %copy-start.7 = (bf16[128,2048]{1,0:T(8,128)(2,1)S(1)}, bf16[128,2048]{1,0:T(8,128)(2,1)}, u32[]{:S(2)}) copy-start(bf16[128,2048]{1,0:T(8,128)(2,1)} %refs_1_.2) | copy-start | bytes 1572868
  133.3 95.2 %copy-start.16 = (bf16[8,128,256]{2,1,0:T(8,128)(2,1)}, bf16[8,128,256]{2,1,0:T(8,128)(2,1)S(1)}, u32[]{:S(2)}) copy-start(bf16[8,128,256]{2,1,0:T(8,128)(2,1)S(1)} %get-tuple-element.74) | copy-start | bytes 1572868
  133.4 95.1 %copy-start.20 = (f32[1,4,2,2,128]{4,3,2,1,0:T(2,128)}, f32[1,4,2,2,128]{4,3,2,1,0:T(2,128)S(1)}, u32[]{:S(2)}) copy-start(f32[1,4,2,2,128]{4,3,2,1,0:T(2,128)S(1)} %get-tuple-element.95) | copy-start | bytes 24580
  228.6 8.0 %copy-start.13 = (f32[128,2048]{1,0:T(8,128)}, f32[128,2048]{1,0:T(8,128)S(1)}, u32[]{:S(2)}) copy-start(f32[128,2048]{1,0:T(8,128)S(1)} %get-tuple-element.62.refs_2_) | copy-start | bytes 3145732
  228.6 8.0 %copy-start.22 = (bf16[8,128,2048]{2,1,0:T(8,128)(2,1)S(1)}, bf16[8,128,2048]{2,1,0:T(8,128)(2,1)}, u32[]{:S(2)}) copy-start(bf16[8,128,2048]{2,1,0:T(8,128)(2,1)} %get-tuple-element.55) | copy-start | bytes 12582916
  228.6 8.0 %copy-start.29 = (bf16[2048,1024]{1,0:T(8,128)(2,1)S(1)}, bf16[2048,1024]{1,0:T(8,128)(2,1)}, u32[]{:S(2)}) copy-start(bf16[2048,1024]{1,0:T(8,128)(2,1)} %get-tuple-element.57) | copy-start | bytes 12582916
  236.5 6.6 %copy-start.32 = (f32[1024,1024]{1,0:T(8,128)}, f32[1024,1024]{1,0:T(8,128)S(1)}, u32[]{:S(2)}) copy-start(f32[1024,1024]{1,0:T(8,128)S(1)} %fusion.7) | copy-start | bytes 12582916
  236.6 6.5 copy-start.31
  243.1 6.1 copy-start.23
  243.1 6.1 copy-start.9
  326.7 11.1 %copy-start.4 = (bf16[8,128,2048]{2,1,0:T(8,128)(2,1)}, bf16[8,128,2048]{2,1,0:T(8,128)(2,1)S(1)}, u32[]{:S(2)}) copy-start(bf16[8,128,2048]{2,1,0:T(8,128)(2,1)S(1)} %get-tuple-element.61) | copy-start | bytes 12582916
  326.7 11.1 %copy-start.18 = (bf16[128,2048]{1,0:T(8,128)(2,1)}, bf16[128,2048]{1,0:T(8,128)(2,1)S(1)}, u32[]{:S(2)}) copy-start(bf16[128,2048]{1,0:T(8,128)(2,1)S(1)} %get-tuple-element.125) | copy-start | bytes 1572868
  326.7 11.1 %copy-start.28 = (bf16[2048,1024]{1,0:T(8,128)(2,1)S(1)}, bf16[2048,1024]{1,0:T(8,128)(2,1)}, u32[]{:S(2)}) copy-start(bf16[2048,1024]{1,0:T(8,128)(2,1)} %get-tuple-element.56) | copy-start | bytes 12582916
  337.8 7.0 %copy-start.25 = (bf16[1024,1024]{1,0:T(8,128)(2,1)}, bf16[1024,1024]{1,0:T(8,128)(2,1)S(1)}, u32[]{:S(2)}) copy-start(bf16[1024,1024]{1,0:T(8,128)(2,1)S(1)} %get-tuple-element.88.refs_5_) | copy-start | bytes 6291460
  337.8 7.0 %copy-start.24 = (bf16[1024,1024]{1,0:T(8,128)(2,1)}, bf16[1024,1024]{1,0:T(8,128)(2,1)S(1)}, u32[]{:S(2)}) copy-start(bf16[1024,1024]{1,0:T(8,128)(2,1)S(1)} %get-tuple-element.87.refs_6_) | copy-start | bytes 6291460
  337.8 7.0 %copy-start.30 = (bf16[2048,1024]{1,0:T(8,128)(2,1)S(1)}, bf16[2048,1024]{1,0:T(8,128)(2,1)}, u32[]{:S(2)}) copy-start(bf16[2048,1024]{1,0:T(8,128)(2,1)} %get-tuple-element.57) | copy-start | bytes 12582916
  353.2 110.5 %copy-start.3 = (bf16[256,2048]{1,0:T(8,128)(2,1)S(1)}, bf16[256,2048]{1,0:T(8,128)(2,1)}, u32[]{:S(2)}) copy-start(bf16[256,2048]{1,0:T(8,128)(2,1)} %get-tuple-element.53.refs_5_.refs_1_) | copy-start | bytes 3145732
  463.8 1.6 copy-start
  466.2 36.8 %copy-start.10 = (f32[128,2048]{1,0:T(8,128)S(1)}, f32[128,2048]{1,0:T(8,128)}, u32[]{:S(2)}) copy-start(f32[128,2048]{1,0:T(8,128)} %get-tuple-element.72.refs_1_) | copy-start | bytes 3145732
  500.9 147.4 %collective-permute-start.2 = (f32[2,128]{1,0:T(2,128)S(1)}, f32[2,128]{1,0:T(2,128)S(1)}, u32[]{:S(2)}, u32[]{:S(2)}) collective-permute-start(f32[2,128]{1,0:T(2,128)S(1)} %bitcast.98), channel_id=1, source_target_pairs={{0,2},{1,3},{2,0},{3,1},{4,6},{5,7},{6,4},{7,5},{8,10},{9,11},{10,... | collective-permute-start | bytes 3080 | tf_op jit(solution)/shard_map/ppermute | solution.py:284
  501.5 146.9 %collective-permute-start.3 = (f32[32,128]{1,0:T(8,128)S(1)}, f32[32,128]{1,0:T(8,128)S(1)}, u32[]{:S(2)}, u32[]{:S(2)}) collective-permute-start(f32[32,128]{1,0:T(8,128)S(1)} %get-tuple-element.83), channel_id=1, source_target_pairs={{0,2},{1,3},{2,0},{3,1},{4,6},{5,7},{6,4},{7,5},{8,10},{9,11},{10,... | collective-permute-start | bytes 49160 | tf_op jit(solution)/shard_map/ppermute | solution.py:284
  605.4 6.8 %copy-start.1 = (bf16[512,2048]{1,0:T(8,128)(2,1)S(1)}, bf16[512,2048]{1,0:T(8,128)(2,1)}, u32[]{:S(2)}) copy-start(bf16[512,2048]{1,0:T(8,128)(2,1)} %get-tuple-element.70.refs_11_.refs_8_) | copy-start | bytes 6291460
  605.4 6.8 %copy-start.15 = (bf16[256,2048]{1,0:T(8,128)(2,1)S(1)}, bf16[256,2048]{1,0:T(8,128)(2,1)}, u32[]{:S(2)}) copy-start(bf16[256,2048]{1,0:T(8,128)(2,1)} %copy-done.14) | copy-start | bytes 3145732
  648.4 3.7 collective-permute-start.4
  649.0 3.6 copy-start.19
  (6 other events, 6.5 us)

commit v7 on v6

--- a/solution.py
+++ b/solution.py
@@ -284,10 +284,6 @@
     return lax.ppermute(values, "shard", shard_perm(lambda index: index ^ 2))
 
 
-def rep_swap(values):
-    return lax.ppermute(values, "rep", [(0, 1), (1, 0)])
-
-
 def by_pair(pair, own, other):
     return jnp.where(pair == 0, own, other), jnp.where(pair == 0, other, own)
 
@@ -312,6 +308,7 @@
         self.left = self.at(jnp.maximum(self.place - 1, 0), self.pair, self.core)
         self.across = self.at(self.place, 1 - self.pair, self.core)
         self.partner = (1 - self.rep, index)
+        self.diagonal = (1 - self.rep, self.across[1])
         self.has_right = self.place < LINE - 1
         self.has_left = self.place > 0
 
@@ -333,7 +330,8 @@
                 greet(self.at(place, self.pair, core))
             greet(self.across)
             greet(self.partner)
-            pl.semaphore_wait(barrier, 2 * LINE + 1)
+            greet(self.diagonal)
+            pl.semaphore_wait(barrier, 2 * LINE + 2)
             return
         greet(self.sibling)
         pl.when(self.has_right)(lambda: greet(self.right))
@@ -506,23 +504,53 @@
     semaphores = ((2,),)
     buffers = ()
     near = True
+
+    def __init__(self, values, start, count, at=0):
+        self.made = values if isinstance(values, PairSum) else None
+        shape = values.outputs[0] if self.made else values
+        self.inputs = [] if self.made else [values]
+        self.start, self.count, self.at, self.slots = start, count, at, at + 1
+        self.outputs = [jax.ShapeDtypeStruct((count, shape.shape[1]), shape.dtype)]
+
+    def bind(self, line, sources, targets, scratch):
+        source = self.made.target if self.made else sources[0]
+        sends, recvs = scratch[0].at[0], scratch[0].at[1]
+        rows = source.at[pl.ds(self.start, self.count), :]
+        self.copy = remote(rows, targets[0], sends, recvs, line.partner)
+
+    def slot(self, t):
+        if t == self.at:
+            self.copy.start()
+
+    def finish(self):
+        self.copy.wait()
+
+
+class Four:
+    semaphores = ((3,),) * 2
+    buffers = ()
+    near = True
     slots = 1
 
-    def __init__(self, values, start, count):
-        self.inputs, self.start, self.count = [values], start, count
-        self.outputs = [jax.ShapeDtypeStruct((count, values.shape[1]), values.dtype)]
+    def __init__(self, values):
+        self.inputs = [values]
+        self.outputs = [jax.ShapeDtypeStruct(values.shape, values.dtype)] * 3
 
     def bind(self, line, sources, targets, scratch):
-        sends, recvs = scratch[0].at[0], scratch[0].at[1]
-        rows = sources[0].at[pl.ds(self.start, self.count), :]
-        self.copy = remote(rows, targets[0], sends, recvs, line.partner)
+        devices = (line.across, line.partner, line.diagonal)
+        self.copies = [
+            remote(sources[0], target, scratch[0].at[index], scratch[1].at[index], device)
+            for index, (target, device) in enumerate(zip(targets, devices))
+        ]
 
     def slot(self, t):
         if t == 0:
-            self.copy.start()
+            for copy in self.copies:
+                copy.start()
 
     def finish(self):
-        self.copy.wait()
+        for copy in self.copies:
+            copy.wait()
 
 
 class Share:
@@ -562,17 +590,20 @@
     semaphores = ((2 * LINE,),) * 4
     buffers = ()
     near = True
-    slots = 3 + 2 * LINE
-
-    def __init__(self, sources, per):
-        rows, width = sources[0].shape[1:]
-        self.inputs, self.per = list(sources), per
-        self.n = width // per
-        self.width = width * len(sources)
-        self.outputs = [jax.ShapeDtypeStruct((rows, 16 * self.width), sources[0].dtype)]
+
+    def __init__(self, sources, per, at=0):
+        self.made = sources if isinstance(sources, Reduce) else None
+        shapes = sources.outputs if self.made else sources
+        self.inputs = [] if self.made else list(sources)
+        self.rows, width = shapes[0].shape[1] // 2, shapes[0].shape[2]
+        self.per, self.at, self.n = per, at, width // per
+        self.width = width * len(shapes)
+        self.slots = at + 2 + 2 * LINE
+        self.outputs = [jax.ShapeDtypeStruct((self.rows, 16 * self.width), shapes[0].dtype)]
 
     def bind(self, line, sources, targets, scratch):
-        self.line, self.sources, self.target = line, sources, targets[0]
+        self.line, self.target = line, targets[0]
+        self.sources = [part[1] for part in self.made.parts] if self.made else sources
         self.z_send, self.z_recv, self.x_send, self.x_recv = scratch
 
     def runs(self, place, core):
@@ -588,7 +619,8 @@
         line = self.line
         place, core = line.piece(p, 1)
         for source, at, there in self.runs(line.place, line.core):
-            piece = source.at[2 * place + core, :, pl.ds(at, self.n)]
+            rows = pl.ds(pl.multiple_of(core * self.rows, self.rows), self.rows)
+            piece = source.at[place, rows, pl.ds(at, self.n)]
             goal = self.target.at[:, there]
             if p == 0:
                 pltpu.make_async_copy(piece, goal, self.z_recv.at[0]).start()
@@ -609,12 +641,13 @@
             remote(goal, goal, self.x_send.at[p], self.x_recv.at[p], line.partner).start()
 
     def slot(self, t):
-        if t < 2 * LINE:
-            self.start(t)
-        if t == 0:
-            self.came(0)
-        if 3 <= t < 2 + 2 * LINE:
-            self.came(t - 2)
+        t -= self.at
+        for p in range(2 * LINE):
+            if t == (0 if self.made else p):
+                self.start(p)
+        for p in range(2 * LINE):
+            if t == (p if self.made or p == 0 else p + 2):
+                self.came(p)
 
     def finish(self):
         ref = self.whole()
@@ -659,8 +692,8 @@
         wide = n if first == "partner" else 2 * n
         self.semaphores = ((self.chunks,),) * (2 * len(rights)) + ((LINE,),) * (2 * len(rights))
         self.buffers = ((self.chunks, rows, wide),) * (2 * len(rights))
-        self.join_at = [3, 5, 8, 10] if first == "partner" else [3, 5, 7, 9]
-        self.last_at = [12, 15, 16, 17] if first == "partner" else [10, 10, 10, 11]
+        self.join_at = [3, 5, 8, 10] if first == "partner" else [3, 4, 5, 7]
+        self.last_at = [12, 15, 16, 17] if first == "partner" else [6, 7, 8, 9]
         self.slots = max(self.last_at) + 1
 
     def bind(self, line, sources, targets, scratch):
@@ -1116,7 +1149,7 @@
         outs[0][rows, :] = (ins[1][rows, :] + total).astype(jnp.bfloat16)
 
     return line_call(
-        collective_id, 8, middle, [parts, d_resid], [(d_resid.shape, jnp.bfloat16)], True, False, moves
+        collective_id, 8, middle, [parts, d_resid], [(d_resid.shape, jnp.bfloat16)], True, False, moves, 48
     )
 
 
@@ -1301,9 +1334,9 @@
 
     def body(line, ins, outs, scratch, tick):
         d_attn, weight, raw, turns, gains, lows, probs, squares = ins[:8]
-        d_low, terms, wide, parts = outs
+        d_low, wide, parts = outs
         full_qkv = ins[10]
-        mine, came, sends, recvs, upstream, unit, d_mixed = scratch
+        mine, came, sends, recvs, upstream, unit, d_mixed, terms = scratch
         tick()
         terms[...] = jnp.zeros_like(terms)
         for which in range(2):
@@ -1355,7 +1388,12 @@
         lax.fori_loop(0, LINE, mix, 0)
         lax.fori_loop(0, blocks, block, 0)
         mine[...] = line_exchange(line, mine, came, sends, recvs)
-        wide[...] = mine[2 * blocks :, :]
+        count = 2 * model_width // length
+        wide[:count, :] = mine[2 * blocks :, :]
+        wide[count:, :] = jnp.zeros((8, length), jnp.float32)
+        for index in range(2 * heads):
+            sums = jnp.sum(terms[:, index * length : (index + 1) * length], axis=0, keepdims=True)
+            wide[count + index : count + index + 1, :] = sums
 
         def last(b, carry):
             for index in range(2):
@@ -1385,12 +1423,11 @@
         [d_attn, weight, raw, turns, gains, lows, probs, squares, *wide_terms, full_qkv],
         [
             (raw.shape, low),
-            ((8, 2 * width), jnp.float32),
-            ((2 * model_width // length, length), jnp.float32),
+            ((2 * model_width // length + 8, length), jnp.float32),
             ((blocks, length, model_width), low),
         ],
         [pltpu.VMEM((blocks, length, 2 * width), jnp.float32) for _ in range(2)]
-        + [pltpu.VMEM((blocks, length, width), low)],
+        + [pltpu.VMEM((blocks, length, width), low), pltpu.VMEM((8, 2 * width), jnp.float32)],
         2 * blocks + 2 * model_width // length,
         moves,
     )
@@ -1500,28 +1537,26 @@
         3,
     )
 
-    d_qkv, head_terms, wide_terms, back_parts, there_first = attend_back(
+    d_qkv, gain_sums, back_parts, there_first = attend_back(
         d_attn_low, full_output, raw, turns, head_gains, lows, probs, squares,
         [attn_gain_term, ffn_gain_term], full_qkv, [Swap(down_part, 0, ff_rows // 2)], 7,
     )
     d_attn_low = d_attn_low.reshape(blocks * length, model_width)
-    hidden_grad, qkv_sum, output_part, ffn_total, there_second = last_block(
+    qkv_sum = Reduce(tokens, [d_qkv.reshape(-1, 3 * width)], "across")
+    output_sum = PairSum(mixed_low, d_attn_low, 1, 5)
+    hidden_grad, _, output_part, ffn_total, there_second, qkv_total, there_output, *there_gains = last_block(
         back_parts,
         d_resid,
         [
-            Reduce(tokens, [d_qkv.reshape(-1, 3 * width)], "across"),
-            PairSum(mixed_low, d_attn_low, 1, 5),
-            Deal([gate_sum.reshape(blocks, length, -1), up_sum.reshape(blocks, length, -1)], 1),
-            Swap(down_part, ff_rows // 2, ff_rows // 2),
+            qkv_sum,
+            output_sum,
+            Deal([gate_sum, up_sum], 1),
+            Swap(down_part, ff_rows // 2, ff_rows // 2, 2),
+            Deal(qkv_sum, 3, 9),
+            Swap(output_sum, 0, length, 8),
+            Four(gain_sums),
         ],
         4,
-    )
-    qkv_total, there_output = line_call(
-        5, 1, None, [], [], False, False,
-        [
-            Deal([qkv_sum.reshape(blocks, length, -1)], 3),
-            Swap(output_part, 0, length),
-        ],
     )
 
     def total_of(first, second):
@@ -1531,13 +1566,12 @@
     grad_gate, grad_up = jnp.split(ffn_total.astype(f32), 2, axis=1)
     grad_output = total_of(output_part, there_output)
     grad_down = total_of(down_part, jnp.concatenate([there_first, there_second]))
-    head_terms = jnp.sum(head_terms, axis=0).reshape(2, 2, HEAD_DIM)
-    own_term, other_term = by_pair(pair, head_terms[:, 0], head_terms[:, 1])
-    head_grads = own_term + pair_swap(other_term)
-    wide_terms = (wide_terms + pair_swap(wide_terms)).reshape(2, 16, length)
-    wide_grads = lax.dynamic_index_in_dim(wide_terms, lax.axis_index("shard"), 1, keepdims=False)
+    gain_sums = (gain_sums + there_gains[0]) + (there_gains[1] + there_gains[2])
+    wide_grads = lax.dynamic_index_in_dim(
+        gain_sums[:32].reshape(2, 16, length), lax.axis_index("shard"), 1, keepdims=False
+    )
+    head_grads = lax.dynamic_index_in_dim(gain_sums[32:36].reshape(2, 2, length), pair, 1, keepdims=False)
     gain_grads = jnp.concatenate([head_grads, wide_grads])
-    gain_grads = gain_grads + rep_swap(gain_grads)
     return (
         hidden_out,
         hidden_grad,

time: 659 us -> 652 us (0.989); the launches traced: 654 us -> 640 us
  Pallas kernels: 569 us -> 558 us
    pallas_call x6 -> x5, Pallas kernels: 481 us -> 470 us  [line_call(): pl.pallas_call(kernel, out_shape=[jax.ShapeDtypeStruct(shape, kind) for s...]
  transfers between devices with their start and end apart: 5 -> 2, of which waited for: 1 -> 0; matrix products, arithmetic and copies ran while one was open for 3% -> 1% of each run, Pallas kernels for 39% -> 19%
where the time goes in v7:
time: 652 us; the launch traced here: 640 us
  Pallas kernels  558 us (86%)
  matrix products  50.2 us (8%)
  local copies, waits for them, and re-layouts  15.8 us (2%)
  other arithmetic  9.87 us (2%)
    pallas_call x5, Pallas kernels, line_call(): pl.pallas_call(kernel, out_shape=[jax.ShapeDtypeStruct(shape, kind) for s...  470 us
    pallas_call x2, Pallas kernels, heads_call(): pl.pallas_call(kernel, out_shape=[jax.ShapeDtypeStruct(shape, kind) for s...  88.3 us
    dot_general x3, matrix products, dot_back(): lax.dot_general(left_side, right_side, (((1,), (1,)), ((), ())), preferre...  29.7 us
  transfers between devices with their start and end apart: 2, of which 0 were waited for; matrix products, arithmetic and copies ran while one was open for 1% of the time, Pallas kernels for 19%

profile of v7, /device:TPU:0, one launch (start us, length us, event | category | flops | bytes accessed | tf_op | source)
XLA Modules:
  0.0 640.3 jit_solution(2771165989878215870)
XLA Ops:
  0.7 0.8 maximum_bitcast_fusion
  1.5 3.0 collective-permute-start
  4.5 0.7 convert_element_type.72
  5.1 0.7 stack.34
  5.9 0.6 pad.4.refs_1_
  6.5 65.2 %shard_map.237 = (bf16[8,128,2048]{2,1,0:T(8,128)(2,1)}, bf16[8,16,128]{2,1,0:T(8,128)(2,1)}, bf16[2048,768]{1,0:T(8,128)(2,1)}, bf16[256,2048]{1,0:T(8,128)(2,1)}) custom-call(bf16[128,2048]{1,0:T(8,128)(2,1)} %refs_1_.2, bf16[16,128]{1,0:T(8,128)(2,1)} %pad.4.refs_1_, bf16[128,2048]{1,0:T(8,128)(2,1)} %refs_2_.2, bf16[128,2048]{1,0:T(8,128)(2,1)} %refs_3_.2, ...), custom_call_target="tpu_custom_call" | custom-call | flops 10000000 | bytes 200000000 | tf_op jit(solution)/shard_map/pallas_call | solution.py:1066
  71.7 0.7 slice.37
  72.4 1.6 collective-permute-start.1
  74.1 0.7 slice_convert_fusion
  75.6 1.9 maximum_cosine_fusion.refs_2_.refs_3_
  77.6 1.2 copy-done.2
  78.8 54.6 %shard_map.238 = (bf16[8,128,2048]{2,1,0:T(8,128)(2,1)}, bf16[8,128,768]{2,1,0:T(8,128)(2,1)S(1)}, f32[8,2,128,128]{3,2,1,0:T(8,128)S(1)}, bf16[8,128,256]{2,1,0...) custom-call(bf16[8,128,2048]{2,1,0:T(8,128)(2,1)} %get-tuple-element.51.refs_0_, ...), custom_call_target="tpu_custom_call" | custom-call | flops 10000000 | bytes 80000000 | tf_op jit(solution)/shard_map/pallas_call | solution.py:1235
  133.5 95.0 %shard_map.239 = (bf16[8,128,2048]{2,1,0:T(8,128)(2,1)}, f32[128,2048]{1,0:T(8,128)S(1)}, f32[128,2048]{1,0:T(8,128)S(1)}, bf16[2048,1024]{1,0:T(8,128)(2,1)}, bf16[1024,2048]{1,0:T(8,128)(2,1)}) custom-call(bf16[8,128,2048]{2,1,0:T(8,128)(2,1)} %get-tuple-element.55.refs_0_, bf16[128,2048]{1,0:T(8,128)(2,1)S(1)} %copy-done.7, f32[1,2048]{1,0:T(1,128)S(1)} %bitcast.58, ...), custom_call_target="tpu_custom_call" | custom-call | flops 10000000 | bytes 200000000 | tf_op jit(solution)/shard_map/pallas_call | solution.py:1066
  228.6 7.9 %fusion.9 = f32[1024,1024]{1,0:T(8,128)S(1)} fusion(bf16[1024,2048]{1,0:T(8,128)(2,1)} %bitcast.64, bf16[2048,1024]{1,0:T(8,128)(2,1)} %get-tuple-element.57), kind=kOutput, calls=%fused_computation.38 | convolution fusion | flops 4294967296 | bytes 12582912 | tf_op jit(solution)/shard_map/dot_general | solution.py:1509
  236.6 6.5 %multiply_convert_fusion.2 = (bf16[1024,1024]{1,0:T(8,128)(2,1)S(1)}, f32[1024,1024]{1,0:T(8,128)}) fusion(f32[1024,1024]{1,0:T(8,128)S(1)} %fusion.9, bf16[1024,2048]{1,0:T(8,128)(2,1)S(1)} %bitcast.66, bf16[2048,1024]{1,0:T(8,128)(2,1)S(1)} %copy-done.24), kind=kOutput, calls=%fused_computation.4 | convolution fusion | flops 4301258752 | bytes 18874368 | tf_op jit(solution)/shard_map/dot_general | solution.py:1510
  243.1 6.1 convolution_convert_fusion
  249.2 69.3 %shard_map.240 = (bf16[8,128,2048]{2,1,0:T(8,128)(2,1)S(1)}, bf16[128,2048]{1,0:T(8,128)(2,1)S(1)}, f32[8,2048]{1,0:T(8,128)S(1)}) custom-call(bf16[8,128,2048]{2,1,0:T(8,128)(2,1)} %bitcast.63, f32[128,2048]{1,0:T(8,128)S(1)} %get-tuple-element.60.refs_1_, bf16[128,2048]{1,0:T(8,128)(2,1)S(1)} %copy-done.9, f32[1,2048]{1,0:T(1,128)S(1)} %bitcast.60), custom_call_target="tpu_custom_call" | custom-call | flops 10000000 | bytes 200000000 | tf_op jit(solution)/shard_map/pallas_call | solution.py:1066
  318.6 10.8 %multiply_convert_fusion = (bf16[1024,1024]{1,0:T(8,128)(2,1)S(1)}, bf16[1024,1024]{1,0:T(8,128)(2,1)S(1)}) fusion(f32[1024,1024]{1,0:T(8,128)} %copy-done.27, f32[1024,1024]{1,0:T(8,128)} %get-tuple-element.109, bf16[1024,2048]{1,0:T(8,128)(2,1)S(1)} %bitcast.54, bf16[1024,2048]{1,0:T(8,128)(2,1)} %get-tuple-element.59), kind=kOutput, calls=%fused_computation.2 | convolution fusion | flops 4308598784 | bytes 20971520 | tf_op jit(solution)/shard_map/dot_general | solution.py:37
  329.4 10.5 %fusion.10 = f32[1024,2048]{1,0:T(8,128)} fusion(bf16[1024,1024]{1,0:T(8,128)(2,1)S(1)} %get-tuple-element.90.refs_5_, bf16[2048,1024]{1,0:T(8,128)(2,1)} %get-tuple-element.57), kind=kOutput, calls=%fused_computation.39 | convolution fusion | flops 4294967296 | bytes 14680064 | tf_op jit(solution)/shard_map/dot_general | solution.py:37
  340.0 8.3 %add_convert_fusion = bf16[1024,2048]{1,0:T(8,128)(2,1)} fusion(f32[1024,2048]{1,0:T(8,128)} %fusion.10, bf16[1024,1024]{1,0:T(8,128)(2,1)S(1)} %get-tuple-element.89.refs_6_, bf16[2048,1024]{1,0:T(8,128)(2,1)S(1)} %copy-done.25), kind=kOutput, calls=%fused_computation | convolution fusion | flops 4299161600 | bytes 18874368 | tf_op jit(solution)/shard_map/dot_general | solution.py:37
  348.3 110.5 %shard_map.241 = (bf16[8,128,2048]{2,1,0:T(8,128)(2,1)}, f32[128,2048]{1,0:T(8,128)}, f32[8,2048]{1,0:T(8,128)}, bf16[4,256,512]{2,1,0:T(8,128)(2,1)}, bf16[4,25...) custom-call(bf16[8,128,2048]{2,1,0:T(8,128)(2,1)} %bitcast.67, bf16[128,2048]{1,0:T(8,128)(2,1)} %refs_1_.3, ...), custom_call_target="tpu_custom_call" | custom-call | flops 10000000 | bytes 200000000 | tf_op jit(solution)/shard_map/pallas_call | solution.py:1066
  458.8 1.6 copy-done
  460.4 0.8 copy-done.15
  461.3 33.7 %shard_map.242 = (bf16[8,128,768]{2,1,0:T(8,128)(2,1)S(1)}, f32[40,128]{1,0:T(8,128)S(1)}, bf16[8,128,2048]{2,1,0:T(8,128)(2,1)}, bf16[256,2048]{1,0:T(8,128)(2,1)S(1)}) custom-call(bf16[8,128,2048]{2,1,0:T(8,128)(2,1)} %get-tuple-element.64.refs_0_, bf16[256,2048]{1,0:T(8,128)(2,1)S(1)} %copy-done.3, f32[8,128,768]{2,1,0:T(8,128)} %get-tuple-element.65.refs_2_, ...), custom_call_target="tpu_custom_call" | custom-call | flops 10000000 | bytes 80000000 | tf_op jit(solution)/shard_map/pallas_call | solution.py:1235
  495.0 1.1 copy-done.10
  496.2 129.8 %shard_map.243 = (bf16[128,2048]{1,0:T(8,128)(2,1)S(1)}, bf16[4,256,384]{2,1,0:T(8,128)(2,1)}, bf16[128,2048]{1,0:T(8,128)(2,1)S(1)}, bf16[128,16384]{1,0:T(8,12...) custom-call(bf16[8,128,2048]{2,1,0:T(8,128)(2,1)} %get-tuple-element, ...), custom_call_target="tpu_custom_call" | custom-call | flops 10000000 | bytes 200000000 | tf_op jit(solution)/shard_map/pallas_call | solution.py:1066
  626.0 6.8 %fusion.6 = (f32[128,8192]{1,0:T(8,128)}, f32[128,8192]{1,0:T(8,128)}) fusion(bf16[128,16384]{1,0:T(8,128)(2,1)} %get-tuple-element.86), kind=kLoop, calls=%fused_computation.35 | loop fusion | bytes 16777216 | tf_op jit(solution)/shard_map/split | solution.py:1566
  632.8 2.8 convert_add_fusion
  635.6 2.1 fusion.7
  637.7 0.5 fusion.2
  638.2 0.8 copy.35
  639.0 0.8 copy.36
  (71 shorter events, 1.0 us)
Async XLA Ops:
  0.6 76.9 %copy-start.23 = (bf16[128]{0:T(256)(128)(2,1)S(1)}, bf16[128]{0:T(256)(128)(2,1)}, u32[]{:S(2)}) copy-start(bf16[128]{0:T(256)(128)(2,1)} %param.21) | copy-start | bytes 772
  0.7 76.9 %copy-start.22 = (bf16[128]{0:T(256)(128)(2,1)S(1)}, bf16[128]{0:T(256)(128)(2,1)}, u32[]{:S(2)}) copy-start(bf16[128]{0:T(256)(128)(2,1)} %param.20) | copy-start | bytes 772
  0.7 76.9 %copy-start.8 = (bf16[128,8192]{1,0:T(8,128)(2,1)S(1)}, bf16[128,8192]{1,0:T(8,128)(2,1)}, u32[]{:S(2)}) copy-start(bf16[128,8192]{1,0:T(8,128)(2,1)} %refs_6_.1) | copy-start | bytes 6291460
  1.5 76.0 %collective-permute-start = (bf16[1,2,128]{2,1,0:T(2,128)(2,1)S(1)}, bf16[1,2,128]{2,1,0:T(2,128)(2,1)S(1)}, u32[]{:S(2)}, u32[]{:S(2)}) collective-permute-start(bf16[1,2,128]{2,1,0:T(2,128)(2,1)S(1)} %maximum_bitcast_fusion), channel_id=1, source_target_pairs={{0,2},{1,3},{2,0},{3,1},{4,6},{5,7},{6,4},{7,5},{8,10},{9,11},{10,... | collective-permute-start | bytes 1544 | tf_op jit(solution)/shard_map/ppermute | solution.py:284
  72.4 61.0 %collective-permute-start.1 = (bf16[4,2,4,128]{3,1,0,2:T(2,128)(2,1)S(1)}, bf16[4,2,4,128]{3,1,0,2:T(2,128)(2,1)S(1)}, u32[]{:S(2)}, u32[]{:S(2)}) collective-permute-start(bf16[4,2,4,128]{3,1,0,2:T(2,128)(2,1)S(1)} %copy.28), channel_id=1, source_target_pairs={{0,2},{1,3},{2,0},{3,1},{4,6},{5,7},{6,4},{7,5},{8,10},{9,11},{10,... | collective-permute-start | bytes 24584 | tf_op jit(solution)/shard_map/ppermute | solution.py:284
  77.6 1.2 copy-start.2
  78.8 54.7 %copy-start.5 = (bf16[128,8192]{1,0:T(8,128)(2,1)S(1)}, bf16[128,8192]{1,0:T(8,128)(2,1)}, u32[]{:S(2)}) copy-start(bf16[128,8192]{1,0:T(8,128)(2,1)} %refs_3_.3) | copy-start | bytes 6291460
  78.8 54.7 %copy-start.6 = (bf16[512,2048]{1,0:T(8,128)(2,1)S(1)}, bf16[512,2048]{1,0:T(8,128)(2,1)}, u32[]{:S(2)}) copy-start(bf16[512,2048]{1,0:T(8,128)(2,1)} %refs_4_.3) | copy-start | bytes 6291460
  78.8 54.7 %copy-start.7 = (bf16[128,2048]{1,0:T(8,128)(2,1)S(1)}, bf16[128,2048]{1,0:T(8,128)(2,1)}, u32[]{:S(2)}) copy-start(bf16[128,2048]{1,0:T(8,128)(2,1)} %refs_1_.2) | copy-start | bytes 1572868
  133.5 95.1 %copy-start.14 = (f32[1,4,2,2,128]{4,3,2,1,0:T(2,128)}, f32[1,4,2,2,128]{4,3,2,1,0:T(2,128)S(1)}, u32[]{:S(2)}) copy-start(f32[1,4,2,2,128]{4,3,2,1,0:T(2,128)S(1)} %get-tuple-element.97) | copy-start | bytes 24580
  228.6 8.0 %copy-start.13 = (f32[128,2048]{1,0:T(8,128)}, f32[128,2048]{1,0:T(8,128)S(1)}, u32[]{:S(2)}) copy-start(f32[128,2048]{1,0:T(8,128)S(1)} %get-tuple-element.63.refs_2_) | copy-start | bytes 3145732
  228.6 8.0 %copy-start.17 = (bf16[8,128,2048]{2,1,0:T(8,128)(2,1)S(1)}, bf16[8,128,2048]{2,1,0:T(8,128)(2,1)}, u32[]{:S(2)}) copy-start(bf16[8,128,2048]{2,1,0:T(8,128)(2,1)} %get-tuple-element.56) | copy-start | bytes 12582916
  228.6 8.0 %copy-start.24 = (bf16[2048,1024]{1,0:T(8,128)(2,1)S(1)}, bf16[2048,1024]{1,0:T(8,128)(2,1)}, u32[]{:S(2)}) copy-start(bf16[2048,1024]{1,0:T(8,128)(2,1)} %get-tuple-element.58) | copy-start | bytes 12582916
  236.6 6.5 %copy-start.27 = (f32[1024,1024]{1,0:T(8,128)}, f32[1024,1024]{1,0:T(8,128)S(1)}, u32[]{:S(2)}) copy-start(f32[1024,1024]{1,0:T(8,128)S(1)} %fusion.9) | copy-start | bytes 12582916
  236.6 6.5 %copy-start.26 = (bf16[1024,2048]{1,0:T(8,128)(2,1)S(1)}, bf16[1024,2048]{1,0:T(8,128)(2,1)}, u32[]{:S(2)}) copy-start(bf16[1024,2048]{1,0:T(8,128)(2,1)} %get-tuple-element.59) | copy-start | bytes 12582916
  243.1 6.1 copy-start.18
  243.1 6.1 copy-start.9
  318.6 10.8 %copy-start.4 = (bf16[8,128,2048]{2,1,0:T(8,128)(2,1)}, bf16[8,128,2048]{2,1,0:T(8,128)(2,1)S(1)}, u32[]{:S(2)}) copy-start(bf16[8,128,2048]{2,1,0:T(8,128)(2,1)S(1)} %get-tuple-element.62) | copy-start | bytes 12582916
  329.4 10.6 %copy-start.20 = (bf16[1024,1024]{1,0:T(8,128)(2,1)}, bf16[1024,1024]{1,0:T(8,128)(2,1)S(1)}, u32[]{:S(2)}) copy-start(bf16[1024,1024]{1,0:T(8,128)(2,1)S(1)} %get-tuple-element.90.refs_5_) | copy-start | bytes 6291460
  329.4 10.5 %copy-start.19 = (bf16[1024,1024]{1,0:T(8,128)(2,1)}, bf16[1024,1024]{1,0:T(8,128)(2,1)S(1)}, u32[]{:S(2)}) copy-start(bf16[1024,1024]{1,0:T(8,128)(2,1)S(1)} %get-tuple-element.89.refs_6_) | copy-start | bytes 6291460
  329.4 10.5 %copy-start.25 = (bf16[2048,1024]{1,0:T(8,128)(2,1)S(1)}, bf16[2048,1024]{1,0:T(8,128)(2,1)}, u32[]{:S(2)}) copy-start(bf16[2048,1024]{1,0:T(8,128)(2,1)} %get-tuple-element.58) | copy-start | bytes 12582916
  348.3 110.5 %copy-start.3 = (bf16[256,2048]{1,0:T(8,128)(2,1)S(1)}, bf16[256,2048]{1,0:T(8,128)(2,1)}, u32[]{:S(2)}) copy-start(bf16[256,2048]{1,0:T(8,128)(2,1)} %get-tuple-element.54.refs_5_.refs_1_) | copy-start | bytes 3145732
  458.8 1.6 copy-start
  460.4 0.8 copy-start.15
  461.3 34.9 %copy-start.11 = (f32[128,2048]{1,0:T(8,128)S(1)}, f32[128,2048]{1,0:T(8,128)}, u32[]{:S(2)}) copy-start(f32[128,2048]{1,0:T(8,128)} %get-tuple-element.73.refs_1_) | copy-start | bytes 3145732
  461.3 34.9 %copy-start.12 = (bf16[4,256,512]{2,1,0:T(8,128)(2,1)S(1)}, bf16[4,256,512]{2,1,0:T(8,128)(2,1)}, u32[]{:S(2)}) copy-start(bf16[4,256,512]{2,1,0:T(8,128)(2,1)} %get-tuple-element.76.refs_6_) | copy-start | bytes 3145732
  495.0 1.1 copy-start.10
  626.0 6.8 %copy-start.21 = (f32[40,128]{1,0:T(8,128)}, f32[40,128]{1,0:T(8,128)S(1)}, u32[]{:S(2)}) copy-start(f32[40,128]{1,0:T(8,128)S(1)} %add_add_fusion) | copy-start | bytes 61444
  626.0 6.8 %copy-start.1 = (bf16[512,2048]{1,0:T(8,128)(2,1)S(1)}, bf16[512,2048]{1,0:T(8,128)(2,1)}, u32[]{:S(2)}) copy-start(bf16[512,2048]{1,0:T(8,128)(2,1)} %get-tuple-element.71.refs_11_.refs_8_) | copy-start | bytes 6291460
  632.8 2.8 copy-start.16
  635.6 2.1 slice-start
  635.6 2.1 slice-start.1

commit v8 on v7

--- a/solution.py
+++ b/solution.py
@@ -432,11 +432,15 @@
 
     def finish(self):
         line = self.line
+        for p in range(1, 2 * LINE):
+            ref = self.rows(line.place, line.pair, line.core, line.rep)
+            remote(ref, ref, self.z_send.at[p], self.z_recv.at[p], line.sibling).wait_send()
+        self.finish_over()
+
+    def finish_over(self):
+        line = self.line
         pair, rep = line.pair, line.rep
         for p in range(2 * LINE):
-            if p > 0:
-                ref = self.rows(line.place, pair, line.core, rep)
-                remote(ref, ref, self.z_send.at[p], self.z_recv.at[p], line.sibling).wait_send()
             self.cross(p, pair, rep, 0).wait_send()
             self.over(p, pair, rep, 0).wait_send()
             if p % 2:
@@ -449,15 +453,100 @@
                 self.over(p, 1 - pair, 1 - rep, 1).wait_recv()
 
 
+class SpreadLine:
+    semaphores = ((2 * LINE,),) * 2
+    buffers = ()
+    near = False
+
+    def __init__(self, weight, at):
+        self.inputs, self.at, self.slots = [weight], at, at + 1
+        shape = (2 * LINE, weight.shape[0] // 2, weight.shape[1] // 8)
+        self.outputs = [jax.ShapeDtypeStruct(shape, weight.dtype)]
+
+    def bind(self, line, sources, targets, scratch):
+        self.line, self.source, self.target = line, sources[0], targets[0]
+        self.sends, self.recvs = scratch
+
+    def slot(self, t):
+        if t != self.at:
+            return
+        line, half, n = self.line, self.target.shape[1], self.target.shape[2] // 2
+        mine = pl.ds(pl.multiple_of(line.rep * half, half), half)
+        for p in range(2 * LINE):
+            place, core = line.piece(p, 1)
+            for q in range(2):
+                column = pl.multiple_of((place * 4 + q * 2 + core) * n, n)
+                piece, goal = self.source.at[mine, pl.ds(column, n)], self.target.at[p, :, pl.ds(q * n, n)]
+                if p == 0:
+                    pltpu.make_async_copy(piece, goal, self.recvs.at[0]).start()
+                else:
+                    device = line.at(place, line.pair, core)
+                    remote(piece, goal, self.sends.at[p], self.recvs.at[p], device).start()
+
+    def finish(self):
+        for p in range(2 * LINE):
+            ref = self.target.at[p]
+            if p == 0:
+                pltpu.make_async_copy(ref, ref, self.recvs.at[0]).wait()
+            else:
+                remote(ref, ref, self.sends.at[p], self.recvs.at[p], self.line.sibling).wait()
+
+
+class SpreadOver(Spread):
+    semaphores = ((2 * LINE,),) + ((2 * LINE, 2),) * 4
+
+    def __init__(self, pieces):
+        self.inputs, self.half = [pieces], pieces.shape[1]
+        shape = (2 * pieces.shape[0] * 2 * pieces.shape[1], pieces.shape[2])
+        self.outputs = [jax.ShapeDtypeStruct(shape, pieces.dtype)]
+        self.slots = 7 + LINE
+
+    def bind(self, line, sources, targets, scratch):
+        self.line, self.pieces, self.target = line, sources[0], targets[0]
+        self.local, self.y_send, self.y_recv, self.x_send, self.x_recv = scratch
+
+    def here(self, p):
+        place, core = self.line.piece(p, -1)
+        goal = self.rows(place, self.line.pair, core, self.line.rep)
+        return pltpu.make_async_copy(self.pieces.at[p], goal, self.local.at[p])
+
+    def cross(self, p, pair, rep, which):
+        place, core = self.line.piece(p, -1)
+        ref = self.rows(place, pair, core, rep)
+        source = ref if which else self.pieces.at[p]
+        return remote(source, ref, self.y_send.at[p, which], self.y_recv.at[p, which], self.line.across)
+
+    def over(self, p, pair, rep, which):
+        place, core = self.line.piece(p, -1)
+        ref = self.rows(place, pair, core, rep)
+        source = ref if which else self.pieces.at[p]
+        return remote(source, ref, self.x_send.at[p, which], self.x_recv.at[p, which], self.line.partner)
+
+    def slot(self, t):
+        line = self.line
+        for p in range(2 * LINE):
+            if t == p // 2:
+                self.cross(p, line.pair, line.rep, 0).start()
+                self.over(p, line.pair, line.rep, 0).start()
+                self.here(p).start()
+            if t == 7 + p // 2:
+                self.onward(p)
+
+    def finish(self):
+        for p in range(2 * LINE):
+            self.here(p).wait()
+        self.finish_over()
+
+
 class Stack:
     buffers = ()
     near = False
 
-    def __init__(self, weight, count):
-        self.inputs, self.count = [weight], count
+    def __init__(self, weight, count, lag):
+        self.inputs, self.count, self.lag = [weight], count, lag
         self.outputs = [jax.ShapeDtypeStruct((2 * weight.shape[0], weight.shape[1]), weight.dtype)]
         self.semaphores = ((1,),) + ((count,),) * 4
-        self.slots = 1 + count
+        self.slots = lag + count
 
     def bind(self, line, sources, targets, sems):
         self.line, self.source, self.target = line, sources[0], targets[0]
@@ -488,9 +577,9 @@
             for k in range(self.count):
                 self.there(k).start()
             self.here().start()
-        if 1 <= t < 1 + self.count:
-            self.there(t - 1).wait_recv()
-            self.onward(t - 1, self.line.rep).start()
+        if self.lag <= t < self.lag + self.count:
+            self.there(t - self.lag).wait_recv()
+            self.onward(t - self.lag, self.line.rep).start()
 
     def finish(self):
         self.here().wait()
@@ -1462,7 +1551,7 @@
         [
             Share(jnp.pad(extra, ((0, 11), (0, 0)))),
             Spread(w_query, w_key, w_value),
-            Stack(w_output, 2),
+            Stack(w_output, 2, 1),
         ],
         0,
     )
@@ -1493,15 +1582,15 @@
     def to_blocks(values):
         return values.astype(jnp.bfloat16).reshape(blocks, -1, model_width)
 
-    attn_parts, lows, probs, mixed_low, squares, raw, full_gate = attend(
-        payload, full_qkv, turns, bias, head_gains, full_output, [Spread(w_gate, plan=Spread.BESIDE_HEADS)], 6
+    attn_parts, lows, probs, mixed_low, squares, raw, full_gate, up_pieces = attend(
+        payload, full_qkv, turns, bias, head_gains, full_output, [Spread(w_gate, plan=Spread.BESIDE_HEADS), SpreadLine(w_up, 5)], 6
     )
     mixed_low = mixed_low.reshape(blocks * length, width)
     resid_low, attn_out, resid, full_up, full_down = attention_block(
         attn_parts,
         hidden_in,
         gain_attn,
-        [Spread(w_up), Stack(w_down, 8)],
+        [SpreadOver(up_pieces), Stack(w_down, 8, 3)],
         1,
     )
     resid_low = resid_low.reshape(blocks * length, model_width)

time: 652 us -> 642 us (0.985)
  Pallas kernels: 558 us -> 545 us
    pallas_call x5, Pallas kernels: 470 us -> 456 us  [line_call(): pl.pallas_call(kernel, out_shape=[jax.ShapeDtypeStruct(shape, kind) for s...]
where the time goes in v8:
time: 642 us; the launch traced here: 629 us
  Pallas kernels  545 us (85%)
  matrix products  52.5 us (8%)
  local copies, waits for them, and re-layouts  15.8 us (2%)
  other arithmetic  9.87 us (2%)
    pallas_call x5, Pallas kernels, line_call(): pl.pallas_call(kernel, out_shape=[jax.ShapeDtypeStruct(shape, kind) for s...  456 us
    pallas_call x2, Pallas kernels, heads_call(): pl.pallas_call(kernel, out_shape=[jax.ShapeDtypeStruct(shape, kind) for s...  88.8 us
    dot_general x3, matrix products, dot_back(): lax.dot_general(left_side, right_side, (((1,), (1,)), ((), ())), preferre...  29.7 us
  transfers between devices with their start and end apart: 2, of which 0 were waited for; matrix products, arithmetic and copies ran while one was open for 1% of the time, Pallas kernels for 19%

profile of v8, /device:TPU:0, one launch (start us, length us, event | category | flops | bytes accessed | tf_op | source)
XLA Modules:
  0.0 629.2 jit_solution(13155586346130064186)
XLA Ops:
  0.7 0.8 maximum_bitcast_fusion
  1.5 3.0 collective-permute-start
  4.5 0.7 convert_element_type.72
  5.1 0.7 stack.34
  5.9 0.6 pad.4.refs_1_
  6.5 65.3 %shard_map.237 = (bf16[8,128,2048]{2,1,0:T(8,128)(2,1)}, bf16[8,16,128]{2,1,0:T(8,128)(2,1)}, bf16[2048,768]{1,0:T(8,128)(2,1)}, bf16[256,2048]{1,0:T(8,128)(2,1)}) custom-call(bf16[128,2048]{1,0:T(8,128)(2,1)} %refs_1_.2, bf16[16,128]{1,0:T(8,128)(2,1)} %pad.4.refs_1_, bf16[128,2048]{1,0:T(8,128)(2,1)} %refs_2_.2, bf16[128,2048]{1,0:T(8,128)(2,1)} %refs_3_.1, ...), custom_call_target="tpu_custom_call" | custom-call | flops 10000000 | bytes 200000000 | tf_op jit(solution)/shard_map/pallas_call | solution.py:1155
  71.7 0.7 slice.37
  72.5 1.6 collective-permute-start.1
  74.1 0.7 slice_convert_fusion
  75.6 1.9 maximum_cosine_fusion.refs_2_.refs_3_
  77.6 1.2 copy-done.2
  78.8 56.1 %shard_map.238 = (bf16[8,128,2048]{2,1,0:T(8,128)(2,1)}, bf16[8,128,768]{2,1,0:T(8,128)(2,1)S(1)}, f32[8,2,128,128]{3,2,1,0:T(8,128)S(1)}, bf16[8,128,256]{2,1,0...) custom-call(bf16[8,128,2048]{2,1,0:T(8,128)(2,1)} %get-tuple-element, ...), custom_call_target="tpu_custom_call" | custom-call | flops 10000000 | bytes 80000000 | tf_op jit(solution)/shard_map/pallas_call | solution.py:1324
  135.0 81.2 %shard_map.239 = (bf16[8,128,2048]{2,1,0:T(8,128)(2,1)}, f32[128,2048]{1,0:T(8,128)S(1)}, f32[128,2048]{1,0:T(8,128)S(1)}, bf16[2048,1024]{1,0:T(8,128)(2,1)}, bf16[1024,2048]{1,0:T(8,128)(2,1)}) custom-call(bf16[8,128,2048]{2,1,0:T(8,128)(2,1)} %get-tuple-element.56.refs_0_, bf16[128,2048]{1,0:T(8,128)(2,1)S(1)} %copy-done.6, f32[1,2048]{1,0:T(1,128)S(1)} %bitcast.58, ...), custom_call_target="tpu_custom_call" | custom-call | flops 10000000 | bytes 200000000 | tf_op jit(solution)/shard_map/pallas_call | solution.py:1155
  216.3 8.6 %fusion.9 = f32[1024,1024]{1,0:T(8,128)} fusion(bf16[1024,2048]{1,0:T(8,128)(2,1)} %bitcast.64, bf16[2048,1024]{1,0:T(8,128)(2,1)S(1)} %copy-done.23), kind=kOutput, calls=%fused_computation.38 | convolution fusion | flops 4294967296 | bytes 12582912 | tf_op jit(solution)/shard_map/dot_general | solution.py:1598
  225.0 8.2 %multiply_convert_fusion.2 = (bf16[1024,1024]{1,0:T(8,128)(2,1)S(1)}, f32[1024,1024]{1,0:T(8,128)}) fusion(f32[1024,1024]{1,0:T(8,128)} %fusion.9, bf16[1024,2048]{1,0:T(8,128)(2,1)S(1)} %bitcast.66, bf16[2048,1024]{1,0:T(8,128)(2,1)S(1)} %copy-done.24), kind=kOutput, calls=%fused_computation.4 | convolution fusion | flops 4301258752 | bytes 18874368 | tf_op jit(solution)/shard_map/dot_general | solution.py:1599
  233.2 6.0 convolution_convert_fusion
  239.2 69.4 %shard_map.240 = (bf16[8,128,2048]{2,1,0:T(8,128)(2,1)S(1)}, bf16[128,2048]{1,0:T(8,128)(2,1)S(1)}, f32[8,2048]{1,0:T(8,128)S(1)}) custom-call(bf16[8,128,2048]{2,1,0:T(8,128)(2,1)} %bitcast.63, f32[128,2048]{1,0:T(8,128)S(1)} %get-tuple-element.62.refs_1_, bf16[128,2048]{1,0:T(8,128)(2,1)S(1)} %copy-done.8, f32[1,2048]{1,0:T(1,128)S(1)} %bitcast.60), custom_call_target="tpu_custom_call" | custom-call | flops 10000000 | bytes 200000000 | tf_op jit(solution)/shard_map/pallas_call | solution.py:1155
  308.6 10.8 %multiply_convert_fusion = (bf16[1024,1024]{1,0:T(8,128)(2,1)S(1)}, bf16[1024,1024]{1,0:T(8,128)(2,1)S(1)}) fusion(f32[1024,1024]{1,0:T(8,128)} %fusion.9, f32[1024,1024]{1,0:T(8,128)} %get-tuple-element.111, bf16[1024,2048]{1,0:T(8,128)(2,1)S(1)} %bitcast.54, bf16[1024,2048]{1,0:T(8,128)(2,1)} %get-tuple-element.61), kind=kOutput, calls=%fused_computation.2 | convolution fusion | flops 4308598784 | bytes 20971520 | tf_op jit(solution)/shard_map/dot_general | solution.py:37
  319.4 10.5 %fusion.10 = f32[1024,2048]{1,0:T(8,128)} fusion(bf16[1024,1024]{1,0:T(8,128)(2,1)S(1)} %get-tuple-element.92.refs_5_, bf16[2048,1024]{1,0:T(8,128)(2,1)} %get-tuple-element.59), kind=kOutput, calls=%fused_computation.39 | convolution fusion | flops 4294967296 | bytes 14680064 | tf_op jit(solution)/shard_map/dot_general | solution.py:37
  330.0 8.3 %add_convert_fusion = bf16[1024,2048]{1,0:T(8,128)(2,1)} fusion(f32[1024,2048]{1,0:T(8,128)} %fusion.10, bf16[1024,1024]{1,0:T(8,128)(2,1)S(1)} %get-tuple-element.91.refs_6_, bf16[2048,1024]{1,0:T(8,128)(2,1)S(1)} %copy-done.25), kind=kOutput, calls=%fused_computation | convolution fusion | flops 4299161600 | bytes 18874368 | tf_op jit(solution)/shard_map/dot_general | solution.py:37
  338.3 109.5 %shard_map.241 = (bf16[8,128,2048]{2,1,0:T(8,128)(2,1)}, f32[128,2048]{1,0:T(8,128)}, f32[8,2048]{1,0:T(8,128)}, bf16[4,256,512]{2,1,0:T(8,128)(2,1)}, bf16[4,25...) custom-call(bf16[8,128,2048]{2,1,0:T(8,128)(2,1)} %bitcast.67, bf16[128,2048]{1,0:T(8,128)(2,1)} %refs_1_.3, ...), custom_call_target="tpu_custom_call" | custom-call | flops 10000000 | bytes 200000000 | tf_op jit(solution)/shard_map/pallas_call | solution.py:1155
  447.8 1.6 copy-done
  449.4 0.8 copy-done.14
  450.2 32.7 %shard_map.242 = (bf16[8,128,768]{2,1,0:T(8,128)(2,1)S(1)}, f32[40,128]{1,0:T(8,128)S(1)}, bf16[8,128,2048]{2,1,0:T(8,128)(2,1)}, bf16[256,2048]{1,0:T(8,128)(2,1)S(1)}) custom-call(bf16[8,128,2048]{2,1,0:T(8,128)(2,1)} %get-tuple-element.66.refs_0_, bf16[256,2048]{1,0:T(8,128)(2,1)S(1)} %copy-done.3, f32[8,128,768]{2,1,0:T(8,128)} %get-tuple-element.67.refs_2_, ...), custom_call_target="tpu_custom_call" | custom-call | flops 10000000 | bytes 80000000 | tf_op jit(solution)/shard_map/pallas_call | solution.py:1324
  483.0 1.1 copy-done.9
  484.1 130.8 %shard_map.243 = (bf16[128,2048]{1,0:T(8,128)(2,1)S(1)}, bf16[4,256,384]{2,1,0:T(8,128)(2,1)}, bf16[128,2048]{1,0:T(8,128)(2,1)S(1)}, bf16[128,16384]{1,0:T(8,12...) custom-call(bf16[8,128,2048]{2,1,0:T(8,128)(2,1)} %get-tuple-element, ...), custom_call_target="tpu_custom_call" | custom-call | flops 10000000 | bytes 200000000 | tf_op jit(solution)/shard_map/pallas_call | solution.py:1155
  615.0 6.8 %fusion.6 = (f32[128,8192]{1,0:T(8,128)}, f32[128,8192]{1,0:T(8,128)}) fusion(bf16[128,16384]{1,0:T(8,128)(2,1)} %get-tuple-element.88), kind=kLoop, calls=%fused_computation.35 | loop fusion | bytes 16777216 | tf_op jit(solution)/shard_map/split | solution.py:1655
  621.8 2.8 convert_add_fusion
  624.5 2.1 fusion.7
  626.7 0.5 fusion.2
  627.2 0.8 copy.35
  628.0 0.8 copy.36
  (69 shorter events, 1.0 us)
Async XLA Ops:
  0.6 76.9 %copy-start.22 = (bf16[128]{0:T(256)(128)(2,1)S(1)}, bf16[128]{0:T(256)(128)(2,1)}, u32[]{:S(2)}) copy-start(bf16[128]{0:T(256)(128)(2,1)} %param.21) | copy-start | bytes 772
  0.7 76.9 %copy-start.21 = (bf16[128]{0:T(256)(128)(2,1)S(1)}, bf16[128]{0:T(256)(128)(2,1)}, u32[]{:S(2)}) copy-start(bf16[128]{0:T(256)(128)(2,1)} %param.20) | copy-start | bytes 772
  0.7 76.9 %copy-start.7 = (bf16[128,8192]{1,0:T(8,128)(2,1)S(1)}, bf16[128,8192]{1,0:T(8,128)(2,1)}, u32[]{:S(2)}) copy-start(bf16[128,8192]{1,0:T(8,128)(2,1)} %refs_6_.1) | copy-start | bytes 6291460
  1.5 76.0 %collective-permute-start = (bf16[1,2,128]{2,1,0:T(2,128)(2,1)S(1)}, bf16[1,2,128]{2,1,0:T(2,128)(2,1)S(1)}, u32[]{:S(2)}, u32[]{:S(2)}) collective-permute-start(bf16[1,2,128]{2,1,0:T(2,128)(2,1)S(1)} %maximum_bitcast_fusion), channel_id=1, source_target_pairs={{0,2},{1,3},{2,0},{3,1},{4,6},{5,7},{6,4},{7,5},{8,10},{9,11},{10,... | collective-permute-start | bytes 1544 | tf_op jit(solution)/shard_map/ppermute | solution.py:284
  72.5 62.5 %collective-permute-start.1 = (bf16[4,2,4,128]{3,1,0,2:T(2,128)(2,1)S(1)}, bf16[4,2,4,128]{3,1,0,2:T(2,128)(2,1)S(1)}, u32[]{:S(2)}, u32[]{:S(2)}) collective-permute-start(bf16[4,2,4,128]{3,1,0,2:T(2,128)(2,1)S(1)} %copy.28), channel_id=1, source_target_pairs={{0,2},{1,3},{2,0},{3,1},{4,6},{5,7},{6,4},{7,5},{8,10},{9,11},{10,... | collective-permute-start | bytes 24584 | tf_op jit(solution)/shard_map/ppermute | solution.py:284
  77.6 1.2 copy-start.2
  78.8 56.2 %copy-start.5 = (bf16[512,2048]{1,0:T(8,128)(2,1)S(1)}, bf16[512,2048]{1,0:T(8,128)(2,1)}, u32[]{:S(2)}) copy-start(bf16[512,2048]{1,0:T(8,128)(2,1)} %refs_4_.3) | copy-start | bytes 6291460
  78.8 56.2 %copy-start.6 = (bf16[128,2048]{1,0:T(8,128)(2,1)S(1)}, bf16[128,2048]{1,0:T(8,128)(2,1)}, u32[]{:S(2)}) copy-start(bf16[128,2048]{1,0:T(8,128)(2,1)} %refs_1_.2) | copy-start | bytes 1572868
  134.9 81.4 %copy-start.23 = (bf16[2048,1024]{1,0:T(8,128)(2,1)S(1)}, bf16[2048,1024]{1,0:T(8,128)(2,1)}, u32[]{:S(2)}) copy-start(bf16[2048,1024]{1,0:T(8,128)(2,1)} %get-tuple-element.59) | copy-start | bytes 12582916
  135.0 89.9 %copy-start.13 = (f32[1,4,2,2,128]{4,3,2,1,0:T(2,128)}, f32[1,4,2,2,128]{4,3,2,1,0:T(2,128)S(1)}, u32[]{:S(2)}) copy-start(f32[1,4,2,2,128]{4,3,2,1,0:T(2,128)S(1)} %get-tuple-element.99) | copy-start | bytes 24580
  216.3 8.7 %copy-start.12 = (f32[128,2048]{1,0:T(8,128)}, f32[128,2048]{1,0:T(8,128)S(1)}, u32[]{:S(2)}) copy-start(f32[128,2048]{1,0:T(8,128)S(1)} %get-tuple-element.65.refs_2_) | copy-start | bytes 3145732
  216.3 8.6 %copy-start.16 = (bf16[8,128,2048]{2,1,0:T(8,128)(2,1)S(1)}, bf16[8,128,2048]{2,1,0:T(8,128)(2,1)}, u32[]{:S(2)}) copy-start(bf16[8,128,2048]{2,1,0:T(8,128)(2,1)} %get-tuple-element.58) | copy-start | bytes 12582916
  216.3 8.6 %copy-start.24 = (bf16[2048,1024]{1,0:T(8,128)(2,1)S(1)}, bf16[2048,1024]{1,0:T(8,128)(2,1)}, u32[]{:S(2)}) copy-start(bf16[2048,1024]{1,0:T(8,128)(2,1)} %get-tuple-element.60) | copy-start | bytes 12582916
  225.0 8.2 %copy-start.26 = (bf16[1024,2048]{1,0:T(8,128)(2,1)S(1)}, bf16[1024,2048]{1,0:T(8,128)(2,1)}, u32[]{:S(2)}) copy-start(bf16[1024,2048]{1,0:T(8,128)(2,1)} %get-tuple-element.61) | copy-start | bytes 12582916
  233.1 6.1 copy-start.17
  233.1 6.0 copy-start.8
  308.6 10.8 %copy-start.4 = (bf16[8,128,2048]{2,1,0:T(8,128)(2,1)}, bf16[8,128,2048]{2,1,0:T(8,128)(2,1)S(1)}, u32[]{:S(2)}) copy-start(bf16[8,128,2048]{2,1,0:T(8,128)(2,1)S(1)} %get-tuple-element.64) | copy-start | bytes 12582916
  319.4 10.5 %copy-start.19 = (bf16[1024,1024]{1,0:T(8,128)(2,1)}, bf16[1024,1024]{1,0:T(8,128)(2,1)S(1)}, u32[]{:S(2)}) copy-start(bf16[1024,1024]{1,0:T(8,128)(2,1)S(1)} %get-tuple-element.92.refs_5_) | copy-start | bytes 6291460
  319.4 10.5 %copy-start.18 = (bf16[1024,1024]{1,0:T(8,128)(2,1)}, bf16[1024,1024]{1,0:T(8,128)(2,1)S(1)}, u32[]{:S(2)}) copy-start(bf16[1024,1024]{1,0:T(8,128)(2,1)S(1)} %get-tuple-element.91.refs_6_) | copy-start | bytes 6291460
  319.4 10.5 %copy-start.25 = (bf16[2048,1024]{1,0:T(8,128)(2,1)S(1)}, bf16[2048,1024]{1,0:T(8,128)(2,1)}, u32[]{:S(2)}) copy-start(bf16[2048,1024]{1,0:T(8,128)(2,1)} %get-tuple-element.60) | copy-start | bytes 12582916
  338.3 109.5 %copy-start.3 = (bf16[256,2048]{1,0:T(8,128)(2,1)S(1)}, bf16[256,2048]{1,0:T(8,128)(2,1)}, u32[]{:S(2)}) copy-start(bf16[256,2048]{1,0:T(8,128)(2,1)} %get-tuple-element.55.refs_5_.refs_1_) | copy-start | bytes 3145732
  447.8 1.6 copy-start
  449.4 0.8 copy-start.14
  450.2 33.9 %copy-start.10 = (f32[128,2048]{1,0:T(8,128)S(1)}, f32[128,2048]{1,0:T(8,128)}, u32[]{:S(2)}) copy-start(f32[128,2048]{1,0:T(8,128)} %get-tuple-element.75.refs_1_) | copy-start | bytes 3145732
  450.2 33.9 %copy-start.11 = (bf16[4,256,512]{2,1,0:T(8,128)(2,1)S(1)}, bf16[4,256,512]{2,1,0:T(8,128)(2,1)}, u32[]{:S(2)}) copy-start(bf16[4,256,512]{2,1,0:T(8,128)(2,1)} %get-tuple-element.78.refs_6_) | copy-start | bytes 3145732
  483.0 1.1 copy-start.9
  615.0 6.8 %copy-start.20 = (f32[40,128]{1,0:T(8,128)}, f32[40,128]{1,0:T(8,128)S(1)}, u32[]{:S(2)}) copy-start(f32[40,128]{1,0:T(8,128)S(1)} %add_add_fusion) | copy-start | bytes 61444
  615.0 6.8 %copy-start.1 = (bf16[512,2048]{1,0:T(8,128)(2,1)S(1)}, bf16[512,2048]{1,0:T(8,128)(2,1)}, u32[]{:S(2)}) copy-start(bf16[512,2048]{1,0:T(8,128)(2,1)} %get-tuple-element.73.refs_11_.refs_8_) | copy-start | bytes 6291460
  621.8 2.8 copy-start.15
  624.5 2.1 slice-start
  624.5 2.1 slice-start.1

commit v9 on v8

--- a/solution.py
+++ b/solution.py
@@ -1628,7 +1628,7 @@
 
     d_qkv, gain_sums, back_parts, there_first = attend_back(
         d_attn_low, full_output, raw, turns, head_gains, lows, probs, squares,
-        [attn_gain_term, ffn_gain_term], full_qkv, [Swap(down_part, 0, ff_rows // 2)], 7,
+        [attn_gain_term, ffn_gain_term], full_qkv, [Swap(down_part, 0, ff_rows // 4)], 7,
     )
     d_attn_low = d_attn_low.reshape(blocks * length, model_width)
     qkv_sum = Reduce(tokens, [d_qkv.reshape(-1, 3 * width)], "across")
@@ -1640,7 +1640,7 @@
             qkv_sum,
             output_sum,
             Deal([gate_sum, up_sum], 1),
-            Swap(down_part, ff_rows // 2, ff_rows // 2, 2),
+            Swap(down_part, ff_rows // 4, 3 * ff_rows // 4, 2),
             Deal(qkv_sum, 3, 9),
             Swap(output_sum, 0, length, 8),
             Four(gain_sums),

time: 642 us -> 639 us (level)
  Pallas kernels: 545 us -> 553 us
  matrix products: 52.5 us -> 45.5 us
    pallas_call x5, Pallas kernels: 456 us -> 468 us  [line_call(): pl.pallas_call(kernel, out_shape=[jax.ShapeDtypeStruct(shape, kind) for s...]
where the time goes in v9:
time: 639 us; the launch traced here: 630 us
  Pallas kernels  553 us (87%)
  matrix products  45.5 us (7%)
  local copies, waits for them, and re-layouts  15.9 us (2%)
  other arithmetic  9.89 us (2%)
    pallas_call x5, Pallas kernels, line_call(): pl.pallas_call(kernel, out_shape=[jax.ShapeDtypeStruct(shape, kind) for s...  468 us
    pallas_call x2, Pallas kernels, heads_call(): pl.pallas_call(kernel, out_shape=[jax.ShapeDtypeStruct(shape, kind) for s...  84.1 us
    dot_general x3, matrix products, dot_back(): lax.dot_general(left_side, right_side, (((1,), (1,)), ((), ())), preferre...  26.2 us
  transfers between devices with their start and end apart: 2, of which 0 were waited for; matrix products, arithmetic and copies ran while one was open for 1% of the time, Pallas kernels for 19%

profile of v9, /device:TPU:0, one launch (start us, length us, event | category | flops | bytes accessed | tf_op | source)
XLA Modules:
  0.0 629.8 jit_solution(6703748617349314126)
XLA Ops:
  0.7 0.8 maximum_bitcast_fusion
  1.5 3.0 collective-permute-start
  4.5 0.7 convert_element_type.72
  5.1 0.7 stack.34
  5.9 0.6 pad.4.refs_1_
  6.5 65.2 %shard_map.237 = (bf16[8,128,2048]{2,1,0:T(8,128)(2,1)}, bf16[8,16,128]{2,1,0:T(8,128)(2,1)}, bf16[2048,768]{1,0:T(8,128)(2,1)}, bf16[256,2048]{1,0:T(8,128)(2,1)}) custom-call(bf16[128,2048]{1,0:T(8,128)(2,1)} %refs_1_.2, bf16[16,128]{1,0:T(8,128)(2,1)} %pad.4.refs_1_, bf16[128,2048]{1,0:T(8,128)(2,1)} %refs_2_.2, bf16[128,2048]{1,0:T(8,128)(2,1)} %refs_3_.1, ...), custom_call_target="tpu_custom_call" | custom-call | flops 10000000 | bytes 200000000 | tf_op jit(solution)/shard_map/pallas_call | solution.py:1155
  71.7 0.7 slice.37
  72.4 1.6 collective-permute-start.1
  74.0 0.7 slice_convert_fusion
  75.6 1.9 maximum_cosine_fusion.refs_2_.refs_3_
  77.6 1.2 copy-done.2
  78.8 56.0 %shard_map.238 = (bf16[8,128,2048]{2,1,0:T(8,128)(2,1)}, bf16[8,128,768]{2,1,0:T(8,128)(2,1)S(1)}, f32[8,2,128,128]{3,2,1,0:T(8,128)S(1)}, bf16[8,128,256]{2,1,0...) custom-call(bf16[8,128,2048]{2,1,0:T(8,128)(2,1)} %get-tuple-element, ...), custom_call_target="tpu_custom_call" | custom-call | flops 10000000 | bytes 80000000 | tf_op jit(solution)/shard_map/pallas_call | solution.py:1324
  134.9 81.2 %shard_map.239 = (bf16[8,128,2048]{2,1,0:T(8,128)(2,1)}, f32[128,2048]{1,0:T(8,128)S(1)}, f32[128,2048]{1,0:T(8,128)S(1)}, bf16[2048,1024]{1,0:T(8,128)(2,1)}, bf16[1024,2048]{1,0:T(8,128)(2,1)}) custom-call(bf16[8,128,2048]{2,1,0:T(8,128)(2,1)} %get-tuple-element.56.refs_0_, bf16[128,2048]{1,0:T(8,128)(2,1)S(1)} %copy-done.6, f32[1,2048]{1,0:T(1,128)S(1)} %bitcast.58, ...), custom_call_target="tpu_custom_call" | custom-call | flops 10000000 | bytes 200000000 | tf_op jit(solution)/shard_map/pallas_call | solution.py:1155
  216.2 6.8 %fusion.9 = f32[1024,1024]{1,0:T(8,128)S(1)} fusion(bf16[1024,2048]{1,0:T(8,128)(2,1)} %bitcast.64, bf16[2048,1024]{1,0:T(8,128)(2,1)S(1)} %copy-done.25), kind=kOutput, calls=%fused_computation.38 | convolution fusion | flops 4294967296 | bytes 12582912 | tf_op jit(solution)/shard_map/dot_general | solution.py:1598
  223.1 6.5 %multiply_convert_fusion.2 = (bf16[1024,1024]{1,0:T(8,128)(2,1)S(1)}, f32[1024,1024]{1,0:T(8,128)}) fusion(f32[1024,1024]{1,0:T(8,128)S(1)} %fusion.9, bf16[1024,2048]{1,0:T(8,128)(2,1)S(1)} %bitcast.66, bf16[2048,1024]{1,0:T(8,128)(2,1)S(1)} %copy-done.27), kind=kOutput, calls=%fused_computation.4 | convolution fusion | flops 4301258752 | bytes 18874368 | tf_op jit(solution)/shard_map/dot_general | solution.py:1599
  229.5 6.1 convolution_convert_fusion
  235.6 69.3 %shard_map.240 = (bf16[8,128,2048]{2,1,0:T(8,128)(2,1)S(1)}, bf16[128,2048]{1,0:T(8,128)(2,1)S(1)}, f32[8,2048]{1,0:T(8,128)S(1)}) custom-call(bf16[8,128,2048]{2,1,0:T(8,128)(2,1)} %bitcast.63, f32[128,2048]{1,0:T(8,128)S(1)} %get-tuple-element.62.refs_1_, bf16[128,2048]{1,0:T(8,128)(2,1)S(1)} %copy-done.8, f32[1,2048]{1,0:T(1,128)S(1)} %bitcast.60), custom_call_target="tpu_custom_call" | custom-call | flops 10000000 | bytes 200000000 | tf_op jit(solution)/shard_map/pallas_call | solution.py:1155
  305.0 10.8 %multiply_convert_fusion = (bf16[1024,1024]{1,0:T(8,128)(2,1)S(1)}, bf16[1024,1024]{1,0:T(8,128)(2,1)S(1)}) fusion(f32[1024,1024]{1,0:T(8,128)} %copy-done.30, f32[1024,1024]{1,0:T(8,128)} %get-tuple-element.111, bf16[1024,2048]{1,0:T(8,128)(2,1)S(1)} %bitcast.54, bf16[1024,2048]{1,0:T(8,128)(2,1)} %get-tuple-element.61), kind=kOutput, calls=%fused_computation.2 | convolution fusion | flops 4308598784 | bytes 20971520 | tf_op jit(solution)/shard_map/dot_general | solution.py:37
  315.9 7.0 %fusion.10 = f32[1024,2048]{1,0:T(8,128)} fusion(bf16[1024,1024]{1,0:T(8,128)(2,1)S(1)} %get-tuple-element.92.refs_5_, bf16[2048,1024]{1,0:T(8,128)(2,1)S(1)} %copy-done.26), kind=kOutput, calls=%fused_computation.39 | convolution fusion | flops 4294967296 | bytes 14680064 | tf_op jit(solution)/shard_map/dot_general | solution.py:37
  322.9 8.4 %add_convert_fusion = bf16[1024,2048]{1,0:T(8,128)(2,1)} fusion(f32[1024,2048]{1,0:T(8,128)} %fusion.10, bf16[1024,1024]{1,0:T(8,128)(2,1)S(1)} %get-tuple-element.91.refs_6_, bf16[2048,1024]{1,0:T(8,128)(2,1)S(1)} %copy-done.28), kind=kOutput, calls=%fused_computation | convolution fusion | flops 4299161600 | bytes 18874368 | tf_op jit(solution)/shard_map/dot_general | solution.py:37
  331.3 109.6 %shard_map.241 = (bf16[8,128,2048]{2,1,0:T(8,128)(2,1)}, f32[128,2048]{1,0:T(8,128)}, f32[8,2048]{1,0:T(8,128)}, bf16[4,256,512]{2,1,0:T(8,128)(2,1)}, bf16[4,25...) custom-call(bf16[8,128,2048]{2,1,0:T(8,128)(2,1)} %bitcast.67, bf16[128,2048]{1,0:T(8,128)(2,1)} %refs_1_.3, ...), custom_call_target="tpu_custom_call" | custom-call | flops 10000000 | bytes 200000000 | tf_op jit(solution)/shard_map/pallas_call | solution.py:1155
  440.9 1.6 copy-done
  442.5 0.8 copy-done.15
  443.3 28.1 %shard_map.242 = (bf16[8,128,768]{2,1,0:T(8,128)(2,1)S(1)}, f32[40,128]{1,0:T(8,128)S(1)}, bf16[8,128,2048]{2,1,0:T(8,128)(2,1)}, bf16[128,2048]{1,0:T(8,128)(2,1)S(1)}) custom-call(bf16[8,128,2048]{2,1,0:T(8,128)(2,1)} %get-tuple-element.66.refs_0_, bf16[256,2048]{1,0:T(8,128)(2,1)S(1)} %copy-done.3, f32[8,128,768]{2,1,0:T(8,128)} %get-tuple-element.67.refs_2_, ...), custom_call_target="tpu_custom_call" | custom-call | flops 10000000 | bytes 80000000 | tf_op jit(solution)/shard_map/pallas_call | solution.py:1324
  471.5 1.1 copy-done.9
  472.6 143.1 %shard_map.243 = (bf16[128,2048]{1,0:T(8,128)(2,1)S(1)}, bf16[4,256,384]{2,1,0:T(8,128)(2,1)}, bf16[128,2048]{1,0:T(8,128)(2,1)S(1)}, bf16[128,16384]{1,0:T(8,12...) custom-call(bf16[8,128,2048]{2,1,0:T(8,128)(2,1)} %get-tuple-element, ...), custom_call_target="tpu_custom_call" | custom-call | flops 10000000 | bytes 200000000 | tf_op jit(solution)/shard_map/pallas_call | solution.py:1155
  615.8 6.8 %fusion.6 = (f32[128,8192]{1,0:T(8,128)}, f32[128,8192]{1,0:T(8,128)}) fusion(bf16[128,16384]{1,0:T(8,128)(2,1)} %get-tuple-element.88), kind=kLoop, calls=%fused_computation.35 | loop fusion | bytes 16777216 | tf_op jit(solution)/shard_map/split | solution.py:1655
  622.5 2.8 convert_add_fusion
  625.4 2.1 fusion.7
  627.5 0.5 fusion.2
  628.0 0.8 copy.35
  628.8 0.8 copy.36
  (77 shorter events, 1.0 us)
Async XLA Ops:
  0.6 76.8 %copy-start.24 = (bf16[128]{0:T(256)(128)(2,1)S(1)}, bf16[128]{0:T(256)(128)(2,1)}, u32[]{:S(2)}) copy-start(bf16[128]{0:T(256)(128)(2,1)} %param.21) | copy-start | bytes 772
  0.7 76.8 %copy-start.23 = (bf16[128]{0:T(256)(128)(2,1)S(1)}, bf16[128]{0:T(256)(128)(2,1)}, u32[]{:S(2)}) copy-start(bf16[128]{0:T(256)(128)(2,1)} %param.20) | copy-start | bytes 772
  0.7 76.9 %copy-start.7 = (bf16[128,8192]{1,0:T(8,128)(2,1)S(1)}, bf16[128,8192]{1,0:T(8,128)(2,1)}, u32[]{:S(2)}) copy-start(bf16[128,8192]{1,0:T(8,128)(2,1)} %refs_6_.1) | copy-start | bytes 6291460
  1.5 76.0 %collective-permute-start = (bf16[1,2,128]{2,1,0:T(2,128)(2,1)S(1)}, bf16[1,2,128]{2,1,0:T(2,128)(2,1)S(1)}, u32[]{:S(2)}, u32[]{:S(2)}) collective-permute-start(bf16[1,2,128]{2,1,0:T(2,128)(2,1)S(1)} %maximum_bitcast_fusion), channel_id=1, source_target_pairs={{0,2},{1,3},{2,0},{3,1},{4,6},{5,7},{6,4},{7,5},{8,10},{9,11},{10,... | collective-permute-start | bytes 1544 | tf_op jit(solution)/shard_map/ppermute | solution.py:284
  72.4 62.4 %collective-permute-start.1 = (bf16[4,2,4,128]{3,1,0,2:T(2,128)(2,1)S(1)}, bf16[4,2,4,128]{3,1,0,2:T(2,128)(2,1)S(1)}, u32[]{:S(2)}, u32[]{:S(2)}) collective-permute-start(bf16[4,2,4,128]{3,1,0,2:T(2,128)(2,1)S(1)} %copy.28), channel_id=1, source_target_pairs={{0,2},{1,3},{2,0},{3,1},{4,6},{5,7},{6,4},{7,5},{8,10},{9,11},{10,... | collective-permute-start | bytes 24584 | tf_op jit(solution)/shard_map/ppermute | solution.py:284
  78.8 56.1 %copy-start.5 = (bf16[512,2048]{1,0:T(8,128)(2,1)S(1)}, bf16[512,2048]{1,0:T(8,128)(2,1)}, u32[]{:S(2)}) copy-start(bf16[512,2048]{1,0:T(8,128)(2,1)} %refs_4_.3) | copy-start | bytes 6291460
  78.8 56.1 %copy-start.6 = (bf16[128,2048]{1,0:T(8,128)(2,1)S(1)}, bf16[128,2048]{1,0:T(8,128)(2,1)}, u32[]{:S(2)}) copy-start(bf16[128,2048]{1,0:T(8,128)(2,1)} %refs_1_.2) | copy-start | bytes 1572868
  134.8 81.4 %copy-start.25 = (bf16[2048,1024]{1,0:T(8,128)(2,1)S(1)}, bf16[2048,1024]{1,0:T(8,128)(2,1)}, u32[]{:S(2)}) copy-start(bf16[2048,1024]{1,0:T(8,128)(2,1)} %get-tuple-element.59) | copy-start | bytes 12582916
  134.9 88.1 %copy-start.14 = (f32[1,4,2,2,128]{4,3,2,1,0:T(2,128)}, f32[1,4,2,2,128]{4,3,2,1,0:T(2,128)S(1)}, u32[]{:S(2)}) copy-start(f32[1,4,2,2,128]{4,3,2,1,0:T(2,128)S(1)} %get-tuple-element.99) | copy-start | bytes 24580
  216.2 6.8 %copy-start.13 = (f32[128,2048]{1,0:T(8,128)}, f32[128,2048]{1,0:T(8,128)S(1)}, u32[]{:S(2)}) copy-start(f32[128,2048]{1,0:T(8,128)S(1)} %get-tuple-element.65.refs_2_) | copy-start | bytes 3145732
  216.2 6.8 %copy-start.17 = (bf16[8,128,2048]{2,1,0:T(8,128)(2,1)S(1)}, bf16[8,128,2048]{2,1,0:T(8,128)(2,1)}, u32[]{:S(2)}) copy-start(bf16[8,128,2048]{2,1,0:T(8,128)(2,1)} %get-tuple-element.58) | copy-start | bytes 12582916
  216.2 6.8 %copy-start.27 = (bf16[2048,1024]{1,0:T(8,128)(2,1)S(1)}, bf16[2048,1024]{1,0:T(8,128)(2,1)}, u32[]{:S(2)}) copy-start(bf16[2048,1024]{1,0:T(8,128)(2,1)} %get-tuple-element.60) | copy-start | bytes 12582916
  223.0 6.5 %copy-start.30 = (f32[1024,1024]{1,0:T(8,128)}, f32[1024,1024]{1,0:T(8,128)S(1)}, u32[]{:S(2)}) copy-start(f32[1024,1024]{1,0:T(8,128)S(1)} %fusion.9) | copy-start | bytes 12582916
  223.1 6.5 %copy-start.29 = (bf16[1024,2048]{1,0:T(8,128)(2,1)S(1)}, bf16[1024,2048]{1,0:T(8,128)(2,1)}, u32[]{:S(2)}) copy-start(bf16[1024,2048]{1,0:T(8,128)(2,1)} %get-tuple-element.61) | copy-start | bytes 12582916
  229.5 6.1 copy-start.18
  229.5 6.1 copy-start.8
  305.0 10.9 %copy-start.4 = (bf16[8,128,2048]{2,1,0:T(8,128)(2,1)}, bf16[8,128,2048]{2,1,0:T(8,128)(2,1)S(1)}, u32[]{:S(2)}) copy-start(bf16[8,128,2048]{2,1,0:T(8,128)(2,1)S(1)} %get-tuple-element.64) | copy-start | bytes 12582916
  305.0 10.9 %copy-start.26 = (bf16[2048,1024]{1,0:T(8,128)(2,1)S(1)}, bf16[2048,1024]{1,0:T(8,128)(2,1)}, u32[]{:S(2)}) copy-start(bf16[2048,1024]{1,0:T(8,128)(2,1)} %get-tuple-element.59) | copy-start | bytes 12582916
  315.9 7.0 %copy-start.20 = (bf16[1024,1024]{1,0:T(8,128)(2,1)}, bf16[1024,1024]{1,0:T(8,128)(2,1)S(1)}, u32[]{:S(2)}) copy-start(bf16[1024,1024]{1,0:T(8,128)(2,1)S(1)} %get-tuple-element.92.refs_5_) | copy-start | bytes 6291460
  315.9 7.0 %copy-start.19 = (bf16[1024,1024]{1,0:T(8,128)(2,1)}, bf16[1024,1024]{1,0:T(8,128)(2,1)S(1)}, u32[]{:S(2)}) copy-start(bf16[1024,1024]{1,0:T(8,128)(2,1)S(1)} %get-tuple-element.91.refs_6_) | copy-start | bytes 6291460
  315.9 7.0 %copy-start.28 = (bf16[2048,1024]{1,0:T(8,128)(2,1)S(1)}, bf16[2048,1024]{1,0:T(8,128)(2,1)}, u32[]{:S(2)}) copy-start(bf16[2048,1024]{1,0:T(8,128)(2,1)} %get-tuple-element.60) | copy-start | bytes 12582916
  331.3 109.6 %copy-start.3 = (bf16[256,2048]{1,0:T(8,128)(2,1)S(1)}, bf16[256,2048]{1,0:T(8,128)(2,1)}, u32[]{:S(2)}) copy-start(bf16[256,2048]{1,0:T(8,128)(2,1)} %get-tuple-element.55.refs_5_.refs_1_) | copy-start | bytes 3145732
  440.9 1.6 copy-start
  443.3 29.3 %copy-start.10 = (f32[128,2048]{1,0:T(8,128)S(1)}, f32[128,2048]{1,0:T(8,128)}, u32[]{:S(2)}) copy-start(f32[128,2048]{1,0:T(8,128)} %get-tuple-element.75.refs_1_) | copy-start | bytes 3145732
  443.3 29.3 %copy-start.11 = (bf16[4,256,512]{2,1,0:T(8,128)(2,1)S(1)}, bf16[4,256,512]{2,1,0:T(8,128)(2,1)}, u32[]{:S(2)}) copy-start(bf16[4,256,512]{2,1,0:T(8,128)(2,1)} %get-tuple-element.78.refs_6_) | copy-start | bytes 3145732
  443.3 29.3 %copy-start.12 = (bf16[4,256,512]{2,1,0:T(8,128)(2,1)S(1)}, bf16[4,256,512]{2,1,0:T(8,128)(2,1)}, u32[]{:S(2)}) copy-start(bf16[4,256,512]{2,1,0:T(8,128)(2,1)} %get-tuple-element.79.refs_7_) | copy-start | bytes 3145732
  615.7 6.8 %copy-start.22 = (f32[40,128]{1,0:T(8,128)}, f32[40,128]{1,0:T(8,128)S(1)}, u32[]{:S(2)}) copy-start(f32[40,128]{1,0:T(8,128)S(1)} %add_add_fusion) | copy-start | bytes 61444
  615.7 6.8 %copy-start.1 = (bf16[512,2048]{1,0:T(8,128)(2,1)S(1)}, bf16[512,2048]{1,0:T(8,128)(2,1)}, u32[]{:S(2)}) copy-start(bf16[512,2048]{1,0:T(8,128)(2,1)} %get-tuple-element.73.refs_11_.refs_8_) | copy-start | bytes 6291460
  615.8 6.8 %copy-start.21 = (bf16[384,2048]{1,0:T(8,128)(2,1)S(1)}, bf16[384,2048]{1,0:T(8,128)(2,1)}, u32[]{:S(2)}) copy-start(bf16[384,2048]{1,0:T(8,128)(2,1)} %get-tuple-element.90) | copy-start | bytes 4718596
  622.5 2.8 copy-start.16
  625.3 2.1 slice-start
  625.3 2.1 slice-start.1
  (3 other events, 3.2 us)
